TPU v7x, 32 devices: a whole 2x2x4 slice. The times are simulated.
32 devices in a mesh: grp: 2 (over x), slab: 16 (over z, y, core).
Axes of the slice: x: 2, y: 2, z: 4, core: 2. Of those that a mesh axis runs over, the one named last changes fastest.
Arguments:
- nodes: bfloat16 [2, 4096, 128], P('grp', 'slab'), may hold values from -6 to 6
- leave_list: int32 [2, 1024], P('grp', 'slab'), may hold values from 0 to 255, as said below
- arrive_list: int32 [2, 4096], P('grp', 'slab'), may hold values from 0 to 319, as said below
- send_list: int32 [2, 2048], P('grp', 'slab'), may hold values from 0 to 255
- neighbours: int32 [2, 4096, 32], P('grp', 'slab'), may hold values from 0 to 383
- valid: int32 [2, 4096, 32], P('grp', 'slab'), may hold values 0 or 1
- w_send: bfloat16 [128, 128], replicated, may hold values from -0.5 to 0.5
- w_recv: bfloat16 [128, 128], replicated, may hold values from -0.5 to 0.5
- w_msg: bfloat16 [128, 128], replicated, may hold values from -0.5 to 0.5
- w_self: bfloat16 [128, 128], replicated, may hold values from -0.5 to 0.5
- w_agg: bfloat16 [128, 128], replicated, may hold values from -0.09375 to 0.09375
- w_out: bfloat16 [128, 128], replicated, may hold values from -0.5 to 0.5
- cotangent: bfloat16 [2, 4096, 128], P('grp', 'slab'), may hold values from -6 to 6
Outputs:
- updated: bfloat16 [2, 4096, 128], P('grp', 'slab')
- grad_nodes: bfloat16 [2, 4096, 128], P('grp', 'slab')
- weight_steps: float32 [6, 128, 128], replicated
Inputs may be any that keep to these rules, and one draw needn't show every extreme that they name: `leave_list`: each slab's 2 * 32 entries are distinct rows of that slab. `arrive_list`: each slab's 256 entries are distinct; they name every incoming row (entries 256 and above) and every own row not in that slab's leave_list, and nothing else.
All inputs are finite; a program needn't handle non-finite values. No bound on the sum of `valid` on one device may be relied on, other than what follows from the above.
Results may differ from a plain program's by a relative error of at most 0.0065.
Values may be sent and summed in bfloat16 or wider, within the bound.
No kernel may reach another device: no remote copies, remote signals or barrier semaphores. Data moves between devices by JAX's collectives and lax.ppermute only.
A program may use at most 64 MiB of HBM per device.

v0:
```python
import math

import jax
import jax.numpy as jnp
from jax import lax
from jax.sharding import PartitionSpec as P


def with_halo(array, sides, width):
    for axis, dim in sides:
        size, length = (lax.axis_size(axis), array.shape[dim])
        up = [(i, (i + 1) % size) for i in range(size)]
        down = [(j, i) for i, j in up]
        last = lax.slice_in_dim(array, length - width, length, axis=dim)
        first = lax.slice_in_dim(array, 0, width, axis=dim)
        before = lax.ppermute(last, axis, up)
        after = lax.ppermute(first, axis, down)
        array = jnp.concatenate([before, array, after], axis=dim)
    return array


def dsilu(value):
    sig = jax.nn.sigmoid(value)
    return sig * (1.0 + value * (1.0 - sig))


def inner(left, right):
    return lax.dot_general(
        left, right, (((0,), (0,)), ((), ())), preferred_element_type=jnp.float32
    )


def by_transpose(left, right):
    return lax.dot_general(
        left, right, (((1,), (1,)), ((), ())), preferred_element_type=jnp.float32
    )


def normalize(total):
    return total / jnp.sqrt(jnp.mean(total * total, axis=(1, 2), keepdims=True) + 1e-06)


def shards(
    nodes,
    leave_list,
    arrive_list,
    send_list,
    neighbours,
    valid,
    w_send,
    w_recv,
    w_msg,
    w_self,
    w_agg,
    w_out,
    cotangent,
):
    plain = nodes[0]
    leave = leave_list[0]
    migr = leave.shape[0] // 2
    moving = jnp.take(plain, leave, axis=0)
    arrived = with_halo(moving, (("slab", 0),), migr)
    pool = jnp.concatenate([plain, arrived[:migr], arrived[3 * migr :]], axis=0)
    moved = jnp.take(pool, arrive_list[0], axis=0)
    sends = send_list[0]
    border = sends.shape[0] // 2
    outgoing = jnp.take(moved, sends, axis=0)
    beside_all = with_halo(outgoing, (("slab", 0),), border)
    table = jnp.concatenate([moved, beside_all[:border], beside_all[3 * border :]], axis=0)
    table_rows = table.shape[0]
    rows, width = moved.shape
    nbr = neighbours[0]
    slots = nbr.shape[1]
    maskf = valid[0].astype(jnp.float32)
    cot = cotangent[0]
    block = math.gcd(rows, 64)
    blocks = rows // block
    centre = jnp.dot(moved, w_send, preferred_element_type=jnp.float32)
    neigh = jnp.dot(table, w_recv, preferred_element_type=jnp.float32).astype(jnp.bfloat16)
    centre_blocks = centre.reshape(blocks, block, width)
    nbr_blocks = nbr.reshape(blocks, block, slots)
    mask_blocks = maskf.reshape(blocks, block, slots)

    def edge_front(centre_blk, nbr_blk):
        gathered = jnp.take(neigh, nbr_blk.reshape(-1), axis=0).reshape(block, slots, width)
        pre = centre_blk[:, None, :] + gathered.astype(jnp.float32)
        hid = jax.nn.silu(pre).astype(jnp.bfloat16).reshape(-1, width)
        pre2 = jnp.dot(hid, w_msg, preferred_element_type=jnp.float32).reshape(block, slots, width)
        return (pre, hid, pre2)

    def aggregate(item):
        pre, hid, pre2 = edge_front(item[0], item[1])
        return jnp.sum(item[2][:, :, None] * jax.nn.silu(pre2), axis=1)

    agg = lax.map(aggregate, (centre_blocks, nbr_blocks, mask_blocks)).reshape(rows, width)
    agg_b = agg.astype(jnp.bfloat16)
    node_pre = jnp.dot(moved, w_self, preferred_element_type=jnp.float32) + jnp.dot(
        agg_b, w_agg, preferred_element_type=jnp.float32
    )
    node_hid = jax.nn.silu(node_pre).astype(jnp.bfloat16)
    updated = (
        moved.astype(jnp.float32) + jnp.dot(node_hid, w_out, preferred_element_type=jnp.float32)
    ).astype(jnp.bfloat16)
    g_out = inner(node_hid, cot)
    d_node_pre = (by_transpose(cot, w_out) * dsilu(node_pre)).astype(jnp.bfloat16)
    g_self = inner(moved, d_node_pre)
    g_agg = inner(agg_b, d_node_pre)
    d_agg_blocks = by_transpose(d_node_pre, w_agg).reshape(blocks, block, width)

    def edge_back(carry, item):
        g_msg_part, d_neigh_part = carry
        centre_blk, nbr_blk, mask_blk, d_agg_blk = item
        pre, hid, pre2 = edge_front(centre_blk, nbr_blk)
        d_pre2 = (
            (mask_blk[:, :, None] * d_agg_blk[:, None, :] * dsilu(pre2))
            .astype(jnp.bfloat16)
            .reshape(-1, width)
        )
        g_msg_part = g_msg_part + inner(hid, d_pre2)
        d_pre = by_transpose(d_pre2, w_msg).reshape(block, slots, width) * dsilu(pre)
        d_neigh_part = d_neigh_part + jax.ops.segment_sum(
            d_pre.reshape(-1, width), nbr_blk.reshape(-1), num_segments=table_rows
        )
        return ((g_msg_part, d_neigh_part), jnp.sum(d_pre, axis=1))

    start = (jnp.zeros((width, width), jnp.float32), jnp.zeros((table_rows, width), jnp.float32))
    (g_msg, d_neigh_sum), d_centre_blocks = lax.scan(
        edge_back, start, (centre_blocks, nbr_blocks, mask_blocks, d_agg_blocks)
    )
    d_centre = d_centre_blocks.reshape(rows, width).astype(jnp.bfloat16)
    d_neigh = d_neigh_sum.astype(jnp.bfloat16)
    g_recv = inner(table, d_neigh)
    g_send = inner(moved, d_centre)
    d_own = by_transpose(d_neigh[:rows], w_recv)
    d_local = (
        cot.astype(jnp.float32)
        + by_transpose(d_node_pre, w_self)
        + by_transpose(d_centre, w_send)
        + d_own
    )
    d_borrowed = by_transpose(d_neigh[rows:], w_recv)
    returned = with_halo(d_borrowed.astype(jnp.bfloat16), (("slab", 0),), border).astype(
        d_borrowed.dtype
    )
    from_lower = returned[:border]
    from_upper = returned[3 * border :]
    d_local = d_local.at[sends[:border]].add(from_lower)
    d_local = d_local.at[sends[border:]].add(from_upper)
    grad_nodes = d_local.astype(jnp.bfloat16)
    grads = jnp.stack([g_send, g_recv, g_msg, g_self, g_agg, g_out])
    total = lax.psum(grads, ("grp", "slab"))
    weight_steps = normalize(total)
    return (updated[None], grad_nodes[None], weight_steps)


def solution(mesh):
    in_specs = (
        P("grp", "slab", None),
        P("grp", "slab"),
        P("grp", "slab"),
        P("grp", "slab"),
        P("grp", "slab", None),
        P("grp", "slab", None),
        P(),
        P(),
        P(),
        P(),
        P(),
        P(),
        P("grp", "slab", None),
    )
    out_specs = (P("grp", "slab", None), P("grp", "slab", None), P())
    return jax.shard_map(shards, mesh=mesh, in_specs=in_specs, out_specs=out_specs, check_vma=False)
```

profile of v0, /device:TPU:0, one launch (start us, length us, event | category | flops | bytes accessed | tf_op | source)
XLA Modules:
  0.0 309.3 jit_solution(18279371742683006188)
XLA Ops:
  8.6 1.5 gather_fusion.2
  10.6 5.1 %collective-permute-start.1 = (bf16[32,128]{1,0:T(8,128)(2,1)S(1)}, bf16[32,128]{1,0:T(8,128)(2,1)S(1)}, u32[]{:S(2)}, u32[]{:S(2)}) collective-permute-start(bf16[32,128]{1,0:T(8,128)(2,1)S(1)} %get-tuple-element.175), channel_id=1, source_target_pairs={{1,0},{2,1},{3,2},{4,3},{5,4},{6,5},{7,6},{8,7},{9,8},{10,9},{11,1... | collective-permute-start | bytes 24584 | tf_op jit(solution)/shard_map/ppermute | solution.py:17
  19.9 4.4 %collective-permute-start.3 = (bf16[64,128]{1,0:T(8,128)(2,1)S(1)}, bf16[64,128]{1,0:T(8,128)(2,1)S(1)}, u32[]{:S(2)}, u32[]{:S(2)}) collective-permute-start(bf16[64,128]{1,0:T(8,128)(2,1)S(1)} %get-tuple-element.173), channel_id=1, source_target_pairs={{1,0},{2,1},{3,2},{4,3},{5,4},{6,5},{7,6},{8,7},{9,8},{10,9},{11,1... | collective-permute-start | bytes 49160 | tf_op jit(solution)/shard_map/ppermute | solution.py:17
  24.5 1.3 collective-permute-done.2
  26.4 32.7 %while.25 = (s32[]{:T(128)}, bf16[4,64,128]{2,1,0:T(8,128)(2,1)S(1)}, f32[4,64,32]{2,1,0:T(8,128)S(1)}, f32[4,64,128]{2,1,0:T(8,128)S(1)}, s32[4,64,32]{2,1,0:T(...) while((s32[]{:T(128)}, bf16[4,64,128]{2,1,0:T(8,128)(2,1)S(1)}, ...), condition=%wide.region_2.4_spmd, body=%wide.region_0.3_spmd.sunk | while | flops 70791168 | bytes 2895973 | solution.py:95
  26.5 6.2 %gather_fusion = bf16[2048,128]{1,0:T(8,128)(2,1)S(1)} fusion(bf16[384,128]{1,0:T(8,128)(2,1)S(1)} %get-tuple-element.313, s32[2048]{0:T(1024)S(1)} %fusion.82), kind=kCustom, calls=%fused_computation.clone.clone.1 | custom fusion | bytes 1056768 | tf_op jit(solution)/shard_map/while/body/eval_jaxpr/jit(_take)/gather | solution.py:85
  34.7 6.2 %gather_fusion = bf16[2048,128]{1,0:T(8,128)(2,1)S(1)} fusion(bf16[384,128]{1,0:T(8,128)(2,1)S(1)} %get-tuple-element.313, s32[2048]{0:T(1024)S(1)} %fusion.82), kind=kCustom, calls=%fused_computation.clone.clone.1 | custom fusion | bytes 1056768 | tf_op jit(solution)/shard_map/while/body/eval_jaxpr/jit(_take)/gather | solution.py:85
  42.9 6.2 %gather_fusion = bf16[2048,128]{1,0:T(8,128)(2,1)S(1)} fusion(bf16[384,128]{1,0:T(8,128)(2,1)S(1)} %get-tuple-element.313, s32[2048]{0:T(1024)S(1)} %fusion.82), kind=kCustom, calls=%fused_computation.clone.clone.1 | custom fusion | bytes 1056768 | tf_op jit(solution)/shard_map/while/body/eval_jaxpr/jit(_take)/gather | solution.py:85
  51.0 6.2 %gather_fusion = bf16[2048,128]{1,0:T(8,128)(2,1)S(1)} fusion(bf16[384,128]{1,0:T(8,128)(2,1)S(1)} %get-tuple-element.313, s32[2048]{0:T(1024)S(1)} %fusion.82), kind=kCustom, calls=%fused_computation.clone.clone.1 | custom fusion | bytes 1056768 | tf_op jit(solution)/shard_map/while/body/eval_jaxpr/jit(_take)/gather | solution.py:85
  64.0 101.9 %while.26 = (s32[]{:T(128)}, f32[128,128]{1,0:T(8,128)}, f32[384,128]{1,0:T(8,128)S(1)}, bf16[4,64,128]{2,1,0:T(8,128)(2,1)}, f32[4,64,128]{2,1,0:T(8,128)S(1)},...) while((s32[]{:T(128)}, f32[128,128]{1,0:T(8,128)}, ...), condition=%wide.region_6.8_spmd.clone, body=%wide.region_3.7_spmd.clone.sunk | while | flops 211070976 | bytes 15293151 | solution.py:127
  64.1 6.2 %gather_fusion.1 = bf16[2048,128]{1,0:T(8,128)(2,1)S(1)} fusion(bf16[384,128]{1,0:T(8,128)(2,1)S(1)} %get-tuple-element.346, s32[2048]{0:T(1024)S(1)} %fusion.87), kind=kCustom, calls=%fused_computation.1.clone.clone.1 | custom fusion | bytes 1056768 | tf_op jit(solution)/shard_map/while/body/eval_jaxpr/jit(_take)/gather | solution.py:85
  71.7 1.3 multiply_convert_fusion.17
  73.8 1.3 fusion.89
  75.1 11.6 %scatter_fusion = f32[384,128]{1,0:T(8,128)S(1)} fusion(f32[384,128]{1,0:T(8,128)S(1)} %get-tuple-element.330, s32[2048]{0:T(1024)S(1)} %reshape.334, f32[2048,128]{1,0:T(8,128)S(1)} %bitcast.171), kind=kCustom, calls=%fused_computation.5.clone.clone.1 | custom fusion | flops 262144 | bytes 3153920 | tf_op jit(solution)/shard_map/while/body/eval_jaxpr/scatter-add | solution.py:121
  87.3 1.5 fusion.88
  89.6 6.2 %gather_fusion.1 = bf16[2048,128]{1,0:T(8,128)(2,1)S(1)} fusion(bf16[384,128]{1,0:T(8,128)(2,1)S(1)} %get-tuple-element.346, s32[2048]{0:T(1024)S(1)} %fusion.87), kind=kCustom, calls=%fused_computation.1.clone.clone.1 | custom fusion | bytes 1056768 | tf_op jit(solution)/shard_map/while/body/eval_jaxpr/jit(_take)/gather | solution.py:85
  97.1 1.3 multiply_convert_fusion.17
  99.2 1.3 fusion.89
  100.6 11.6 %scatter_fusion = f32[384,128]{1,0:T(8,128)S(1)} fusion(f32[384,128]{1,0:T(8,128)S(1)} %get-tuple-element.330, s32[2048]{0:T(1024)S(1)} %reshape.334, f32[2048,128]{1,0:T(8,128)S(1)} %bitcast.171), kind=kCustom, calls=%fused_computation.5.clone.clone.1 | custom fusion | flops 262144 | bytes 3153920 | tf_op jit(solution)/shard_map/while/body/eval_jaxpr/scatter-add | solution.py:121
  112.8 1.5 fusion.88
  115.1 6.2 %gather_fusion.1 = bf16[2048,128]{1,0:T(8,128)(2,1)S(1)} fusion(bf16[384,128]{1,0:T(8,128)(2,1)S(1)} %get-tuple-element.346, s32[2048]{0:T(1024)S(1)} %fusion.87), kind=kCustom, calls=%fused_computation.1.clone.clone.1 | custom fusion | bytes 1056768 | tf_op jit(solution)/shard_map/while/body/eval_jaxpr/jit(_take)/gather | solution.py:85
  122.6 1.3 multiply_convert_fusion.17
  124.7 1.3 fusion.89
  126.1 11.6 %scatter_fusion = f32[384,128]{1,0:T(8,128)S(1)} fusion(f32[384,128]{1,0:T(8,128)S(1)} %get-tuple-element.330, s32[2048]{0:T(1024)S(1)} %reshape.334, f32[2048,128]{1,0:T(8,128)S(1)} %bitcast.171), kind=kCustom, calls=%fused_computation.5.clone.clone.1 | custom fusion | flops 262144 | bytes 3153920 | tf_op jit(solution)/shard_map/while/body/eval_jaxpr/scatter-add | solution.py:121
  138.3 1.5 fusion.88
  140.5 6.2 %gather_fusion.1 = bf16[2048,128]{1,0:T(8,128)(2,1)S(1)} fusion(bf16[384,128]{1,0:T(8,128)(2,1)S(1)} %get-tuple-element.346, s32[2048]{0:T(1024)S(1)} %fusion.87), kind=kCustom, calls=%fused_computation.1.clone.clone.1 | custom fusion | bytes 1056768 | tf_op jit(solution)/shard_map/while/body/eval_jaxpr/jit(_take)/gather | solution.py:85
  148.0 1.3 multiply_convert_fusion.17
  150.2 1.3 fusion.89
  151.5 11.6 %scatter_fusion = f32[384,128]{1,0:T(8,128)S(1)} fusion(f32[384,128]{1,0:T(8,128)S(1)} %get-tuple-element.330, s32[2048]{0:T(1024)S(1)} %reshape.334, f32[2048,128]{1,0:T(8,128)S(1)} %bitcast.171), kind=kCustom, calls=%fused_computation.5.clone.clone.1 | custom fusion | flops 262144 | bytes 3153920 | tf_op jit(solution)/shard_map/while/body/eval_jaxpr/scatter-add | solution.py:121
  163.7 1.5 fusion.88
  171.8 4.5 %collective-permute-start.5 = (bf16[64,128]{1,0:T(8,128)(2,1)S(1)}, bf16[64,128]{1,0:T(8,128)(2,1)S(1)}, u32[]{:S(2)}, u32[]{:S(2)}) collective-permute-start(bf16[64,128]{1,0:T(8,128)(2,1)S(1)} %get-tuple-element.171), channel_id=1, source_target_pairs={{1,0},{2,1},{3,2},{4,3},{5,4},{6,5},{7,6},{8,7},{9,8},{10,9},{11,1... | collective-permute-start | bytes 49160 | tf_op jit(solution)/shard_map/ppermute | solution.py:17
  180.4 120.0 %all-reduce.2.cloned.1.call-done = f32[6,128,128]{2,1,0:T(8,128)} async-done(((f32[6,128,128]{2,1,0:T(8,128)}), f32[6,128,128]{2,1,0:T(8,128)}) %all-reduce.2.cloned.1.call-update) | async-done | bytes 393232 | tf_op jit(solution)/shard_map/psum | solution.py:151
  (207 shorter events, 45.1 us)
Async XLA Ops:
  7.2 18.6 %copy-start = (bf16[128,128]{1,0:T(8,128)(2,1)S(1)}, bf16[128,128]{1,0:T(8,128)(2,1)}, u32[]{:S(2)}) copy-start(bf16[128,128]{1,0:T(8,128)(2,1)} %param.26) | copy-start | bytes 98308
  7.2 293.2 %all-reduce.2.cloned.1.call-start = ((), (), s32[]{:S(2)}) async-start(), calls=%async_computation | async-start | bytes 786432 | tf_op jit(solution)/shard_map/psum | solution.py:151
  10.1 6.3 %copy-start.19 = (s32[1,256,32]{1,2,0:T(8,128)S(1)}, s32[1,256,32]{1,2,0:T(8,128)}, u32[]{:S(2)}) copy-start(s32[1,256,32]{1,2,0:T(8,128)} %param.24) | copy-start | bytes 98308
  10.1 7.2 %collective-permute-start = (bf16[32,128]{1,0:T(8,128)(2,1)S(1)}, bf16[32,128]{1,0:T(8,128)(2,1)S(1)}, u32[]{:S(2)}, u32[]{:S(2)}) collective-permute-start(bf16[32,128]{1,0:T(8,128)(2,1)S(1)} %get-tuple-element.174), channel_id=1, source_target_pairs={{0,1},{1,2},{2,3},{3,4},{4,5},{5,6},{6,7},{7,8},{8,9},{9,10},{10,1... | collective-permute-start | bytes 24584 | tf_op jit(solution)/shard_map/ppermute | solution.py:16
  10.6 6.7 %collective-permute-start.1 = (bf16[32,128]{1,0:T(8,128)(2,1)S(1)}, bf16[32,128]{1,0:T(8,128)(2,1)S(1)}, u32[]{:S(2)}, u32[]{:S(2)}) collective-permute-start(bf16[32,128]{1,0:T(8,128)(2,1)S(1)} %get-tuple-element.175), channel_id=1, source_target_pairs={{1,0},{2,1},{3,2},{4,3},{5,4},{6,5},{7,6},{8,7},{9,8},{10,9},{11,1... | collective-permute-start | bytes 24584 | tf_op jit(solution)/shard_map/ppermute | solution.py:17
  16.4 0.8 copy-start.18
  17.2 0.8 copy-start.4
  19.8 4.5 %copy-start.12 = (bf16[128,128]{1,0:T(8,128)(2,1)S(1)}, bf16[128,128]{1,0:T(8,128)(2,1)}, u32[]{:S(2)}) copy-start(bf16[128,128]{1,0:T(8,128)(2,1)} %param.25) | copy-start | bytes 98308
  19.8 5.9 %collective-permute-start.2 = (bf16[64,128]{1,0:T(8,128)(2,1)S(1)}, bf16[64,128]{1,0:T(8,128)(2,1)S(1)}, u32[]{:S(2)}, u32[]{:S(2)}) collective-permute-start(bf16[64,128]{1,0:T(8,128)(2,1)S(1)} %get-tuple-element.172), channel_id=1, source_target_pairs={{0,1},{1,2},{2,3},{3,4},{4,5},{5,6},{6,7},{7,8},{8,9},{9,10},{10,1... | collective-permute-start | bytes 49160 | tf_op jit(solution)/shard_map/ppermute | solution.py:16
  19.9 5.9 %collective-permute-start.3 = (bf16[64,128]{1,0:T(8,128)(2,1)S(1)}, bf16[64,128]{1,0:T(8,128)(2,1)S(1)}, u32[]{:S(2)}, u32[]{:S(2)}) collective-permute-start(bf16[64,128]{1,0:T(8,128)(2,1)S(1)} %get-tuple-element.173), channel_id=1, source_target_pairs={{1,0},{2,1},{3,2},{4,3},{5,4},{6,5},{7,6},{8,7},{9,8},{10,9},{11,1... | collective-permute-start | bytes 49160 | tf_op jit(solution)/shard_map/ppermute | solution.py:17
  26.4 32.7 %copy-start.8 = (bf16[128,128]{1,0:T(8,128)(2,1)S(1)}, bf16[128,128]{1,0:T(8,128)(2,1)}, u32[]{:S(2)}) copy-start(bf16[128,128]{1,0:T(8,128)(2,1)} %param.29) | copy-start | bytes 98308
  59.1 0.8 copy-start.11
  59.9 0.8 copy-start.16
  59.9 0.8 copy-start.22
  60.7 1.8 copy-start.9
  73.0 0.8 copy-start.28
  75.1 12.2 %copy-start.13 = (f32[128,128]{1,0:T(8,128)S(1)}, f32[128,128]{1,0:T(8,128)}, u32[]{:S(2)}) copy-start(f32[128,128]{1,0:T(8,128)} %get-tuple-element.329) | copy-start | bytes 196612 | tf_op jit(solution)/shard_map/while
  98.4 0.8 copy-start.28
  100.6 12.2 %copy-start.13 = (f32[128,128]{1,0:T(8,128)S(1)}, f32[128,128]{1,0:T(8,128)}, u32[]{:S(2)}) copy-start(f32[128,128]{1,0:T(8,128)} %get-tuple-element.329) | copy-start | bytes 196612 | tf_op jit(solution)/shard_map/while
  123.9 0.8 copy-start.28
  126.1 12.2 %copy-start.13 = (f32[128,128]{1,0:T(8,128)S(1)}, f32[128,128]{1,0:T(8,128)}, u32[]{:S(2)}) copy-start(f32[128,128]{1,0:T(8,128)} %get-tuple-element.329) | copy-start | bytes 196612 | tf_op jit(solution)/shard_map/while
  149.4 0.8 copy-start.28
  151.5 12.2 %copy-start.13 = (f32[128,128]{1,0:T(8,128)S(1)}, f32[128,128]{1,0:T(8,128)}, u32[]{:S(2)}) copy-start(f32[128,128]{1,0:T(8,128)} %get-tuple-element.329) | copy-start | bytes 196612 | tf_op jit(solution)/shard_map/while
  167.7 0.8 copy-start.15
  168.5 0.8 copy-start.3
  169.4 0.9 copy-start.10
  169.4 0.9 copy-start.17
  170.5 0.9 copy-start.5
  170.5 1.1 copy-start.7
  171.8 5.9 %collective-permute-start.4 = (bf16[64,128]{1,0:T(8,128)(2,1)S(1)}, bf16[64,128]{1,0:T(8,128)(2,1)S(1)}, u32[]{:S(2)}, u32[]{:S(2)}) collective-permute-start(bf16[64,128]{1,0:T(8,128)(2,1)S(1)} %get-tuple-element.170), channel_id=1, source_target_pairs={{0,1},{1,2},{2,3},{3,4},{4,5},{5,6},{6,7},{7,8},{8,9},{9,10},{10,1... | collective-permute-start | bytes 49160 | tf_op jit(solution)/shard_map/ppermute | solution.py:16
  171.8 5.9 %collective-permute-start.5 = (bf16[64,128]{1,0:T(8,128)(2,1)S(1)}, bf16[64,128]{1,0:T(8,128)(2,1)S(1)}, u32[]{:S(2)}, u32[]{:S(2)}) collective-permute-start(bf16[64,128]{1,0:T(8,128)(2,1)S(1)} %get-tuple-element.171), channel_id=1, source_target_pairs={{1,0},{2,1},{3,2},{4,3},{5,4},{6,5},{7,6},{8,7},{9,8},{10,9},{11,1... | collective-permute-start | bytes 49160 | tf_op jit(solution)/shard_map/ppermute | solution.py:17
  300.4 1.2 copy-start.1
  (13 other events, 8.6 us)
Sparse Core Ops, SparseCore 0:
  171.4 128.9 all-reduce.1
where the time goes:
time: 311 us; the launch traced here: 309 us
  waiting for transfers between devices  123 us (40%)
  local copies, waits for them, and re-layouts  71.9 us (23%)
  other arithmetic  57.9 us (19%)
  matrix products  27.3 us (9%)
  starting transfers between devices  14.6 us (5%)
  between operations  14.4 us (5%)
    psum x1, waiting for transfers between devices, shards(): total = lax.psum(grads, ('grp', 'slab'))  120 us
    gather x8, local copies, waits for them, and re-layouts, edge_front(): jnp.take(neigh, nbr_blk.reshape(-1), axis=0).reshape(block, slots, width)  49.4 us
    scatter-add x4, other arithmetic, edge_back(): jax.ops.segment_sum(d_pre.reshape(-1, width), nbr_blk.reshape(-1), num_se...  46.3 us
    ppermute x3, starting transfers between devices, with_halo(): after = lax.ppermute(first, axis, down)  14 us
    dot_general x8, matrix products, edge_front(): jnp.dot(hid, w_msg, preferred_element_type=jnp.float32)  10.3 us
    unnamed x54, local copies, waits for them, and re-layouts  8.13 us
    dot_general x9, matrix products, inner(): lax.dot_general(left, right, (((0,), (0,)), ((), ())), preferred_element_...  7.97 us
    dot_general x10, matrix products, by_transpose(): lax.dot_general(left, right, (((1,), (1,)), ((), ())), preferred_element_...  7.65 us
  transfers between devices with their start and end apart: 7, of which 4 were waited for; matrix products, arithmetic and copies ran while one was open for 1% of the time, Pallas kernels for 0%

commit v1 on v0

v1 whole, which is shorter than its diff:
```python
import functools

import jax
import jax.numpy as jnp
from jax import lax
from jax.experimental import pallas as pl
from jax.experimental.pallas import tpu as pltpu
from jax.sharding import PartitionSpec as P

F32 = jnp.float32
BF16 = jnp.bfloat16
CODE_ROWS = 16
LANES = 128


def nn(left, right):
    return lax.dot_general(left, right, (((1,), (0,)), ((), ())), preferred_element_type=F32)


def nt(left, right):
    return lax.dot_general(left, right, (((1,), (1,)), ((), ())), preferred_element_type=F32)


def tn(left, right):
    return lax.dot_general(left, right, (((0,), (0,)), ((), ())), preferred_element_type=F32)


def hot_columns(row, count):
    sub = lax.broadcasted_iota(jnp.int32, (count, row.shape[1]), 0)
    return jnp.where(sub == row, 1.0, 0.0).astype(BF16)


def sigmoid(value):
    return 0.5 * jnp.tanh(0.5 * value) + 0.5


def pack_kernel(nodes, leave, arrive, sends, to_up, to_down, far_up, far_down):
    rows = nodes.shape[1]
    migr = leave.shape[1] // 2
    border = sends.shape[1] // 2
    own = nodes[0]
    leaving = tn(hot_columns(leave[...], rows), own).astype(BF16)
    sub = lax.broadcasted_iota(jnp.int32, (rows, 2 * border), 0)
    column = jnp.transpose(
        jnp.broadcast_to(arrive[...].astype(F32), (2 * border, rows)), (1, 0)
    )
    source = jnp.sum(jnp.where(sub == sends[...], column, 0.0), axis=0, keepdims=True)
    source = source.astype(jnp.int32)
    held = tn(hot_columns(source, rows), own).astype(BF16)
    code = jnp.where(source >= rows, source - rows, -1).astype(F32)
    for out, far, part in ((to_down, far_down, 0), (to_up, far_up, 1)):
        out[:border] = held[part * border : (part + 1) * border]
        moving = leaving[part * migr : (part + 1) * migr]
        out[border : border + migr] = moving
        far[...] = moving
        shifted = code if part == 0 else pltpu.roll(code, border, 1)
        out[border + migr :] = jnp.broadcast_to(shifted, (CODE_ROWS, 2 * border)).astype(BF16)


def layer_kernel(
    chunk,
    nodes,
    arrive,
    nbr,
    valid,
    cotangent,
    w_send,
    w_recv,
    w_msg,
    w_self,
    w_agg,
    w_out,
    my_up,
    my_down,
    low,
    high,
    low_far,
    high_far,
    updated,
    d_local,
    back_low,
    back_high,
    grads,
    nbr_s,
    valid_s,
    nbr_t,
    hid_s,
    ds1_s,
    ds2_s,
    agg_s,
    dcen_s,
    dneigh_s,
    gmsg_s,
):
    rows, width = nodes.shape[1:]
    slots = nbr.shape[2]
    migr = low_far.shape[0]
    border = low.shape[0] - migr - CODE_ROWS
    table_rows = rows + 2 * border

    pool = jnp.concatenate(
        [nodes[0], low[border : border + migr], high[border : border + migr]], axis=0
    )
    moved = tn(hot_columns(arrive[...], pool.shape[0]), pool).astype(BF16)

    def halo(message, first, second):
        code = message[border + migr : border + migr + 8].astype(F32)[:1]
        code = code.astype(jnp.int32)
        source = jnp.concatenate([first, second], axis=0)
        extra = tn(hot_columns(code, 2 * migr), source)
        return (message[:border].astype(F32) + extra[:border]).astype(BF16)

    below = halo(low[...], low_far[...], my_down[border : border + migr])
    above = halo(high[...], my_up[border : border + migr], high_far[...])
    table = jnp.concatenate([moved, below, above], axis=0)

    centre = nn(moved, w_send[...])
    neigh = nn(table, w_recv[...]).astype(BF16)
    msg = w_msg[...]
    nbr_s[:, :slots] = nbr[0]
    valid_s[:, :slots] = valid[0].astype(F32)
    nbr_t[...] = jnp.transpose(nbr_s[...], (1, 0))
    agg_s[...] = jnp.zeros_like(agg_s)

    lane = lax.broadcasted_iota(jnp.int32, (rows, table_rows), 1)

    @pl.loop(0, slots // chunk)
    def forward(step):
        first = step * chunk
        shift = lax.rem(LANES - first, LANES)
        near = pltpu.roll(nbr_s[...], shift, 1)
        keep = pltpu.roll(valid_s[...], shift, 1)
        hot = jnp.concatenate(
            [
                jnp.where(lane == near[:, j : j + 1], 1.0, 0.0).astype(BF16)
                for j in range(chunk)
            ],
            axis=0,
        )
        gathered = nn(hot, neigh)
        hids = []
        for j in range(chunk):
            pre = centre + gathered[j * rows : (j + 1) * rows]
            sig = sigmoid(pre)
            hid = pre * sig
            ds1_s[pl.ds((first + j) * rows, rows)] = sig + hid * (1.0 - sig)
            hids.append(hid.astype(BF16))
        hid = jnp.concatenate(hids, axis=0)
        hid_s[pl.ds(first * rows, chunk * rows)] = hid
        pre2s = nn(hid, msg)
        total = agg_s[...]
        for j in range(chunk):
            pre2 = pre2s[j * rows : (j + 1) * rows]
            sig = sigmoid(pre2)
            act = pre2 * sig
            mask = keep[:, j : j + 1]
            total = total + mask * act
            ds2_s[pl.ds((first + j) * rows, rows)] = mask * (sig + act * (1.0 - sig))
        agg_s[...] = total

    agg_b = agg_s[...].astype(BF16)
    node_pre = nn(moved, w_self[...]) + nn(agg_b, w_agg[...])
    sig = sigmoid(node_pre)
    act = node_pre * sig
    node_hid = act.astype(BF16)
    updated[0] = (moved.astype(F32) + nn(node_hid, w_out[...])).astype(BF16)
    cot = cotangent[0]
    d_node = (nt(cot, w_out[...]) * (sig + act * (1.0 - sig))).astype(BF16)
    d_agg = nt(d_node, w_agg[...])

    dcen_s[...] = jnp.zeros_like(dcen_s)
    dneigh_s[...] = jnp.zeros_like(dneigh_s)
    gmsg_s[...] = jnp.zeros_like(gmsg_s)

    @pl.loop(0, slots // chunk)
    def backward(step):
        first = step * chunk
        span = pl.ds(first * rows, chunk * rows)
        d_pre2 = jnp.concatenate(
            [
                (d_agg * ds2_s[pl.ds((first + j) * rows, rows)]).astype(BF16)
                for j in range(chunk)
            ],
            axis=0,
        )
        gmsg_s[...] += tn(hid_s[span], d_pre2)
        d_pre = nt(d_pre2, msg) * ds1_s[span]
        total = dcen_s[...]
        for j in range(chunk):
            total = total + d_pre[j * rows : (j + 1) * rows]
        dcen_s[...] = total
        hot = jnp.concatenate(
            [hot_columns(nbr_t[pl.ds(first + j, 1)], table_rows) for j in range(chunk)], axis=1
        )
        dneigh_s[...] += nn(hot, d_pre.astype(BF16))

    d_centre = dcen_s[...].astype(BF16)
    d_neigh = dneigh_s[...].astype(BF16)
    d_table = nt(d_neigh, w_recv[...])
    d_local[...] = (
        cot.astype(F32) + nt(d_node, w_self[...]) + nt(d_centre, w_send[...]) + d_table[:rows]
    )
    back_low[...] = d_table[rows : rows + border].astype(BF16)
    back_high[...] = d_table[rows + border :].astype(BF16)
    parts = (
        tn(moved, d_centre),
        tn(table, d_neigh),
        gmsg_s[...],
        tn(moved, d_node),
        tn(agg_b, d_node),
        tn(node_hid, cot),
    )
    for m, part in enumerate(parts):
        grads[m * width : (m + 1) * width] = part.astype(BF16)


def finish_kernel(d_local, sends, from_high, from_low, grad_nodes):
    rows = d_local.shape[0]
    returned = jnp.concatenate([from_low[...], from_high[...]], axis=0)
    extra = nn(hot_columns(sends[...], rows), returned)
    grad_nodes[0] = (d_local[...] + extra).astype(BF16)


def sum_kernel(parts, out):
    count = parts.shape[0]
    total = jnp.sum(parts[...].astype(F32), axis=0).astype(BF16)
    out[...] = jnp.broadcast_to(total[None], out.shape)


def norm_kernel(total, steps):
    count, width = steps.shape[0], steps.shape[1]
    for m in range(count):
        part = total[m * width : (m + 1) * width].astype(F32)
        mean = jnp.sum(jnp.sum(part * part, axis=0, keepdims=True), axis=1, keepdims=True)
        mean = mean / (part.shape[0] * part.shape[1])
        steps[m] = part / jnp.sqrt(mean + 1e-06)


def call(kernel, outs, scratch=(), limit=48):
    return pl.pallas_call(
        kernel,
        out_shape=[jax.ShapeDtypeStruct(shape, kind) for shape, kind in outs],
        scratch_shapes=scratch,
        compiler_params=pltpu.CompilerParams(vmem_limit_bytes=limit * 1024 * 1024),
    )


def shards(
    nodes,
    leave_list,
    arrive_list,
    send_list,
    neighbours,
    valid,
    w_send,
    w_recv,
    w_msg,
    w_self,
    w_agg,
    w_out,
    cotangent,
):
    rows, width = nodes.shape[1:]
    slots = neighbours.shape[2]
    migr = leave_list.shape[1] // 2
    border = send_list.shape[1] // 2
    table_rows = rows + 2 * border
    size = lax.axis_size("slab")
    devices = size * lax.axis_size("grp")

    def shift(array, by):
        return lax.ppermute(array, "slab", [(i, (i + by) % size) for i in range(size)])

    message = (border + migr + CODE_ROWS, width)
    to_up, to_down, far_up, far_down = call(
        pack_kernel,
        [(message, BF16), (message, BF16), ((migr, width), BF16), ((migr, width), BF16)],
    )(nodes, leave_list, arrive_list, send_list)
    low, high = shift(to_up, 1), shift(to_down, -1)
    low_far, high_far = shift(far_up, 2), shift(far_down, -2)

    matrices = 6
    edges = rows * slots
    share = -(-matrices * width // (8 * devices)) * 8
    chunk = 4
    updated, d_local, back_low, back_high, grads = call(
        functools.partial(layer_kernel, chunk),
        [
            ((1, rows, width), BF16),
            ((rows, width), F32),
            ((border, width), BF16),
            ((border, width), BF16),
            ((matrices * width, width), BF16),
        ],
        [
            pltpu.VMEM((rows, LANES), jnp.int32),
            pltpu.VMEM((rows, LANES), F32),
            pltpu.VMEM((LANES, rows), jnp.int32),
            pltpu.VMEM((edges, width), BF16),
            pltpu.VMEM((edges, width), F32),
            pltpu.VMEM((edges, width), F32),
            pltpu.VMEM((rows, width), F32),
            pltpu.VMEM((rows, width), F32),
            pltpu.VMEM((table_rows, width), F32),
            pltpu.VMEM((width, width), F32),
        ],
    )(
        nodes,
        arrive_list,
        neighbours,
        valid,
        cotangent,
        w_send,
        w_recv,
        w_msg,
        w_self,
        w_agg,
        w_out,
        to_up,
        to_down,
        low,
        high,
        low_far,
        high_far,
    )
    from_high = shift(back_low, -1)
    from_low = shift(back_high, 1)
    (grad_nodes,) = call(finish_kernel, [((1, rows, width), BF16)])(
        d_local, send_list, from_high, from_low
    )

    if share * devices > matrices * width:
        grads = jnp.pad(grads, ((0, share * devices - matrices * width), (0, 0)))
    axes = ("grp", "slab")
    parts = lax.all_to_all(
        grads.reshape(devices, share, width), axes, split_axis=0, concat_axis=0, tiled=True
    )
    (shared,) = call(sum_kernel, [((devices, share, width), BF16)])(parts)
    total = lax.all_to_all(shared, axes, split_axis=0, concat_axis=0, tiled=True)
    total = total.reshape(devices * share, width)[: matrices * width]
    (weight_steps,) = call(norm_kernel, [((matrices, width, width), F32)])(total)
    return (updated, grad_nodes, weight_steps)


def solution(mesh):
    rows = P("grp", "slab", None)
    lists = P("grp", "slab")
    in_specs = (rows, lists, lists, lists, rows, rows, P(), P(), P(), P(), P(), P(), rows)
    out_specs = (rows, rows, P())
    return jax.shard_map(shards, mesh=mesh, in_specs=in_specs, out_specs=out_specs, check_vma=False)
```

time: 311 us -> 59.6 us (0.19)
  waiting for transfers between devices: 123 us -> 7.22 us
  local copies, waits for them, and re-layouts: 71.9 us -> 3.07 us
  other arithmetic: 57.9 us -> 0 us
  matrix products: 27.3 us -> 0 us
  Pallas kernels: 0 us -> 15.9 us
  blocking collectives: 0 us -> 15.1 us
  between operations: 14.4 us -> 0.8 us
    psum x1 -> x0, waiting for transfers between devices: 120 us -> none  [shards(): total = lax.psum(grads, ('grp', 'slab'))]
    gather x11 -> x0, local copies, waits for them, and re-layouts: 52.4 us -> none  [the longest x8 49.4 us: edge_front(): jnp.take(neigh, nbr_blk.reshape(-1), axis=0).reshape(block, slots, width)]
    scatter-add x6 -> x0, other arithmetic: 48.3 us -> none  [the longest x4 46.3 us: edge_back(): jax.ops.segment_sum(d_pre.reshape(-1, width), nbr_blk.reshape(-1), num_se...]
    dot_general x32 -> x0, matrix products: 27.3 us -> none  [the longest x8 10.3 us: edge_front(): jnp.dot(hid, w_msg, preferred_element_type=jnp.float32)]
    pallas_call x0 -> x5, Pallas kernels: none -> 15.9 us  [the longest x1 13.2 us: shards(): call(functools.partial(layer_kernel, chunk), [((1, rows, width), BF16), (...]
    all_to_all x0 -> x1, blocking collectives: none -> 15.1 us  [shards(): lax.all_to_all(grads.reshape(devices, share, width), axes, split_axis=0,...]
    convert_element_type x14 -> x0, other arithmetic: 5.71 us -> none  [the longest x8 4.33 us: edge_front(): hid = jax.nn.silu(pre).astype(jnp.bfloat16).reshape(-1, width)]
    unnamed x54 -> x34, local copies, waits for them, and re-layouts: 8.13 us -> 3.07 us
  transfers between devices with their start and end apart: 7 -> 7, of which waited for: 4 -> 3; matrix products, arithmetic and copies ran while one was open for 1% -> 0% of each run, Pallas kernels for 0% -> 1%
where the time goes in v1:
time: 59.6 us; the launch traced here: 59.4 us
  starting transfers between devices  17.2 us (29%)
  Pallas kernels  15.9 us (27%)
  blocking collectives  15.1 us (25%)
  waiting for transfers between devices  7.22 us (12%)
  local copies, waits for them, and re-layouts  3.07 us (5%)
  between operations  0.8 us (1%)
    all_to_all x1, blocking collectives, shards(): lax.all_to_all(grads.reshape(devices, share, width), axes, split_axis=0,...  15.1 us
    ppermute x6, starting transfers between devices, shift(): lax.ppermute(array, 'slab', [(i, (i + by) % size) for i in range(size)])  14.7 us
    pallas_call x1, Pallas kernels, shards(): call(functools.partial(layer_kernel, chunk), [((1, rows, width), BF16), (...  13.2 us
    ppermute x6, waiting for transfers between devices, shift(): lax.ppermute(array, 'slab', [(i, (i + by) % size) for i in range(size)])  7.21 us
    unnamed x34, local copies, waits for them, and re-layouts  3.07 us
    all_to_all x1, starting transfers between devices, shards(): lax.all_to_all(shared, axes, split_axis=0, concat_axis=0, tiled=True)  2.59 us
  transfers between devices with their start and end apart: 7, of which 3 were waited for; matrix products, arithmetic and copies ran while one was open for 0% of the time, Pallas kernels for 1%

profile of v1, /device:TPU:0, one launch (start us, length us, event | category | flops | bytes accessed | tf_op | source)
XLA Modules:
  0.0 59.4 jit_solution(12881491339204368763)
XLA Ops:
  0.6 0.0 copy-start
  0.6 0.8 %copy-done = bf16[1,256,128]{2,1,0:T(8,128)(2,1)S(1)} copy-done((bf16[1,256,128]{2,1,0:T(8,128)(2,1)S(1)}, bf16[1,256,128]{2,1,0:T(8,128)(2,1)}, u32[]{:S(2)}) %copy-start) | copy-done | bytes 65560
  1.5 0.7 %copy-done.9 = s32[1,256]{1,0:T(1,128)S(1)} copy-done((s32[1,256]{1,0:T(1,128)S(1)}, s32[1,256]{1,0:T(1,128)}, u32[]{:S(2)}) %copy-start.9) | copy-done | bytes 1048
  2.2 0.7 %copy-done.11 = s32[1,128]{1,0:T(1,128)S(1)} copy-done((s32[1,128]{1,0:T(1,128)S(1)}, s32[1,128]{1,0:T(1,128)}, u32[]{:S(2)}) %copy-start.11) | copy-done | bytes 536
  2.8 0.7 %copy-done.13 = s32[1,64]{1,0:T(1,128)S(1)} copy-done((s32[1,64]{1,0:T(1,128)S(1)}, s32[1,64]{1,0:T(1,128)}, u32[]{:S(2)}) %copy-start.13) | copy-done | bytes 280
  3.5 0.3 shard_map.148
  3.8 0.5 collective-permute-start
  4.3 5.1 %collective-permute-start.1 = (bf16[112,128]{1,0:T(8,128)(2,1)S(1)}, bf16[112,128]{1,0:T(8,128)(2,1)S(1)}, u32[]{:S(2)}, u32[]{:S(2)}) collective-permute-start(bf16[112,128]{1,0:T(8,128)(2,1)S(1)} %get-tuple-element.13.my_down), channel_id=1, source_target_pairs={{0,15},{1,0},{2,1},{3,2},{4,3},{5,4},{6,5},{7,6},{8,7},{9,8},{10,9... | collective-permute-start | bytes 86024 | tf_op jit(solution)/shard_map/ppermute | solution.py:272
  9.4 0.0 collective-permute-start.2
  9.4 4.7 %collective-permute-start.3 = (bf16[32,128]{1,0:T(8,128)(2,1)S(1)}, bf16[32,128]{1,0:T(8,128)(2,1)S(1)}, u32[]{:S(2)}, u32[]{:S(2)}) collective-permute-start(bf16[32,128]{1,0:T(8,128)(2,1)S(1)} %get-tuple-element.15), channel_id=1, source_target_pairs={{0,14},{1,15},{2,0},{3,1},{4,2},{5,3},{6,4},{7,5},{8,6},{9,7},{10,... | collective-permute-start | bytes 24584 | tf_op jit(solution)/shard_map/ppermute | solution.py:272
  14.1 0.0 copy-start.7
  14.1 0.0 copy-start.8
  14.2 0.1 copy.16.nbr
  14.3 0.0 copy-start.1
  14.3 0.0 copy-start.2
  14.3 0.0 copy-start.3
  14.3 0.1 copy.17.valid
  14.4 1.3 %collective-permute-done.2.low_far = bf16[32,128]{1,0:T(8,128)(2,1)S(1)} collective-permute-done((bf16[32,128]{1,0:T(8,128)(2,1)S(1)}, bf16[32,128]{1,0:T(8,128)(2,1)S(1)}, u32[]{:S(2)}, u32[]{:S(2)}) %collective-permute-start.2) | collective-permute-done | bytes 8224 | tf_op jit(solution)/shard_map/ppermute | solution.py:272
  15.7 0.0 collective-permute-done.3.high_far
  15.7 0.0 collective-permute-done.low
  15.7 0.0 collective-permute-done.1.high
  15.8 13.2 %shard_map.149 = (bf16[1,256,128]{2,1,0:T(8,128)(2,1)}, f32[256,128]{1,0:T(8,128)S(1)}, bf16[64,128]{1,0:T(8,128)(2,1)S(1)}, bf16[64,128]{1,0:T(8,128)(2,1)S(1)}, bf16[768,128]{1,0:T(8,128)(2,1)S(1)}) custom-call(bf16[1,256,128]{2,1,0:T(8,128)(2,1)S(1)} %copy-done.1, s32[1,256]{1,0:T(1,128)S(1)} %copy-done.10, s32[1,256,32]{2,1,0:T(8,128)S(1)} %copy.16.nbr, ...), custom_call_target="tpu_custom_call" | custom-call | tf_op jit(solution)/shard_map/pallas_call | solution.py:286
  29.0 15.1 %all_to_all.10.parts = bf16[32,24,128]{2,1,0:T(8,128)(2,1)S(1)} all-to-all(bf16[32,24,128]{2,1,0:T(8,128)(2,1)S(1)} %bitcast.3), channel_id=1, replica_groups=mesh['grp'=2,'slab'=16] {'grp','slab'}, dimensions={0} | all-to-all | bytes 393216 | tf_op jit(solution)/shard_map/all_to_all | solution.py:335
  44.1 0.7 %shard_map.151 = bf16[32,24,128]{2,1,0:T(8,128)(2,1)} custom-call(bf16[32,24,128]{2,1,0:T(8,128)(2,1)S(1)} %all_to_all.10.parts), custom_call_target="tpu_custom_call" | custom-call | tf_op jit(solution)/shard_map/pallas_call | solution.py:338
  44.9 2.6 %all-to-all-start.1 = ((bf16[32,24,128]{2,1,0:T(8,128)(2,1)}), bf16[32,24,128]{2,1,0:T(8,128)(2,1)S(1)}, u32[]{:S(2)}, u32[]{:S(2)}) async-start(bf16[32,24,128]{2,1,0:T(8,128)(2,1)} %shard_map.151), calls=%async_computation.1 | async-start | bytes 393216 | tf_op jit(solution)/shard_map/all_to_all | solution.py:339
  47.5 4.4 %collective-permute-start.4 = (bf16[64,128]{1,0:T(8,128)(2,1)S(1)}, bf16[64,128]{1,0:T(8,128)(2,1)S(1)}, u32[]{:S(2)}, u32[]{:S(2)}) collective-permute-start(bf16[64,128]{1,0:T(8,128)(2,1)S(1)} %get-tuple-element.18), channel_id=1, source_target_pairs={{0,15},{1,0},{2,1},{3,2},{4,3},{5,4},{6,5},{7,6},{8,7},{9,8},{10,9... | collective-permute-start | bytes 49160 | tf_op jit(solution)/shard_map/ppermute | solution.py:272
  51.8 0.0 collective-permute-start.5
  51.8 1.4 %collective-permute-done.4.from_high = bf16[64,128]{1,0:T(8,128)(2,1)S(1)} collective-permute-done((bf16[64,128]{1,0:T(8,128)(2,1)S(1)}, bf16[64,128]{1,0:T(8,128)(2,1)S(1)}, u32[]{:S(2)}, u32[]{:S(2)}) %collective-permute-start.4) | collective-permute-done | bytes 16416 | tf_op jit(solution)/shard_map/ppermute | solution.py:272
  53.3 4.4 %collective-permute-done.5.from_low = bf16[64,128]{1,0:T(8,128)(2,1)S(1)} collective-permute-done((bf16[64,128]{1,0:T(8,128)(2,1)S(1)}, bf16[64,128]{1,0:T(8,128)(2,1)S(1)}, u32[]{:S(2)}, u32[]{:S(2)}) %collective-permute-start.5) | collective-permute-done | bytes 16416 | tf_op jit(solution)/shard_map/ppermute | solution.py:272
  57.7 0.8 %shard_map.150 = bf16[1,256,128]{2,1,0:T(8,128)(2,1)} custom-call(f32[256,128]{1,0:T(8,128)S(1)} %get-tuple-element.17.d_local, s32[1,128]{1,0:T(1,128)S(1)} %copy-done.12, bf16[64,128]{1,0:T(8,128)(2,1)S(1)} %collective-permute-done.4.from_high, bf16[64,128]{1,0:T(8,128)(2,1)S(1)} %collective-permute-done.5.from_low), custom_call_target="tpu_custom_call" | custom-call | tf_op jit(solution)/shard_map/pallas_call | solution.py:328
  58.5 0.0 all-to-all-done.1
  58.5 0.9 %shard_map.152 = f32[6,128,128]{2,1,0:T(8,128)} custom-call(bf16[768,128]{1,0:T(8,128)(2,1)S(1)} %bitcast.2), custom_call_target="tpu_custom_call" | custom-call | tf_op jit(solution)/shard_map/pallas_call | solution.py:341
  (22 shorter events, 0.0 us)
Async XLA Ops:
  0.6 0.8 %copy-start = (bf16[1,256,128]{2,1,0:T(8,128)(2,1)S(1)}, bf16[1,256,128]{2,1,0:T(8,128)(2,1)}, u32[]{:S(2)}) copy-start(bf16[1,256,128]{2,1,0:T(8,128)(2,1)} %nodes.3) | copy-start | bytes 196612
  1.5 0.7 %copy-start.9 = (s32[1,256]{1,0:T(1,128)S(1)}, s32[1,256]{1,0:T(1,128)}, u32[]{:S(2)}) copy-start(s32[1,256]{1,0:T(1,128)} %arrive.3) | copy-start | bytes 3076
  2.2 0.7 %copy-start.11 = (s32[1,128]{1,0:T(1,128)S(1)}, s32[1,128]{1,0:T(1,128)}, u32[]{:S(2)}) copy-start(s32[1,128]{1,0:T(1,128)} %sends.3) | copy-start | bytes 1540
  2.8 0.7 %copy-start.13 = (s32[1,64]{1,0:T(1,128)S(1)}, s32[1,64]{1,0:T(1,128)}, u32[]{:S(2)}) copy-start(s32[1,64]{1,0:T(1,128)} %leave.1) | copy-start | bytes 772
  3.5 10.7 %copy-start.14 = (s32[1,256,32]{1,2,0:T(8,128)S(1)}, s32[1,256,32]{1,2,0:T(8,128)}, u32[]{:S(2)}) copy-start(s32[1,256,32]{1,2,0:T(8,128)} %param.17) | copy-start | bytes 98308
  3.5 10.8 %copy-start.15 = (s32[1,256,32]{1,2,0:T(8,128)S(1)}, s32[1,256,32]{1,2,0:T(8,128)}, u32[]{:S(2)}) copy-start(s32[1,256,32]{1,2,0:T(8,128)} %param.18) | copy-start | bytes 98308
  3.8 11.9 %collective-permute-start = (bf16[112,128]{1,0:T(8,128)(2,1)S(1)}, bf16[112,128]{1,0:T(8,128)(2,1)S(1)}, u32[]{:S(2)}, u32[]{:S(2)}) collective-permute-start(bf16[112,128]{1,0:T(8,128)(2,1)S(1)} %get-tuple-element.12.my_up), channel_id=1, source_target_pairs={{0,1},{1,2},{2,3},{3,4},{4,5},{5,6},{6,7},{7,8},{8,9},{9,10},{10,1... | collective-permute-start | bytes 86024 | tf_op jit(solution)/shard_map/ppermute | solution.py:272
  4.3 11.4 %copy-start.10 = (s32[1,256]{1,0:T(1,128)S(1)}, s32[1,256]{1,0:T(1,128)}, u32[]{:S(2)}) copy-start(s32[1,256]{1,0:T(1,128)} %arrive.3) | copy-start | bytes 3076
  4.3 11.4 %collective-permute-start.1 = (bf16[112,128]{1,0:T(8,128)(2,1)S(1)}, bf16[112,128]{1,0:T(8,128)(2,1)S(1)}, u32[]{:S(2)}, u32[]{:S(2)}) collective-permute-start(bf16[112,128]{1,0:T(8,128)(2,1)S(1)} %get-tuple-element.13.my_down), channel_id=1, source_target_pairs={{0,15},{1,0},{2,1},{3,2},{4,3},{5,4},{6,5},{7,6},{8,7},{9,8},{10,9... | collective-permute-start | bytes 86024 | tf_op jit(solution)/shard_map/ppermute | solution.py:272
  9.4 6.3 %collective-permute-start.2 = (bf16[32,128]{1,0:T(8,128)(2,1)S(1)}, bf16[32,128]{1,0:T(8,128)(2,1)S(1)}, u32[]{:S(2)}, u32[]{:S(2)}) collective-permute-start(bf16[32,128]{1,0:T(8,128)(2,1)S(1)} %get-tuple-element.14), channel_id=1, source_target_pairs={{0,2},{1,3},{2,4},{3,5},{4,6},{5,7},{6,8},{7,9},{8,10},{9,11},{10,... | collective-permute-start | bytes 24584 | tf_op jit(solution)/shard_map/ppermute | solution.py:272
  9.4 6.3 %collective-permute-start.3 = (bf16[32,128]{1,0:T(8,128)(2,1)S(1)}, bf16[32,128]{1,0:T(8,128)(2,1)S(1)}, u32[]{:S(2)}, u32[]{:S(2)}) collective-permute-start(bf16[32,128]{1,0:T(8,128)(2,1)S(1)} %get-tuple-element.15), channel_id=1, source_target_pairs={{0,14},{1,15},{2,0},{3,1},{4,2},{5,3},{6,4},{7,5},{8,6},{9,7},{10,... | collective-permute-start | bytes 24584 | tf_op jit(solution)/shard_map/ppermute | solution.py:272
  14.1 1.6 %copy-start.4 = (bf16[128,128]{1,0:T(8,128)(2,1)S(1)}, bf16[128,128]{1,0:T(8,128)(2,1)}, u32[]{:S(2)}) copy-start(bf16[128,128]{1,0:T(8,128)(2,1)} %w_recv.1) | copy-start | bytes 98308
  14.1 1.7 %copy-start.5 = (bf16[128,128]{1,0:T(8,128)(2,1)S(1)}, bf16[128,128]{1,0:T(8,128)(2,1)}, u32[]{:S(2)}) copy-start(bf16[128,128]{1,0:T(8,128)(2,1)} %w_msg.1) | copy-start | bytes 98308
  14.1 1.7 %copy-start.6 = (bf16[128,128]{1,0:T(8,128)(2,1)S(1)}, bf16[128,128]{1,0:T(8,128)(2,1)}, u32[]{:S(2)}) copy-start(bf16[128,128]{1,0:T(8,128)(2,1)} %w_self.1) | copy-start | bytes 98308
  14.1 1.7 %copy-start.7 = (bf16[128,128]{1,0:T(8,128)(2,1)S(1)}, bf16[128,128]{1,0:T(8,128)(2,1)}, u32[]{:S(2)}) copy-start(bf16[128,128]{1,0:T(8,128)(2,1)} %w_agg.1) | copy-start | bytes 98308
  14.1 1.7 %copy-start.8 = (bf16[128,128]{1,0:T(8,128)(2,1)S(1)}, bf16[128,128]{1,0:T(8,128)(2,1)}, u32[]{:S(2)}) copy-start(bf16[128,128]{1,0:T(8,128)(2,1)} %w_out.1) | copy-start | bytes 98308
  14.3 1.6 %copy-start.1 = (bf16[1,256,128]{2,1,0:T(8,128)(2,1)S(1)}, bf16[1,256,128]{2,1,0:T(8,128)(2,1)}, u32[]{:S(2)}) copy-start(bf16[1,256,128]{2,1,0:T(8,128)(2,1)} %nodes.3) | copy-start | bytes 196612
  14.3 1.6 %copy-start.2 = (bf16[1,256,128]{2,1,0:T(8,128)(2,1)S(1)}, bf16[1,256,128]{2,1,0:T(8,128)(2,1)}, u32[]{:S(2)}) copy-start(bf16[1,256,128]{2,1,0:T(8,128)(2,1)} %cotangent.1) | copy-start | bytes 196612
  14.3 1.6 %copy-start.3 = (bf16[128,128]{1,0:T(8,128)(2,1)S(1)}, bf16[128,128]{1,0:T(8,128)(2,1)}, u32[]{:S(2)}) copy-start(bf16[128,128]{1,0:T(8,128)(2,1)} %w_send.1) | copy-start | bytes 98308
  44.9 13.6 %all-to-all-start.1 = ((bf16[32,24,128]{2,1,0:T(8,128)(2,1)}), bf16[32,24,128]{2,1,0:T(8,128)(2,1)S(1)}, u32[]{:S(2)}, u32[]{:S(2)}) async-start(bf16[32,24,128]{2,1,0:T(8,128)(2,1)} %shard_map.151), calls=%async_computation.1 | async-start | bytes 393216 | tf_op jit(solution)/shard_map/all_to_all | solution.py:339
  47.5 5.8 %collective-permute-start.4 = (bf16[64,128]{1,0:T(8,128)(2,1)S(1)}, bf16[64,128]{1,0:T(8,128)(2,1)S(1)}, u32[]{:S(2)}, u32[]{:S(2)}) collective-permute-start(bf16[64,128]{1,0:T(8,128)(2,1)S(1)} %get-tuple-element.18), channel_id=1, source_target_pairs={{0,15},{1,0},{2,1},{3,2},{4,3},{5,4},{6,5},{7,6},{8,7},{9,8},{10,9... | collective-permute-start | bytes 49160 | tf_op jit(solution)/shard_map/ppermute | solution.py:272
  51.8 5.9 %copy-start.12 = (s32[1,128]{1,0:T(1,128)S(1)}, s32[1,128]{1,0:T(1,128)}, u32[]{:S(2)}) copy-start(s32[1,128]{1,0:T(1,128)} %sends.3) | copy-start | bytes 1540
  51.8 5.9 %collective-permute-start.5 = (bf16[64,128]{1,0:T(8,128)(2,1)S(1)}, bf16[64,128]{1,0:T(8,128)(2,1)S(1)}, u32[]{:S(2)}, u32[]{:S(2)}) collective-permute-start(bf16[64,128]{1,0:T(8,128)(2,1)S(1)} %get-tuple-element.19), channel_id=1, source_target_pairs={{0,1},{1,2},{2,3},{3,4},{4,5},{5,6},{6,7},{7,8},{8,9},{9,10},{10,1... | collective-permute-start | bytes 49160 | tf_op jit(solution)/shard_map/ppermute | solution.py:272

commit v2 on v1

--- a/solution.py
+++ b/solution.py
@@ -11,6 +11,7 @@
 BF16 = jnp.bfloat16
 CODE_ROWS = 16
 LANES = 128
+SLAB = ("outer", "inner")
 
 
 def nn(left, right):
@@ -34,7 +35,20 @@
     return 0.5 * jnp.tanh(0.5 * value) + 0.5
 
 
-def pack_kernel(nodes, leave, arrive, sends, to_up, to_down, far_up, far_down):
+def pack_kernel(
+    nodes_h, leave_h, arrive_h, sends_h, to_up, far_up, to_down, far_down,
+    nodes, leave, arrive, sends, done,
+):
+    copies = [
+        pltpu.make_async_copy(source, target, done.at[n])
+        for n, (source, target) in enumerate(
+            ((leave_h, leave), (arrive_h, arrive), (sends_h, sends), (nodes_h, nodes))
+        )
+    ]
+    for copy in copies:
+        copy.start()
+    for copy in copies:
+        copy.wait()
     rows = nodes.shape[1]
     migr = leave.shape[1] // 2
     border = sends.shape[1] // 2
@@ -52,9 +66,11 @@
         out[:border] = held[part * border : (part + 1) * border]
         moving = leaving[part * migr : (part + 1) * migr]
         out[border : border + migr] = moving
-        far[...] = moving
+        far[:migr] = moving
+        far[migr:] = jnp.zeros_like(far[migr:])
         shifted = code if part == 0 else pltpu.roll(code, border, 1)
-        out[border + migr :] = jnp.broadcast_to(shifted, (CODE_ROWS, 2 * border)).astype(BF16)
+        tail = out.shape[0] - border - migr
+        out[border + migr :] = jnp.broadcast_to(shifted, (tail, 2 * border)).astype(BF16)
 
 
 def layer_kernel(
@@ -73,8 +89,8 @@
     my_up,
     my_down,
     low,
+    low_far,
     high,
-    low_far,
     high_far,
     updated,
     d_local,
@@ -83,7 +99,6 @@
     grads,
     nbr_s,
     valid_s,
-    nbr_t,
     hid_s,
     ds1_s,
     ds2_s,
@@ -93,9 +108,9 @@
     gmsg_s,
 ):
     rows, width = nodes.shape[1:]
-    slots = nbr.shape[2]
-    migr = low_far.shape[0]
-    border = low.shape[0] - migr - CODE_ROWS
+    slots = nbr.shape[1]
+    border = back_low.shape[0]
+    migr = high.shape[0] - border - CODE_ROWS
     table_rows = rows + 2 * border
 
     pool = jnp.concatenate(
@@ -110,16 +125,16 @@
         extra = tn(hot_columns(code, 2 * migr), source)
         return (message[:border].astype(F32) + extra[:border]).astype(BF16)
 
-    below = halo(low[...], low_far[...], my_down[border : border + migr])
-    above = halo(high[...], my_up[border : border + migr], high_far[...])
+    below = halo(low[...], low_far[:migr], my_down[border : border + migr])
+    above = halo(high[...], my_up[border : border + migr], high_far[:migr])
     table = jnp.concatenate([moved, below, above], axis=0)
 
     centre = nn(moved, w_send[...])
     neigh = nn(table, w_recv[...]).astype(BF16)
     msg = w_msg[...]
-    nbr_s[:, :slots] = nbr[0]
-    valid_s[:, :slots] = valid[0].astype(F32)
-    nbr_t[...] = jnp.transpose(nbr_s[...], (1, 0))
+    fill = jnp.zeros((LANES - slots, rows), jnp.int32)
+    nbr_s[...] = jnp.transpose(jnp.concatenate([nbr[0], fill], axis=0), (1, 0))
+    valid_s[...] = jnp.transpose(jnp.concatenate([valid[0], fill], axis=0), (1, 0)).astype(F32)
     agg_s[...] = jnp.zeros_like(agg_s)
 
     lane = lax.broadcasted_iota(jnp.int32, (rows, table_rows), 1)
@@ -190,7 +205,7 @@
             total = total + d_pre[j * rows : (j + 1) * rows]
         dcen_s[...] = total
         hot = jnp.concatenate(
-            [hot_columns(nbr_t[pl.ds(first + j, 1)], table_rows) for j in range(chunk)], axis=1
+            [hot_columns(nbr[0, pl.ds(first + j, 1)], table_rows) for j in range(chunk)], axis=1
         )
         dneigh_s[...] += nn(hot, d_pre.astype(BF16))
 
@@ -236,9 +251,11 @@
         steps[m] = part / jnp.sqrt(mean + 1e-06)
 
 
-def call(kernel, outs, scratch=(), limit=48):
+def call(kernel, outs, scratch=(), limit=48, space=None):
+    specs = {} if space is None else {"in_specs": [pl.BlockSpec(memory_space=pl.ANY)] * space}
     return pl.pallas_call(
         kernel,
+        **specs,
         out_shape=[jax.ShapeDtypeStruct(shape, kind) for shape, kind in outs],
         scratch_shapes=scratch,
         compiler_params=pltpu.CompilerParams(vmem_limit_bytes=limit * 1024 * 1024),
@@ -265,23 +282,25 @@
     migr = leave_list.shape[1] // 2
     border = send_list.shape[1] // 2
     table_rows = rows + 2 * border
-    size = lax.axis_size("slab")
-    devices = size * lax.axis_size("grp")
+    size = lax.axis_size(SLAB)
 
     def shift(array, by):
-        return lax.ppermute(array, "slab", [(i, (i + by) % size) for i in range(size)])
+        return lax.ppermute(array, SLAB, [(i, (i + by) % size) for i in range(size)])
 
     message = (border + migr + CODE_ROWS, width)
-    to_up, to_down, far_up, far_down = call(
+    message_up = (border + migr + 2 * CODE_ROWS, width)
+    to_up, far_up, to_down, far_down = call(
         pack_kernel,
-        [(message, BF16), (message, BF16), ((migr, width), BF16), ((migr, width), BF16)],
+        [(message_up, BF16)] * 2 + [(message, BF16)] * 2,
+        [pltpu.VMEM(a.shape, a.dtype) for a in (nodes, leave_list, arrive_list, send_list)]
+        + [pltpu.SemaphoreType.DMA((4,))],
+        space=4,
     )(nodes, leave_list, arrive_list, send_list)
-    low, high = shift(to_up, 1), shift(to_down, -1)
-    low_far, high_far = shift(far_up, 2), shift(far_down, -2)
+    low, low_far = shift(to_up, 1), shift(far_up, 2)
+    high, high_far = shift(to_down, -1), shift(far_down, -2)
 
     matrices = 6
     edges = rows * slots
-    share = -(-matrices * width // (8 * devices)) * 8
     chunk = 4
     updated, d_local, back_low, back_high, grads = call(
         functools.partial(layer_kernel, chunk),
@@ -295,7 +314,6 @@
         [
             pltpu.VMEM((rows, LANES), jnp.int32),
             pltpu.VMEM((rows, LANES), F32),
-            pltpu.VMEM((LANES, rows), jnp.int32),
             pltpu.VMEM((edges, width), BF16),
             pltpu.VMEM((edges, width), F32),
             pltpu.VMEM((edges, width), F32),
@@ -307,8 +325,8 @@
     )(
         nodes,
         arrive_list,
-        neighbours,
-        valid,
+        jnp.swapaxes(neighbours, 1, 2),
+        jnp.swapaxes(valid, 1, 2),
         cotangent,
         w_send,
         w_recv,
@@ -319,8 +337,8 @@
         to_up,
         to_down,
         low,
+        low_far,
         high,
-        low_far,
         high_far,
     )
     from_high = shift(back_low, -1)
@@ -329,22 +347,30 @@
         d_local, send_list, from_high, from_low
     )
 
-    if share * devices > matrices * width:
-        grads = jnp.pad(grads, ((0, share * devices - matrices * width), (0, 0)))
-    axes = ("grp", "slab")
+    plane = ("grp", "inner")
+    near = lax.axis_size("grp") * lax.axis_size("inner")
+    far = lax.axis_size("outer")
+    share = matrices * width // near
     parts = lax.all_to_all(
-        grads.reshape(devices, share, width), axes, split_axis=0, concat_axis=0, tiled=True
-    )
-    (shared,) = call(sum_kernel, [((devices, share, width), BF16)])(parts)
-    total = lax.all_to_all(shared, axes, split_axis=0, concat_axis=0, tiled=True)
-    total = total.reshape(devices * share, width)[: matrices * width]
+        grads.reshape(near, share, width), plane, split_axis=0, concat_axis=0, tiled=True
+    )
+    (partial,) = call(sum_kernel, [((far, share, width), BF16)])(parts)
+    parts = lax.all_to_all(partial, "outer", split_axis=0, concat_axis=0, tiled=True)
+    (shared,) = call(sum_kernel, [((near, share, width), BF16)])(parts)
+    total = lax.all_to_all(shared, plane, split_axis=0, concat_axis=0, tiled=True)
+    total = total.reshape(matrices * width, width)
     (weight_steps,) = call(norm_kernel, [((matrices, width, width), F32)])(total)
     return (updated, grad_nodes, weight_steps)
 
 
 def solution(mesh):
-    rows = P("grp", "slab", None)
-    lists = P("grp", "slab")
+    inner = 4
+    groups, slabs = mesh.devices.shape
+    mesh = jax.sharding.Mesh(
+        mesh.devices.reshape(groups, slabs // inner, inner), ("grp", "outer", "inner")
+    )
+    rows = P("grp", SLAB, None)
+    lists = P("grp", SLAB)
     in_specs = (rows, lists, lists, lists, rows, rows, P(), P(), P(), P(), P(), P(), rows)
     out_specs = (rows, rows, P())
     return jax.shard_map(shards, mesh=mesh, in_specs=in_specs, out_specs=out_specs, check_vma=False)

time: 59.6 us -> 67.5 us (1.13); the launches traced: 59.4 us -> 66.6 us
  local copies, waits for them, and re-layouts: 3.07 us -> 9.56 us
  blocking collectives: 15.1 us -> 19.7 us
  starting transfers between devices: 17.2 us -> 13.2 us
    unnamed x34 -> x30, local copies, waits for them, and re-layouts: 3.07 us -> 9.56 us
    ppermute x6, starting transfers between devices: 14.7 us -> 9.76 us  [shift(): lax.ppermute(array, SLAB, [(i, (i + by) % size) for i in range(size)])]
    all_to_all x1 -> x2, blocking collectives: 15.1 us -> 19.7 us  [the longest x1 10.1 us: shards(): lax.all_to_all(partial, 'outer', split_axis=0, concat_axis=0, tiled=True)]
    all_to_all x1, starting transfers between devices: 2.59 us -> 3.39 us  [shards(): lax.all_to_all(shared, plane, split_axis=0, concat_axis=0, tiled=True)]
  transfers between devices with their start and end apart: 7 -> 7, of which waited for: 3 -> 4; matrix products, arithmetic and copies ran while one was open for 0% -> 0% of each run, Pallas kernels for 1% -> 1%
where the time goes in v2:
time: 67.5 us; the launch traced here: 66.6 us
  blocking collectives  19.7 us (29%)
  Pallas kernels  16.1 us (24%)
  starting transfers between devices  13.2 us (20%)
  local copies, waits for them, and re-layouts  9.56 us (14%)
  waiting for transfers between devices  7.42 us (11%)
  between operations  0.69 us (1%)
    pallas_call x1, Pallas kernels, shards(): call(functools.partial(layer_kernel, chunk), [((1, rows, width), BF16), (...  13.2 us
    all_to_all x1, blocking collectives, shards(): lax.all_to_all(partial, 'outer', split_axis=0, concat_axis=0, tiled=True)  10.1 us
    ppermute x6, starting transfers between devices, shift(): lax.ppermute(array, SLAB, [(i, (i + by) % size) for i in range(size)])  9.76 us
    unnamed x30, local copies, waits for them, and re-layouts  9.56 us
    all_to_all x1, blocking collectives, shards(): lax.all_to_all(grads.reshape(near, share, width), plane, split_axis=0, co...  9.54 us
    ppermute x6, waiting for transfers between devices, shift(): lax.ppermute(array, SLAB, [(i, (i + by) % size) for i in range(size)])  7.42 us
    all_to_all x1, starting transfers between devices, shards(): lax.all_to_all(shared, plane, split_axis=0, concat_axis=0, tiled=True)  3.39 us
  transfers between devices with their start and end apart: 7, of which 4 were waited for; matrix products, arithmetic and copies ran while one was open for 0% of the time, Pallas kernels for 1%

profile of v2, /device:TPU:0, one launch (start us, length us, event | category | flops | bytes accessed | tf_op | source)
XLA Modules:
  0.0 66.6 jit_solution(4166123348491525210)
XLA Ops:
  0.6 0.8 %copy-done = bf16[1,256,128]{2,1,0:T(8,128)(2,1)S(1)} copy-done((bf16[1,256,128]{2,1,0:T(8,128)(2,1)S(1)}, bf16[1,256,128]{2,1,0:T(8,128)(2,1)}, u32[]{:S(2)}) %copy-start) | copy-done | bytes 65560
  1.5 0.7 %copy-done.10 = s32[1,256]{1,0:T(1,128)S(1)} copy-done((s32[1,256]{1,0:T(1,128)S(1)}, s32[1,256]{1,0:T(1,128)}, u32[]{:S(2)}) %copy-start.10) | copy-done | bytes 1048
  2.2 0.7 copy-done.12
  2.8 0.7 copy-done.14
  3.5 0.5 shard_map.148
  3.9 3.0 %collective-permute-start.1 = (bf16[128,128]{1,0:T(8,128)(2,1)S(1)}, bf16[128,128]{1,0:T(8,128)(2,1)S(1)}, u32[]{:S(2)}, u32[]{:S(2)}) collective-permute-start(bf16[128,128]{1,0:T(8,128)(2,1)S(1)} %get-tuple-element.14), channel_id=1, source_target_pairs={{0,2},{1,3},{2,4},{3,5},{4,6},{5,7},{6,8},{7,9},{8,10},{9,11},{10,... | collective-permute-start | bytes 98312 | tf_op jit(solution)/shard_map/ppermute | solution.py:288
  7.0 0.0 collective-permute-start
  7.0 3.2 %collective-permute-start.3 = (bf16[112,128]{1,0:T(8,128)(2,1)S(1)}, bf16[112,128]{1,0:T(8,128)(2,1)S(1)}, u32[]{:S(2)}, u32[]{:S(2)}) collective-permute-start(bf16[112,128]{1,0:T(8,128)(2,1)S(1)} %get-tuple-element.15), channel_id=1, source_target_pairs={{0,14},{1,15},{2,0},{3,1},{4,2},{5,3},{6,4},{7,5},{8,6},{9,7},{10,... | collective-permute-start | bytes 86024 | tf_op jit(solution)/shard_map/ppermute | solution.py:288
  10.1 1.4 %collective-permute-start.2 = (bf16[112,128]{1,0:T(8,128)(2,1)S(1)}, bf16[112,128]{1,0:T(8,128)(2,1)S(1)}, u32[]{:S(2)}, u32[]{:S(2)}) collective-permute-start(bf16[112,128]{1,0:T(8,128)(2,1)S(1)} %get-tuple-element.13.my_down), channel_id=1, source_target_pairs={{0,15},{1,0},{2,1},{3,2},{4,3},{5,4},{6,5},{7,6},{8,7},{9,8},{10,9... | collective-permute-start | bytes 86024 | tf_op jit(solution)/shard_map/ppermute | solution.py:288
  11.5 0.2 collective-permute-done.3.high_far
  11.7 1.4 %collective-permute-done.2.high = bf16[112,128]{1,0:T(8,128)(2,1)S(1)} collective-permute-done((bf16[112,128]{1,0:T(8,128)(2,1)S(1)}, bf16[112,128]{1,0:T(8,128)(2,1)S(1)}, u32[]{:S(2)}, u32[]{:S(2)}) %collective-permute-start.2) | collective-permute-done | bytes 28704 | tf_op jit(solution)/shard_map/ppermute | solution.py:288
  13.1 0.0 collective-permute-done.1.low_far
  13.1 0.0 collective-permute-done.low
  13.1 0.7 %copy-done.11 = s32[1,256]{1,0:T(1,128)S(1)} copy-done((s32[1,256]{1,0:T(1,128)S(1)}, s32[1,256]{1,0:T(1,128)}, u32[]{:S(2)}) %copy-start.11) | copy-done | bytes 1048
  13.8 0.8 %copy-done.2 = s32[1,256,32]{1,2,0:T(8,128)S(1)} copy-done((s32[1,256,32]{1,2,0:T(8,128)S(1)}, s32[1,256,32]{1,2,0:T(8,128)}, u32[]{:S(2)}) %copy-start.2) | copy-done | bytes 32792
  14.5 0.8 %copy-done.3 = s32[1,256,32]{1,2,0:T(8,128)S(1)} copy-done((s32[1,256,32]{1,2,0:T(8,128)S(1)}, s32[1,256,32]{1,2,0:T(8,128)}, u32[]{:S(2)}) %copy-start.3) | copy-done | bytes 32792
  15.3 0.8 %copy-done.4 = bf16[128,128]{1,0:T(8,128)(2,1)S(1)} copy-done((bf16[128,128]{1,0:T(8,128)(2,1)S(1)}, bf16[128,128]{1,0:T(8,128)(2,1)}, u32[]{:S(2)}) %copy-start.4) | copy-done | bytes 32792
  16.1 0.8 %copy-done.5 = bf16[128,128]{1,0:T(8,128)(2,1)S(1)} copy-done((bf16[128,128]{1,0:T(8,128)(2,1)S(1)}, bf16[128,128]{1,0:T(8,128)(2,1)}, u32[]{:S(2)}) %copy-start.5) | copy-done | bytes 32792
  16.8 0.8 %copy-done.6 = bf16[128,128]{1,0:T(8,128)(2,1)S(1)} copy-done((bf16[128,128]{1,0:T(8,128)(2,1)S(1)}, bf16[128,128]{1,0:T(8,128)(2,1)}, u32[]{:S(2)}) %copy-start.6) | copy-done | bytes 32792
  17.6 0.8 %copy-done.7 = bf16[128,128]{1,0:T(8,128)(2,1)S(1)} copy-done((bf16[128,128]{1,0:T(8,128)(2,1)S(1)}, bf16[128,128]{1,0:T(8,128)(2,1)}, u32[]{:S(2)}) %copy-start.7) | copy-done | bytes 32792
  18.3 0.8 %copy-done.8 = bf16[128,128]{1,0:T(8,128)(2,1)S(1)} copy-done((bf16[128,128]{1,0:T(8,128)(2,1)S(1)}, bf16[128,128]{1,0:T(8,128)(2,1)}, u32[]{:S(2)}) %copy-start.8) | copy-done | bytes 32792
  19.1 0.8 %copy-done.9 = bf16[128,128]{1,0:T(8,128)(2,1)S(1)} copy-done((bf16[128,128]{1,0:T(8,128)(2,1)S(1)}, bf16[128,128]{1,0:T(8,128)(2,1)}, u32[]{:S(2)}) %copy-start.9) | copy-done | bytes 32792
  19.8 13.2 %shard_map.149 = (bf16[1,256,128]{2,1,0:T(8,128)(2,1)}, f32[256,128]{1,0:T(8,128)S(1)}, bf16[64,128]{1,0:T(8,128)(2,1)S(1)}, bf16[64,128]{1,0:T(8,128)(2,1)S(1)}, bf16[768,128]{1,0:T(8,128)(2,1)S(1)}) custom-call(bf16[1,256,128]{2,1,0:T(8,128)(2,1)S(1)} %copy-done, s32[1,256]{1,0:T(1,128)S(1)} %copy-done.11, s32[1,32,256]{2,1,0:T(8,128)S(1)} %bitcast.6, ...), custom_call_target="tpu_custom_call" | custom-call | tf_op jit(solution)/shard_map/pallas_call | solution.py:305
  33.1 9.5 %all_to_all.15.parts = bf16[8,96,128]{2,1,0:T(8,128)(2,1)S(1)} all-to-all(bf16[8,96,128]{2,1,0:T(8,128)(2,1)S(1)} %bitcast.5), channel_id=1, replica_groups=mesh['grp'=2,'outer'=4,'inner'=4] {'grp','inner'}, dimensions={0} | all-to-all | bytes 393216 | tf_op jit(solution)/shard_map/all_to_all | solution.py:354
  42.7 10.1 %all_to_all.16.parts = bf16[4,96,128]{2,1,0:T(8,128)(2,1)S(1)} all-to-all(bf16[4,96,128]{2,1,0:T(8,128)(2,1)S(1)} %shard_map.151), channel_id=1, replica_groups=mesh['grp'=2,'outer'=4,'inner'=4] {'outer'}, dimensions={0} | all-to-all | bytes 196608 | tf_op jit(solution)/shard_map/all_to_all | solution.py:358
  52.8 0.7 %shard_map.152 = bf16[8,96,128]{2,1,0:T(8,128)(2,1)} custom-call(bf16[4,96,128]{2,1,0:T(8,128)(2,1)S(1)} %all_to_all.16.parts), custom_call_target="tpu_custom_call" | custom-call | tf_op jit(solution)/shard_map/pallas_call | solution.py:359
  53.5 3.4 %all-to-all-start.2 = ((bf16[8,96,128]{2,1,0:T(8,128)(2,1)}), bf16[8,96,128]{2,1,0:T(8,128)(2,1)S(1)}, u32[]{:S(2)}, u32[]{:S(2)}) async-start(bf16[8,96,128]{2,1,0:T(8,128)(2,1)} %shard_map.152), calls=%async_computation.2 | async-start | bytes 393216 | tf_op jit(solution)/shard_map/all_to_all | solution.py:360
  56.9 2.2 %collective-permute-start.4 = (bf16[64,128]{1,0:T(8,128)(2,1)S(1)}, bf16[64,128]{1,0:T(8,128)(2,1)S(1)}, u32[]{:S(2)}, u32[]{:S(2)}) collective-permute-start(bf16[64,128]{1,0:T(8,128)(2,1)S(1)} %get-tuple-element.18), channel_id=1, source_target_pairs={{0,15},{1,0},{2,1},{3,2},{4,3},{5,4},{6,5},{7,6},{8,7},{9,8},{10,9... | collective-permute-start | bytes 49160 | tf_op jit(solution)/shard_map/ppermute | solution.py:288
  59.0 1.4 %collective-permute-done.4.from_high = bf16[64,128]{1,0:T(8,128)(2,1)S(1)} collective-permute-done((bf16[64,128]{1,0:T(8,128)(2,1)S(1)}, bf16[64,128]{1,0:T(8,128)(2,1)S(1)}, u32[]{:S(2)}, u32[]{:S(2)}) %collective-permute-start.4) | collective-permute-done | bytes 16416 | tf_op jit(solution)/shard_map/ppermute | solution.py:288
  60.5 4.4 %collective-permute-done.5.from_low = bf16[64,128]{1,0:T(8,128)(2,1)S(1)} collective-permute-done((bf16[64,128]{1,0:T(8,128)(2,1)S(1)}, bf16[64,128]{1,0:T(8,128)(2,1)S(1)}, u32[]{:S(2)}, u32[]{:S(2)}) %collective-permute-start.5) | collective-permute-done | bytes 16416 | tf_op jit(solution)/shard_map/ppermute | solution.py:288
  64.9 0.8 %shard_map.150 = bf16[1,256,128]{2,1,0:T(8,128)(2,1)} custom-call(f32[256,128]{1,0:T(8,128)S(1)} %get-tuple-element.17.d_local, s32[1,128]{1,0:T(1,128)S(1)} %copy-done.13, bf16[64,128]{1,0:T(8,128)(2,1)S(1)} %collective-permute-done.4.from_high, bf16[64,128]{1,0:T(8,128)(2,1)S(1)} %collective-permute-done.5.from_low), custom_call_target="tpu_custom_call" | custom-call | tf_op jit(solution)/shard_map/pallas_call | solution.py:346
  65.7 0.9 %shard_map.153 = f32[6,128,128]{2,1,0:T(8,128)} custom-call(bf16[768,128]{1,0:T(8,128)(2,1)S(1)} %bitcast.4), custom_call_target="tpu_custom_call" | custom-call | tf_op jit(solution)/shard_map/pallas_call | solution.py:362
  (20 shorter events, 0.1 us)
Async XLA Ops:
  0.6 0.8 %copy-start = (bf16[1,256,128]{2,1,0:T(8,128)(2,1)S(1)}, bf16[1,256,128]{2,1,0:T(8,128)(2,1)}, u32[]{:S(2)}) copy-start(bf16[1,256,128]{2,1,0:T(8,128)(2,1)} %nodes.1) | copy-start | bytes 196612
  1.5 0.7 %copy-start.10 = (s32[1,256]{1,0:T(1,128)S(1)}, s32[1,256]{1,0:T(1,128)}, u32[]{:S(2)}) copy-start(s32[1,256]{1,0:T(1,128)} %arrive.1) | copy-start | bytes 3076
  2.2 0.7 copy-start.12
  2.8 0.7 copy-start.14
  3.5 9.6 %copy-start.1 = (bf16[1,256,128]{2,1,0:T(8,128)(2,1)S(1)}, bf16[1,256,128]{2,1,0:T(8,128)(2,1)}, u32[]{:S(2)}) copy-start(bf16[1,256,128]{2,1,0:T(8,128)(2,1)} %cotangent.1) | copy-start | bytes 196612
  3.9 9.2 %collective-permute-start.1 = (bf16[128,128]{1,0:T(8,128)(2,1)S(1)}, bf16[128,128]{1,0:T(8,128)(2,1)S(1)}, u32[]{:S(2)}, u32[]{:S(2)}) collective-permute-start(bf16[128,128]{1,0:T(8,128)(2,1)S(1)} %get-tuple-element.14), channel_id=1, source_target_pairs={{0,2},{1,3},{2,4},{3,5},{4,6},{5,7},{6,8},{7,9},{8,10},{9,11},{10,... | collective-permute-start | bytes 98312 | tf_op jit(solution)/shard_map/ppermute | solution.py:288
  7.0 6.1 %collective-permute-start = (bf16[128,128]{1,0:T(8,128)(2,1)S(1)}, bf16[128,128]{1,0:T(8,128)(2,1)S(1)}, u32[]{:S(2)}, u32[]{:S(2)}) collective-permute-start(bf16[128,128]{1,0:T(8,128)(2,1)S(1)} %get-tuple-element.12.my_up), channel_id=1, source_target_pairs={{0,1},{1,2},{2,3},{3,4},{4,5},{5,6},{6,7},{7,8},{8,9},{9,10},{10,1... | collective-permute-start | bytes 98312 | tf_op jit(solution)/shard_map/ppermute | solution.py:288
  7.0 4.7 %collective-permute-start.3 = (bf16[112,128]{1,0:T(8,128)(2,1)S(1)}, bf16[112,128]{1,0:T(8,128)(2,1)S(1)}, u32[]{:S(2)}, u32[]{:S(2)}) collective-permute-start(bf16[112,128]{1,0:T(8,128)(2,1)S(1)} %get-tuple-element.15), channel_id=1, source_target_pairs={{0,14},{1,15},{2,0},{3,1},{4,2},{5,3},{6,4},{7,5},{8,6},{9,7},{10,... | collective-permute-start | bytes 86024 | tf_op jit(solution)/shard_map/ppermute | solution.py:288
  10.1 3.0 %collective-permute-start.2 = (bf16[112,128]{1,0:T(8,128)(2,1)S(1)}, bf16[112,128]{1,0:T(8,128)(2,1)S(1)}, u32[]{:S(2)}, u32[]{:S(2)}) collective-permute-start(bf16[112,128]{1,0:T(8,128)(2,1)S(1)} %get-tuple-element.13.my_down), channel_id=1, source_target_pairs={{0,15},{1,0},{2,1},{3,2},{4,3},{5,4},{6,5},{7,6},{8,7},{9,8},{10,9... | collective-permute-start | bytes 86024 | tf_op jit(solution)/shard_map/ppermute | solution.py:288
  13.1 0.7 %copy-start.11 = (s32[1,256]{1,0:T(1,128)S(1)}, s32[1,256]{1,0:T(1,128)}, u32[]{:S(2)}) copy-start(s32[1,256]{1,0:T(1,128)} %arrive.1) | copy-start | bytes 3076
  13.8 0.8 %copy-start.2 = (s32[1,256,32]{1,2,0:T(8,128)S(1)}, s32[1,256,32]{1,2,0:T(8,128)}, u32[]{:S(2)}) copy-start(s32[1,256,32]{1,2,0:T(8,128)} %param.17) | copy-start | bytes 98308
  14.5 0.8 %copy-start.3 = (s32[1,256,32]{1,2,0:T(8,128)S(1)}, s32[1,256,32]{1,2,0:T(8,128)}, u32[]{:S(2)}) copy-start(s32[1,256,32]{1,2,0:T(8,128)} %param.18) | copy-start | bytes 98308
  15.3 0.8 %copy-start.4 = (bf16[128,128]{1,0:T(8,128)(2,1)S(1)}, bf16[128,128]{1,0:T(8,128)(2,1)}, u32[]{:S(2)}) copy-start(bf16[128,128]{1,0:T(8,128)(2,1)} %w_send.1) | copy-start | bytes 98308
  16.1 0.8 %copy-start.5 = (bf16[128,128]{1,0:T(8,128)(2,1)S(1)}, bf16[128,128]{1,0:T(8,128)(2,1)}, u32[]{:S(2)}) copy-start(bf16[128,128]{1,0:T(8,128)(2,1)} %w_recv.1) | copy-start | bytes 98308
  16.8 0.8 %copy-start.6 = (bf16[128,128]{1,0:T(8,128)(2,1)S(1)}, bf16[128,128]{1,0:T(8,128)(2,1)}, u32[]{:S(2)}) copy-start(bf16[128,128]{1,0:T(8,128)(2,1)} %w_msg.1) | copy-start | bytes 98308
  17.6 0.8 %copy-start.7 = (bf16[128,128]{1,0:T(8,128)(2,1)S(1)}, bf16[128,128]{1,0:T(8,128)(2,1)}, u32[]{:S(2)}) copy-start(bf16[128,128]{1,0:T(8,128)(2,1)} %w_self.1) | copy-start | bytes 98308
  18.3 0.8 %copy-start.8 = (bf16[128,128]{1,0:T(8,128)(2,1)S(1)}, bf16[128,128]{1,0:T(8,128)(2,1)}, u32[]{:S(2)}) copy-start(bf16[128,128]{1,0:T(8,128)(2,1)} %w_agg.1) | copy-start | bytes 98308
  19.1 0.8 %copy-start.9 = (bf16[128,128]{1,0:T(8,128)(2,1)S(1)}, bf16[128,128]{1,0:T(8,128)(2,1)}, u32[]{:S(2)}) copy-start(bf16[128,128]{1,0:T(8,128)(2,1)} %w_out.1) | copy-start | bytes 98308
  53.5 12.2 %all-to-all-start.2 = ((bf16[8,96,128]{2,1,0:T(8,128)(2,1)}), bf16[8,96,128]{2,1,0:T(8,128)(2,1)S(1)}, u32[]{:S(2)}, u32[]{:S(2)}) async-start(bf16[8,96,128]{2,1,0:T(8,128)(2,1)} %shard_map.152), calls=%async_computation.2 | async-start | bytes 393216 | tf_op jit(solution)/shard_map/all_to_all | solution.py:360
  56.9 3.6 %collective-permute-start.4 = (bf16[64,128]{1,0:T(8,128)(2,1)S(1)}, bf16[64,128]{1,0:T(8,128)(2,1)S(1)}, u32[]{:S(2)}, u32[]{:S(2)}) collective-permute-start(bf16[64,128]{1,0:T(8,128)(2,1)S(1)} %get-tuple-element.18), channel_id=1, source_target_pairs={{0,15},{1,0},{2,1},{3,2},{4,3},{5,4},{6,5},{7,6},{8,7},{9,8},{10,9... | collective-permute-start | bytes 49160 | tf_op jit(solution)/shard_map/ppermute | solution.py:288
  59.0 5.9 %copy-start.13 = (s32[1,128]{1,0:T(1,128)S(1)}, s32[1,128]{1,0:T(1,128)}, u32[]{:S(2)}) copy-start(s32[1,128]{1,0:T(1,128)} %sends.1) | copy-start | bytes 1540
  59.0 5.9 %collective-permute-start.5 = (bf16[64,128]{1,0:T(8,128)(2,1)S(1)}, bf16[64,128]{1,0:T(8,128)(2,1)S(1)}, u32[]{:S(2)}, u32[]{:S(2)}) collective-permute-start(bf16[64,128]{1,0:T(8,128)(2,1)S(1)} %get-tuple-element.19), channel_id=1, source_target_pairs={{0,1},{1,2},{2,3},{3,4},{4,5},{5,6},{6,7},{7,8},{8,9},{9,10},{10,1... | collective-permute-start | bytes 49160 | tf_op jit(solution)/shard_map/ppermute | solution.py:288

commit v3 on v1

v3 whole, which is shorter than its diff:
```python
import functools

import jax
import jax.numpy as jnp
from jax import lax
from jax.experimental import pallas as pl
from jax.experimental.pallas import tpu as pltpu
from jax.sharding import PartitionSpec as P

F32 = jnp.float32
BF16 = jnp.bfloat16
CODE_ROWS = 16
LANES = 128
FAR = -1e30
PAIRS = 2


def nn(left, right):
    return lax.dot_general(left, right, (((1,), (0,)), ((), ())), preferred_element_type=F32)


def nt(left, right):
    return lax.dot_general(left, right, (((1,), (1,)), ((), ())), preferred_element_type=F32)


def tn(left, right):
    return lax.dot_general(left, right, (((0,), (0,)), ((), ())), preferred_element_type=F32)


def hot_columns(row, count):
    sub = lax.broadcasted_iota(jnp.int32, (count, row.shape[1]), 0)
    return jnp.where(sub == row, 1.0, 0.0).astype(BF16)


def silu_parts(half):
    tan = jnp.tanh(half)
    part = half * tan
    return half + part, (1.0 + tan) * ((1.0 + half) - part)


def first_kernel(out):
    out[...] = jnp.zeros_like(out)


def pack_kernel(_, nodes, leave, arrive, sends, to_up, far_up, to_down, far_down):
    rows = nodes.shape[1]
    migr = leave.shape[1] // 2
    border = sends.shape[1] // 2
    own = nodes[0]
    leaving = tn(hot_columns(leave[...], rows), own).astype(BF16)
    sub = lax.broadcasted_iota(jnp.int32, (rows, 2 * border), 0)
    column = jnp.transpose(
        jnp.broadcast_to(arrive[...].astype(F32), (2 * border, rows)), (1, 0)
    )
    source = jnp.sum(jnp.where(sub == sends[...], column, 0.0), axis=0, keepdims=True)
    source = source.astype(jnp.int32)
    rest = tn(hot_columns(source, rows), own).astype(BF16)
    code = jnp.where(source >= rows, source - rows, -1).astype(F32)
    for out, far, part in ((to_down, far_down, 0), (to_up, far_up, 1)):
        out[:border] = rest[part * border : (part + 1) * border]
        moving = leaving[part * migr : (part + 1) * migr]
        out[border : border + migr] = moving
        far[:migr] = moving
        far[migr:] = jnp.zeros_like(far[migr:])
        shifted = code if part == 0 else pltpu.roll(code, border, 1)
        tail = out.shape[0] - border - migr
        out[border + migr :] = jnp.broadcast_to(shifted, (tail, 2 * border)).astype(BF16)


def layer_kernel(
    nodes,
    arrive,
    my_up,
    my_down,
    low,
    low_far,
    high,
    high_far,
    nbr,
    valid,
    w_send,
    w_recv,
    w_msg,
    w_self,
    w_agg,
    w_out,
    cotangent,
    updated,
    back_low,
    back_high,
    grads,
    d_node_o,
    d_centre_o,
    d_neigh_o,
    nbr_s,
    neigh_s,
    wide_s,
    hid_s,
    ds1_s,
    ds2_s,
    agg_s,
    dcen_s,
    dneigh_s,
    gmsg_s,
):
    rows, width = nodes.shape[1:]
    slots = nbr.shape[1]
    border = back_low.shape[0]
    migr = high.shape[0] - border - CODE_ROWS
    table_rows = rows + 2 * border
    chunk = 2 * PAIRS
    steps = slots // chunk

    pool = jnp.concatenate(
        [nodes[0], low[border : border + migr], high[border : border + migr]], axis=0
    )
    moved = tn(hot_columns(arrive[...], pool.shape[0]), pool).astype(BF16)

    def halo(message, first, second):
        code = message[border + migr : border + migr + 8].astype(F32)[:1]
        code = code.astype(jnp.int32)
        source = jnp.concatenate([first, second], axis=0)
        extra = tn(hot_columns(code, 2 * migr), source)
        return (message[:border].astype(F32) + extra[:border]).astype(BF16)

    below = halo(low[...], low_far[:migr], my_down[border : border + migr])
    above = halo(high[...], my_up[border : border + migr], high_far[:migr])
    table = jnp.concatenate([moved, below, above], axis=0)

    half_centre = 0.5 * nn(moved, w_send[...])
    half_neigh = (0.5 * nn(table, w_recv[...]).astype(BF16).astype(F32)).astype(BF16)
    none = jnp.zeros((table_rows, width), BF16)
    neigh_s[...] = jnp.concatenate(
        [
            jnp.concatenate([half_neigh, none], axis=1),
            jnp.concatenate([none, half_neigh], axis=1),
        ],
        axis=0,
    )
    half_msg = 0.5 * w_msg[...].astype(F32)
    none = jnp.zeros((width, width), F32)
    for part, block in enumerate((half_msg, jnp.transpose(half_msg, (1, 0)))):
        wide_s[part] = jnp.concatenate(
            [
                jnp.concatenate([block, none], axis=1),
                jnp.concatenate([none, block], axis=1),
            ],
            axis=0,
        ).astype(BF16)
    index = jnp.where(valid[0] == 1, nbr[0], -1)
    fill = jnp.zeros((LANES - slots, rows), jnp.int32)
    nbr_s[...] = jnp.transpose(jnp.concatenate([index, fill], axis=0), (1, 0))
    agg_s[...] = jnp.zeros_like(agg_s)

    lane = lax.broadcasted_iota(jnp.int32, (rows, table_rows), 1).astype(jnp.int16)
    one = jnp.ones((rows, table_rows), BF16)
    zero = jnp.zeros((rows, table_rows), BF16)

    @pl.loop(0, steps)
    def forward(step):
        near = pltpu.roll(nbr_s[...], lax.rem(LANES - step * chunk, LANES), 1)
        ids = [jnp.broadcast_to(near[:, j : j + 1], (rows, LANES)) for j in range(chunk)]
        hots = []
        for j in range(chunk):
            short = ids[j].astype(jnp.int16)
            short = jnp.concatenate([short] * (table_rows // LANES), axis=1)
            hots.append(jnp.where(short == lane, one, zero))
        hot = jnp.concatenate(
            [
                jnp.concatenate([hots[2 * p], hots[2 * p + 1]], axis=1)
                for p in range(PAIRS)
            ],
            axis=0,
        )
        gathered = nn(hot, neigh_s[...])
        base = step * (PAIRS * rows)
        for p in range(PAIRS):
            for side in range(2):
                cols = slice(side * width, (side + 1) * width)
                half = half_centre + gathered[p * rows : (p + 1) * rows, cols]
                half = jnp.where(ids[2 * p + side] < 0, FAR, half)
                act, slope = silu_parts(half)
                span = pl.ds(base + p * rows, rows)
                ds1_s[span, cols] = slope
                hid_s[span, cols] = act.astype(BF16)
        halves = nn(hid_s[pl.ds(base, PAIRS * rows)], wide_s[0])
        total = agg_s[...]
        for p in range(PAIRS):
            for side in range(2):
                cols = slice(side * width, (side + 1) * width)
                act, slope = silu_parts(halves[p * rows : (p + 1) * rows, cols])
                total = total + act
                ds2_s[pl.ds(base + p * rows, rows), cols] = slope
        agg_s[...] = total

    agg_b = agg_s[...].astype(BF16)
    node_pre = nn(moved, w_self[...]) + nn(agg_b, w_agg[...])
    act, slope = silu_parts(0.5 * node_pre)
    node_hid = act.astype(BF16)
    updated[0] = (moved.astype(F32) + nn(node_hid, w_out[...])).astype(BF16)
    cot = cotangent[0]
    d_node = (nt(cot, w_out[...]) * (0.5 * slope)).astype(BF16)
    half_d_agg = 0.5 * nt(d_node, w_agg[...])

    dcen_s[...] = jnp.zeros_like(dcen_s)
    dneigh_s[...] = jnp.zeros_like(dneigh_s)
    gmsg_s[...] = jnp.zeros_like(gmsg_s)
    sub = lax.broadcasted_iota(jnp.int32, (table_rows, rows), 0).astype(jnp.int16)
    one_t = jnp.ones((table_rows, rows), BF16)
    zero_t = jnp.zeros((table_rows, rows), BF16)

    def stack(wide):
        return jnp.concatenate(
            [
                wide[p * rows : (p + 1) * rows, side * width : (side + 1) * width]
                for p in range(PAIRS)
                for side in range(2)
            ],
            axis=0,
        )

    @pl.loop(0, steps)
    def backward(step):
        span = pl.ds(step * (PAIRS * rows), PAIRS * rows)
        d_agg = jnp.concatenate([half_d_agg, half_d_agg], axis=1)
        d_agg = jnp.concatenate([d_agg] * PAIRS, axis=0)
        d_pre2 = (d_agg * ds2_s[span]).astype(BF16)
        d_pre = nn(d_pre2, wide_s[1]) * ds1_s[span]
        gmsg_s[...] += tn(stack(hid_s[span]), stack(d_pre2))
        d_pre = stack(d_pre)
        total = dcen_s[...]
        for j in range(chunk):
            total = total + d_pre[j * rows : (j + 1) * rows]
        dcen_s[...] = total
        hots = []
        for j in range(chunk):
            row = jnp.broadcast_to(nbr[0, pl.ds(step * chunk + j, 1)], (16, rows))
            short = jnp.concatenate([row.astype(jnp.int16)] * (table_rows // 16), axis=0)
            hots.append(jnp.where(short == sub, one_t, zero_t))
        dneigh_s[...] += nn(jnp.concatenate(hots, axis=1), d_pre.astype(BF16))

    d_centre = dcen_s[...].astype(BF16)
    d_neigh = dneigh_s[...].astype(BF16)
    d_borrowed = nt(d_neigh[rows:], w_recv[...]).astype(BF16)
    back_low[...] = d_borrowed[:border]
    back_high[...] = d_borrowed[border:]
    d_node_o[...] = d_node
    d_centre_o[...] = d_centre
    d_neigh_o[...] = d_neigh[:rows]
    parts = (
        tn(moved, d_centre),
        tn(table, d_neigh),
        gmsg_s[...],
        tn(moved, d_node),
        tn(agg_b, d_node),
        tn(node_hid, cot),
    )
    for m, part in enumerate(parts):
        grads[m * width : (m + 1) * width] = part.astype(BF16)
    used = len(parts) * width
    if grads.shape[0] > used:
        grads[used:] = jnp.zeros_like(grads[used:])


def finish_kernel(
    cotangent, d_node, d_centre, d_neigh, w_self, w_send, w_recv, sends, from_low, from_high, out
):
    rows = d_node.shape[0]
    returned = jnp.concatenate([from_low[...], from_high[...]], axis=0)
    out[0] = (
        cotangent[0].astype(F32)
        + nt(d_node[...], w_self[...])
        + nt(d_centre[...], w_send[...])
        + nt(d_neigh[...], w_recv[...])
        + nn(hot_columns(sends[...], rows), returned)
    ).astype(BF16)


def sum_kernel(parts, out):
    total = jnp.sum(parts[...].astype(F32), axis=0).astype(BF16)
    out[...] = jnp.broadcast_to(total[None], out.shape)


def norm_kernel(total, steps):
    count, width = steps.shape[0], steps.shape[1]
    for m in range(count):
        part = total[m * width : (m + 1) * width].astype(F32)
        mean = jnp.sum(jnp.sum(part * part, axis=0, keepdims=True), axis=1, keepdims=True)
        mean = mean / (part.shape[0] * part.shape[1])
        steps[m] = part / jnp.sqrt(mean + 1e-06)


def call(kernel, outs, scratch=()):
    return pl.pallas_call(
        kernel,
        out_shape=[jax.ShapeDtypeStruct(shape, kind) for shape, kind in outs],
        scratch_shapes=scratch,
        compiler_params=pltpu.CompilerParams(vmem_limit_bytes=40 * 1024 * 1024),
        cost_estimate=pl.CostEstimate(flops=2 * 10**9, bytes_accessed=1024, transcendentals=0),
    )


def shards(
    nodes,
    leave_list,
    arrive_list,
    send_list,
    neighbours,
    valid,
    w_send,
    w_recv,
    w_msg,
    w_self,
    w_agg,
    w_out,
    cotangent,
):
    rows, width = nodes.shape[1:]
    slots = neighbours.shape[2]
    migr = leave_list.shape[1] // 2
    border = send_list.shape[1] // 2
    table_rows = rows + 2 * border
    size = lax.axis_size("slab")
    devices = size * lax.axis_size("grp")
    axes = ("grp", "slab")

    def shift(array, by):
        return lax.ppermute(array, "slab", [(i, (i + by) % size) for i in range(size)])

    message = (border + migr + CODE_ROWS, width)
    message_up = (message[0] + CODE_ROWS, width)
    (token,) = call(first_kernel, [((8, LANES), F32)])()
    to_up, far_up, to_down, far_down = call(
        pack_kernel,
        [(message_up, BF16)] * 2 + [(message, BF16)] * 2,
    )(token, nodes, leave_list, arrive_list, send_list)
    low, low_far = shift(to_up, 1), shift(far_up, 2)
    high, high_far = shift(to_down, -1), shift(far_down, -2)

    matrices = 6
    pair_rows = rows * slots // 2
    share = -(-matrices * width // (8 * devices)) * 8
    sources = (
        nodes,
        arrive_list,
        to_up,
        to_down,
        low,
        low_far,
        high,
        high_far,
        jnp.swapaxes(neighbours, 1, 2),
        jnp.swapaxes(valid, 1, 2),
        w_send,
        w_recv,
        w_msg,
        w_self,
        w_agg,
        w_out,
        cotangent,
    )
    updated, back_low, back_high, grads, d_node, d_centre, d_neigh = call(
        layer_kernel,
        [
            ((1, rows, width), BF16),
            ((border, width), BF16),
            ((border, width), BF16),
            ((devices * share, width), BF16),
            ((rows, width), BF16),
            ((rows, width), BF16),
            ((rows, width), BF16),
        ],
        [
            pltpu.VMEM((rows, LANES), jnp.int32),
            pltpu.VMEM((2 * table_rows, 2 * width), BF16),
            pltpu.VMEM((2, 2 * width, 2 * width), BF16),
            pltpu.VMEM((pair_rows, 2 * width), BF16),
            pltpu.VMEM((pair_rows, 2 * width), F32),
            pltpu.VMEM((pair_rows, 2 * width), F32),
            pltpu.VMEM((rows, width), F32),
            pltpu.VMEM((rows, width), F32),
            pltpu.VMEM((table_rows, width), F32),
            pltpu.VMEM((width, width), F32),
        ],
    )(*sources)
    from_low = shift(back_high, 1)
    from_high = shift(back_low, -1)
    parts = lax.all_to_all(
        grads.reshape(devices, share, width), axes, split_axis=0, concat_axis=0, tiled=True
    )
    sources = (
        cotangent,
        d_node,
        d_centre,
        d_neigh,
        w_self,
        w_send,
        w_recv,
        send_list,
        from_low,
        from_high,
    )
    (grad_nodes,) = call(
        finish_kernel,
        [((1, rows, width), BF16)],
    )(*sources)
    (shared,) = call(sum_kernel, [((devices, share, width), BF16)])(parts)
    total = lax.all_to_all(shared, axes, split_axis=0, concat_axis=0, tiled=True)
    total = total.reshape(devices * share, width)[: matrices * width]
    (weight_steps,) = call(norm_kernel, [((matrices, width, width), F32)])(total)
    return (updated, grad_nodes, weight_steps)


def solution(mesh):
    rows = P("grp", "slab", None)
    lists = P("grp", "slab")
    in_specs = (rows, lists, lists, lists, rows, rows, P(), P(), P(), P(), P(), P(), rows)
    out_specs = (rows, rows, P())
    return jax.shard_map(shards, mesh=mesh, in_specs=in_specs, out_specs=out_specs, check_vma=False)
```

time: 59.6 us -> 54 us (0.906)
  starting transfers between devices: 17.2 us -> 14.7 us
  local copies, waits for them, and re-layouts: 3.07 us -> 0.88 us
  waiting for transfers between devices: 7.22 us -> 5.76 us
  Pallas kernels: 15.9 us -> 17.2 us
  blocking collectives: 15.1 us -> 14.4 us
    ppermute x6, starting transfers between devices: 14.7 us -> 12.1 us  [shift(): lax.ppermute(array, 'slab', [(i, (i + by) % size) for i in range(size)])]
    unnamed x34 -> x26, local copies, waits for them, and re-layouts: 3.07 us -> 0.88 us
    ppermute x6, waiting for transfers between devices: 7.21 us -> 5.75 us  [shift(): lax.ppermute(array, 'slab', [(i, (i + by) % size) for i in range(size)])]
    pallas_call x3 -> x4, Pallas kernels: 14.3 us -> 15.6 us  [the longest x1 14.4 us: shards(): call(layer_kernel, [((1, rows, width), BF16), ((border, width), BF16), ((...]
    all_to_all x1, blocking collectives: 15.1 us -> 14.4 us  [shards(): lax.all_to_all(grads.reshape(devices, share, width), axes, split_axis=0,...]
  transfers between devices with their start and end apart: 7 -> 7, of which waited for: 3 -> 3; matrix products, arithmetic and copies ran while one was open for 0% -> 0% of each run, Pallas kernels for 1% -> 2%
where the time goes in v3:
time: 54 us; the launch traced here: 53.8 us
  Pallas kernels  17.2 us (32%)
  starting transfers between devices  14.7 us (27%)
  blocking collectives  14.4 us (27%)
  waiting for transfers between devices  5.76 us (11%)
  local copies, waits for them, and re-layouts  0.88 us (2%)
  between operations  0.82 us (2%)
    all_to_all x1, blocking collectives, shards(): lax.all_to_all(grads.reshape(devices, share, width), axes, split_axis=0,...  14.4 us
    pallas_call x1, Pallas kernels, shards(): call(layer_kernel, [((1, rows, width), BF16), ((border, width), BF16), ((...  14.4 us
    ppermute x6, starting transfers between devices, shift(): lax.ppermute(array, 'slab', [(i, (i + by) % size) for i in range(size)])  12.1 us
    ppermute x6, waiting for transfers between devices, shift(): lax.ppermute(array, 'slab', [(i, (i + by) % size) for i in range(size)])  5.75 us
    all_to_all x1, starting transfers between devices, shards(): lax.all_to_all(shared, axes, split_axis=0, concat_axis=0, tiled=True)  2.59 us
  transfers between devices with their start and end apart: 7, of which 3 were waited for; matrix products, arithmetic and copies ran while one was open for 0% of the time, Pallas kernels for 2%

profile of v3, /device:TPU:0, one launch (start us, length us, event | category | flops | bytes accessed | tf_op | source)
XLA Modules:
  0.0 53.8 jit_solution(8247966261215497186)
XLA Ops:
  0.6 0.0 copy-start.12
  0.6 0.0 copy-start.10
  0.7 0.6 %copy-done.12 = s32[1,128]{1,0:T(1,128)S(1)} copy-done((s32[1,128]{1,0:T(1,128)S(1)}, s32[1,128]{1,0:T(1,128)}, u32[]{:S(2)}) %copy-start.12) | copy-done | bytes 536
  1.3 0.0 copy-done.10
  1.3 0.2 copy-done
  1.5 0.0 copy-done.11
  1.5 0.0 copy-start.4
  1.5 0.0 copy-start.5
  1.5 0.0 copy-start.6
  1.6 0.0 copy-start.7
  1.6 0.0 copy-start.8
  1.6 0.0 copy-start.9
  1.6 0.3 shard_map.149
  1.9 3.0 %collective-permute-start.1 = (bf16[128,128]{1,0:T(8,128)(2,1)S(1)}, bf16[128,128]{1,0:T(8,128)(2,1)S(1)}, u32[]{:S(2)}, u32[]{:S(2)}) collective-permute-start(bf16[128,128]{1,0:T(8,128)(2,1)S(1)} %get-tuple-element.16), channel_id=1, source_target_pairs={{0,2},{1,3},{2,4},{3,5},{4,6},{5,7},{6,8},{7,9},{8,10},{9,11},{10,... | collective-permute-start | bytes 98312 | tf_op jit(solution)/shard_map/ppermute | solution.py:328
  5.0 0.0 collective-permute-start
  5.0 3.2 %collective-permute-start.3 = (bf16[112,128]{1,0:T(8,128)(2,1)S(1)}, bf16[112,128]{1,0:T(8,128)(2,1)S(1)}, u32[]{:S(2)}, u32[]{:S(2)}) collective-permute-start(bf16[112,128]{1,0:T(8,128)(2,1)S(1)} %get-tuple-element.17), channel_id=1, source_target_pairs={{0,14},{1,15},{2,0},{3,1},{4,2},{5,3},{6,4},{7,5},{8,6},{9,7},{10,... | collective-permute-start | bytes 86024 | tf_op jit(solution)/shard_map/ppermute | solution.py:328
  8.1 1.4 %collective-permute-start.2 = (bf16[112,128]{1,0:T(8,128)(2,1)S(1)}, bf16[112,128]{1,0:T(8,128)(2,1)S(1)}, u32[]{:S(2)}, u32[]{:S(2)}) collective-permute-start(bf16[112,128]{1,0:T(8,128)(2,1)S(1)} %get-tuple-element.15.my_down), channel_id=1, source_target_pairs={{0,15},{1,0},{2,1},{3,2},{4,3},{5,4},{6,5},{7,6},{8,7},{9,8},{10,9... | collective-permute-start | bytes 86024 | tf_op jit(solution)/shard_map/ppermute | solution.py:328
  9.5 0.2 collective-permute-done.3.high_far
  9.7 1.4 %collective-permute-done.2.high = bf16[112,128]{1,0:T(8,128)(2,1)S(1)} collective-permute-done((bf16[112,128]{1,0:T(8,128)(2,1)S(1)}, bf16[112,128]{1,0:T(8,128)(2,1)S(1)}, u32[]{:S(2)}, u32[]{:S(2)}) %collective-permute-start.2) | collective-permute-done | bytes 28704 | tf_op jit(solution)/shard_map/ppermute | solution.py:328
  11.1 0.0 collective-permute-done.1.low_far
  11.1 0.0 collective-permute-done.low
  11.2 14.4 %shard_map.150 = (bf16[1,256,128]{2,1,0:T(8,128)(2,1)}, bf16[64,128]{1,0:T(8,128)(2,1)S(1)}, bf16[64,128]{1,0:T(8,128)(2,1)S(1)}, bf16[768,128]{1,0:T(8,128)(2,1...) custom-call(bf16[1,256,128]{2,1,0:T(8,128)(2,1)S(1)} %copy-done, ...), custom_call_target="tpu_custom_call" | custom-call | flops 2000000000 | bytes 1024 | tf_op jit(solution)/shard_map/pallas_call | solution.py:362
  25.6 14.4 %all_to_all.10.parts = bf16[32,24,128]{2,1,0:T(8,128)(2,1)S(1)} all-to-all(bf16[32,24,128]{2,1,0:T(8,128)(2,1)S(1)} %bitcast.5), channel_id=1, replica_groups=mesh['grp'=2,'slab'=16] {'grp','slab'}, dimensions={0} | all-to-all | bytes 393216 | tf_op jit(solution)/shard_map/all_to_all | solution.py:388
  40.0 0.7 %shard_map.152 = bf16[32,24,128]{2,1,0:T(8,128)(2,1)} custom-call(bf16[32,24,128]{2,1,0:T(8,128)(2,1)S(1)} %all_to_all.10.parts), custom_call_target="tpu_custom_call" | custom-call | flops 2000000000 | bytes 1024 | tf_op jit(solution)/shard_map/pallas_call | solution.py:407
  40.7 2.6 %all-to-all-start.1 = ((bf16[32,24,128]{2,1,0:T(8,128)(2,1)}), bf16[32,24,128]{2,1,0:T(8,128)(2,1)S(1)}, u32[]{:S(2)}, u32[]{:S(2)}) async-start(bf16[32,24,128]{2,1,0:T(8,128)(2,1)} %shard_map.152), calls=%async_computation.1 | async-start | bytes 393216 | tf_op jit(solution)/shard_map/all_to_all | solution.py:408
  43.3 0.4 collective-permute-start.4
  43.8 4.0 %collective-permute-start.5 = (bf16[64,128]{1,0:T(8,128)(2,1)S(1)}, bf16[64,128]{1,0:T(8,128)(2,1)S(1)}, u32[]{:S(2)}, u32[]{:S(2)}) collective-permute-start(bf16[64,128]{1,0:T(8,128)(2,1)S(1)} %get-tuple-element.23), channel_id=1, source_target_pairs={{0,15},{1,0},{2,1},{3,2},{4,3},{5,4},{6,5},{7,6},{8,7},{9,8},{10,9... | collective-permute-start | bytes 49160 | tf_op jit(solution)/shard_map/ppermute | solution.py:328
  47.8 4.2 %collective-permute-done.4.from_low = bf16[64,128]{1,0:T(8,128)(2,1)S(1)} collective-permute-done((bf16[64,128]{1,0:T(8,128)(2,1)S(1)}, bf16[64,128]{1,0:T(8,128)(2,1)S(1)}, u32[]{:S(2)}, u32[]{:S(2)}) %collective-permute-start.4) | collective-permute-done | bytes 16416 | tf_op jit(solution)/shard_map/ppermute | solution.py:328
  52.0 0.0 collective-permute-done.5.from_high
  52.0 0.9 %shard_map.151 = bf16[1,256,128]{2,1,0:T(8,128)(2,1)} custom-call(bf16[1,256,128]{2,1,0:T(8,128)(2,1)S(1)} %copy-done.1, bf16[256,128]{1,0:T(8,128)(2,1)S(1)} %get-tuple-element.19.d_node, bf16[256,128]{1,0:T(8,128)(2,1)S(1)} %get-tuple-element.20.d_centre, bf16[256,128]{1,0:T(8,128)(2,1)S(1)} %get-tuple-element.21.d_neigh, bf16[128,128]{1,0:T(8,128)(2,1)S(1)} %copy-done.9, ...), custom_call_target="tpu_custom_call" | custom-call | flops 2000000000 | bytes 1024 | tf_op jit(solution)/shard_map/pallas_call | solution.py:403
  52.9 0.0 all-to-all-done.1
  52.9 0.9 %shard_map.153 = f32[6,128,128]{2,1,0:T(8,128)} custom-call(bf16[768,128]{1,0:T(8,128)(2,1)S(1)} %bitcast.4), custom_call_target="tpu_custom_call" | custom-call | flops 2000000000 | bytes 1024 | tf_op jit(solution)/shard_map/pallas_call | solution.py:410
  (15 shorter events, 0.0 us)
Async XLA Ops:
  0.6 0.7 %copy-start.12 = (s32[1,128]{1,0:T(1,128)S(1)}, s32[1,128]{1,0:T(1,128)}, u32[]{:S(2)}) copy-start(s32[1,128]{1,0:T(1,128)} %sends.3) | copy-start | bytes 1540
  0.6 0.7 %copy-start.10 = (s32[1,256]{1,0:T(1,128)S(1)}, s32[1,256]{1,0:T(1,128)}, u32[]{:S(2)}) copy-start(s32[1,256]{1,0:T(1,128)} %arrive.3) | copy-start | bytes 3076
  0.7 0.9 %copy-start = (bf16[1,256,128]{2,1,0:T(8,128)(2,1)S(1)}, bf16[1,256,128]{2,1,0:T(8,128)(2,1)}, u32[]{:S(2)}) copy-start(bf16[1,256,128]{2,1,0:T(8,128)(2,1)} %nodes.3) | copy-start | bytes 196612
  0.7 0.8 %copy-start.11 = (s32[1,64]{1,0:T(1,128)S(1)}, s32[1,64]{1,0:T(1,128)}, u32[]{:S(2)}) copy-start(s32[1,64]{1,0:T(1,128)} %leave.1) | copy-start | bytes 772
  1.5 9.6 %copy-start.1 = (bf16[1,256,128]{2,1,0:T(8,128)(2,1)S(1)}, bf16[1,256,128]{2,1,0:T(8,128)(2,1)}, u32[]{:S(2)}) copy-start(bf16[1,256,128]{2,1,0:T(8,128)(2,1)} %cotangent.3) | copy-start | bytes 196612
  1.5 9.6 %copy-start.2 = (s32[1,256,32]{1,2,0:T(8,128)S(1)}, s32[1,256,32]{1,2,0:T(8,128)}, u32[]{:S(2)}) copy-start(s32[1,256,32]{1,2,0:T(8,128)} %param.17) | copy-start | bytes 98308
  1.5 9.6 %copy-start.3 = (s32[1,256,32]{1,2,0:T(8,128)S(1)}, s32[1,256,32]{1,2,0:T(8,128)}, u32[]{:S(2)}) copy-start(s32[1,256,32]{1,2,0:T(8,128)} %param.18) | copy-start | bytes 98308
  1.5 9.6 %copy-start.4 = (bf16[128,128]{1,0:T(8,128)(2,1)S(1)}, bf16[128,128]{1,0:T(8,128)(2,1)}, u32[]{:S(2)}) copy-start(bf16[128,128]{1,0:T(8,128)(2,1)} %w_msg.1) | copy-start | bytes 98308
  1.5 9.6 %copy-start.5 = (bf16[128,128]{1,0:T(8,128)(2,1)S(1)}, bf16[128,128]{1,0:T(8,128)(2,1)}, u32[]{:S(2)}) copy-start(bf16[128,128]{1,0:T(8,128)(2,1)} %w_agg.1) | copy-start | bytes 98308
  1.5 9.6 %copy-start.6 = (bf16[128,128]{1,0:T(8,128)(2,1)S(1)}, bf16[128,128]{1,0:T(8,128)(2,1)}, u32[]{:S(2)}) copy-start(bf16[128,128]{1,0:T(8,128)(2,1)} %w_out.1) | copy-start | bytes 98308
  1.6 9.6 %copy-start.7 = (bf16[128,128]{1,0:T(8,128)(2,1)S(1)}, bf16[128,128]{1,0:T(8,128)(2,1)}, u32[]{:S(2)}) copy-start(bf16[128,128]{1,0:T(8,128)(2,1)} %w_send.3) | copy-start | bytes 98308
  1.6 9.6 %copy-start.8 = (bf16[128,128]{1,0:T(8,128)(2,1)S(1)}, bf16[128,128]{1,0:T(8,128)(2,1)}, u32[]{:S(2)}) copy-start(bf16[128,128]{1,0:T(8,128)(2,1)} %w_recv.3) | copy-start | bytes 98308
  1.6 9.6 %copy-start.9 = (bf16[128,128]{1,0:T(8,128)(2,1)S(1)}, bf16[128,128]{1,0:T(8,128)(2,1)}, u32[]{:S(2)}) copy-start(bf16[128,128]{1,0:T(8,128)(2,1)} %w_self.3) | copy-start | bytes 98308
  1.9 9.2 %collective-permute-start.1 = (bf16[128,128]{1,0:T(8,128)(2,1)S(1)}, bf16[128,128]{1,0:T(8,128)(2,1)S(1)}, u32[]{:S(2)}, u32[]{:S(2)}) collective-permute-start(bf16[128,128]{1,0:T(8,128)(2,1)S(1)} %get-tuple-element.16), channel_id=1, source_target_pairs={{0,2},{1,3},{2,4},{3,5},{4,6},{5,7},{6,8},{7,9},{8,10},{9,11},{10,... | collective-permute-start | bytes 98312 | tf_op jit(solution)/shard_map/ppermute | solution.py:328
  5.0 6.1 %collective-permute-start = (bf16[128,128]{1,0:T(8,128)(2,1)S(1)}, bf16[128,128]{1,0:T(8,128)(2,1)S(1)}, u32[]{:S(2)}, u32[]{:S(2)}) collective-permute-start(bf16[128,128]{1,0:T(8,128)(2,1)S(1)} %get-tuple-element.14.my_up), channel_id=1, source_target_pairs={{0,1},{1,2},{2,3},{3,4},{4,5},{5,6},{6,7},{7,8},{8,9},{9,10},{10,1... | collective-permute-start | bytes 98312 | tf_op jit(solution)/shard_map/ppermute | solution.py:328
  5.0 4.7 %collective-permute-start.3 = (bf16[112,128]{1,0:T(8,128)(2,1)S(1)}, bf16[112,128]{1,0:T(8,128)(2,1)S(1)}, u32[]{:S(2)}, u32[]{:S(2)}) collective-permute-start(bf16[112,128]{1,0:T(8,128)(2,1)S(1)} %get-tuple-element.17), channel_id=1, source_target_pairs={{0,14},{1,15},{2,0},{3,1},{4,2},{5,3},{6,4},{7,5},{8,6},{9,7},{10,... | collective-permute-start | bytes 86024 | tf_op jit(solution)/shard_map/ppermute | solution.py:328
  8.1 3.0 %collective-permute-start.2 = (bf16[112,128]{1,0:T(8,128)(2,1)S(1)}, bf16[112,128]{1,0:T(8,128)(2,1)S(1)}, u32[]{:S(2)}, u32[]{:S(2)}) collective-permute-start(bf16[112,128]{1,0:T(8,128)(2,1)S(1)} %get-tuple-element.15.my_down), channel_id=1, source_target_pairs={{0,15},{1,0},{2,1},{3,2},{4,3},{5,4},{6,5},{7,6},{8,7},{9,8},{10,9... | collective-permute-start | bytes 86024 | tf_op jit(solution)/shard_map/ppermute | solution.py:328
  40.7 12.2 %all-to-all-start.1 = ((bf16[32,24,128]{2,1,0:T(8,128)(2,1)}), bf16[32,24,128]{2,1,0:T(8,128)(2,1)S(1)}, u32[]{:S(2)}, u32[]{:S(2)}) async-start(bf16[32,24,128]{2,1,0:T(8,128)(2,1)} %shard_map.152), calls=%async_computation.1 | async-start | bytes 393216 | tf_op jit(solution)/shard_map/all_to_all | solution.py:408
  43.3 8.7 %collective-permute-start.4 = (bf16[64,128]{1,0:T(8,128)(2,1)S(1)}, bf16[64,128]{1,0:T(8,128)(2,1)S(1)}, u32[]{:S(2)}, u32[]{:S(2)}) collective-permute-start(bf16[64,128]{1,0:T(8,128)(2,1)S(1)} %get-tuple-element.22), channel_id=1, source_target_pairs={{0,1},{1,2},{2,3},{3,4},{4,5},{5,6},{6,7},{7,8},{8,9},{9,10},{10,1... | collective-permute-start | bytes 49160 | tf_op jit(solution)/shard_map/ppermute | solution.py:328
  43.8 8.2 %collective-permute-start.5 = (bf16[64,128]{1,0:T(8,128)(2,1)S(1)}, bf16[64,128]{1,0:T(8,128)(2,1)S(1)}, u32[]{:S(2)}, u32[]{:S(2)}) collective-permute-start(bf16[64,128]{1,0:T(8,128)(2,1)S(1)} %get-tuple-element.23), channel_id=1, source_target_pairs={{0,15},{1,0},{2,1},{3,2},{4,3},{5,4},{6,5},{7,6},{8,7},{9,8},{10,9... | collective-permute-start | bytes 49160 | tf_op jit(solution)/shard_map/ppermute | solution.py:328

commit v4 on v3

--- a/solution.py
+++ b/solution.py
@@ -12,7 +12,7 @@
 CODE_ROWS = 16
 LANES = 128
 FAR = -1e30
-PAIRS = 2
+PAIRS = 4
 
 
 def nn(left, right):

time: 54 us -> 51.2 us (0.948)
  Pallas kernels: 17.2 us -> 14.3 us
    pallas_call x1, Pallas kernels: 14.4 us -> 11.5 us  [shards(): call(layer_kernel, [((1, rows, width), BF16), ((border, width), BF16), ((...]
where the time goes in v4:
time: 51.2 us; the launch traced here: 51 us
  starting transfers between devices  14.7 us (29%)
  blocking collectives  14.5 us (28%)
  Pallas kernels  14.3 us (28%)
  waiting for transfers between devices  5.76 us (11%)
  local copies, waits for them, and re-layouts  0.88 us (2%)
  between operations  0.82 us (2%)
    all_to_all x1, blocking collectives, shards(): lax.all_to_all(grads.reshape(devices, share, width), axes, split_axis=0,...  14.5 us
    ppermute x6, starting transfers between devices, shift(): lax.ppermute(array, 'slab', [(i, (i + by) % size) for i in range(size)])  12.1 us
    pallas_call x1, Pallas kernels, shards(): call(layer_kernel, [((1, rows, width), BF16), ((border, width), BF16), ((...  11.5 us
    ppermute x6, waiting for transfers between devices, shift(): lax.ppermute(array, 'slab', [(i, (i + by) % size) for i in range(size)])  5.75 us
    all_to_all x1, starting transfers between devices, shards(): lax.all_to_all(shared, axes, split_axis=0, concat_axis=0, tiled=True)  2.59 us
  transfers between devices with their start and end apart: 7, of which 3 were waited for; matrix products, arithmetic and copies ran while one was open for 0% of the time, Pallas kernels for 2%

profile of v4, /device:TPU:0, one launch (start us, length us, event | category | flops | bytes accessed | tf_op | source)
XLA Modules:
  0.0 51.0 jit_solution(4566689666168533650)
XLA Ops:
  0.6 0.0 copy-start.12
  0.6 0.0 copy-start.10
  0.7 0.6 %copy-done.12 = s32[1,128]{1,0:T(1,128)S(1)} copy-done((s32[1,128]{1,0:T(1,128)S(1)}, s32[1,128]{1,0:T(1,128)}, u32[]{:S(2)}) %copy-start.12) | copy-done | bytes 536
  1.3 0.0 copy-done.10
  1.3 0.2 copy-done
  1.5 0.0 copy-start.4
  1.5 0.0 copy-start.5
  1.5 0.0 copy-start.6
  1.6 0.0 copy-start.7
  1.6 0.0 copy-start.8
  1.6 0.0 copy-start.9
  1.6 0.3 shard_map.149
  1.9 3.0 %collective-permute-start.1 = (bf16[128,128]{1,0:T(8,128)(2,1)S(1)}, bf16[128,128]{1,0:T(8,128)(2,1)S(1)}, u32[]{:S(2)}, u32[]{:S(2)}) collective-permute-start(bf16[128,128]{1,0:T(8,128)(2,1)S(1)} %get-tuple-element.16), channel_id=1, source_target_pairs={{0,2},{1,3},{2,4},{3,5},{4,6},{5,7},{6,8},{7,9},{8,10},{9,11},{10,... | collective-permute-start | bytes 98312 | tf_op jit(solution)/shard_map/ppermute | solution.py:328
  5.0 0.0 collective-permute-start
  5.0 3.2 %collective-permute-start.3 = (bf16[112,128]{1,0:T(8,128)(2,1)S(1)}, bf16[112,128]{1,0:T(8,128)(2,1)S(1)}, u32[]{:S(2)}, u32[]{:S(2)}) collective-permute-start(bf16[112,128]{1,0:T(8,128)(2,1)S(1)} %get-tuple-element.17), channel_id=1, source_target_pairs={{0,14},{1,15},{2,0},{3,1},{4,2},{5,3},{6,4},{7,5},{8,6},{9,7},{10,... | collective-permute-start | bytes 86024 | tf_op jit(solution)/shard_map/ppermute | solution.py:328
  8.1 1.4 %collective-permute-start.2 = (bf16[112,128]{1,0:T(8,128)(2,1)S(1)}, bf16[112,128]{1,0:T(8,128)(2,1)S(1)}, u32[]{:S(2)}, u32[]{:S(2)}) collective-permute-start(bf16[112,128]{1,0:T(8,128)(2,1)S(1)} %get-tuple-element.15.my_down), channel_id=1, source_target_pairs={{0,15},{1,0},{2,1},{3,2},{4,3},{5,4},{6,5},{7,6},{8,7},{9,8},{10,9... | collective-permute-start | bytes 86024 | tf_op jit(solution)/shard_map/ppermute | solution.py:328
  9.5 0.2 collective-permute-done.3.high_far
  9.7 1.4 %collective-permute-done.2.high = bf16[112,128]{1,0:T(8,128)(2,1)S(1)} collective-permute-done((bf16[112,128]{1,0:T(8,128)(2,1)S(1)}, bf16[112,128]{1,0:T(8,128)(2,1)S(1)}, u32[]{:S(2)}, u32[]{:S(2)}) %collective-permute-start.2) | collective-permute-done | bytes 28704 | tf_op jit(solution)/shard_map/ppermute | solution.py:328
  11.1 0.0 collective-permute-done.1.low_far
  11.1 0.0 collective-permute-done.low
  11.1 0.0 copy-done.1
  11.2 11.5 %shard_map.150 = (bf16[1,256,128]{2,1,0:T(8,128)(2,1)}, bf16[64,128]{1,0:T(8,128)(2,1)S(1)}, bf16[64,128]{1,0:T(8,128)(2,1)S(1)}, bf16[768,128]{1,0:T(8,128)(2,1...) custom-call(bf16[1,256,128]{2,1,0:T(8,128)(2,1)S(1)} %copy-done, ...), custom_call_target="tpu_custom_call" | custom-call | flops 2000000000 | bytes 1024 | tf_op jit(solution)/shard_map/pallas_call | solution.py:362
  22.7 14.5 %all_to_all.10.parts = bf16[32,24,128]{2,1,0:T(8,128)(2,1)S(1)} all-to-all(bf16[32,24,128]{2,1,0:T(8,128)(2,1)S(1)} %bitcast.5), channel_id=1, replica_groups=mesh['grp'=2,'slab'=16] {'grp','slab'}, dimensions={0} | all-to-all | bytes 393216 | tf_op jit(solution)/shard_map/all_to_all | solution.py:388
  37.2 0.7 %shard_map.152 = bf16[32,24,128]{2,1,0:T(8,128)(2,1)} custom-call(bf16[32,24,128]{2,1,0:T(8,128)(2,1)S(1)} %all_to_all.10.parts), custom_call_target="tpu_custom_call" | custom-call | flops 2000000000 | bytes 1024 | tf_op jit(solution)/shard_map/pallas_call | solution.py:407
  37.9 2.6 %all-to-all-start.1 = ((bf16[32,24,128]{2,1,0:T(8,128)(2,1)}), bf16[32,24,128]{2,1,0:T(8,128)(2,1)S(1)}, u32[]{:S(2)}, u32[]{:S(2)}) async-start(bf16[32,24,128]{2,1,0:T(8,128)(2,1)} %shard_map.152), calls=%async_computation.1 | async-start | bytes 393216 | tf_op jit(solution)/shard_map/all_to_all | solution.py:408
  40.5 0.4 collective-permute-start.4
  40.9 4.0 %collective-permute-start.5 = (bf16[64,128]{1,0:T(8,128)(2,1)S(1)}, bf16[64,128]{1,0:T(8,128)(2,1)S(1)}, u32[]{:S(2)}, u32[]{:S(2)}) collective-permute-start(bf16[64,128]{1,0:T(8,128)(2,1)S(1)} %get-tuple-element.23), channel_id=1, source_target_pairs={{0,15},{1,0},{2,1},{3,2},{4,3},{5,4},{6,5},{7,6},{8,7},{9,8},{10,9... | collective-permute-start | bytes 49160 | tf_op jit(solution)/shard_map/ppermute | solution.py:328
  45.0 4.2 %collective-permute-done.4.from_low = bf16[64,128]{1,0:T(8,128)(2,1)S(1)} collective-permute-done((bf16[64,128]{1,0:T(8,128)(2,1)S(1)}, bf16[64,128]{1,0:T(8,128)(2,1)S(1)}, u32[]{:S(2)}, u32[]{:S(2)}) %collective-permute-start.4) | collective-permute-done | bytes 16416 | tf_op jit(solution)/shard_map/ppermute | solution.py:328
  49.2 0.0 collective-permute-done.5.from_high
  49.2 0.9 %shard_map.151 = bf16[1,256,128]{2,1,0:T(8,128)(2,1)} custom-call(bf16[1,256,128]{2,1,0:T(8,128)(2,1)S(1)} %copy-done.1, bf16[256,128]{1,0:T(8,128)(2,1)S(1)} %get-tuple-element.19.d_node, bf16[256,128]{1,0:T(8,128)(2,1)S(1)} %get-tuple-element.20.d_centre, bf16[256,128]{1,0:T(8,128)(2,1)S(1)} %get-tuple-element.21.d_neigh, bf16[128,128]{1,0:T(8,128)(2,1)S(1)} %copy-done.9, ...), custom_call_target="tpu_custom_call" | custom-call | flops 2000000000 | bytes 1024 | tf_op jit(solution)/shard_map/pallas_call | solution.py:403
  50.0 0.0 all-to-all-done.1
  50.1 0.9 %shard_map.153 = f32[6,128,128]{2,1,0:T(8,128)} custom-call(bf16[768,128]{1,0:T(8,128)(2,1)S(1)} %bitcast.4), custom_call_target="tpu_custom_call" | custom-call | flops 2000000000 | bytes 1024 | tf_op jit(solution)/shard_map/pallas_call | solution.py:410
  (15 shorter events, 0.0 us)
Async XLA Ops:
  0.6 0.7 %copy-start.12 = (s32[1,128]{1,0:T(1,128)S(1)}, s32[1,128]{1,0:T(1,128)}, u32[]{:S(2)}) copy-start(s32[1,128]{1,0:T(1,128)} %sends.3) | copy-start | bytes 1540
  0.6 0.7 %copy-start.10 = (s32[1,256]{1,0:T(1,128)S(1)}, s32[1,256]{1,0:T(1,128)}, u32[]{:S(2)}) copy-start(s32[1,256]{1,0:T(1,128)} %arrive.3) | copy-start | bytes 3076
  0.7 0.9 %copy-start = (bf16[1,256,128]{2,1,0:T(8,128)(2,1)S(1)}, bf16[1,256,128]{2,1,0:T(8,128)(2,1)}, u32[]{:S(2)}) copy-start(bf16[1,256,128]{2,1,0:T(8,128)(2,1)} %nodes.3) | copy-start | bytes 196612
  0.7 0.8 %copy-start.11 = (s32[1,64]{1,0:T(1,128)S(1)}, s32[1,64]{1,0:T(1,128)}, u32[]{:S(2)}) copy-start(s32[1,64]{1,0:T(1,128)} %leave.1) | copy-start | bytes 772
  1.5 9.6 %copy-start.1 = (bf16[1,256,128]{2,1,0:T(8,128)(2,1)S(1)}, bf16[1,256,128]{2,1,0:T(8,128)(2,1)}, u32[]{:S(2)}) copy-start(bf16[1,256,128]{2,1,0:T(8,128)(2,1)} %cotangent.3) | copy-start | bytes 196612
  1.5 9.6 %copy-start.2 = (s32[1,256,32]{1,2,0:T(8,128)S(1)}, s32[1,256,32]{1,2,0:T(8,128)}, u32[]{:S(2)}) copy-start(s32[1,256,32]{1,2,0:T(8,128)} %param.17) | copy-start | bytes 98308
  1.5 9.6 %copy-start.3 = (s32[1,256,32]{1,2,0:T(8,128)S(1)}, s32[1,256,32]{1,2,0:T(8,128)}, u32[]{:S(2)}) copy-start(s32[1,256,32]{1,2,0:T(8,128)} %param.18) | copy-start | bytes 98308
  1.5 9.6 %copy-start.4 = (bf16[128,128]{1,0:T(8,128)(2,1)S(1)}, bf16[128,128]{1,0:T(8,128)(2,1)}, u32[]{:S(2)}) copy-start(bf16[128,128]{1,0:T(8,128)(2,1)} %w_msg.1) | copy-start | bytes 98308
  1.5 9.6 %copy-start.5 = (bf16[128,128]{1,0:T(8,128)(2,1)S(1)}, bf16[128,128]{1,0:T(8,128)(2,1)}, u32[]{:S(2)}) copy-start(bf16[128,128]{1,0:T(8,128)(2,1)} %w_agg.1) | copy-start | bytes 98308
  1.5 9.6 %copy-start.6 = (bf16[128,128]{1,0:T(8,128)(2,1)S(1)}, bf16[128,128]{1,0:T(8,128)(2,1)}, u32[]{:S(2)}) copy-start(bf16[128,128]{1,0:T(8,128)(2,1)} %w_out.1) | copy-start | bytes 98308
  1.6 9.6 %copy-start.7 = (bf16[128,128]{1,0:T(8,128)(2,1)S(1)}, bf16[128,128]{1,0:T(8,128)(2,1)}, u32[]{:S(2)}) copy-start(bf16[128,128]{1,0:T(8,128)(2,1)} %w_send.3) | copy-start | bytes 98308
  1.6 9.6 %copy-start.8 = (bf16[128,128]{1,0:T(8,128)(2,1)S(1)}, bf16[128,128]{1,0:T(8,128)(2,1)}, u32[]{:S(2)}) copy-start(bf16[128,128]{1,0:T(8,128)(2,1)} %w_recv.3) | copy-start | bytes 98308
  1.6 9.6 %copy-start.9 = (bf16[128,128]{1,0:T(8,128)(2,1)S(1)}, bf16[128,128]{1,0:T(8,128)(2,1)}, u32[]{:S(2)}) copy-start(bf16[128,128]{1,0:T(8,128)(2,1)} %w_self.3) | copy-start | bytes 98308
  1.9 9.2 %collective-permute-start.1 = (bf16[128,128]{1,0:T(8,128)(2,1)S(1)}, bf16[128,128]{1,0:T(8,128)(2,1)S(1)}, u32[]{:S(2)}, u32[]{:S(2)}) collective-permute-start(bf16[128,128]{1,0:T(8,128)(2,1)S(1)} %get-tuple-element.16), channel_id=1, source_target_pairs={{0,2},{1,3},{2,4},{3,5},{4,6},{5,7},{6,8},{7,9},{8,10},{9,11},{10,... | collective-permute-start | bytes 98312 | tf_op jit(solution)/shard_map/ppermute | solution.py:328
  5.0 6.1 %collective-permute-start = (bf16[128,128]{1,0:T(8,128)(2,1)S(1)}, bf16[128,128]{1,0:T(8,128)(2,1)S(1)}, u32[]{:S(2)}, u32[]{:S(2)}) collective-permute-start(bf16[128,128]{1,0:T(8,128)(2,1)S(1)} %get-tuple-element.14.my_up), channel_id=1, source_target_pairs={{0,1},{1,2},{2,3},{3,4},{4,5},{5,6},{6,7},{7,8},{8,9},{9,10},{10,1... | collective-permute-start | bytes 98312 | tf_op jit(solution)/shard_map/ppermute | solution.py:328
  5.0 4.7 %collective-permute-start.3 = (bf16[112,128]{1,0:T(8,128)(2,1)S(1)}, bf16[112,128]{1,0:T(8,128)(2,1)S(1)}, u32[]{:S(2)}, u32[]{:S(2)}) collective-permute-start(bf16[112,128]{1,0:T(8,128)(2,1)S(1)} %get-tuple-element.17), channel_id=1, source_target_pairs={{0,14},{1,15},{2,0},{3,1},{4,2},{5,3},{6,4},{7,5},{8,6},{9,7},{10,... | collective-permute-start | bytes 86024 | tf_op jit(solution)/shard_map/ppermute | solution.py:328
  8.1 3.0 %collective-permute-start.2 = (bf16[112,128]{1,0:T(8,128)(2,1)S(1)}, bf16[112,128]{1,0:T(8,128)(2,1)S(1)}, u32[]{:S(2)}, u32[]{:S(2)}) collective-permute-start(bf16[112,128]{1,0:T(8,128)(2,1)S(1)} %get-tuple-element.15.my_down), channel_id=1, source_target_pairs={{0,15},{1,0},{2,1},{3,2},{4,3},{5,4},{6,5},{7,6},{8,7},{9,8},{10,9... | collective-permute-start | bytes 86024 | tf_op jit(solution)/shard_map/ppermute | solution.py:328
  37.9 12.2 %all-to-all-start.1 = ((bf16[32,24,128]{2,1,0:T(8,128)(2,1)}), bf16[32,24,128]{2,1,0:T(8,128)(2,1)S(1)}, u32[]{:S(2)}, u32[]{:S(2)}) async-start(bf16[32,24,128]{2,1,0:T(8,128)(2,1)} %shard_map.152), calls=%async_computation.1 | async-start | bytes 393216 | tf_op jit(solution)/shard_map/all_to_all | solution.py:408
  40.5 8.7 %collective-permute-start.4 = (bf16[64,128]{1,0:T(8,128)(2,1)S(1)}, bf16[64,128]{1,0:T(8,128)(2,1)S(1)}, u32[]{:S(2)}, u32[]{:S(2)}) collective-permute-start(bf16[64,128]{1,0:T(8,128)(2,1)S(1)} %get-tuple-element.22), channel_id=1, source_target_pairs={{0,1},{1,2},{2,3},{3,4},{4,5},{5,6},{6,7},{7,8},{8,9},{9,10},{10,1... | collective-permute-start | bytes 49160 | tf_op jit(solution)/shard_map/ppermute | solution.py:328
  40.9 8.2 %collective-permute-start.5 = (bf16[64,128]{1,0:T(8,128)(2,1)S(1)}, bf16[64,128]{1,0:T(8,128)(2,1)S(1)}, u32[]{:S(2)}, u32[]{:S(2)}) collective-permute-start(bf16[64,128]{1,0:T(8,128)(2,1)S(1)} %get-tuple-element.23), channel_id=1, source_target_pairs={{0,15},{1,0},{2,1},{3,2},{4,3},{5,4},{6,5},{7,6},{8,7},{9,8},{10,9... | collective-permute-start | bytes 49160 | tf_op jit(solution)/shard_map/ppermute | solution.py:328

commit v5 on v4

--- a/solution.py
+++ b/solution.py
@@ -12,7 +12,7 @@
 CODE_ROWS = 16
 LANES = 128
 FAR = -1e30
-PAIRS = 4
+PAIRS = 8
 
 
 def nn(left, right):

time: 51.2 us -> 50 us (0.977)
  Pallas kernels: 14.3 us -> 13.2 us
    pallas_call x1, Pallas kernels: 11.5 us -> 10.3 us  [shards(): call(layer_kernel, [((1, rows, width), BF16), ((border, width), BF16), ((...]
where the time goes in v5:
time: 50 us; the launch traced here: 49.8 us
  starting transfers between devices  14.7 us (29%)
  blocking collectives  14.5 us (29%)
  Pallas kernels  13.2 us (26%)
  waiting for transfers between devices  5.76 us (12%)
  local copies, waits for them, and re-layouts  0.88 us (2%)
  between operations  0.82 us (2%)
    all_to_all x1, blocking collectives, shards(): lax.all_to_all(grads.reshape(devices, share, width), axes, split_axis=0,...  14.5 us
    ppermute x6, starting transfers between devices, shift(): lax.ppermute(array, 'slab', [(i, (i + by) % size) for i in range(size)])  12.1 us
    pallas_call x1, Pallas kernels, shards(): call(layer_kernel, [((1, rows, width), BF16), ((border, width), BF16), ((...  10.3 us
    ppermute x6, waiting for transfers between devices, shift(): lax.ppermute(array, 'slab', [(i, (i + by) % size) for i in range(size)])  5.75 us
    all_to_all x1, starting transfers between devices, shards(): lax.all_to_all(shared, axes, split_axis=0, concat_axis=0, tiled=True)  2.59 us
  transfers between devices with their start and end apart: 7, of which 3 were waited for; matrix products, arithmetic and copies ran while one was open for 0% of the time, Pallas kernels for 2%

profile of v5, /device:TPU:0, one launch (start us, length us, event | category | flops | bytes accessed | tf_op | source)
XLA Modules:
  0.0 49.8 jit_solution(5259267695735663285)
XLA Ops:
  0.6 0.0 copy-start.12
  0.6 0.0 copy-start.10
  0.7 0.6 %copy-done.12 = s32[1,128]{1,0:T(1,128)S(1)} copy-done((s32[1,128]{1,0:T(1,128)S(1)}, s32[1,128]{1,0:T(1,128)}, u32[]{:S(2)}) %copy-start.12) | copy-done | bytes 536
  1.3 0.0 copy-done.10
  1.3 0.2 copy-done
  1.5 0.0 copy-done.11
  1.5 0.0 copy-start.4
  1.5 0.0 copy-start.5
  1.5 0.0 copy-start.6
  1.6 0.0 copy-start.7
  1.6 0.0 copy-start.8
  1.6 0.0 copy-start.9
  1.6 0.3 shard_map.149
  1.9 3.0 %collective-permute-start.1 = (bf16[128,128]{1,0:T(8,128)(2,1)S(1)}, bf16[128,128]{1,0:T(8,128)(2,1)S(1)}, u32[]{:S(2)}, u32[]{:S(2)}) collective-permute-start(bf16[128,128]{1,0:T(8,128)(2,1)S(1)} %get-tuple-element.16), channel_id=1, source_target_pairs={{0,2},{1,3},{2,4},{3,5},{4,6},{5,7},{6,8},{7,9},{8,10},{9,11},{10,... | collective-permute-start | bytes 98312 | tf_op jit(solution)/shard_map/ppermute | solution.py:328
  5.0 0.0 collective-permute-start
  5.0 3.2 %collective-permute-start.3 = (bf16[112,128]{1,0:T(8,128)(2,1)S(1)}, bf16[112,128]{1,0:T(8,128)(2,1)S(1)}, u32[]{:S(2)}, u32[]{:S(2)}) collective-permute-start(bf16[112,128]{1,0:T(8,128)(2,1)S(1)} %get-tuple-element.17), channel_id=1, source_target_pairs={{0,14},{1,15},{2,0},{3,1},{4,2},{5,3},{6,4},{7,5},{8,6},{9,7},{10,... | collective-permute-start | bytes 86024 | tf_op jit(solution)/shard_map/ppermute | solution.py:328
  8.1 1.4 %collective-permute-start.2 = (bf16[112,128]{1,0:T(8,128)(2,1)S(1)}, bf16[112,128]{1,0:T(8,128)(2,1)S(1)}, u32[]{:S(2)}, u32[]{:S(2)}) collective-permute-start(bf16[112,128]{1,0:T(8,128)(2,1)S(1)} %get-tuple-element.15.my_down), channel_id=1, source_target_pairs={{0,15},{1,0},{2,1},{3,2},{4,3},{5,4},{6,5},{7,6},{8,7},{9,8},{10,9... | collective-permute-start | bytes 86024 | tf_op jit(solution)/shard_map/ppermute | solution.py:328
  9.5 0.2 collective-permute-done.3.high_far
  9.7 1.4 %collective-permute-done.2.high = bf16[112,128]{1,0:T(8,128)(2,1)S(1)} collective-permute-done((bf16[112,128]{1,0:T(8,128)(2,1)S(1)}, bf16[112,128]{1,0:T(8,128)(2,1)S(1)}, u32[]{:S(2)}, u32[]{:S(2)}) %collective-permute-start.2) | collective-permute-done | bytes 28704 | tf_op jit(solution)/shard_map/ppermute | solution.py:328
  11.1 0.0 collective-permute-done.1.low_far
  11.1 0.0 collective-permute-done.low
  11.2 10.3 %shard_map.150 = (bf16[1,256,128]{2,1,0:T(8,128)(2,1)}, bf16[64,128]{1,0:T(8,128)(2,1)S(1)}, bf16[64,128]{1,0:T(8,128)(2,1)S(1)}, bf16[768,128]{1,0:T(8,128)(2,1...) custom-call(bf16[1,256,128]{2,1,0:T(8,128)(2,1)S(1)} %copy-done, ...), custom_call_target="tpu_custom_call" | custom-call | flops 2000000000 | bytes 1024 | tf_op jit(solution)/shard_map/pallas_call | solution.py:362
  21.5 14.5 %all_to_all.10.parts = bf16[32,24,128]{2,1,0:T(8,128)(2,1)S(1)} all-to-all(bf16[32,24,128]{2,1,0:T(8,128)(2,1)S(1)} %bitcast.5), channel_id=1, replica_groups=mesh['grp'=2,'slab'=16] {'grp','slab'}, dimensions={0} | all-to-all | bytes 393216 | tf_op jit(solution)/shard_map/all_to_all | solution.py:388
  36.0 0.7 %shard_map.152 = bf16[32,24,128]{2,1,0:T(8,128)(2,1)} custom-call(bf16[32,24,128]{2,1,0:T(8,128)(2,1)S(1)} %all_to_all.10.parts), custom_call_target="tpu_custom_call" | custom-call | flops 2000000000 | bytes 1024 | tf_op jit(solution)/shard_map/pallas_call | solution.py:407
  36.7 2.6 %all-to-all-start.1 = ((bf16[32,24,128]{2,1,0:T(8,128)(2,1)}), bf16[32,24,128]{2,1,0:T(8,128)(2,1)S(1)}, u32[]{:S(2)}, u32[]{:S(2)}) async-start(bf16[32,24,128]{2,1,0:T(8,128)(2,1)} %shard_map.152), calls=%async_computation.1 | async-start | bytes 393216 | tf_op jit(solution)/shard_map/all_to_all | solution.py:408
  39.3 0.4 collective-permute-start.4
  39.8 4.0 %collective-permute-start.5 = (bf16[64,128]{1,0:T(8,128)(2,1)S(1)}, bf16[64,128]{1,0:T(8,128)(2,1)S(1)}, u32[]{:S(2)}, u32[]{:S(2)}) collective-permute-start(bf16[64,128]{1,0:T(8,128)(2,1)S(1)} %get-tuple-element.23), channel_id=1, source_target_pairs={{0,15},{1,0},{2,1},{3,2},{4,3},{5,4},{6,5},{7,6},{8,7},{9,8},{10,9... | collective-permute-start | bytes 49160 | tf_op jit(solution)/shard_map/ppermute | solution.py:328
  43.8 4.2 %collective-permute-done.4.from_low = bf16[64,128]{1,0:T(8,128)(2,1)S(1)} collective-permute-done((bf16[64,128]{1,0:T(8,128)(2,1)S(1)}, bf16[64,128]{1,0:T(8,128)(2,1)S(1)}, u32[]{:S(2)}, u32[]{:S(2)}) %collective-permute-start.4) | collective-permute-done | bytes 16416 | tf_op jit(solution)/shard_map/ppermute | solution.py:328
  48.0 0.0 collective-permute-done.5.from_high
  48.0 0.9 %shard_map.151 = bf16[1,256,128]{2,1,0:T(8,128)(2,1)} custom-call(bf16[1,256,128]{2,1,0:T(8,128)(2,1)S(1)} %copy-done.1, bf16[256,128]{1,0:T(8,128)(2,1)S(1)} %get-tuple-element.19.d_node, bf16[256,128]{1,0:T(8,128)(2,1)S(1)} %get-tuple-element.20.d_centre, bf16[256,128]{1,0:T(8,128)(2,1)S(1)} %get-tuple-element.21.d_neigh, bf16[128,128]{1,0:T(8,128)(2,1)S(1)} %copy-done.9, ...), custom_call_target="tpu_custom_call" | custom-call | flops 2000000000 | bytes 1024 | tf_op jit(solution)/shard_map/pallas_call | solution.py:403
  48.9 0.0 all-to-all-done.1
  48.9 0.9 %shard_map.153 = f32[6,128,128]{2,1,0:T(8,128)} custom-call(bf16[768,128]{1,0:T(8,128)(2,1)S(1)} %bitcast.4), custom_call_target="tpu_custom_call" | custom-call | flops 2000000000 | bytes 1024 | tf_op jit(solution)/shard_map/pallas_call | solution.py:410
  (15 shorter events, 0.0 us)
Async XLA Ops:
  0.6 0.7 %copy-start.12 = (s32[1,128]{1,0:T(1,128)S(1)}, s32[1,128]{1,0:T(1,128)}, u32[]{:S(2)}) copy-start(s32[1,128]{1,0:T(1,128)} %sends.3) | copy-start | bytes 1540
  0.6 0.7 %copy-start.10 = (s32[1,256]{1,0:T(1,128)S(1)}, s32[1,256]{1,0:T(1,128)}, u32[]{:S(2)}) copy-start(s32[1,256]{1,0:T(1,128)} %arrive.3) | copy-start | bytes 3076
  0.7 0.9 %copy-start = (bf16[1,256,128]{2,1,0:T(8,128)(2,1)S(1)}, bf16[1,256,128]{2,1,0:T(8,128)(2,1)}, u32[]{:S(2)}) copy-start(bf16[1,256,128]{2,1,0:T(8,128)(2,1)} %nodes.3) | copy-start | bytes 196612
  0.7 0.8 %copy-start.11 = (s32[1,64]{1,0:T(1,128)S(1)}, s32[1,64]{1,0:T(1,128)}, u32[]{:S(2)}) copy-start(s32[1,64]{1,0:T(1,128)} %leave.1) | copy-start | bytes 772
  1.5 9.6 %copy-start.1 = (bf16[1,256,128]{2,1,0:T(8,128)(2,1)S(1)}, bf16[1,256,128]{2,1,0:T(8,128)(2,1)}, u32[]{:S(2)}) copy-start(bf16[1,256,128]{2,1,0:T(8,128)(2,1)} %cotangent.3) | copy-start | bytes 196612
  1.5 9.6 %copy-start.2 = (s32[1,256,32]{1,2,0:T(8,128)S(1)}, s32[1,256,32]{1,2,0:T(8,128)}, u32[]{:S(2)}) copy-start(s32[1,256,32]{1,2,0:T(8,128)} %param.17) | copy-start | bytes 98308
  1.5 9.6 %copy-start.3 = (s32[1,256,32]{1,2,0:T(8,128)S(1)}, s32[1,256,32]{1,2,0:T(8,128)}, u32[]{:S(2)}) copy-start(s32[1,256,32]{1,2,0:T(8,128)} %param.18) | copy-start | bytes 98308
  1.5 9.6 %copy-start.4 = (bf16[128,128]{1,0:T(8,128)(2,1)S(1)}, bf16[128,128]{1,0:T(8,128)(2,1)}, u32[]{:S(2)}) copy-start(bf16[128,128]{1,0:T(8,128)(2,1)} %w_msg.1) | copy-start | bytes 98308
  1.5 9.6 %copy-start.5 = (bf16[128,128]{1,0:T(8,128)(2,1)S(1)}, bf16[128,128]{1,0:T(8,128)(2,1)}, u32[]{:S(2)}) copy-start(bf16[128,128]{1,0:T(8,128)(2,1)} %w_agg.1) | copy-start | bytes 98308
  1.5 9.6 %copy-start.6 = (bf16[128,128]{1,0:T(8,128)(2,1)S(1)}, bf16[128,128]{1,0:T(8,128)(2,1)}, u32[]{:S(2)}) copy-start(bf16[128,128]{1,0:T(8,128)(2,1)} %w_out.1) | copy-start | bytes 98308
  1.6 9.6 %copy-start.7 = (bf16[128,128]{1,0:T(8,128)(2,1)S(1)}, bf16[128,128]{1,0:T(8,128)(2,1)}, u32[]{:S(2)}) copy-start(bf16[128,128]{1,0:T(8,128)(2,1)} %w_send.3) | copy-start | bytes 98308
  1.6 9.6 %copy-start.8 = (bf16[128,128]{1,0:T(8,128)(2,1)S(1)}, bf16[128,128]{1,0:T(8,128)(2,1)}, u32[]{:S(2)}) copy-start(bf16[128,128]{1,0:T(8,128)(2,1)} %w_recv.3) | copy-start | bytes 98308
  1.6 9.6 %copy-start.9 = (bf16[128,128]{1,0:T(8,128)(2,1)S(1)}, bf16[128,128]{1,0:T(8,128)(2,1)}, u32[]{:S(2)}) copy-start(bf16[128,128]{1,0:T(8,128)(2,1)} %w_self.3) | copy-start | bytes 98308
  1.9 9.2 %collective-permute-start.1 = (bf16[128,128]{1,0:T(8,128)(2,1)S(1)}, bf16[128,128]{1,0:T(8,128)(2,1)S(1)}, u32[]{:S(2)}, u32[]{:S(2)}) collective-permute-start(bf16[128,128]{1,0:T(8,128)(2,1)S(1)} %get-tuple-element.16), channel_id=1, source_target_pairs={{0,2},{1,3},{2,4},{3,5},{4,6},{5,7},{6,8},{7,9},{8,10},{9,11},{10,... | collective-permute-start | bytes 98312 | tf_op jit(solution)/shard_map/ppermute | solution.py:328
  5.0 6.1 %collective-permute-start = (bf16[128,128]{1,0:T(8,128)(2,1)S(1)}, bf16[128,128]{1,0:T(8,128)(2,1)S(1)}, u32[]{:S(2)}, u32[]{:S(2)}) collective-permute-start(bf16[128,128]{1,0:T(8,128)(2,1)S(1)} %get-tuple-element.14.my_up), channel_id=1, source_target_pairs={{0,1},{1,2},{2,3},{3,4},{4,5},{5,6},{6,7},{7,8},{8,9},{9,10},{10,1... | collective-permute-start | bytes 98312 | tf_op jit(solution)/shard_map/ppermute | solution.py:328
  5.0 4.7 %collective-permute-start.3 = (bf16[112,128]{1,0:T(8,128)(2,1)S(1)}, bf16[112,128]{1,0:T(8,128)(2,1)S(1)}, u32[]{:S(2)}, u32[]{:S(2)}) collective-permute-start(bf16[112,128]{1,0:T(8,128)(2,1)S(1)} %get-tuple-element.17), channel_id=1, source_target_pairs={{0,14},{1,15},{2,0},{3,1},{4,2},{5,3},{6,4},{7,5},{8,6},{9,7},{10,... | collective-permute-start | bytes 86024 | tf_op jit(solution)/shard_map/ppermute | solution.py:328
  8.1 3.0 %collective-permute-start.2 = (bf16[112,128]{1,0:T(8,128)(2,1)S(1)}, bf16[112,128]{1,0:T(8,128)(2,1)S(1)}, u32[]{:S(2)}, u32[]{:S(2)}) collective-permute-start(bf16[112,128]{1,0:T(8,128)(2,1)S(1)} %get-tuple-element.15.my_down), channel_id=1, source_target_pairs={{0,15},{1,0},{2,1},{3,2},{4,3},{5,4},{6,5},{7,6},{8,7},{9,8},{10,9... | collective-permute-start | bytes 86024 | tf_op jit(solution)/shard_map/ppermute | solution.py:328
  36.7 12.2 %all-to-all-start.1 = ((bf16[32,24,128]{2,1,0:T(8,128)(2,1)}), bf16[32,24,128]{2,1,0:T(8,128)(2,1)S(1)}, u32[]{:S(2)}, u32[]{:S(2)}) async-start(bf16[32,24,128]{2,1,0:T(8,128)(2,1)} %shard_map.152), calls=%async_computation.1 | async-start | bytes 393216 | tf_op jit(solution)/shard_map/all_to_all | solution.py:408
  39.3 8.7 %collective-permute-start.4 = (bf16[64,128]{1,0:T(8,128)(2,1)S(1)}, bf16[64,128]{1,0:T(8,128)(2,1)S(1)}, u32[]{:S(2)}, u32[]{:S(2)}) collective-permute-start(bf16[64,128]{1,0:T(8,128)(2,1)S(1)} %get-tuple-element.22), channel_id=1, source_target_pairs={{0,1},{1,2},{2,3},{3,4},{4,5},{5,6},{6,7},{7,8},{8,9},{9,10},{10,1... | collective-permute-start | bytes 49160 | tf_op jit(solution)/shard_map/ppermute | solution.py:328
  39.8 8.2 %collective-permute-start.5 = (bf16[64,128]{1,0:T(8,128)(2,1)S(1)}, bf16[64,128]{1,0:T(8,128)(2,1)S(1)}, u32[]{:S(2)}, u32[]{:S(2)}) collective-permute-start(bf16[64,128]{1,0:T(8,128)(2,1)S(1)} %get-tuple-element.23), channel_id=1, source_target_pairs={{0,15},{1,0},{2,1},{3,2},{4,3},{5,4},{6,5},{7,6},{8,7},{9,8},{10,9... | collective-permute-start | bytes 49160 | tf_op jit(solution)/shard_map/ppermute | solution.py:328

commit v6 on v5

--- a/solution.py
+++ b/solution.py
@@ -93,6 +93,7 @@
     d_centre_o,
     d_neigh_o,
     nbr_s,
+    row_s,
     neigh_s,
     wide_s,
     hid_s,
@@ -127,16 +128,12 @@
     above = halo(high[...], my_up[border : border + migr], high_far[:migr])
     table = jnp.concatenate([moved, below, above], axis=0)
 
+    half_rows = table_rows // 2
+    hot_rows = -(-(half_rows + 1) // LANES) * LANES
     half_centre = 0.5 * nn(moved, w_send[...])
     half_neigh = (0.5 * nn(table, w_recv[...]).astype(BF16).astype(F32)).astype(BF16)
-    none = jnp.zeros((table_rows, width), BF16)
-    neigh_s[...] = jnp.concatenate(
-        [
-            jnp.concatenate([half_neigh, none], axis=1),
-            jnp.concatenate([none, half_neigh], axis=1),
-        ],
-        axis=0,
-    )
+    neigh_s[:half_rows] = jnp.concatenate([half_neigh[:half_rows], half_neigh[half_rows:]], axis=1)
+    neigh_s[half_rows:] = jnp.full((hot_rows - half_rows, 2 * width), FAR, BF16)
     half_msg = 0.5 * w_msg[...].astype(F32)
     none = jnp.zeros((width, width), F32)
     for part, block in enumerate((half_msg, jnp.transpose(half_msg, (1, 0)))):
@@ -147,39 +144,39 @@
             ],
             axis=0,
         ).astype(BF16)
-    index = jnp.where(valid[0] == 1, nbr[0], -1)
+    upper = nbr[0] >= half_rows
+    low_row = jnp.where(upper, nbr[0] - half_rows, nbr[0])
+    row_s[...] = low_row
+    index = jnp.where(valid[0] == 1, low_row, half_rows) + jnp.where(upper, hot_rows, 0)
     fill = jnp.zeros((LANES - slots, rows), jnp.int32)
     nbr_s[...] = jnp.transpose(jnp.concatenate([index, fill], axis=0), (1, 0))
     agg_s[...] = jnp.zeros_like(agg_s)
 
-    lane = lax.broadcasted_iota(jnp.int32, (rows, table_rows), 1).astype(jnp.int16)
-    one = jnp.ones((rows, table_rows), BF16)
-    zero = jnp.zeros((rows, table_rows), BF16)
+    lane = lax.broadcasted_iota(jnp.int32, (rows, hot_rows), 1).astype(jnp.int16)
+    one = jnp.ones((rows, hot_rows), BF16)
+    zero = jnp.zeros((rows, hot_rows), BF16)
+
+    def slot_ids(step):
+        near = pltpu.roll(nbr_s[...], lax.rem(LANES - step * chunk, LANES), 1)
+        return [jnp.broadcast_to(near[:, j : j + 1], (rows, LANES)) for j in range(chunk)]
 
     @pl.loop(0, steps)
     def forward(step):
-        near = pltpu.roll(nbr_s[...], lax.rem(LANES - step * chunk, LANES), 1)
-        ids = [jnp.broadcast_to(near[:, j : j + 1], (rows, LANES)) for j in range(chunk)]
+        ids = slot_ids(step)
         hots = []
         for j in range(chunk):
-            short = ids[j].astype(jnp.int16)
-            short = jnp.concatenate([short] * (table_rows // LANES), axis=1)
+            short = (ids[j] & (hot_rows - 1)).astype(jnp.int16)
+            short = jnp.concatenate([short] * (hot_rows // LANES), axis=1)
             hots.append(jnp.where(short == lane, one, zero))
-        hot = jnp.concatenate(
-            [
-                jnp.concatenate([hots[2 * p], hots[2 * p + 1]], axis=1)
-                for p in range(PAIRS)
-            ],
-            axis=0,
-        )
-        gathered = nn(hot, neigh_s[...])
+        gathered = nn(jnp.concatenate(hots, axis=0), neigh_s[...])
         base = step * (PAIRS * rows)
         for p in range(PAIRS):
             for side in range(2):
                 cols = slice(side * width, (side + 1) * width)
-                half = half_centre + gathered[p * rows : (p + 1) * rows, cols]
-                half = jnp.where(ids[2 * p + side] < 0, FAR, half)
-                act, slope = silu_parts(half)
+                j = 2 * p + side
+                pick = gathered[j * rows : (j + 1) * rows]
+                pick = jnp.where(ids[j] >= hot_rows, pick[:, width:], pick[:, :width])
+                act, slope = silu_parts(half_centre + pick)
                 span = pl.ds(base + p * rows, rows)
                 ds1_s[span, cols] = slope
                 hid_s[span, cols] = act.astype(BF16)
@@ -205,42 +202,43 @@
     dcen_s[...] = jnp.zeros_like(dcen_s)
     dneigh_s[...] = jnp.zeros_like(dneigh_s)
     gmsg_s[...] = jnp.zeros_like(gmsg_s)
-    sub = lax.broadcasted_iota(jnp.int32, (table_rows, rows), 0).astype(jnp.int16)
-    one_t = jnp.ones((table_rows, rows), BF16)
-    zero_t = jnp.zeros((table_rows, rows), BF16)
-
-    def stack(wide):
-        return jnp.concatenate(
-            [
-                wide[p * rows : (p + 1) * rows, side * width : (side + 1) * width]
-                for p in range(PAIRS)
-                for side in range(2)
-            ],
-            axis=0,
-        )
+    sub = lax.broadcasted_iota(jnp.int32, (half_rows, rows), 0).astype(jnp.int16)
+    one_t = jnp.ones((half_rows, rows), BF16)
+    zero_t = jnp.zeros((half_rows, rows), BF16)
+    none = jnp.zeros((rows, width), BF16)
+    border_id = jnp.full((rows, width), hot_rows, jnp.int16)
 
     @pl.loop(0, steps)
     def backward(step):
+        ids = slot_ids(step)
         span = pl.ds(step * (PAIRS * rows), PAIRS * rows)
         d_agg = jnp.concatenate([half_d_agg, half_d_agg], axis=1)
         d_agg = jnp.concatenate([d_agg] * PAIRS, axis=0)
         d_pre2 = (d_agg * ds2_s[span]).astype(BF16)
         d_pre = nn(d_pre2, wide_s[1]) * ds1_s[span]
-        gmsg_s[...] += tn(stack(hid_s[span]), stack(d_pre2))
-        d_pre = stack(d_pre)
+        gmsg_s[...] += tn(hid_s[span], d_pre2)
         total = dcen_s[...]
+        hots, wides = [], []
         for j in range(chunk):
-            total = total + d_pre[j * rows : (j + 1) * rows]
+            p, side = divmod(j, 2)
+            part = d_pre[p * rows : (p + 1) * rows, side * width : (side + 1) * width]
+            total = total + part
+            part = part.astype(BF16)
+            is_up = ids[j].astype(jnp.int16) >= border_id
+            wides.append(
+                jnp.concatenate(
+                    [jnp.where(is_up, none, part), jnp.where(is_up, part, none)], axis=1
+                )
+            )
+            row = jnp.broadcast_to(row_s[pl.ds(step * chunk + j, 1)], (16, rows))
+            short = jnp.concatenate([row.astype(jnp.int16)] * (half_rows // 16), axis=0)
+            hots.append(jnp.where(short == sub, one_t, zero_t))
         dcen_s[...] = total
-        hots = []
-        for j in range(chunk):
-            row = jnp.broadcast_to(nbr[0, pl.ds(step * chunk + j, 1)], (16, rows))
-            short = jnp.concatenate([row.astype(jnp.int16)] * (table_rows // 16), axis=0)
-            hots.append(jnp.where(short == sub, one_t, zero_t))
-        dneigh_s[...] += nn(jnp.concatenate(hots, axis=1), d_pre.astype(BF16))
+        dneigh_s[...] += nn(jnp.concatenate(hots, axis=1), jnp.concatenate(wides, axis=0))
 
     d_centre = dcen_s[...].astype(BF16)
     d_neigh = dneigh_s[...].astype(BF16)
+    d_neigh = jnp.concatenate([d_neigh[:, :width], d_neigh[:, width:]], axis=0)
     d_borrowed = nt(d_neigh[rows:], w_recv[...]).astype(BF16)
     back_low[...] = d_borrowed[:border]
     back_high[...] = d_borrowed[border:]
@@ -250,7 +248,7 @@
     parts = (
         tn(moved, d_centre),
         tn(table, d_neigh),
-        gmsg_s[...],
+        gmsg_s[:width, :width] + gmsg_s[width:, width:],
         tn(moved, d_node),
         tn(agg_b, d_node),
         tn(node_hid, cot),
@@ -339,6 +337,8 @@
 
     matrices = 6
     pair_rows = rows * slots // 2
+    half_rows = table_rows // 2
+    hot_rows = -(-(half_rows + 1) // LANES) * LANES
     share = -(-matrices * width // (8 * devices)) * 8
     sources = (
         nodes,
@@ -372,15 +372,16 @@
         ],
         [
             pltpu.VMEM((rows, LANES), jnp.int32),
-            pltpu.VMEM((2 * table_rows, 2 * width), BF16),
+            pltpu.VMEM((slots, rows), jnp.int32),
+            pltpu.VMEM((hot_rows, 2 * width), BF16),
             pltpu.VMEM((2, 2 * width, 2 * width), BF16),
             pltpu.VMEM((pair_rows, 2 * width), BF16),
             pltpu.VMEM((pair_rows, 2 * width), F32),
             pltpu.VMEM((pair_rows, 2 * width), F32),
             pltpu.VMEM((rows, width), F32),
             pltpu.VMEM((rows, width), F32),
-            pltpu.VMEM((table_rows, width), F32),
-            pltpu.VMEM((width, width), F32),
+            pltpu.VMEM((half_rows, 2 * width), F32),
+            pltpu.VMEM((2 * width, 2 * width), F32),
         ],
     )(*sources)
     from_low = shift(back_high, 1)

time: 50 us -> 48.4 us (0.968)
  Pallas kernels: 13.2 us -> 11.5 us
    pallas_call x1, Pallas kernels: 10.3 us -> 8.64 us  [shards(): call(layer_kernel, [((1, rows, width), BF16), ((border, width), BF16), ((...]
where the time goes in v6:
time: 48.4 us; the launch traced here: 48.1 us
  starting transfers between devices  14.7 us (30%)
  blocking collectives  14.5 us (30%)
  Pallas kernels  11.5 us (24%)
  waiting for transfers between devices  5.76 us (12%)
  local copies, waits for them, and re-layouts  0.88 us (2%)
  between operations  0.82 us (2%)
    all_to_all x1, blocking collectives, shards(): lax.all_to_all(grads.reshape(devices, share, width), axes, split_axis=0,...  14.5 us
    ppermute x6, starting transfers between devices, shift(): lax.ppermute(array, 'slab', [(i, (i + by) % size) for i in range(size)])  12.1 us
    pallas_call x1, Pallas kernels, shards(): call(layer_kernel, [((1, rows, width), BF16), ((border, width), BF16), ((...  8.64 us
    ppermute x6, waiting for transfers between devices, shift(): lax.ppermute(array, 'slab', [(i, (i + by) % size) for i in range(size)])  5.75 us
    all_to_all x1, starting transfers between devices, shards(): lax.all_to_all(shared, axes, split_axis=0, concat_axis=0, tiled=True)  2.59 us
  transfers between devices with their start and end apart: 7, of which 3 were waited for; matrix products, arithmetic and copies ran while one was open for 0% of the time, Pallas kernels for 2%

profile of v6, /device:TPU:0, one launch (start us, length us, event | category | flops | bytes accessed | tf_op | source)
XLA Modules:
  0.0 48.1 jit_solution(2126051974230493055)
XLA Ops:
  0.6 0.0 copy-start.12
  0.6 0.0 copy-start.10
  0.7 0.0 copy-start
  0.7 0.6 %copy-done.12 = s32[1,128]{1,0:T(1,128)S(1)} copy-done((s32[1,128]{1,0:T(1,128)S(1)}, s32[1,128]{1,0:T(1,128)}, u32[]{:S(2)}) %copy-start.12) | copy-done | bytes 536
  1.3 0.0 copy-done.10
  1.3 0.2 copy-done
  1.5 0.0 copy-start.4
  1.5 0.0 copy-start.5
  1.5 0.0 copy-start.6
  1.6 0.0 copy-start.7
  1.6 0.0 copy-start.8
  1.6 0.0 copy-start.9
  1.6 0.3 shard_map.149
  1.9 3.0 %collective-permute-start.1 = (bf16[128,128]{1,0:T(8,128)(2,1)S(1)}, bf16[128,128]{1,0:T(8,128)(2,1)S(1)}, u32[]{:S(2)}, u32[]{:S(2)}) collective-permute-start(bf16[128,128]{1,0:T(8,128)(2,1)S(1)} %get-tuple-element.16), channel_id=1, source_target_pairs={{0,2},{1,3},{2,4},{3,5},{4,6},{5,7},{6,8},{7,9},{8,10},{9,11},{10,... | collective-permute-start | bytes 98312 | tf_op jit(solution)/shard_map/ppermute | solution.py:326
  5.0 0.0 collective-permute-start
  5.0 3.2 %collective-permute-start.3 = (bf16[112,128]{1,0:T(8,128)(2,1)S(1)}, bf16[112,128]{1,0:T(8,128)(2,1)S(1)}, u32[]{:S(2)}, u32[]{:S(2)}) collective-permute-start(bf16[112,128]{1,0:T(8,128)(2,1)S(1)} %get-tuple-element.17), channel_id=1, source_target_pairs={{0,14},{1,15},{2,0},{3,1},{4,2},{5,3},{6,4},{7,5},{8,6},{9,7},{10,... | collective-permute-start | bytes 86024 | tf_op jit(solution)/shard_map/ppermute | solution.py:326
  8.1 1.4 %collective-permute-start.2 = (bf16[112,128]{1,0:T(8,128)(2,1)S(1)}, bf16[112,128]{1,0:T(8,128)(2,1)S(1)}, u32[]{:S(2)}, u32[]{:S(2)}) collective-permute-start(bf16[112,128]{1,0:T(8,128)(2,1)S(1)} %get-tuple-element.15.my_down), channel_id=1, source_target_pairs={{0,15},{1,0},{2,1},{3,2},{4,3},{5,4},{6,5},{7,6},{8,7},{9,8},{10,9... | collective-permute-start | bytes 86024 | tf_op jit(solution)/shard_map/ppermute | solution.py:326
  9.5 0.2 collective-permute-done.3.high_far
  9.7 1.4 %collective-permute-done.2.high = bf16[112,128]{1,0:T(8,128)(2,1)S(1)} collective-permute-done((bf16[112,128]{1,0:T(8,128)(2,1)S(1)}, bf16[112,128]{1,0:T(8,128)(2,1)S(1)}, u32[]{:S(2)}, u32[]{:S(2)}) %collective-permute-start.2) | collective-permute-done | bytes 28704 | tf_op jit(solution)/shard_map/ppermute | solution.py:326
  11.1 0.0 collective-permute-done.1.low_far
  11.1 0.0 collective-permute-done.low
  11.2 8.6 %shard_map.150 = (bf16[1,256,128]{2,1,0:T(8,128)(2,1)}, bf16[64,128]{1,0:T(8,128)(2,1)S(1)}, bf16[64,128]{1,0:T(8,128)(2,1)S(1)}, bf16[768,128]{1,0:T(8,128)(2,1...) custom-call(bf16[1,256,128]{2,1,0:T(8,128)(2,1)S(1)} %copy-done, ...), custom_call_target="tpu_custom_call" | custom-call | flops 2000000000 | bytes 1024 | tf_op jit(solution)/shard_map/pallas_call | solution.py:362
  19.8 14.5 %all_to_all.10.parts = bf16[32,24,128]{2,1,0:T(8,128)(2,1)S(1)} all-to-all(bf16[32,24,128]{2,1,0:T(8,128)(2,1)S(1)} %bitcast.5), channel_id=1, replica_groups=mesh['grp'=2,'slab'=16] {'grp','slab'}, dimensions={0} | all-to-all | bytes 393216 | tf_op jit(solution)/shard_map/all_to_all | solution.py:389
  34.3 0.7 %shard_map.152 = bf16[32,24,128]{2,1,0:T(8,128)(2,1)} custom-call(bf16[32,24,128]{2,1,0:T(8,128)(2,1)S(1)} %all_to_all.10.parts), custom_call_target="tpu_custom_call" | custom-call | flops 2000000000 | bytes 1024 | tf_op jit(solution)/shard_map/pallas_call | solution.py:408
  35.1 2.6 %all-to-all-start.1 = ((bf16[32,24,128]{2,1,0:T(8,128)(2,1)}), bf16[32,24,128]{2,1,0:T(8,128)(2,1)S(1)}, u32[]{:S(2)}, u32[]{:S(2)}) async-start(bf16[32,24,128]{2,1,0:T(8,128)(2,1)} %shard_map.152), calls=%async_computation.1 | async-start | bytes 393216 | tf_op jit(solution)/shard_map/all_to_all | solution.py:409
  37.7 0.4 collective-permute-start.4
  38.1 4.0 %collective-permute-start.5 = (bf16[64,128]{1,0:T(8,128)(2,1)S(1)}, bf16[64,128]{1,0:T(8,128)(2,1)S(1)}, u32[]{:S(2)}, u32[]{:S(2)}) collective-permute-start(bf16[64,128]{1,0:T(8,128)(2,1)S(1)} %get-tuple-element.23), channel_id=1, source_target_pairs={{0,15},{1,0},{2,1},{3,2},{4,3},{5,4},{6,5},{7,6},{8,7},{9,8},{10,9... | collective-permute-start | bytes 49160 | tf_op jit(solution)/shard_map/ppermute | solution.py:326
  42.1 4.2 %collective-permute-done.4.from_low = bf16[64,128]{1,0:T(8,128)(2,1)S(1)} collective-permute-done((bf16[64,128]{1,0:T(8,128)(2,1)S(1)}, bf16[64,128]{1,0:T(8,128)(2,1)S(1)}, u32[]{:S(2)}, u32[]{:S(2)}) %collective-permute-start.4) | collective-permute-done | bytes 16416 | tf_op jit(solution)/shard_map/ppermute | solution.py:326
  46.3 0.0 collective-permute-done.5.from_high
  46.3 0.9 %shard_map.151 = bf16[1,256,128]{2,1,0:T(8,128)(2,1)} custom-call(bf16[1,256,128]{2,1,0:T(8,128)(2,1)S(1)} %copy-done.1, bf16[256,128]{1,0:T(8,128)(2,1)S(1)} %get-tuple-element.19.d_node, bf16[256,128]{1,0:T(8,128)(2,1)S(1)} %get-tuple-element.20.d_centre, bf16[256,128]{1,0:T(8,128)(2,1)S(1)} %get-tuple-element.21.d_neigh, bf16[128,128]{1,0:T(8,128)(2,1)S(1)} %copy-done.9, ...), custom_call_target="tpu_custom_call" | custom-call | flops 2000000000 | bytes 1024 | tf_op jit(solution)/shard_map/pallas_call | solution.py:404
  47.2 0.0 all-to-all-done.1
  47.2 0.9 %shard_map.153 = f32[6,128,128]{2,1,0:T(8,128)} custom-call(bf16[768,128]{1,0:T(8,128)(2,1)S(1)} %bitcast.4), custom_call_target="tpu_custom_call" | custom-call | flops 2000000000 | bytes 1024 | tf_op jit(solution)/shard_map/pallas_call | solution.py:411
  (15 shorter events, 0.0 us)
Async XLA Ops:
  0.6 0.7 %copy-start.12 = (s32[1,128]{1,0:T(1,128)S(1)}, s32[1,128]{1,0:T(1,128)}, u32[]{:S(2)}) copy-start(s32[1,128]{1,0:T(1,128)} %sends.3) | copy-start | bytes 1540
  0.6 0.7 %copy-start.10 = (s32[1,256]{1,0:T(1,128)S(1)}, s32[1,256]{1,0:T(1,128)}, u32[]{:S(2)}) copy-start(s32[1,256]{1,0:T(1,128)} %arrive.3) | copy-start | bytes 3076
  0.7 0.9 %copy-start = (bf16[1,256,128]{2,1,0:T(8,128)(2,1)S(1)}, bf16[1,256,128]{2,1,0:T(8,128)(2,1)}, u32[]{:S(2)}) copy-start(bf16[1,256,128]{2,1,0:T(8,128)(2,1)} %nodes.3) | copy-start | bytes 196612
  0.7 0.8 %copy-start.11 = (s32[1,64]{1,0:T(1,128)S(1)}, s32[1,64]{1,0:T(1,128)}, u32[]{:S(2)}) copy-start(s32[1,64]{1,0:T(1,128)} %leave.1) | copy-start | bytes 772
  1.5 9.6 %copy-start.1 = (bf16[1,256,128]{2,1,0:T(8,128)(2,1)S(1)}, bf16[1,256,128]{2,1,0:T(8,128)(2,1)}, u32[]{:S(2)}) copy-start(bf16[1,256,128]{2,1,0:T(8,128)(2,1)} %cotangent.3) | copy-start | bytes 196612
  1.5 9.6 %copy-start.2 = (s32[1,256,32]{1,2,0:T(8,128)S(1)}, s32[1,256,32]{1,2,0:T(8,128)}, u32[]{:S(2)}) copy-start(s32[1,256,32]{1,2,0:T(8,128)} %param.17) | copy-start | bytes 98308
  1.5 9.6 %copy-start.3 = (s32[1,256,32]{1,2,0:T(8,128)S(1)}, s32[1,256,32]{1,2,0:T(8,128)}, u32[]{:S(2)}) copy-start(s32[1,256,32]{1,2,0:T(8,128)} %param.18) | copy-start | bytes 98308
  1.5 9.6 %copy-start.4 = (bf16[128,128]{1,0:T(8,128)(2,1)S(1)}, bf16[128,128]{1,0:T(8,128)(2,1)}, u32[]{:S(2)}) copy-start(bf16[128,128]{1,0:T(8,128)(2,1)} %w_msg.1) | copy-start | bytes 98308
  1.5 9.6 %copy-start.5 = (bf16[128,128]{1,0:T(8,128)(2,1)S(1)}, bf16[128,128]{1,0:T(8,128)(2,1)}, u32[]{:S(2)}) copy-start(bf16[128,128]{1,0:T(8,128)(2,1)} %w_agg.1) | copy-start | bytes 98308
  1.5 9.6 %copy-start.6 = (bf16[128,128]{1,0:T(8,128)(2,1)S(1)}, bf16[128,128]{1,0:T(8,128)(2,1)}, u32[]{:S(2)}) copy-start(bf16[128,128]{1,0:T(8,128)(2,1)} %w_out.1) | copy-start | bytes 98308
  1.6 9.6 %copy-start.7 = (bf16[128,128]{1,0:T(8,128)(2,1)S(1)}, bf16[128,128]{1,0:T(8,128)(2,1)}, u32[]{:S(2)}) copy-start(bf16[128,128]{1,0:T(8,128)(2,1)} %w_send.3) | copy-start | bytes 98308
  1.6 9.6 %copy-start.8 = (bf16[128,128]{1,0:T(8,128)(2,1)S(1)}, bf16[128,128]{1,0:T(8,128)(2,1)}, u32[]{:S(2)}) copy-start(bf16[128,128]{1,0:T(8,128)(2,1)} %w_recv.3) | copy-start | bytes 98308
  1.6 9.6 %copy-start.9 = (bf16[128,128]{1,0:T(8,128)(2,1)S(1)}, bf16[128,128]{1,0:T(8,128)(2,1)}, u32[]{:S(2)}) copy-start(bf16[128,128]{1,0:T(8,128)(2,1)} %w_self.3) | copy-start | bytes 98308
  1.9 9.2 %collective-permute-start.1 = (bf16[128,128]{1,0:T(8,128)(2,1)S(1)}, bf16[128,128]{1,0:T(8,128)(2,1)S(1)}, u32[]{:S(2)}, u32[]{:S(2)}) collective-permute-start(bf16[128,128]{1,0:T(8,128)(2,1)S(1)} %get-tuple-element.16), channel_id=1, source_target_pairs={{0,2},{1,3},{2,4},{3,5},{4,6},{5,7},{6,8},{7,9},{8,10},{9,11},{10,... | collective-permute-start | bytes 98312 | tf_op jit(solution)/shard_map/ppermute | solution.py:326
  5.0 6.1 %collective-permute-start = (bf16[128,128]{1,0:T(8,128)(2,1)S(1)}, bf16[128,128]{1,0:T(8,128)(2,1)S(1)}, u32[]{:S(2)}, u32[]{:S(2)}) collective-permute-start(bf16[128,128]{1,0:T(8,128)(2,1)S(1)} %get-tuple-element.14.my_up), channel_id=1, source_target_pairs={{0,1},{1,2},{2,3},{3,4},{4,5},{5,6},{6,7},{7,8},{8,9},{9,10},{10,1... | collective-permute-start | bytes 98312 | tf_op jit(solution)/shard_map/ppermute | solution.py:326
  5.0 4.7 %collective-permute-start.3 = (bf16[112,128]{1,0:T(8,128)(2,1)S(1)}, bf16[112,128]{1,0:T(8,128)(2,1)S(1)}, u32[]{:S(2)}, u32[]{:S(2)}) collective-permute-start(bf16[112,128]{1,0:T(8,128)(2,1)S(1)} %get-tuple-element.17), channel_id=1, source_target_pairs={{0,14},{1,15},{2,0},{3,1},{4,2},{5,3},{6,4},{7,5},{8,6},{9,7},{10,... | collective-permute-start | bytes 86024 | tf_op jit(solution)/shard_map/ppermute | solution.py:326
  8.1 3.0 %collective-permute-start.2 = (bf16[112,128]{1,0:T(8,128)(2,1)S(1)}, bf16[112,128]{1,0:T(8,128)(2,1)S(1)}, u32[]{:S(2)}, u32[]{:S(2)}) collective-permute-start(bf16[112,128]{1,0:T(8,128)(2,1)S(1)} %get-tuple-element.15.my_down), channel_id=1, source_target_pairs={{0,15},{1,0},{2,1},{3,2},{4,3},{5,4},{6,5},{7,6},{8,7},{9,8},{10,9... | collective-permute-start | bytes 86024 | tf_op jit(solution)/shard_map/ppermute | solution.py:326
  35.1 12.2 %all-to-all-start.1 = ((bf16[32,24,128]{2,1,0:T(8,128)(2,1)}), bf16[32,24,128]{2,1,0:T(8,128)(2,1)S(1)}, u32[]{:S(2)}, u32[]{:S(2)}) async-start(bf16[32,24,128]{2,1,0:T(8,128)(2,1)} %shard_map.152), calls=%async_computation.1 | async-start | bytes 393216 | tf_op jit(solution)/shard_map/all_to_all | solution.py:409
  37.7 8.7 %collective-permute-start.4 = (bf16[64,128]{1,0:T(8,128)(2,1)S(1)}, bf16[64,128]{1,0:T(8,128)(2,1)S(1)}, u32[]{:S(2)}, u32[]{:S(2)}) collective-permute-start(bf16[64,128]{1,0:T(8,128)(2,1)S(1)} %get-tuple-element.22), channel_id=1, source_target_pairs={{0,1},{1,2},{2,3},{3,4},{4,5},{5,6},{6,7},{7,8},{8,9},{9,10},{10,1... | collective-permute-start | bytes 49160 | tf_op jit(solution)/shard_map/ppermute | solution.py:326
  38.1 8.2 %collective-permute-start.5 = (bf16[64,128]{1,0:T(8,128)(2,1)S(1)}, bf16[64,128]{1,0:T(8,128)(2,1)S(1)}, u32[]{:S(2)}, u32[]{:S(2)}) collective-permute-start(bf16[64,128]{1,0:T(8,128)(2,1)S(1)} %get-tuple-element.23), channel_id=1, source_target_pairs={{0,15},{1,0},{2,1},{3,2},{4,3},{5,4},{6,5},{7,6},{8,7},{9,8},{10,9... | collective-permute-start | bytes 49160 | tf_op jit(solution)/shard_map/ppermute | solution.py:326

commit v7 on v6

--- a/solution.py
+++ b/solution.py
@@ -61,7 +61,8 @@
         moving = leaving[part * migr : (part + 1) * migr]
         out[border : border + migr] = moving
         far[:migr] = moving
-        far[migr:] = jnp.zeros_like(far[migr:])
+        if far.shape[0] > migr:
+            far[migr:] = jnp.zeros_like(far[migr:])
         shifted = code if part == 0 else pltpu.roll(code, border, 1)
         tail = out.shape[0] - border - migr
         out[border + migr :] = jnp.broadcast_to(shifted, (tail, 2 * border)).astype(BF16)
@@ -274,7 +275,7 @@
     ).astype(BF16)
 
 
-def sum_kernel(parts, out):
+def sum_kernel(parts, _, __, out):
     total = jnp.sum(parts[...].astype(F32), axis=0).astype(BF16)
     out[...] = jnp.broadcast_to(total[None], out.shape)
 
@@ -325,12 +326,12 @@
     def shift(array, by):
         return lax.ppermute(array, "slab", [(i, (i + by) % size) for i in range(size)])
 
-    message = (border + migr + CODE_ROWS, width)
-    message_up = (message[0] + CODE_ROWS, width)
+    down_rows = border + migr + CODE_ROWS
+    lengths = (down_rows + 2 * CODE_ROWS, down_rows + CODE_ROWS, down_rows, migr)
     (token,) = call(first_kernel, [((8, LANES), F32)])()
     to_up, far_up, to_down, far_down = call(
         pack_kernel,
-        [(message_up, BF16)] * 2 + [(message, BF16)] * 2,
+        [((length, width), BF16) for length in lengths],
     )(token, nodes, leave_list, arrive_list, send_list)
     low, low_far = shift(to_up, 1), shift(far_up, 2)
     high, high_far = shift(to_down, -1), shift(far_down, -2)
@@ -405,7 +406,7 @@
         finish_kernel,
         [((1, rows, width), BF16)],
     )(*sources)
-    (shared,) = call(sum_kernel, [((devices, share, width), BF16)])(parts)
+    (shared,) = call(sum_kernel, [((devices, share, width), BF16)])(parts, from_low, from_high)
     total = lax.all_to_all(shared, axes, split_axis=0, concat_axis=0, tiled=True)
     total = total.reshape(devices * share, width)[: matrices * width]
     (weight_steps,) = call(norm_kernel, [((matrices, width, width), F32)])(total)

time: 48.4 us -> 49.4 us (1.021)
  blocking collectives: 14.5 us -> 0 us
  waiting for transfers between devices: 5.76 us -> 15.4 us
  starting transfers between devices: 14.7 us -> 20 us
    all_to_all x1 -> x0, blocking collectives: 14.5 us -> none  [shards(): lax.all_to_all(grads.reshape(devices, share, width), axes, split_axis=0,...]
    all_to_all x1, waiting for transfers between devices: 0.01 us -> 8.01 us  [shards(): lax.all_to_all(shared, axes, split_axis=0, concat_axis=0, tiled=True)]
    all_to_all x0 -> x1, starting transfers between devices: none -> 4.6 us  [shards(): lax.all_to_all(grads.reshape(devices, share, width), axes, split_axis=0,...]
    ppermute x6, waiting for transfers between devices: 5.75 us -> 7.22 us  [shift(): lax.ppermute(array, 'slab', [(i, (i + by) % size) for i in range(size)])]
  transfers between devices with their start and end apart: 7 -> 8, of which waited for: 3 -> 4; matrix products, arithmetic and copies ran while one was open for 0% -> 0% of each run, Pallas kernels for 2% -> 2%
where the time goes in v7:
time: 49.4 us; the launch traced here: 48.9 us
  starting transfers between devices  20 us (40%)
  waiting for transfers between devices  15.4 us (31%)
  Pallas kernels  11.8 us (24%)
  local copies, waits for them, and re-layouts  0.88 us (2%)
  between operations  0.83 us (2%)
    ppermute x6, starting transfers between devices, shift(): lax.ppermute(array, 'slab', [(i, (i + by) % size) for i in range(size)])  12.3 us
    pallas_call x1, Pallas kernels, shards(): call(layer_kernel, [((1, rows, width), BF16), ((border, width), BF16), ((...  8.98 us
    all_to_all x1, waiting for transfers between devices, shards(): lax.all_to_all(shared, axes, split_axis=0, concat_axis=0, tiled=True)  8.01 us
    ppermute x6, waiting for transfers between devices, shift(): lax.ppermute(array, 'slab', [(i, (i + by) % size) for i in range(size)])  7.22 us
    all_to_all x1, starting transfers between devices, shards(): lax.all_to_all(grads.reshape(devices, share, width), axes, split_axis=0,...  4.6 us
    all_to_all x1, starting transfers between devices, shards(): lax.all_to_all(shared, axes, split_axis=0, concat_axis=0, tiled=True)  3.05 us
  transfers between devices with their start and end apart: 8, of which 4 were waited for; matrix products, arithmetic and copies ran while one was open for 0% of the time, Pallas kernels for 2%

profile of v7, /device:TPU:0, one launch (start us, length us, event | category | flops | bytes accessed | tf_op | source)
XLA Modules:
  0.0 48.9 jit_solution(14273601727922158742)
XLA Ops:
  0.6 0.0 copy-start.12
  0.6 0.0 copy-start.10
  0.7 0.6 %copy-done.12 = s32[1,128]{1,0:T(1,128)S(1)} copy-done((s32[1,128]{1,0:T(1,128)S(1)}, s32[1,128]{1,0:T(1,128)}, u32[]{:S(2)}) %copy-start.12) | copy-done | bytes 536
  1.3 0.0 copy-done.10
  1.3 0.2 copy-done
  1.5 0.0 copy-start.4
  1.5 0.0 copy-start.5
  1.5 0.0 copy-start.6
  1.6 0.0 copy-start.7
  1.6 0.0 copy-start.8
  1.6 0.0 copy-start.9
  1.6 0.3 shard_map.149
  1.9 0.5 %collective-permute-start = (bf16[144,128]{1,0:T(8,128)(2,1)S(1)}, bf16[144,128]{1,0:T(8,128)(2,1)S(1)}, u32[]{:S(2)}, u32[]{:S(2)}) collective-permute-start(bf16[144,128]{1,0:T(8,128)(2,1)S(1)} %get-tuple-element.14.my_up), channel_id=1, source_target_pairs={{0,1},{1,2},{2,3},{3,4},{4,5},{5,6},{6,7},{7,8},{8,9},{9,10},{10,1... | collective-permute-start | bytes 110600 | tf_op jit(solution)/shard_map/ppermute | solution.py:327
  2.4 2.6 %collective-permute-start.1 = (bf16[128,128]{1,0:T(8,128)(2,1)S(1)}, bf16[128,128]{1,0:T(8,128)(2,1)S(1)}, u32[]{:S(2)}, u32[]{:S(2)}) collective-permute-start(bf16[128,128]{1,0:T(8,128)(2,1)S(1)} %get-tuple-element.16), channel_id=1, source_target_pairs={{0,2},{1,3},{2,4},{3,5},{4,6},{5,7},{6,8},{7,9},{8,10},{9,11},{10,... | collective-permute-start | bytes 98312 | tf_op jit(solution)/shard_map/ppermute | solution.py:327
  5.0 4.1 %collective-permute-start.2 = (bf16[112,128]{1,0:T(8,128)(2,1)S(1)}, bf16[112,128]{1,0:T(8,128)(2,1)S(1)}, u32[]{:S(2)}, u32[]{:S(2)}) collective-permute-start(bf16[112,128]{1,0:T(8,128)(2,1)S(1)} %get-tuple-element.15.my_down), channel_id=1, source_target_pairs={{0,15},{1,0},{2,1},{3,2},{4,3},{5,4},{6,5},{7,6},{8,7},{9,8},{10,9... | collective-permute-start | bytes 86024 | tf_op jit(solution)/shard_map/ppermute | solution.py:327
  9.1 0.6 %collective-permute-start.3 = (bf16[32,128]{1,0:T(8,128)(2,1)S(1)}, bf16[32,128]{1,0:T(8,128)(2,1)S(1)}, u32[]{:S(2)}, u32[]{:S(2)}) collective-permute-start(bf16[32,128]{1,0:T(8,128)(2,1)S(1)} %get-tuple-element.17), channel_id=1, source_target_pairs={{0,14},{1,15},{2,0},{3,1},{4,2},{5,3},{6,4},{7,5},{8,6},{9,7},{10,... | collective-permute-start | bytes 24584 | tf_op jit(solution)/shard_map/ppermute | solution.py:327
  9.7 3.0 %collective-permute-done.3.high_far = bf16[32,128]{1,0:T(8,128)(2,1)S(1)} collective-permute-done((bf16[32,128]{1,0:T(8,128)(2,1)S(1)}, bf16[32,128]{1,0:T(8,128)(2,1)S(1)}, u32[]{:S(2)}, u32[]{:S(2)}) %collective-permute-start.3) | collective-permute-done | bytes 8224 | tf_op jit(solution)/shard_map/ppermute | solution.py:327
  12.8 0.0 collective-permute-done.2.high
  12.8 0.0 collective-permute-done.1.low_far
  12.8 0.0 collective-permute-done.low
  12.9 9.0 %shard_map.150 = (bf16[1,256,128]{2,1,0:T(8,128)(2,1)}, bf16[64,128]{1,0:T(8,128)(2,1)S(1)}, bf16[64,128]{1,0:T(8,128)(2,1)S(1)}, bf16[768,128]{1,0:T(8,128)(2,1...) custom-call(bf16[1,256,128]{2,1,0:T(8,128)(2,1)S(1)} %copy-done, ...), custom_call_target="tpu_custom_call" | custom-call | flops 2000000000 | bytes 1024 | tf_op jit(solution)/shard_map/pallas_call | solution.py:363
  21.9 4.6 %all-to-all-start = ((bf16[32,24,128]{2,1,0:T(8,128)(2,1)}), bf16[32,24,128]{2,1,0:T(8,128)(2,1)S(1)}, u32[]{:S(2)}, u32[]{:S(2)}) async-start(bf16[32,24,128]{2,1,0:T(8,128)(2,1)} %bitcast.2), calls=%async_computation | async-start | bytes 393216 | tf_op jit(solution)/shard_map/all_to_all | solution.py:390
  26.5 0.3 collective-permute-start.4
  26.8 4.2 %collective-permute-start.5 = (bf16[64,128]{1,0:T(8,128)(2,1)S(1)}, bf16[64,128]{1,0:T(8,128)(2,1)S(1)}, u32[]{:S(2)}, u32[]{:S(2)}) collective-permute-start(bf16[64,128]{1,0:T(8,128)(2,1)S(1)} %get-tuple-element.23), channel_id=1, source_target_pairs={{0,15},{1,0},{2,1},{3,2},{4,3},{5,4},{6,5},{7,6},{8,7},{9,8},{10,9... | collective-permute-start | bytes 49160 | tf_op jit(solution)/shard_map/ppermute | solution.py:327
  31.0 4.2 %collective-permute-done.4.from_low._ = bf16[64,128]{1,0:T(8,128)(2,1)S(1)} collective-permute-done((bf16[64,128]{1,0:T(8,128)(2,1)S(1)}, bf16[64,128]{1,0:T(8,128)(2,1)S(1)}, u32[]{:S(2)}, u32[]{:S(2)}) %collective-permute-start.4) | collective-permute-done | bytes 16416 | tf_op jit(solution)/shard_map/ppermute | solution.py:327
  35.1 0.0 collective-permute-done.5.from_high.__
  35.2 0.2 all-to-all-done.parts
  35.3 0.7 %shard_map.152 = bf16[32,24,128]{2,1,0:T(8,128)(2,1)} custom-call(bf16[32,24,128]{2,1,0:T(8,128)(2,1)S(1)} %all-to-all-done.parts, bf16[64,128]{1,0:T(8,128)(2,1)S(1)} %collective-permute-done.4.from_low._, bf16[64,128]{1,0:T(8,128)(2,1)S(1)} %collective-permute-done.5.from_high.__), custom_call_target="tpu_custom_call" | custom-call | flops 2000000000 | bytes 1024 | tf_op jit(solution)/shard_map/pallas_call | solution.py:409
  36.1 3.0 %all-to-all-start.1 = ((bf16[32,24,128]{2,1,0:T(8,128)(2,1)}), bf16[32,24,128]{2,1,0:T(8,128)(2,1)S(1)}, u32[]{:S(2)}, u32[]{:S(2)}) async-start(bf16[32,24,128]{2,1,0:T(8,128)(2,1)} %shard_map.152), calls=%async_computation.1 | async-start | bytes 393216 | tf_op jit(solution)/shard_map/all_to_all | solution.py:410
  39.1 0.9 %shard_map.151 = bf16[1,256,128]{2,1,0:T(8,128)(2,1)} custom-call(bf16[1,256,128]{2,1,0:T(8,128)(2,1)S(1)} %copy-done.1, bf16[256,128]{1,0:T(8,128)(2,1)S(1)} %get-tuple-element.19.d_node, bf16[256,128]{1,0:T(8,128)(2,1)S(1)} %get-tuple-element.20.d_centre, bf16[256,128]{1,0:T(8,128)(2,1)S(1)} %get-tuple-element.21.d_neigh, bf16[128,128]{1,0:T(8,128)(2,1)S(1)} %copy-done.9, ...), custom_call_target="tpu_custom_call" | custom-call | flops 2000000000 | bytes 1024 | tf_op jit(solution)/shard_map/pallas_call | solution.py:405
  40.0 8.0 %all-to-all-done.1 = bf16[32,24,128]{2,1,0:T(8,128)(2,1)S(1)} async-done(((bf16[32,24,128]{2,1,0:T(8,128)(2,1)}), bf16[32,24,128]{2,1,0:T(8,128)(2,1)S(1)}, u32[]{:S(2)}, u32[]{:S(2)}) %all-to-all-start.1) | async-done | bytes 196640 | tf_op jit(solution)/shard_map/all_to_all | solution.py:410
  48.0 0.9 %shard_map.153 = f32[6,128,128]{2,1,0:T(8,128)} custom-call(bf16[768,128]{1,0:T(8,128)(2,1)S(1)} %bitcast.4), custom_call_target="tpu_custom_call" | custom-call | flops 2000000000 | bytes 1024 | tf_op jit(solution)/shard_map/pallas_call | solution.py:412
  (16 shorter events, 0.0 us)
Async XLA Ops:
  0.6 0.7 %copy-start.12 = (s32[1,128]{1,0:T(1,128)S(1)}, s32[1,128]{1,0:T(1,128)}, u32[]{:S(2)}) copy-start(s32[1,128]{1,0:T(1,128)} %sends.3) | copy-start | bytes 1540
  0.6 0.7 %copy-start.10 = (s32[1,256]{1,0:T(1,128)S(1)}, s32[1,256]{1,0:T(1,128)}, u32[]{:S(2)}) copy-start(s32[1,256]{1,0:T(1,128)} %arrive.3) | copy-start | bytes 3076
  0.7 0.9 %copy-start = (bf16[1,256,128]{2,1,0:T(8,128)(2,1)S(1)}, bf16[1,256,128]{2,1,0:T(8,128)(2,1)}, u32[]{:S(2)}) copy-start(bf16[1,256,128]{2,1,0:T(8,128)(2,1)} %nodes.3) | copy-start | bytes 196612
  0.7 0.8 %copy-start.11 = (s32[1,64]{1,0:T(1,128)S(1)}, s32[1,64]{1,0:T(1,128)}, u32[]{:S(2)}) copy-start(s32[1,64]{1,0:T(1,128)} %leave.1) | copy-start | bytes 772
  1.5 11.3 %copy-start.1 = (bf16[1,256,128]{2,1,0:T(8,128)(2,1)S(1)}, bf16[1,256,128]{2,1,0:T(8,128)(2,1)}, u32[]{:S(2)}) copy-start(bf16[1,256,128]{2,1,0:T(8,128)(2,1)} %cotangent.3) | copy-start | bytes 196612
  1.5 11.3 %copy-start.2 = (s32[1,256,32]{1,2,0:T(8,128)S(1)}, s32[1,256,32]{1,2,0:T(8,128)}, u32[]{:S(2)}) copy-start(s32[1,256,32]{1,2,0:T(8,128)} %param.17) | copy-start | bytes 98308
  1.5 11.3 %copy-start.3 = (s32[1,256,32]{1,2,0:T(8,128)S(1)}, s32[1,256,32]{1,2,0:T(8,128)}, u32[]{:S(2)}) copy-start(s32[1,256,32]{1,2,0:T(8,128)} %param.18) | copy-start | bytes 98308
  1.5 11.3 %copy-start.4 = (bf16[128,128]{1,0:T(8,128)(2,1)S(1)}, bf16[128,128]{1,0:T(8,128)(2,1)}, u32[]{:S(2)}) copy-start(bf16[128,128]{1,0:T(8,128)(2,1)} %w_msg.1) | copy-start | bytes 98308
  1.5 11.3 %copy-start.5 = (bf16[128,128]{1,0:T(8,128)(2,1)S(1)}, bf16[128,128]{1,0:T(8,128)(2,1)}, u32[]{:S(2)}) copy-start(bf16[128,128]{1,0:T(8,128)(2,1)} %w_agg.1) | copy-start | bytes 98308
  1.5 11.3 %copy-start.6 = (bf16[128,128]{1,0:T(8,128)(2,1)S(1)}, bf16[128,128]{1,0:T(8,128)(2,1)}, u32[]{:S(2)}) copy-start(bf16[128,128]{1,0:T(8,128)(2,1)} %w_out.1) | copy-start | bytes 98308
  1.6 11.3 %copy-start.7 = (bf16[128,128]{1,0:T(8,128)(2,1)S(1)}, bf16[128,128]{1,0:T(8,128)(2,1)}, u32[]{:S(2)}) copy-start(bf16[128,128]{1,0:T(8,128)(2,1)} %w_send.3) | copy-start | bytes 98308
  1.6 11.3 %copy-start.8 = (bf16[128,128]{1,0:T(8,128)(2,1)S(1)}, bf16[128,128]{1,0:T(8,128)(2,1)}, u32[]{:S(2)}) copy-start(bf16[128,128]{1,0:T(8,128)(2,1)} %w_recv.3) | copy-start | bytes 98308
  1.6 11.3 %copy-start.9 = (bf16[128,128]{1,0:T(8,128)(2,1)S(1)}, bf16[128,128]{1,0:T(8,128)(2,1)}, u32[]{:S(2)}) copy-start(bf16[128,128]{1,0:T(8,128)(2,1)} %w_self.3) | copy-start | bytes 98308
  1.9 10.8 %collective-permute-start = (bf16[144,128]{1,0:T(8,128)(2,1)S(1)}, bf16[144,128]{1,0:T(8,128)(2,1)S(1)}, u32[]{:S(2)}, u32[]{:S(2)}) collective-permute-start(bf16[144,128]{1,0:T(8,128)(2,1)S(1)} %get-tuple-element.14.my_up), channel_id=1, source_target_pairs={{0,1},{1,2},{2,3},{3,4},{4,5},{5,6},{6,7},{7,8},{8,9},{9,10},{10,1... | collective-permute-start | bytes 110600 | tf_op jit(solution)/shard_map/ppermute | solution.py:327
  2.4 10.3 %collective-permute-start.1 = (bf16[128,128]{1,0:T(8,128)(2,1)S(1)}, bf16[128,128]{1,0:T(8,128)(2,1)S(1)}, u32[]{:S(2)}, u32[]{:S(2)}) collective-permute-start(bf16[128,128]{1,0:T(8,128)(2,1)S(1)} %get-tuple-element.16), channel_id=1, source_target_pairs={{0,2},{1,3},{2,4},{3,5},{4,6},{5,7},{6,8},{7,9},{8,10},{9,11},{10,... | collective-permute-start | bytes 98312 | tf_op jit(solution)/shard_map/ppermute | solution.py:327
  5.0 7.8 %collective-permute-start.2 = (bf16[112,128]{1,0:T(8,128)(2,1)S(1)}, bf16[112,128]{1,0:T(8,128)(2,1)S(1)}, u32[]{:S(2)}, u32[]{:S(2)}) collective-permute-start(bf16[112,128]{1,0:T(8,128)(2,1)S(1)} %get-tuple-element.15.my_down), channel_id=1, source_target_pairs={{0,15},{1,0},{2,1},{3,2},{4,3},{5,4},{6,5},{7,6},{8,7},{9,8},{10,9... | collective-permute-start | bytes 86024 | tf_op jit(solution)/shard_map/ppermute | solution.py:327
  9.1 3.7 %collective-permute-start.3 = (bf16[32,128]{1,0:T(8,128)(2,1)S(1)}, bf16[32,128]{1,0:T(8,128)(2,1)S(1)}, u32[]{:S(2)}, u32[]{:S(2)}) collective-permute-start(bf16[32,128]{1,0:T(8,128)(2,1)S(1)} %get-tuple-element.17), channel_id=1, source_target_pairs={{0,14},{1,15},{2,0},{3,1},{4,2},{5,3},{6,4},{7,5},{8,6},{9,7},{10,... | collective-permute-start | bytes 24584 | tf_op jit(solution)/shard_map/ppermute | solution.py:327
  21.9 13.5 %all-to-all-start = ((bf16[32,24,128]{2,1,0:T(8,128)(2,1)}), bf16[32,24,128]{2,1,0:T(8,128)(2,1)S(1)}, u32[]{:S(2)}, u32[]{:S(2)}) async-start(bf16[32,24,128]{2,1,0:T(8,128)(2,1)} %bitcast.2), calls=%async_computation | async-start | bytes 393216 | tf_op jit(solution)/shard_map/all_to_all | solution.py:390
  26.5 8.7 %collective-permute-start.4 = (bf16[64,128]{1,0:T(8,128)(2,1)S(1)}, bf16[64,128]{1,0:T(8,128)(2,1)S(1)}, u32[]{:S(2)}, u32[]{:S(2)}) collective-permute-start(bf16[64,128]{1,0:T(8,128)(2,1)S(1)} %get-tuple-element.22), channel_id=1, source_target_pairs={{0,1},{1,2},{2,3},{3,4},{4,5},{5,6},{6,7},{7,8},{8,9},{9,10},{10,1... | collective-permute-start | bytes 49160 | tf_op jit(solution)/shard_map/ppermute | solution.py:327
  26.8 8.4 %collective-permute-start.5 = (bf16[64,128]{1,0:T(8,128)(2,1)S(1)}, bf16[64,128]{1,0:T(8,128)(2,1)S(1)}, u32[]{:S(2)}, u32[]{:S(2)}) collective-permute-start(bf16[64,128]{1,0:T(8,128)(2,1)S(1)} %get-tuple-element.23), channel_id=1, source_target_pairs={{0,15},{1,0},{2,1},{3,2},{4,3},{5,4},{6,5},{7,6},{8,7},{9,8},{10,9... | collective-permute-start | bytes 49160 | tf_op jit(solution)/shard_map/ppermute | solution.py:327
  36.1 11.9 %all-to-all-start.1 = ((bf16[32,24,128]{2,1,0:T(8,128)(2,1)}), bf16[32,24,128]{2,1,0:T(8,128)(2,1)S(1)}, u32[]{:S(2)}, u32[]{:S(2)}) async-start(bf16[32,24,128]{2,1,0:T(8,128)(2,1)} %shard_map.152), calls=%async_computation.1 | async-start | bytes 393216 | tf_op jit(solution)/shard_map/all_to_all | solution.py:410

commit v8 on v6

--- a/solution.py
+++ b/solution.py
@@ -67,6 +67,57 @@
         out[border + migr :] = jnp.broadcast_to(shifted, (tail, 2 * border)).astype(BF16)
 
 
+def prep_kernel(nbr, valid, w_msg, w_out, cotangent, hot_o, hot_t_o, wide_o, ids_o, d_hid_o):
+    slots, rows = nbr.shape[1:]
+    width = w_msg.shape[0]
+    half_rows, hot_rows = hot_t_o.shape[0], hot_o.shape[1]
+    chunk = 4
+    half_msg = 0.5 * w_msg[...].astype(F32)
+    none = jnp.zeros((width, width), F32)
+    for part, block in enumerate((half_msg, jnp.transpose(half_msg, (1, 0)))):
+        wide_o[part] = jnp.concatenate(
+            [
+                jnp.concatenate([block, none], axis=1),
+                jnp.concatenate([none, block], axis=1),
+            ],
+            axis=0,
+        ).astype(BF16)
+    d_hid_o[...] = nt(cotangent[0], w_out[...])
+    upper = nbr[0] >= half_rows
+    low_row = jnp.where(upper, nbr[0] - half_rows, nbr[0])
+    index = jnp.where(valid[0] == 1, low_row, half_rows) + jnp.where(upper, hot_rows, 0)
+    fill = jnp.zeros((LANES - slots, rows), jnp.int32)
+    ids_o[...] = jnp.transpose(jnp.concatenate([index, fill], axis=0), (1, 0))
+
+    lane = lax.broadcasted_iota(jnp.int32, (rows, hot_rows), 1).astype(jnp.int16)
+    one = jnp.ones((rows, hot_rows), BF16)
+    zero = jnp.zeros((rows, hot_rows), BF16)
+    sub = lax.broadcasted_iota(jnp.int32, (half_rows, rows), 0).astype(jnp.int16)
+    one_t = jnp.ones((half_rows, rows), BF16)
+    zero_t = jnp.zeros((half_rows, rows), BF16)
+
+    @pl.loop(0, slots // chunk)
+    def build(step):
+        for j, short in enumerate(slot_ids(ids_o, step, chunk)):
+            slot = step * chunk + j
+            short = (short & (hot_rows - 1)).astype(jnp.int16)
+            short = jnp.concatenate([short] * (hot_rows // LANES), axis=1)
+            hot_o[pl.ds(slot * rows, rows)] = jnp.where(short == lane, one, zero)
+            row = nbr[0, pl.ds(slot, 1)]
+            row = jnp.where(row >= half_rows, row - half_rows, row)
+            short = jnp.broadcast_to(row, (16, rows)).astype(jnp.int16)
+            short = jnp.concatenate([short] * (half_rows // 16), axis=0)
+            hot_t_o[:, pl.ds(pl.multiple_of(slot * rows, LANES), rows)] = jnp.where(
+                short == sub, one_t, zero_t
+            )
+
+
+def slot_ids(ids, step, chunk):
+    near = pltpu.roll(ids[...], lax.rem(LANES - step * chunk, LANES), 1)
+    shape = (ids.shape[0], LANES)
+    return [jnp.broadcast_to(near[:, j : j + 1], shape) for j in range(chunk)]
+
+
 def layer_kernel(
     nodes,
     arrive,
@@ -76,11 +127,13 @@
     low_far,
     high,
     high_far,
-    nbr,
-    valid,
+    hot,
+    hot_t,
+    wide,
+    nbr_ids,
+    d_hid,
     w_send,
     w_recv,
-    w_msg,
     w_self,
     w_agg,
     w_out,
@@ -92,10 +145,7 @@
     d_node_o,
     d_centre_o,
     d_neigh_o,
-    nbr_s,
-    row_s,
     neigh_s,
-    wide_s,
     hid_s,
     ds1_s,
     ds2_s,
@@ -105,9 +155,9 @@
     gmsg_s,
 ):
     rows, width = nodes.shape[1:]
-    slots = nbr.shape[1]
+    slots = hot.shape[0] // rows
     border = back_low.shape[0]
-    migr = high.shape[0] - border - CODE_ROWS
+    migr = low.shape[0] - border - CODE_ROWS
     table_rows = rows + 2 * border
     chunk = 2 * PAIRS
     steps = slots // chunk
@@ -128,47 +178,17 @@
     above = halo(high[...], my_up[border : border + migr], high_far[:migr])
     table = jnp.concatenate([moved, below, above], axis=0)
 
-    half_rows = table_rows // 2
-    hot_rows = -(-(half_rows + 1) // LANES) * LANES
+    half_rows, hot_rows = hot_t.shape[0], hot.shape[1]
     half_centre = 0.5 * nn(moved, w_send[...])
     half_neigh = (0.5 * nn(table, w_recv[...]).astype(BF16).astype(F32)).astype(BF16)
     neigh_s[:half_rows] = jnp.concatenate([half_neigh[:half_rows], half_neigh[half_rows:]], axis=1)
     neigh_s[half_rows:] = jnp.full((hot_rows - half_rows, 2 * width), FAR, BF16)
-    half_msg = 0.5 * w_msg[...].astype(F32)
-    none = jnp.zeros((width, width), F32)
-    for part, block in enumerate((half_msg, jnp.transpose(half_msg, (1, 0)))):
-        wide_s[part] = jnp.concatenate(
-            [
-                jnp.concatenate([block, none], axis=1),
-                jnp.concatenate([none, block], axis=1),
-            ],
-            axis=0,
-        ).astype(BF16)
-    upper = nbr[0] >= half_rows
-    low_row = jnp.where(upper, nbr[0] - half_rows, nbr[0])
-    row_s[...] = low_row
-    index = jnp.where(valid[0] == 1, low_row, half_rows) + jnp.where(upper, hot_rows, 0)
-    fill = jnp.zeros((LANES - slots, rows), jnp.int32)
-    nbr_s[...] = jnp.transpose(jnp.concatenate([index, fill], axis=0), (1, 0))
     agg_s[...] = jnp.zeros_like(agg_s)
-
-    lane = lax.broadcasted_iota(jnp.int32, (rows, hot_rows), 1).astype(jnp.int16)
-    one = jnp.ones((rows, hot_rows), BF16)
-    zero = jnp.zeros((rows, hot_rows), BF16)
-
-    def slot_ids(step):
-        near = pltpu.roll(nbr_s[...], lax.rem(LANES - step * chunk, LANES), 1)
-        return [jnp.broadcast_to(near[:, j : j + 1], (rows, LANES)) for j in range(chunk)]
 
     @pl.loop(0, steps)
     def forward(step):
-        ids = slot_ids(step)
-        hots = []
-        for j in range(chunk):
-            short = (ids[j] & (hot_rows - 1)).astype(jnp.int16)
-            short = jnp.concatenate([short] * (hot_rows // LANES), axis=1)
-            hots.append(jnp.where(short == lane, one, zero))
-        gathered = nn(jnp.concatenate(hots, axis=0), neigh_s[...])
+        ids = slot_ids(nbr_ids, step, chunk)
+        gathered = nn(hot[pl.ds(step * (chunk * rows), chunk * rows)], neigh_s[...])
         base = step * (PAIRS * rows)
         for p in range(PAIRS):
             for side in range(2):
@@ -180,7 +200,7 @@
                 span = pl.ds(base + p * rows, rows)
                 ds1_s[span, cols] = slope
                 hid_s[span, cols] = act.astype(BF16)
-        halves = nn(hid_s[pl.ds(base, PAIRS * rows)], wide_s[0])
+        halves = nn(hid_s[pl.ds(base, PAIRS * rows)], wide[0])
         total = agg_s[...]
         for p in range(PAIRS):
             for side in range(2):
@@ -196,29 +216,26 @@
     node_hid = act.astype(BF16)
     updated[0] = (moved.astype(F32) + nn(node_hid, w_out[...])).astype(BF16)
     cot = cotangent[0]
-    d_node = (nt(cot, w_out[...]) * (0.5 * slope)).astype(BF16)
+    d_node = (d_hid[...] * (0.5 * slope)).astype(BF16)
     half_d_agg = 0.5 * nt(d_node, w_agg[...])
 
     dcen_s[...] = jnp.zeros_like(dcen_s)
     dneigh_s[...] = jnp.zeros_like(dneigh_s)
     gmsg_s[...] = jnp.zeros_like(gmsg_s)
-    sub = lax.broadcasted_iota(jnp.int32, (half_rows, rows), 0).astype(jnp.int16)
-    one_t = jnp.ones((half_rows, rows), BF16)
-    zero_t = jnp.zeros((half_rows, rows), BF16)
     none = jnp.zeros((rows, width), BF16)
     border_id = jnp.full((rows, width), hot_rows, jnp.int16)
 
     @pl.loop(0, steps)
     def backward(step):
-        ids = slot_ids(step)
+        ids = slot_ids(nbr_ids, step, chunk)
         span = pl.ds(step * (PAIRS * rows), PAIRS * rows)
         d_agg = jnp.concatenate([half_d_agg, half_d_agg], axis=1)
         d_agg = jnp.concatenate([d_agg] * PAIRS, axis=0)
         d_pre2 = (d_agg * ds2_s[span]).astype(BF16)
-        d_pre = nn(d_pre2, wide_s[1]) * ds1_s[span]
+        d_pre = nn(d_pre2, wide[1]) * ds1_s[span]
         gmsg_s[...] += tn(hid_s[span], d_pre2)
         total = dcen_s[...]
-        hots, wides = [], []
+        wides = []
         for j in range(chunk):
             p, side = divmod(j, 2)
             part = d_pre[p * rows : (p + 1) * rows, side * width : (side + 1) * width]
@@ -230,11 +247,9 @@
                     [jnp.where(is_up, none, part), jnp.where(is_up, part, none)], axis=1
                 )
             )
-            row = jnp.broadcast_to(row_s[pl.ds(step * chunk + j, 1)], (16, rows))
-            short = jnp.concatenate([row.astype(jnp.int16)] * (half_rows // 16), axis=0)
-            hots.append(jnp.where(short == sub, one_t, zero_t))
         dcen_s[...] = total
-        dneigh_s[...] += nn(jnp.concatenate(hots, axis=1), jnp.concatenate(wides, axis=0))
+        edges = pl.ds(pl.multiple_of(step * (chunk * rows), LANES), chunk * rows)
+        dneigh_s[...] += nn(hot_t[:, edges], jnp.concatenate(wides, axis=0))
 
     d_centre = dcen_s[...].astype(BF16)
     d_neigh = dneigh_s[...].astype(BF16)
@@ -326,11 +341,11 @@
         return lax.ppermute(array, "slab", [(i, (i + by) % size) for i in range(size)])
 
     message = (border + migr + CODE_ROWS, width)
-    message_up = (message[0] + CODE_ROWS, width)
+    message_down = (message[0] + CODE_ROWS, width)
     (token,) = call(first_kernel, [((8, LANES), F32)])()
     to_up, far_up, to_down, far_down = call(
         pack_kernel,
-        [(message_up, BF16)] * 2 + [(message, BF16)] * 2,
+        [(message, BF16)] * 2 + [(message_down, BF16)] * 2,
     )(token, nodes, leave_list, arrive_list, send_list)
     low, low_far = shift(to_up, 1), shift(far_up, 2)
     high, high_far = shift(to_down, -1), shift(far_down, -2)
@@ -340,6 +355,17 @@
     half_rows = table_rows // 2
     hot_rows = -(-(half_rows + 1) // LANES) * LANES
     share = -(-matrices * width // (8 * devices)) * 8
+    edges = rows * slots
+    hot, hot_t, wide, ids, d_hid = call(
+        prep_kernel,
+        [
+            ((edges, hot_rows), BF16),
+            ((half_rows, edges), BF16),
+            ((2, 2 * width, 2 * width), BF16),
+            ((rows, LANES), jnp.int32),
+            ((rows, width), F32),
+        ],
+    )(jnp.swapaxes(neighbours, 1, 2), jnp.swapaxes(valid, 1, 2), w_msg, w_out, cotangent)
     sources = (
         nodes,
         arrive_list,
@@ -349,11 +375,13 @@
         low_far,
         high,
         high_far,
-        jnp.swapaxes(neighbours, 1, 2),
-        jnp.swapaxes(valid, 1, 2),
+        hot,
+        hot_t,
+        wide,
+        ids,
+        d_hid,
         w_send,
         w_recv,
-        w_msg,
         w_self,
         w_agg,
         w_out,
@@ -371,10 +399,7 @@
             ((rows, width), BF16),
         ],
         [
-            pltpu.VMEM((rows, LANES), jnp.int32),
-            pltpu.VMEM((slots, rows), jnp.int32),
             pltpu.VMEM((hot_rows, 2 * width), BF16),
-            pltpu.VMEM((2, 2 * width, 2 * width), BF16),
             pltpu.VMEM((pair_rows, 2 * width), BF16),
             pltpu.VMEM((pair_rows, 2 * width), F32),
             pltpu.VMEM((pair_rows, 2 * width), F32),

time: 48.4 us -> 47.7 us (0.986)
  Pallas kernels: 11.5 us -> 13.3 us
  waiting for transfers between devices: 5.76 us -> 4.2 us
  blocking collectives: 14.5 us -> 13.5 us
    pallas_call x1 -> x2, Pallas kernels: 0.34 us -> 2.84 us  [the longest x1 2.49 us: shards(): call(prep_kernel, [((edges, hot_rows), BF16), ((half_rows, edges), BF16),...]
    ppermute x6, waiting for transfers between devices: 5.75 us -> 4.2 us  [shift(): lax.ppermute(array, 'slab', [(i, (i + by) % size) for i in range(size)])]
    all_to_all x1, blocking collectives: 14.5 us -> 13.5 us  [shards(): lax.all_to_all(grads.reshape(devices, share, width), axes, split_axis=0,...]
    pallas_call x1, Pallas kernels: 8.64 us -> 7.97 us  [shards(): call(layer_kernel, [((1, rows, width), BF16), ((border, width), BF16), ((...]
  transfers between devices with their start and end apart: 7 -> 7, of which waited for: 3 -> 1; matrix products, arithmetic and copies ran while one was open for 0% -> 0% of each run, Pallas kernels for 2% -> 7%
where the time goes in v8:
time: 47.7 us; the launch traced here: 47.4 us
  starting transfers between devices  14.7 us (31%)
  blocking collectives  13.5 us (28%)
  Pallas kernels  13.3 us (28%)
  waiting for transfers between devices  4.2 us (9%)
  local copies, waits for them, and re-layouts  0.88 us (2%)
  between operations  0.83 us (2%)
    all_to_all x1, blocking collectives, shards(): lax.all_to_all(grads.reshape(devices, share, width), axes, split_axis=0,...  13.5 us
    ppermute x6, starting transfers between devices, shift(): lax.ppermute(array, 'slab', [(i, (i + by) % size) for i in range(size)])  12.1 us
    pallas_call x1, Pallas kernels, shards(): call(layer_kernel, [((1, rows, width), BF16), ((border, width), BF16), ((...  7.97 us
    ppermute x6, waiting for transfers between devices, shift(): lax.ppermute(array, 'slab', [(i, (i + by) % size) for i in range(size)])  4.2 us
    all_to_all x1, starting transfers between devices, shards(): lax.all_to_all(shared, axes, split_axis=0, concat_axis=0, tiled=True)  2.59 us
    pallas_call x1, Pallas kernels, shards(): call(prep_kernel, [((edges, hot_rows), BF16), ((half_rows, edges), BF16),...  2.49 us
  transfers between devices with their start and end apart: 7, of which 1 were waited for; matrix products, arithmetic and copies ran while one was open for 0% of the time, Pallas kernels for 7%

profile of v8, /device:TPU:0, one launch (start us, length us, event | category | flops | bytes accessed | tf_op | source)
XLA Modules:
  0.0 47.4 jit_solution(17522883559243474494)
XLA Ops:
  0.6 0.0 copy-start.12
  0.6 0.0 copy-start.7
  0.7 0.6 %copy-done.12 = s32[1,128]{1,0:T(1,128)S(1)} copy-done((s32[1,128]{1,0:T(1,128)S(1)}, s32[1,128]{1,0:T(1,128)}, u32[]{:S(2)}) %copy-start.12) | copy-done | bytes 536
  1.3 0.0 copy-done.7
  1.3 0.2 copy-done
  1.5 0.0 copy-start.9
  1.5 0.0 copy-start.10
  1.5 0.3 shard_map.149
  1.9 0.0 copy-start.3
  1.9 0.0 copy-start.4
  1.9 0.0 copy-start.5
  1.9 0.0 copy-start.6
  1.9 3.0 %collective-permute-start.1 = (bf16[112,128]{1,0:T(8,128)(2,1)S(1)}, bf16[112,128]{1,0:T(8,128)(2,1)S(1)}, u32[]{:S(2)}, u32[]{:S(2)}) collective-permute-start(bf16[112,128]{1,0:T(8,128)(2,1)S(1)} %get-tuple-element.21), channel_id=1, source_target_pairs={{0,2},{1,3},{2,4},{3,5},{4,6},{5,7},{6,8},{7,9},{8,10},{9,11},{10,... | collective-permute-start | bytes 86024 | tf_op jit(solution)/shard_map/ppermute | solution.py:341
  5.0 0.0 collective-permute-start
  5.0 3.2 %collective-permute-start.3 = (bf16[128,128]{1,0:T(8,128)(2,1)S(1)}, bf16[128,128]{1,0:T(8,128)(2,1)S(1)}, u32[]{:S(2)}, u32[]{:S(2)}) collective-permute-start(bf16[128,128]{1,0:T(8,128)(2,1)S(1)} %get-tuple-element.22), channel_id=1, source_target_pairs={{0,14},{1,15},{2,0},{3,1},{4,2},{5,3},{6,4},{7,5},{8,6},{9,7},{10,... | collective-permute-start | bytes 98312 | tf_op jit(solution)/shard_map/ppermute | solution.py:341
  8.1 1.4 %collective-permute-start.2 = (bf16[128,128]{1,0:T(8,128)(2,1)S(1)}, bf16[128,128]{1,0:T(8,128)(2,1)S(1)}, u32[]{:S(2)}, u32[]{:S(2)}) collective-permute-start(bf16[128,128]{1,0:T(8,128)(2,1)S(1)} %get-tuple-element.20.my_down), channel_id=1, source_target_pairs={{0,15},{1,0},{2,1},{3,2},{4,3},{5,4},{6,5},{7,6},{8,7},{9,8},{10,9... | collective-permute-start | bytes 98312 | tf_op jit(solution)/shard_map/ppermute | solution.py:341
  9.6 2.5 %shard_map.150 = (bf16[8192,256]{1,0:T(8,128)(2,1)S(1)}, bf16[192,8192]{1,0:T(8,128)(2,1)S(1)}, bf16[2,256,256]{2,1,0:T(8,128)(2,1)S(1)}, s32[256,128]{1,0:T(8,128)S(1)}, f32[256,128]{1,0:T(8,128)S(1)}) custom-call(s32[1,32,256]{2,1,0:T(8,128)S(1)} %bitcast.6, s32[1,32,256]{2,1,0:T(8,128)S(1)} %bitcast.7, bf16[128,128]{1,0:T(8,128)(2,1)S(1)} %copy-done.10, ...), custom_call_target="tpu_custom_call" | custom-call | flops 2000000000 | bytes 1024 | tf_op jit(solution)/shard_map/pallas_call | solution.py:359
  12.1 0.0 collective-permute-done.1.low_far
  12.1 0.0 collective-permute-done.low
  12.1 0.0 collective-permute-done.3.high_far
  12.1 0.0 collective-permute-done.2.high
  12.1 8.0 %shard_map.151 = (bf16[1,256,128]{2,1,0:T(8,128)(2,1)}, bf16[64,128]{1,0:T(8,128)(2,1)S(1)}, bf16[64,128]{1,0:T(8,128)(2,1)S(1)}, bf16[768,128]{1,0:T(8,128)(2,1...) custom-call(bf16[1,256,128]{2,1,0:T(8,128)(2,1)S(1)} %copy-done, ...), custom_call_target="tpu_custom_call" | custom-call | flops 2000000000 | bytes 1024 | tf_op jit(solution)/shard_map/pallas_call | solution.py:390
  20.1 13.5 %all_to_all.10.parts = bf16[32,24,128]{2,1,0:T(8,128)(2,1)S(1)} all-to-all(bf16[32,24,128]{2,1,0:T(8,128)(2,1)S(1)} %bitcast.5), channel_id=1, replica_groups=mesh['grp'=2,'slab'=16] {'grp','slab'}, dimensions={0} | all-to-all | bytes 393216 | tf_op jit(solution)/shard_map/all_to_all | solution.py:414
  33.6 0.7 %shard_map.153 = bf16[32,24,128]{2,1,0:T(8,128)(2,1)} custom-call(bf16[32,24,128]{2,1,0:T(8,128)(2,1)S(1)} %all_to_all.10.parts), custom_call_target="tpu_custom_call" | custom-call | flops 2000000000 | bytes 1024 | tf_op jit(solution)/shard_map/pallas_call | solution.py:433
  34.4 2.6 %all-to-all-start.1 = ((bf16[32,24,128]{2,1,0:T(8,128)(2,1)}), bf16[32,24,128]{2,1,0:T(8,128)(2,1)S(1)}, u32[]{:S(2)}, u32[]{:S(2)}) async-start(bf16[32,24,128]{2,1,0:T(8,128)(2,1)} %shard_map.153), calls=%async_computation.1 | async-start | bytes 393216 | tf_op jit(solution)/shard_map/all_to_all | solution.py:434
  37.0 0.4 collective-permute-start.4
  37.4 4.0 %collective-permute-start.5 = (bf16[64,128]{1,0:T(8,128)(2,1)S(1)}, bf16[64,128]{1,0:T(8,128)(2,1)S(1)}, u32[]{:S(2)}, u32[]{:S(2)}) collective-permute-start(bf16[64,128]{1,0:T(8,128)(2,1)S(1)} %get-tuple-element.33), channel_id=1, source_target_pairs={{0,15},{1,0},{2,1},{3,2},{4,3},{5,4},{6,5},{7,6},{8,7},{9,8},{10,9... | collective-permute-start | bytes 49160 | tf_op jit(solution)/shard_map/ppermute | solution.py:341
  41.5 4.2 %collective-permute-done.4.from_low = bf16[64,128]{1,0:T(8,128)(2,1)S(1)} collective-permute-done((bf16[64,128]{1,0:T(8,128)(2,1)S(1)}, bf16[64,128]{1,0:T(8,128)(2,1)S(1)}, u32[]{:S(2)}, u32[]{:S(2)}) %collective-permute-start.4) | collective-permute-done | bytes 16416 | tf_op jit(solution)/shard_map/ppermute | solution.py:341
  45.6 0.0 collective-permute-done.5.from_high
  45.6 0.9 %shard_map.152 = bf16[1,256,128]{2,1,0:T(8,128)(2,1)} custom-call(bf16[1,256,128]{2,1,0:T(8,128)(2,1)S(1)} %copy-done.1, bf16[256,128]{1,0:T(8,128)(2,1)S(1)} %get-tuple-element.29.d_node, bf16[256,128]{1,0:T(8,128)(2,1)S(1)} %get-tuple-element.30.d_centre, bf16[256,128]{1,0:T(8,128)(2,1)S(1)} %get-tuple-element.31.d_neigh, bf16[128,128]{1,0:T(8,128)(2,1)S(1)} %copy-done.6, ...), custom_call_target="tpu_custom_call" | custom-call | flops 2000000000 | bytes 1024 | tf_op jit(solution)/shard_map/pallas_call | solution.py:429
  46.5 0.0 all-to-all-done.1
  46.5 0.9 %shard_map.154 = f32[6,128,128]{2,1,0:T(8,128)} custom-call(bf16[768,128]{1,0:T(8,128)(2,1)S(1)} %bitcast.4), custom_call_target="tpu_custom_call" | custom-call | flops 2000000000 | bytes 1024 | tf_op jit(solution)/shard_map/pallas_call | solution.py:436
  (16 shorter events, 0.0 us)
Async XLA Ops:
  0.6 0.7 %copy-start.12 = (s32[1,128]{1,0:T(1,128)S(1)}, s32[1,128]{1,0:T(1,128)}, u32[]{:S(2)}) copy-start(s32[1,128]{1,0:T(1,128)} %sends.3) | copy-start | bytes 1540
  0.6 0.7 %copy-start.7 = (s32[1,256]{1,0:T(1,128)S(1)}, s32[1,256]{1,0:T(1,128)}, u32[]{:S(2)}) copy-start(s32[1,256]{1,0:T(1,128)} %arrive.3) | copy-start | bytes 3076
  0.7 0.9 %copy-start = (bf16[1,256,128]{2,1,0:T(8,128)(2,1)S(1)}, bf16[1,256,128]{2,1,0:T(8,128)(2,1)}, u32[]{:S(2)}) copy-start(bf16[1,256,128]{2,1,0:T(8,128)(2,1)} %nodes.3) | copy-start | bytes 196612
  0.7 0.8 %copy-start.11 = (s32[1,64]{1,0:T(1,128)S(1)}, s32[1,64]{1,0:T(1,128)}, u32[]{:S(2)}) copy-start(s32[1,64]{1,0:T(1,128)} %leave.1) | copy-start | bytes 772
  1.5 8.0 %copy-start.1 = (bf16[1,256,128]{2,1,0:T(8,128)(2,1)S(1)}, bf16[1,256,128]{2,1,0:T(8,128)(2,1)}, u32[]{:S(2)}) copy-start(bf16[1,256,128]{2,1,0:T(8,128)(2,1)} %cotangent.5) | copy-start | bytes 196612
  1.5 8.0 %copy-start.2 = (bf16[128,128]{1,0:T(8,128)(2,1)S(1)}, bf16[128,128]{1,0:T(8,128)(2,1)}, u32[]{:S(2)}) copy-start(bf16[128,128]{1,0:T(8,128)(2,1)} %w_out.3) | copy-start | bytes 98308
  1.5 8.0 %copy-start.8 = (s32[1,256,32]{1,2,0:T(8,128)S(1)}, s32[1,256,32]{1,2,0:T(8,128)}, u32[]{:S(2)}) copy-start(s32[1,256,32]{1,2,0:T(8,128)} %param.17) | copy-start | bytes 98308
  1.5 8.0 %copy-start.9 = (s32[1,256,32]{1,2,0:T(8,128)S(1)}, s32[1,256,32]{1,2,0:T(8,128)}, u32[]{:S(2)}) copy-start(s32[1,256,32]{1,2,0:T(8,128)} %param.18) | copy-start | bytes 98308
  1.5 8.0 %copy-start.10 = (bf16[128,128]{1,0:T(8,128)(2,1)S(1)}, bf16[128,128]{1,0:T(8,128)(2,1)}, u32[]{:S(2)}) copy-start(bf16[128,128]{1,0:T(8,128)(2,1)} %w_msg.1) | copy-start | bytes 98308
  1.9 10.2 %copy-start.3 = (bf16[128,128]{1,0:T(8,128)(2,1)S(1)}, bf16[128,128]{1,0:T(8,128)(2,1)}, u32[]{:S(2)}) copy-start(bf16[128,128]{1,0:T(8,128)(2,1)} %w_agg.1) | copy-start | bytes 98308
  1.9 10.2 %copy-start.4 = (bf16[128,128]{1,0:T(8,128)(2,1)S(1)}, bf16[128,128]{1,0:T(8,128)(2,1)}, u32[]{:S(2)}) copy-start(bf16[128,128]{1,0:T(8,128)(2,1)} %w_send.3) | copy-start | bytes 98308
  1.9 10.2 %copy-start.5 = (bf16[128,128]{1,0:T(8,128)(2,1)S(1)}, bf16[128,128]{1,0:T(8,128)(2,1)}, u32[]{:S(2)}) copy-start(bf16[128,128]{1,0:T(8,128)(2,1)} %w_recv.3) | copy-start | bytes 98308
  1.9 10.2 %copy-start.6 = (bf16[128,128]{1,0:T(8,128)(2,1)S(1)}, bf16[128,128]{1,0:T(8,128)(2,1)}, u32[]{:S(2)}) copy-start(bf16[128,128]{1,0:T(8,128)(2,1)} %w_self.3) | copy-start | bytes 98308
  1.9 10.1 %collective-permute-start.1 = (bf16[112,128]{1,0:T(8,128)(2,1)S(1)}, bf16[112,128]{1,0:T(8,128)(2,1)S(1)}, u32[]{:S(2)}, u32[]{:S(2)}) collective-permute-start(bf16[112,128]{1,0:T(8,128)(2,1)S(1)} %get-tuple-element.21), channel_id=1, source_target_pairs={{0,2},{1,3},{2,4},{3,5},{4,6},{5,7},{6,8},{7,9},{8,10},{9,11},{10,... | collective-permute-start | bytes 86024 | tf_op jit(solution)/shard_map/ppermute | solution.py:341
  5.0 7.1 %collective-permute-start = (bf16[112,128]{1,0:T(8,128)(2,1)S(1)}, bf16[112,128]{1,0:T(8,128)(2,1)S(1)}, u32[]{:S(2)}, u32[]{:S(2)}) collective-permute-start(bf16[112,128]{1,0:T(8,128)(2,1)S(1)} %get-tuple-element.19.my_up), channel_id=1, source_target_pairs={{0,1},{1,2},{2,3},{3,4},{4,5},{5,6},{6,7},{7,8},{8,9},{9,10},{10,1... | collective-permute-start | bytes 86024 | tf_op jit(solution)/shard_map/ppermute | solution.py:341
  5.0 7.1 %collective-permute-start.3 = (bf16[128,128]{1,0:T(8,128)(2,1)S(1)}, bf16[128,128]{1,0:T(8,128)(2,1)S(1)}, u32[]{:S(2)}, u32[]{:S(2)}) collective-permute-start(bf16[128,128]{1,0:T(8,128)(2,1)S(1)} %get-tuple-element.22), channel_id=1, source_target_pairs={{0,14},{1,15},{2,0},{3,1},{4,2},{5,3},{6,4},{7,5},{8,6},{9,7},{10,... | collective-permute-start | bytes 98312 | tf_op jit(solution)/shard_map/ppermute | solution.py:341
  8.1 4.0 %collective-permute-start.2 = (bf16[128,128]{1,0:T(8,128)(2,1)S(1)}, bf16[128,128]{1,0:T(8,128)(2,1)S(1)}, u32[]{:S(2)}, u32[]{:S(2)}) collective-permute-start(bf16[128,128]{1,0:T(8,128)(2,1)S(1)} %get-tuple-element.20.my_down), channel_id=1, source_target_pairs={{0,15},{1,0},{2,1},{3,2},{4,3},{5,4},{6,5},{7,6},{8,7},{9,8},{10,9... | collective-permute-start | bytes 98312 | tf_op jit(solution)/shard_map/ppermute | solution.py:341
  34.4 12.2 %all-to-all-start.1 = ((bf16[32,24,128]{2,1,0:T(8,128)(2,1)}), bf16[32,24,128]{2,1,0:T(8,128)(2,1)S(1)}, u32[]{:S(2)}, u32[]{:S(2)}) async-start(bf16[32,24,128]{2,1,0:T(8,128)(2,1)} %shard_map.153), calls=%async_computation.1 | async-start | bytes 393216 | tf_op jit(solution)/shard_map/all_to_all | solution.py:434
  37.0 8.7 %collective-permute-start.4 = (bf16[64,128]{1,0:T(8,128)(2,1)S(1)}, bf16[64,128]{1,0:T(8,128)(2,1)S(1)}, u32[]{:S(2)}, u32[]{:S(2)}) collective-permute-start(bf16[64,128]{1,0:T(8,128)(2,1)S(1)} %get-tuple-element.32), channel_id=1, source_target_pairs={{0,1},{1,2},{2,3},{3,4},{4,5},{5,6},{6,7},{7,8},{8,9},{9,10},{10,1... | collective-permute-start | bytes 49160 | tf_op jit(solution)/shard_map/ppermute | solution.py:341
  37.4 8.2 %collective-permute-start.5 = (bf16[64,128]{1,0:T(8,128)(2,1)S(1)}, bf16[64,128]{1,0:T(8,128)(2,1)S(1)}, u32[]{:S(2)}, u32[]{:S(2)}) collective-permute-start(bf16[64,128]{1,0:T(8,128)(2,1)S(1)} %get-tuple-element.33), channel_id=1, source_target_pairs={{0,15},{1,0},{2,1},{3,2},{4,3},{5,4},{6,5},{7,6},{8,7},{9,8},{10,9... | collective-permute-start | bytes 49160 | tf_op jit(solution)/shard_map/ppermute | solution.py:341

commit v9 on v8

--- a/solution.py
+++ b/solution.py
@@ -12,7 +12,7 @@
 CODE_ROWS = 16
 LANES = 128
 FAR = -1e30
-PAIRS = 8
+PAIRS = 16
 
 
 def nn(left, right):

time: 47.7 us -> 47.4 us (level)
  no operation moved by 1% of the time
where the time goes in v9:
time: 47.4 us; the launch traced here: 47.2 us
  starting transfers between devices  14.7 us (31%)
  blocking collectives  13.5 us (28%)
  Pallas kernels  13.1 us (28%)
  waiting for transfers between devices  4.2 us (9%)
  local copies, waits for them, and re-layouts  0.88 us (2%)
  between operations  0.84 us (2%)
    all_to_all x1, blocking collectives, shards(): lax.all_to_all(grads.reshape(devices, share, width), axes, split_axis=0,...  13.5 us
    ppermute x6, starting transfers between devices, shift(): lax.ppermute(array, 'slab', [(i, (i + by) % size) for i in range(size)])  12.1 us
    pallas_call x1, Pallas kernels, shards(): call(layer_kernel, [((1, rows, width), BF16), ((border, width), BF16), ((...  7.74 us
    ppermute x6, waiting for transfers between devices, shift(): lax.ppermute(array, 'slab', [(i, (i + by) % size) for i in range(size)])  4.2 us
    all_to_all x1, starting transfers between devices, shards(): lax.all_to_all(shared, axes, split_axis=0, concat_axis=0, tiled=True)  2.59 us
    pallas_call x1, Pallas kernels, shards(): call(prep_kernel, [((edges, hot_rows), BF16), ((half_rows, edges), BF16),...  2.49 us
  transfers between devices with their start and end apart: 7, of which 1 were waited for; matrix products, arithmetic and copies ran while one was open for 0% of the time, Pallas kernels for 7%

profile of v9, /device:TPU:0, one launch (start us, length us, event | category | flops | bytes accessed | tf_op | source)
XLA Modules:
  0.0 47.2 jit_solution(15103680613166738630)
XLA Ops:
  0.7 0.6 %copy-done.12 = s32[1,128]{1,0:T(1,128)S(1)} copy-done((s32[1,128]{1,0:T(1,128)S(1)}, s32[1,128]{1,0:T(1,128)}, u32[]{:S(2)}) %copy-start.12) | copy-done | bytes 536
  1.3 0.0 copy-done.7
  1.3 0.2 copy-done
  1.5 0.0 copy-start.9
  1.5 0.0 copy-start.10
  1.5 0.3 shard_map.149
  1.9 0.0 copy-start.3
  1.9 0.0 copy-start.4
  1.9 0.0 copy-start.5
  1.9 0.0 copy-start.6
  1.9 3.0 %collective-permute-start.1 = (bf16[112,128]{1,0:T(8,128)(2,1)S(1)}, bf16[112,128]{1,0:T(8,128)(2,1)S(1)}, u32[]{:S(2)}, u32[]{:S(2)}) collective-permute-start(bf16[112,128]{1,0:T(8,128)(2,1)S(1)} %get-tuple-element.21), channel_id=1, source_target_pairs={{0,2},{1,3},{2,4},{3,5},{4,6},{5,7},{6,8},{7,9},{8,10},{9,11},{10,... | collective-permute-start | bytes 86024 | tf_op jit(solution)/shard_map/ppermute | solution.py:341
  5.0 0.0 collective-permute-start
  5.0 3.2 %collective-permute-start.3 = (bf16[128,128]{1,0:T(8,128)(2,1)S(1)}, bf16[128,128]{1,0:T(8,128)(2,1)S(1)}, u32[]{:S(2)}, u32[]{:S(2)}) collective-permute-start(bf16[128,128]{1,0:T(8,128)(2,1)S(1)} %get-tuple-element.22), channel_id=1, source_target_pairs={{0,14},{1,15},{2,0},{3,1},{4,2},{5,3},{6,4},{7,5},{8,6},{9,7},{10,... | collective-permute-start | bytes 98312 | tf_op jit(solution)/shard_map/ppermute | solution.py:341
  8.1 1.4 %collective-permute-start.2 = (bf16[128,128]{1,0:T(8,128)(2,1)S(1)}, bf16[128,128]{1,0:T(8,128)(2,1)S(1)}, u32[]{:S(2)}, u32[]{:S(2)}) collective-permute-start(bf16[128,128]{1,0:T(8,128)(2,1)S(1)} %get-tuple-element.20.my_down), channel_id=1, source_target_pairs={{0,15},{1,0},{2,1},{3,2},{4,3},{5,4},{6,5},{7,6},{8,7},{9,8},{10,9... | collective-permute-start | bytes 98312 | tf_op jit(solution)/shard_map/ppermute | solution.py:341
  9.5 0.0 copy-done.9
  9.6 2.5 %shard_map.150 = (bf16[8192,256]{1,0:T(8,128)(2,1)S(1)}, bf16[192,8192]{1,0:T(8,128)(2,1)S(1)}, bf16[2,256,256]{2,1,0:T(8,128)(2,1)S(1)}, s32[256,128]{1,0:T(8,128)S(1)}, f32[256,128]{1,0:T(8,128)S(1)}) custom-call(s32[1,32,256]{2,1,0:T(8,128)S(1)} %bitcast.6, s32[1,32,256]{2,1,0:T(8,128)S(1)} %bitcast.7, bf16[128,128]{1,0:T(8,128)(2,1)S(1)} %copy-done.10, ...), custom_call_target="tpu_custom_call" | custom-call | flops 2000000000 | bytes 1024 | tf_op jit(solution)/shard_map/pallas_call | solution.py:359
  12.1 0.0 collective-permute-done.1.low_far
  12.1 0.0 collective-permute-done.low
  12.1 0.0 collective-permute-done.3.high_far
  12.1 0.0 collective-permute-done.2.high
  12.1 0.0 copy-done.3
  12.1 7.7 %shard_map.151 = (bf16[1,256,128]{2,1,0:T(8,128)(2,1)}, bf16[64,128]{1,0:T(8,128)(2,1)S(1)}, bf16[64,128]{1,0:T(8,128)(2,1)S(1)}, bf16[768,128]{1,0:T(8,128)(2,1...) custom-call(bf16[1,256,128]{2,1,0:T(8,128)(2,1)S(1)} %copy-done, ...), custom_call_target="tpu_custom_call" | custom-call | flops 2000000000 | bytes 1024 | tf_op jit(solution)/shard_map/pallas_call | solution.py:390
  19.9 13.5 %all_to_all.10.parts = bf16[32,24,128]{2,1,0:T(8,128)(2,1)S(1)} all-to-all(bf16[32,24,128]{2,1,0:T(8,128)(2,1)S(1)} %bitcast.5), channel_id=1, replica_groups=mesh['grp'=2,'slab'=16] {'grp','slab'}, dimensions={0} | all-to-all | bytes 393216 | tf_op jit(solution)/shard_map/all_to_all | solution.py:414
  33.4 0.7 %shard_map.153 = bf16[32,24,128]{2,1,0:T(8,128)(2,1)} custom-call(bf16[32,24,128]{2,1,0:T(8,128)(2,1)S(1)} %all_to_all.10.parts), custom_call_target="tpu_custom_call" | custom-call | flops 2000000000 | bytes 1024 | tf_op jit(solution)/shard_map/pallas_call | solution.py:433
  34.1 2.6 %all-to-all-start.1 = ((bf16[32,24,128]{2,1,0:T(8,128)(2,1)}), bf16[32,24,128]{2,1,0:T(8,128)(2,1)S(1)}, u32[]{:S(2)}, u32[]{:S(2)}) async-start(bf16[32,24,128]{2,1,0:T(8,128)(2,1)} %shard_map.153), calls=%async_computation.1 | async-start | bytes 393216 | tf_op jit(solution)/shard_map/all_to_all | solution.py:434
  36.7 0.4 collective-permute-start.4
  37.2 4.0 %collective-permute-start.5 = (bf16[64,128]{1,0:T(8,128)(2,1)S(1)}, bf16[64,128]{1,0:T(8,128)(2,1)S(1)}, u32[]{:S(2)}, u32[]{:S(2)}) collective-permute-start(bf16[64,128]{1,0:T(8,128)(2,1)S(1)} %get-tuple-element.33), channel_id=1, source_target_pairs={{0,15},{1,0},{2,1},{3,2},{4,3},{5,4},{6,5},{7,6},{8,7},{9,8},{10,9... | collective-permute-start | bytes 49160 | tf_op jit(solution)/shard_map/ppermute | solution.py:341
  41.2 4.2 %collective-permute-done.4.from_low = bf16[64,128]{1,0:T(8,128)(2,1)S(1)} collective-permute-done((bf16[64,128]{1,0:T(8,128)(2,1)S(1)}, bf16[64,128]{1,0:T(8,128)(2,1)S(1)}, u32[]{:S(2)}, u32[]{:S(2)}) %collective-permute-start.4) | collective-permute-done | bytes 16416 | tf_op jit(solution)/shard_map/ppermute | solution.py:341
  45.4 0.0 collective-permute-done.5.from_high
  45.4 0.9 %shard_map.152 = bf16[1,256,128]{2,1,0:T(8,128)(2,1)} custom-call(bf16[1,256,128]{2,1,0:T(8,128)(2,1)S(1)} %copy-done.1, bf16[256,128]{1,0:T(8,128)(2,1)S(1)} %get-tuple-element.29.d_node, bf16[256,128]{1,0:T(8,128)(2,1)S(1)} %get-tuple-element.30.d_centre, bf16[256,128]{1,0:T(8,128)(2,1)S(1)} %get-tuple-element.31.d_neigh, bf16[128,128]{1,0:T(8,128)(2,1)S(1)} %copy-done.6, ...), custom_call_target="tpu_custom_call" | custom-call | flops 2000000000 | bytes 1024 | tf_op jit(solution)/shard_map/pallas_call | solution.py:429
  46.3 0.0 all-to-all-done.1
  46.3 0.9 %shard_map.154 = f32[6,128,128]{2,1,0:T(8,128)} custom-call(bf16[768,128]{1,0:T(8,128)(2,1)S(1)} %bitcast.4), custom_call_target="tpu_custom_call" | custom-call | flops 2000000000 | bytes 1024 | tf_op jit(solution)/shard_map/pallas_call | solution.py:436
  (16 shorter events, 0.0 us)
Async XLA Ops:
  0.6 0.7 %copy-start.12 = (s32[1,128]{1,0:T(1,128)S(1)}, s32[1,128]{1,0:T(1,128)}, u32[]{:S(2)}) copy-start(s32[1,128]{1,0:T(1,128)} %sends.3) | copy-start | bytes 1540
  0.6 0.7 %copy-start.7 = (s32[1,256]{1,0:T(1,128)S(1)}, s32[1,256]{1,0:T(1,128)}, u32[]{:S(2)}) copy-start(s32[1,256]{1,0:T(1,128)} %arrive.3) | copy-start | bytes 3076
  0.7 0.9 %copy-start = (bf16[1,256,128]{2,1,0:T(8,128)(2,1)S(1)}, bf16[1,256,128]{2,1,0:T(8,128)(2,1)}, u32[]{:S(2)}) copy-start(bf16[1,256,128]{2,1,0:T(8,128)(2,1)} %nodes.3) | copy-start | bytes 196612
  0.7 0.8 %copy-start.11 = (s32[1,64]{1,0:T(1,128)S(1)}, s32[1,64]{1,0:T(1,128)}, u32[]{:S(2)}) copy-start(s32[1,64]{1,0:T(1,128)} %leave.1) | copy-start | bytes 772
  1.5 8.0 %copy-start.1 = (bf16[1,256,128]{2,1,0:T(8,128)(2,1)S(1)}, bf16[1,256,128]{2,1,0:T(8,128)(2,1)}, u32[]{:S(2)}) copy-start(bf16[1,256,128]{2,1,0:T(8,128)(2,1)} %cotangent.5) | copy-start | bytes 196612
  1.5 8.0 %copy-start.2 = (bf16[128,128]{1,0:T(8,128)(2,1)S(1)}, bf16[128,128]{1,0:T(8,128)(2,1)}, u32[]{:S(2)}) copy-start(bf16[128,128]{1,0:T(8,128)(2,1)} %w_out.3) | copy-start | bytes 98308
  1.5 8.0 %copy-start.8 = (s32[1,256,32]{1,2,0:T(8,128)S(1)}, s32[1,256,32]{1,2,0:T(8,128)}, u32[]{:S(2)}) copy-start(s32[1,256,32]{1,2,0:T(8,128)} %param.17) | copy-start | bytes 98308
  1.5 8.0 %copy-start.9 = (s32[1,256,32]{1,2,0:T(8,128)S(1)}, s32[1,256,32]{1,2,0:T(8,128)}, u32[]{:S(2)}) copy-start(s32[1,256,32]{1,2,0:T(8,128)} %param.18) | copy-start | bytes 98308
  1.5 8.0 %copy-start.10 = (bf16[128,128]{1,0:T(8,128)(2,1)S(1)}, bf16[128,128]{1,0:T(8,128)(2,1)}, u32[]{:S(2)}) copy-start(bf16[128,128]{1,0:T(8,128)(2,1)} %w_msg.1) | copy-start | bytes 98308
  1.9 10.2 %copy-start.3 = (bf16[128,128]{1,0:T(8,128)(2,1)S(1)}, bf16[128,128]{1,0:T(8,128)(2,1)}, u32[]{:S(2)}) copy-start(bf16[128,128]{1,0:T(8,128)(2,1)} %w_agg.1) | copy-start | bytes 98308
  1.9 10.2 %copy-start.4 = (bf16[128,128]{1,0:T(8,128)(2,1)S(1)}, bf16[128,128]{1,0:T(8,128)(2,1)}, u32[]{:S(2)}) copy-start(bf16[128,128]{1,0:T(8,128)(2,1)} %w_send.3) | copy-start | bytes 98308
  1.9 10.2 %copy-start.5 = (bf16[128,128]{1,0:T(8,128)(2,1)S(1)}, bf16[128,128]{1,0:T(8,128)(2,1)}, u32[]{:S(2)}) copy-start(bf16[128,128]{1,0:T(8,128)(2,1)} %w_recv.3) | copy-start | bytes 98308
  1.9 10.2 %copy-start.6 = (bf16[128,128]{1,0:T(8,128)(2,1)S(1)}, bf16[128,128]{1,0:T(8,128)(2,1)}, u32[]{:S(2)}) copy-start(bf16[128,128]{1,0:T(8,128)(2,1)} %w_self.3) | copy-start | bytes 98308
  1.9 10.1 %collective-permute-start.1 = (bf16[112,128]{1,0:T(8,128)(2,1)S(1)}, bf16[112,128]{1,0:T(8,128)(2,1)S(1)}, u32[]{:S(2)}, u32[]{:S(2)}) collective-permute-start(bf16[112,128]{1,0:T(8,128)(2,1)S(1)} %get-tuple-element.21), channel_id=1, source_target_pairs={{0,2},{1,3},{2,4},{3,5},{4,6},{5,7},{6,8},{7,9},{8,10},{9,11},{10,... | collective-permute-start | bytes 86024 | tf_op jit(solution)/shard_map/ppermute | solution.py:341
  5.0 7.1 %collective-permute-start = (bf16[112,128]{1,0:T(8,128)(2,1)S(1)}, bf16[112,128]{1,0:T(8,128)(2,1)S(1)}, u32[]{:S(2)}, u32[]{:S(2)}) collective-permute-start(bf16[112,128]{1,0:T(8,128)(2,1)S(1)} %get-tuple-element.19.my_up), channel_id=1, source_target_pairs={{0,1},{1,2},{2,3},{3,4},{4,5},{5,6},{6,7},{7,8},{8,9},{9,10},{10,1... | collective-permute-start | bytes 86024 | tf_op jit(solution)/shard_map/ppermute | solution.py:341
  5.0 7.1 %collective-permute-start.3 = (bf16[128,128]{1,0:T(8,128)(2,1)S(1)}, bf16[128,128]{1,0:T(8,128)(2,1)S(1)}, u32[]{:S(2)}, u32[]{:S(2)}) collective-permute-start(bf16[128,128]{1,0:T(8,128)(2,1)S(1)} %get-tuple-element.22), channel_id=1, source_target_pairs={{0,14},{1,15},{2,0},{3,1},{4,2},{5,3},{6,4},{7,5},{8,6},{9,7},{10,... | collective-permute-start | bytes 98312 | tf_op jit(solution)/shard_map/ppermute | solution.py:341
  8.1 4.0 %collective-permute-start.2 = (bf16[128,128]{1,0:T(8,128)(2,1)S(1)}, bf16[128,128]{1,0:T(8,128)(2,1)S(1)}, u32[]{:S(2)}, u32[]{:S(2)}) collective-permute-start(bf16[128,128]{1,0:T(8,128)(2,1)S(1)} %get-tuple-element.20.my_down), channel_id=1, source_target_pairs={{0,15},{1,0},{2,1},{3,2},{4,3},{5,4},{6,5},{7,6},{8,7},{9,8},{10,9... | collective-permute-start | bytes 98312 | tf_op jit(solution)/shard_map/ppermute | solution.py:341
  34.1 12.2 %all-to-all-start.1 = ((bf16[32,24,128]{2,1,0:T(8,128)(2,1)}), bf16[32,24,128]{2,1,0:T(8,128)(2,1)S(1)}, u32[]{:S(2)}, u32[]{:S(2)}) async-start(bf16[32,24,128]{2,1,0:T(8,128)(2,1)} %shard_map.153), calls=%async_computation.1 | async-start | bytes 393216 | tf_op jit(solution)/shard_map/all_to_all | solution.py:434
  36.7 8.7 %collective-permute-start.4 = (bf16[64,128]{1,0:T(8,128)(2,1)S(1)}, bf16[64,128]{1,0:T(8,128)(2,1)S(1)}, u32[]{:S(2)}, u32[]{:S(2)}) collective-permute-start(bf16[64,128]{1,0:T(8,128)(2,1)S(1)} %get-tuple-element.32), channel_id=1, source_target_pairs={{0,1},{1,2},{2,3},{3,4},{4,5},{5,6},{6,7},{7,8},{8,9},{9,10},{10,1... | collective-permute-start | bytes 49160 | tf_op jit(solution)/shard_map/ppermute | solution.py:341
  37.2 8.2 %collective-permute-start.5 = (bf16[64,128]{1,0:T(8,128)(2,1)S(1)}, bf16[64,128]{1,0:T(8,128)(2,1)S(1)}, u32[]{:S(2)}, u32[]{:S(2)}) collective-permute-start(bf16[64,128]{1,0:T(8,128)(2,1)S(1)} %get-tuple-element.33), channel_id=1, source_target_pairs={{0,15},{1,0},{2,1},{3,2},{4,3},{5,4},{6,5},{7,6},{8,7},{9,8},{10,9... | collective-permute-start | bytes 49160 | tf_op jit(solution)/shard_map/ppermute | solution.py:341

commit v10 on v9

--- a/solution.py
+++ b/solution.py
@@ -12,7 +12,8 @@
 CODE_ROWS = 16
 LANES = 128
 FAR = -1e30
-PAIRS = 16
+GROUP = 4
+BLOCK = 64
 
 
 def nn(left, right):
@@ -151,16 +152,14 @@
     ds2_s,
     agg_s,
     dcen_s,
-    dneigh_s,
-    gmsg_s,
+    dpre2_s,
+    dpre_s,
 ):
     rows, width = nodes.shape[1:]
     slots = hot.shape[0] // rows
     border = back_low.shape[0]
     migr = low.shape[0] - border - CODE_ROWS
     table_rows = rows + 2 * border
-    chunk = 2 * PAIRS
-    steps = slots // chunk
 
     pool = jnp.concatenate(
         [nodes[0], low[border : border + migr], high[border : border + migr]], axis=0
@@ -183,32 +182,34 @@
     half_neigh = (0.5 * nn(table, w_recv[...]).astype(BF16).astype(F32)).astype(BF16)
     neigh_s[:half_rows] = jnp.concatenate([half_neigh[:half_rows], half_neigh[half_rows:]], axis=1)
     neigh_s[half_rows:] = jnp.full((hot_rows - half_rows, 2 * width), FAR, BF16)
-    agg_s[...] = jnp.zeros_like(agg_s)
-
-    @pl.loop(0, steps)
-    def forward(step):
-        ids = slot_ids(nbr_ids, step, chunk)
-        gathered = nn(hot[pl.ds(step * (chunk * rows), chunk * rows)], neigh_s[...])
-        base = step * (PAIRS * rows)
-        for p in range(PAIRS):
-            for side in range(2):
-                cols = slice(side * width, (side + 1) * width)
-                j = 2 * p + side
-                pick = gathered[j * rows : (j + 1) * rows]
-                pick = jnp.where(ids[j] >= hot_rows, pick[:, width:], pick[:, :width])
-                act, slope = silu_parts(half_centre + pick)
-                span = pl.ds(base + p * rows, rows)
-                ds1_s[span, cols] = slope
-                hid_s[span, cols] = act.astype(BF16)
-        halves = nn(hid_s[pl.ds(base, PAIRS * rows)], wide[0])
-        total = agg_s[...]
-        for p in range(PAIRS):
-            for side in range(2):
-                cols = slice(side * width, (side + 1) * width)
-                act, slope = silu_parts(halves[p * rows : (p + 1) * rows, cols])
+    ids = slot_ids(nbr_ids, 0, slots)
+    blocks = [slice(start, start + BLOCK) for start in range(0, rows, BLOCK)]
+    sides = (slice(0, width), slice(width, 2 * width))
+
+    for first in range(0, slots, GROUP):
+        gathered = nn(hot[first * rows : (first + GROUP) * rows], neigh_s[...])
+        for j in range(GROUP):
+            pair, side = divmod(first + j, 2)
+            for block in blocks:
+                pick = gathered[j * rows + block.start : j * rows + block.stop]
+                pick = jnp.where(
+                    ids[first + j][block] >= hot_rows, pick[:, sides[1]], pick[:, sides[0]]
+                )
+                act, slope = silu_parts(half_centre[block] + pick)
+                at = slice(pair * rows + block.start, pair * rows + block.stop)
+                ds1_s[at, sides[side]] = slope
+                hid_s[at, sides[side]] = act.astype(BF16)
+        base = first // 2 * rows
+        halves = nn(hid_s[base : base + GROUP // 2 * rows], wide[0])
+        for block in blocks:
+            total = jnp.zeros((BLOCK, width), F32) if first == 0 else agg_s[block]
+            for j in range(GROUP):
+                pair, side = divmod(j, 2)
+                at = slice(pair * rows + block.start, pair * rows + block.stop)
+                act, slope = silu_parts(halves[at, sides[side]])
                 total = total + act
-                ds2_s[pl.ds(base + p * rows, rows), cols] = slope
-        agg_s[...] = total
+                ds2_s[base + at.start : base + at.stop, sides[side]] = slope
+            agg_s[block] = total
 
     agg_b = agg_s[...].astype(BF16)
     node_pre = nn(moved, w_self[...]) + nn(agg_b, w_agg[...])
@@ -219,40 +220,34 @@
     d_node = (d_hid[...] * (0.5 * slope)).astype(BF16)
     half_d_agg = 0.5 * nt(d_node, w_agg[...])
 
-    dcen_s[...] = jnp.zeros_like(dcen_s)
-    dneigh_s[...] = jnp.zeros_like(dneigh_s)
-    gmsg_s[...] = jnp.zeros_like(gmsg_s)
-    none = jnp.zeros((rows, width), BF16)
-    border_id = jnp.full((rows, width), hot_rows, jnp.int16)
-
-    @pl.loop(0, steps)
-    def backward(step):
-        ids = slot_ids(nbr_ids, step, chunk)
-        span = pl.ds(step * (PAIRS * rows), PAIRS * rows)
-        d_agg = jnp.concatenate([half_d_agg, half_d_agg], axis=1)
-        d_agg = jnp.concatenate([d_agg] * PAIRS, axis=0)
-        d_pre2 = (d_agg * ds2_s[span]).astype(BF16)
-        d_pre = nn(d_pre2, wide[1]) * ds1_s[span]
-        gmsg_s[...] += tn(hid_s[span], d_pre2)
-        total = dcen_s[...]
-        wides = []
-        for j in range(chunk):
-            p, side = divmod(j, 2)
-            part = d_pre[p * rows : (p + 1) * rows, side * width : (side + 1) * width]
-            total = total + part
-            part = part.astype(BF16)
-            is_up = ids[j].astype(jnp.int16) >= border_id
-            wides.append(
-                jnp.concatenate(
-                    [jnp.where(is_up, none, part), jnp.where(is_up, part, none)], axis=1
-                )
-            )
-        dcen_s[...] = total
-        edges = pl.ds(pl.multiple_of(step * (chunk * rows), LANES), chunk * rows)
-        dneigh_s[...] += nn(hot_t[:, edges], jnp.concatenate(wides, axis=0))
+    none = jnp.zeros((BLOCK, width), BF16)
+    border_id = jnp.full((BLOCK, width), hot_rows, jnp.int16)
+    for first in range(0, slots, GROUP):
+        base = first // 2 * rows
+        span = slice(base, base + GROUP // 2 * rows)
+        for pair in range(GROUP // 2):
+            for block in blocks:
+                at = slice(base + pair * rows + block.start, base + pair * rows + block.stop)
+                for side in sides:
+                    dpre2_s[at, side] = (half_d_agg[block] * ds2_s[at, side]).astype(BF16)
+        d_hids = nn(dpre2_s[span], wide[1])
+        for block in blocks:
+            total = jnp.zeros((BLOCK, width), F32) if first == 0 else dcen_s[block]
+            for j in range(GROUP):
+                pair, side = divmod(j, 2)
+                at = slice(pair * rows + block.start, pair * rows + block.stop)
+                part = d_hids[at, sides[side]] * ds1_s[base + at.start : base + at.stop, sides[side]]
+                total = total + part
+                part = part.astype(BF16)
+                is_up = ids[first + j][block].astype(jnp.int16) >= border_id
+                at = slice((first + j) * rows + block.start, (first + j) * rows + block.stop)
+                dpre_s[at, sides[0]] = jnp.where(is_up, none, part)
+                dpre_s[at, sides[1]] = jnp.where(is_up, part, none)
+            dcen_s[block] = total
+    gmsg = tn(hid_s[...], dpre2_s[...])
+    d_neigh = nn(hot_t[...], dpre_s[...]).astype(BF16)
 
     d_centre = dcen_s[...].astype(BF16)
-    d_neigh = dneigh_s[...].astype(BF16)
     d_neigh = jnp.concatenate([d_neigh[:, :width], d_neigh[:, width:]], axis=0)
     d_borrowed = nt(d_neigh[rows:], w_recv[...]).astype(BF16)
     back_low[...] = d_borrowed[:border]
@@ -263,7 +258,7 @@
     parts = (
         tn(moved, d_centre),
         tn(table, d_neigh),
-        gmsg_s[:width, :width] + gmsg_s[width:, width:],
+        gmsg[:width, :width] + gmsg[width:, width:],
         tn(moved, d_node),
         tn(agg_b, d_node),
         tn(node_hid, cot),
@@ -405,8 +400,8 @@
             pltpu.VMEM((pair_rows, 2 * width), F32),
             pltpu.VMEM((rows, width), F32),
             pltpu.VMEM((rows, width), F32),
-            pltpu.VMEM((half_rows, 2 * width), F32),
-            pltpu.VMEM((2 * width, 2 * width), F32),
+            pltpu.VMEM((pair_rows, 2 * width), BF16),
+            pltpu.VMEM((edges, 2 * width), BF16),
         ],
     )(*sources)
     from_low = shift(back_high, 1)

time: 47.4 us -> 48.5 us (1.023)
  Pallas kernels: 13.1 us -> 14.2 us
    pallas_call x1, Pallas kernels: 7.74 us -> 8.84 us  [shards(): call(layer_kernel, [((1, rows, width), BF16), ((border, width), BF16), ((...]
where the time goes in v10:
time: 48.5 us; the launch traced here: 48.3 us
  starting transfers between devices  14.7 us (30%)
  Pallas kernels  14.2 us (29%)
  blocking collectives  13.5 us (28%)
  waiting for transfers between devices  4.2 us (9%)
  local copies, waits for them, and re-layouts  0.88 us (2%)
  between operations  0.83 us (2%)
    all_to_all x1, blocking collectives, shards(): lax.all_to_all(grads.reshape(devices, share, width), axes, split_axis=0,...  13.5 us
    ppermute x6, starting transfers between devices, shift(): lax.ppermute(array, 'slab', [(i, (i + by) % size) for i in range(size)])  12.1 us
    pallas_call x1, Pallas kernels, shards(): call(layer_kernel, [((1, rows, width), BF16), ((border, width), BF16), ((...  8.84 us
    ppermute x6, waiting for transfers between devices, shift(): lax.ppermute(array, 'slab', [(i, (i + by) % size) for i in range(size)])  4.2 us
    all_to_all x1, starting transfers between devices, shards(): lax.all_to_all(shared, axes, split_axis=0, concat_axis=0, tiled=True)  2.59 us
    pallas_call x1, Pallas kernels, shards(): call(prep_kernel, [((edges, hot_rows), BF16), ((half_rows, edges), BF16),...  2.49 us
  transfers between devices with their start and end apart: 7, of which 1 were waited for; matrix products, arithmetic and copies ran while one was open for 0% of the time, Pallas kernels for 7%

profile of v10, /device:TPU:0, one launch (start us, length us, event | category | flops | bytes accessed | tf_op | source)
XLA Modules:
  0.0 48.3 jit_solution(177028498251413842)
XLA Ops:
  0.6 0.0 copy-start.12
  0.6 0.0 copy-start.7
  0.7 0.6 %copy-done.12 = s32[1,128]{1,0:T(1,128)S(1)} copy-done((s32[1,128]{1,0:T(1,128)S(1)}, s32[1,128]{1,0:T(1,128)}, u32[]{:S(2)}) %copy-start.12) | copy-done | bytes 536
  1.3 0.0 copy-done.7
  1.3 0.2 copy-done
  1.5 0.0 copy-start.9
  1.5 0.0 copy-start.10
  1.5 0.3 shard_map.149
  1.9 0.0 copy-start.3
  1.9 0.0 copy-start.4
  1.9 0.0 copy-start.5
  1.9 0.0 copy-start.6
  1.9 3.0 %collective-permute-start.1 = (bf16[112,128]{1,0:T(8,128)(2,1)S(1)}, bf16[112,128]{1,0:T(8,128)(2,1)S(1)}, u32[]{:S(2)}, u32[]{:S(2)}) collective-permute-start(bf16[112,128]{1,0:T(8,128)(2,1)S(1)} %get-tuple-element.21), channel_id=1, source_target_pairs={{0,2},{1,3},{2,4},{3,5},{4,6},{5,7},{6,8},{7,9},{8,10},{9,11},{10,... | collective-permute-start | bytes 86024 | tf_op jit(solution)/shard_map/ppermute | solution.py:336
  5.0 0.0 collective-permute-start
  5.0 3.2 %collective-permute-start.3 = (bf16[128,128]{1,0:T(8,128)(2,1)S(1)}, bf16[128,128]{1,0:T(8,128)(2,1)S(1)}, u32[]{:S(2)}, u32[]{:S(2)}) collective-permute-start(bf16[128,128]{1,0:T(8,128)(2,1)S(1)} %get-tuple-element.22), channel_id=1, source_target_pairs={{0,14},{1,15},{2,0},{3,1},{4,2},{5,3},{6,4},{7,5},{8,6},{9,7},{10,... | collective-permute-start | bytes 98312 | tf_op jit(solution)/shard_map/ppermute | solution.py:336
  8.1 1.4 %collective-permute-start.2 = (bf16[128,128]{1,0:T(8,128)(2,1)S(1)}, bf16[128,128]{1,0:T(8,128)(2,1)S(1)}, u32[]{:S(2)}, u32[]{:S(2)}) collective-permute-start(bf16[128,128]{1,0:T(8,128)(2,1)S(1)} %get-tuple-element.20.my_down), channel_id=1, source_target_pairs={{0,15},{1,0},{2,1},{3,2},{4,3},{5,4},{6,5},{7,6},{8,7},{9,8},{10,9... | collective-permute-start | bytes 98312 | tf_op jit(solution)/shard_map/ppermute | solution.py:336
  9.6 2.5 %shard_map.150 = (bf16[8192,256]{1,0:T(8,128)(2,1)S(1)}, bf16[192,8192]{1,0:T(8,128)(2,1)S(1)}, bf16[2,256,256]{2,1,0:T(8,128)(2,1)S(1)}, s32[256,128]{1,0:T(8,128)S(1)}, f32[256,128]{1,0:T(8,128)S(1)}) custom-call(s32[1,32,256]{2,1,0:T(8,128)S(1)} %bitcast.6, s32[1,32,256]{2,1,0:T(8,128)S(1)} %bitcast.7, bf16[128,128]{1,0:T(8,128)(2,1)S(1)} %copy-done.10, ...), custom_call_target="tpu_custom_call" | custom-call | flops 2000000000 | bytes 1024 | tf_op jit(solution)/shard_map/pallas_call | solution.py:354
  12.1 0.0 collective-permute-done.1.low_far
  12.1 0.0 collective-permute-done.low
  12.1 0.0 collective-permute-done.3.high_far
  12.1 0.0 collective-permute-done.2.high
  12.1 8.8 %shard_map.151 = (bf16[1,256,128]{2,1,0:T(8,128)(2,1)}, bf16[64,128]{1,0:T(8,128)(2,1)S(1)}, bf16[64,128]{1,0:T(8,128)(2,1)S(1)}, bf16[768,128]{1,0:T(8,128)(2,1...) custom-call(bf16[1,256,128]{2,1,0:T(8,128)(2,1)S(1)} %copy-done, ...), custom_call_target="tpu_custom_call" | custom-call | flops 2000000000 | bytes 1024 | tf_op jit(solution)/shard_map/pallas_call | solution.py:385
  21.0 13.5 %all_to_all.10.parts = bf16[32,24,128]{2,1,0:T(8,128)(2,1)S(1)} all-to-all(bf16[32,24,128]{2,1,0:T(8,128)(2,1)S(1)} %bitcast.5), channel_id=1, replica_groups=mesh['grp'=2,'slab'=16] {'grp','slab'}, dimensions={0} | all-to-all | bytes 393216 | tf_op jit(solution)/shard_map/all_to_all | solution.py:409
  34.5 0.7 %shard_map.153 = bf16[32,24,128]{2,1,0:T(8,128)(2,1)} custom-call(bf16[32,24,128]{2,1,0:T(8,128)(2,1)S(1)} %all_to_all.10.parts), custom_call_target="tpu_custom_call" | custom-call | flops 2000000000 | bytes 1024 | tf_op jit(solution)/shard_map/pallas_call | solution.py:428
  35.2 2.6 %all-to-all-start.1 = ((bf16[32,24,128]{2,1,0:T(8,128)(2,1)}), bf16[32,24,128]{2,1,0:T(8,128)(2,1)S(1)}, u32[]{:S(2)}, u32[]{:S(2)}) async-start(bf16[32,24,128]{2,1,0:T(8,128)(2,1)} %shard_map.153), calls=%async_computation.1 | async-start | bytes 393216 | tf_op jit(solution)/shard_map/all_to_all | solution.py:429
  37.8 0.4 collective-permute-start.4
  38.3 4.0 %collective-permute-start.5 = (bf16[64,128]{1,0:T(8,128)(2,1)S(1)}, bf16[64,128]{1,0:T(8,128)(2,1)S(1)}, u32[]{:S(2)}, u32[]{:S(2)}) collective-permute-start(bf16[64,128]{1,0:T(8,128)(2,1)S(1)} %get-tuple-element.33), channel_id=1, source_target_pairs={{0,15},{1,0},{2,1},{3,2},{4,3},{5,4},{6,5},{7,6},{8,7},{9,8},{10,9... | collective-permute-start | bytes 49160 | tf_op jit(solution)/shard_map/ppermute | solution.py:336
  42.3 4.2 %collective-permute-done.4.from_low = bf16[64,128]{1,0:T(8,128)(2,1)S(1)} collective-permute-done((bf16[64,128]{1,0:T(8,128)(2,1)S(1)}, bf16[64,128]{1,0:T(8,128)(2,1)S(1)}, u32[]{:S(2)}, u32[]{:S(2)}) %collective-permute-start.4) | collective-permute-done | bytes 16416 | tf_op jit(solution)/shard_map/ppermute | solution.py:336
  46.5 0.0 collective-permute-done.5.from_high
  46.5 0.9 %shard_map.152 = bf16[1,256,128]{2,1,0:T(8,128)(2,1)} custom-call(bf16[1,256,128]{2,1,0:T(8,128)(2,1)S(1)} %copy-done.1, bf16[256,128]{1,0:T(8,128)(2,1)S(1)} %get-tuple-element.29.d_node, bf16[256,128]{1,0:T(8,128)(2,1)S(1)} %get-tuple-element.30.d_centre, bf16[256,128]{1,0:T(8,128)(2,1)S(1)} %get-tuple-element.31.d_neigh, bf16[128,128]{1,0:T(8,128)(2,1)S(1)} %copy-done.6, ...), custom_call_target="tpu_custom_call" | custom-call | flops 2000000000 | bytes 1024 | tf_op jit(solution)/shard_map/pallas_call | solution.py:424
  47.4 0.0 all-to-all-done.1
  47.4 0.9 %shard_map.154 = f32[6,128,128]{2,1,0:T(8,128)} custom-call(bf16[768,128]{1,0:T(8,128)(2,1)S(1)} %bitcast.4), custom_call_target="tpu_custom_call" | custom-call | flops 2000000000 | bytes 1024 | tf_op jit(solution)/shard_map/pallas_call | solution.py:431
  (16 shorter events, 0.0 us)
Async XLA Ops:
  0.6 0.7 %copy-start.12 = (s32[1,128]{1,0:T(1,128)S(1)}, s32[1,128]{1,0:T(1,128)}, u32[]{:S(2)}) copy-start(s32[1,128]{1,0:T(1,128)} %sends.3) | copy-start | bytes 1540
  0.6 0.7 %copy-start.7 = (s32[1,256]{1,0:T(1,128)S(1)}, s32[1,256]{1,0:T(1,128)}, u32[]{:S(2)}) copy-start(s32[1,256]{1,0:T(1,128)} %arrive.3) | copy-start | bytes 3076
  0.7 0.9 %copy-start = (bf16[1,256,128]{2,1,0:T(8,128)(2,1)S(1)}, bf16[1,256,128]{2,1,0:T(8,128)(2,1)}, u32[]{:S(2)}) copy-start(bf16[1,256,128]{2,1,0:T(8,128)(2,1)} %nodes.3) | copy-start | bytes 196612
  0.7 0.8 %copy-start.11 = (s32[1,64]{1,0:T(1,128)S(1)}, s32[1,64]{1,0:T(1,128)}, u32[]{:S(2)}) copy-start(s32[1,64]{1,0:T(1,128)} %leave.1) | copy-start | bytes 772
  1.5 8.0 %copy-start.1 = (bf16[1,256,128]{2,1,0:T(8,128)(2,1)S(1)}, bf16[1,256,128]{2,1,0:T(8,128)(2,1)}, u32[]{:S(2)}) copy-start(bf16[1,256,128]{2,1,0:T(8,128)(2,1)} %cotangent.5) | copy-start | bytes 196612
  1.5 8.0 %copy-start.2 = (bf16[128,128]{1,0:T(8,128)(2,1)S(1)}, bf16[128,128]{1,0:T(8,128)(2,1)}, u32[]{:S(2)}) copy-start(bf16[128,128]{1,0:T(8,128)(2,1)} %w_out.3) | copy-start | bytes 98308
  1.5 8.0 %copy-start.8 = (s32[1,256,32]{1,2,0:T(8,128)S(1)}, s32[1,256,32]{1,2,0:T(8,128)}, u32[]{:S(2)}) copy-start(s32[1,256,32]{1,2,0:T(8,128)} %param.17) | copy-start | bytes 98308
  1.5 8.0 %copy-start.9 = (s32[1,256,32]{1,2,0:T(8,128)S(1)}, s32[1,256,32]{1,2,0:T(8,128)}, u32[]{:S(2)}) copy-start(s32[1,256,32]{1,2,0:T(8,128)} %param.18) | copy-start | bytes 98308
  1.5 8.0 %copy-start.10 = (bf16[128,128]{1,0:T(8,128)(2,1)S(1)}, bf16[128,128]{1,0:T(8,128)(2,1)}, u32[]{:S(2)}) copy-start(bf16[128,128]{1,0:T(8,128)(2,1)} %w_msg.1) | copy-start | bytes 98308
  1.9 10.2 %copy-start.3 = (bf16[128,128]{1,0:T(8,128)(2,1)S(1)}, bf16[128,128]{1,0:T(8,128)(2,1)}, u32[]{:S(2)}) copy-start(bf16[128,128]{1,0:T(8,128)(2,1)} %w_agg.1) | copy-start | bytes 98308
  1.9 10.2 %copy-start.4 = (bf16[128,128]{1,0:T(8,128)(2,1)S(1)}, bf16[128,128]{1,0:T(8,128)(2,1)}, u32[]{:S(2)}) copy-start(bf16[128,128]{1,0:T(8,128)(2,1)} %w_send.3) | copy-start | bytes 98308
  1.9 10.2 %copy-start.5 = (bf16[128,128]{1,0:T(8,128)(2,1)S(1)}, bf16[128,128]{1,0:T(8,128)(2,1)}, u32[]{:S(2)}) copy-start(bf16[128,128]{1,0:T(8,128)(2,1)} %w_recv.3) | copy-start | bytes 98308
  1.9 10.2 %copy-start.6 = (bf16[128,128]{1,0:T(8,128)(2,1)S(1)}, bf16[128,128]{1,0:T(8,128)(2,1)}, u32[]{:S(2)}) copy-start(bf16[128,128]{1,0:T(8,128)(2,1)} %w_self.3) | copy-start | bytes 98308
  1.9 10.1 %collective-permute-start.1 = (bf16[112,128]{1,0:T(8,128)(2,1)S(1)}, bf16[112,128]{1,0:T(8,128)(2,1)S(1)}, u32[]{:S(2)}, u32[]{:S(2)}) collective-permute-start(bf16[112,128]{1,0:T(8,128)(2,1)S(1)} %get-tuple-element.21), channel_id=1, source_target_pairs={{0,2},{1,3},{2,4},{3,5},{4,6},{5,7},{6,8},{7,9},{8,10},{9,11},{10,... | collective-permute-start | bytes 86024 | tf_op jit(solution)/shard_map/ppermute | solution.py:336
  5.0 7.1 %collective-permute-start = (bf16[112,128]{1,0:T(8,128)(2,1)S(1)}, bf16[112,128]{1,0:T(8,128)(2,1)S(1)}, u32[]{:S(2)}, u32[]{:S(2)}) collective-permute-start(bf16[112,128]{1,0:T(8,128)(2,1)S(1)} %get-tuple-element.19.my_up), channel_id=1, source_target_pairs={{0,1},{1,2},{2,3},{3,4},{4,5},{5,6},{6,7},{7,8},{8,9},{9,10},{10,1... | collective-permute-start | bytes 86024 | tf_op jit(solution)/shard_map/ppermute | solution.py:336
  5.0 7.1 %collective-permute-start.3 = (bf16[128,128]{1,0:T(8,128)(2,1)S(1)}, bf16[128,128]{1,0:T(8,128)(2,1)S(1)}, u32[]{:S(2)}, u32[]{:S(2)}) collective-permute-start(bf16[128,128]{1,0:T(8,128)(2,1)S(1)} %get-tuple-element.22), channel_id=1, source_target_pairs={{0,14},{1,15},{2,0},{3,1},{4,2},{5,3},{6,4},{7,5},{8,6},{9,7},{10,... | collective-permute-start | bytes 98312 | tf_op jit(solution)/shard_map/ppermute | solution.py:336
  8.1 4.0 %collective-permute-start.2 = (bf16[128,128]{1,0:T(8,128)(2,1)S(1)}, bf16[128,128]{1,0:T(8,128)(2,1)S(1)}, u32[]{:S(2)}, u32[]{:S(2)}) collective-permute-start(bf16[128,128]{1,0:T(8,128)(2,1)S(1)} %get-tuple-element.20.my_down), channel_id=1, source_target_pairs={{0,15},{1,0},{2,1},{3,2},{4,3},{5,4},{6,5},{7,6},{8,7},{9,8},{10,9... | collective-permute-start | bytes 98312 | tf_op jit(solution)/shard_map/ppermute | solution.py:336
  35.2 12.2 %all-to-all-start.1 = ((bf16[32,24,128]{2,1,0:T(8,128)(2,1)}), bf16[32,24,128]{2,1,0:T(8,128)(2,1)S(1)}, u32[]{:S(2)}, u32[]{:S(2)}) async-start(bf16[32,24,128]{2,1,0:T(8,128)(2,1)} %shard_map.153), calls=%async_computation.1 | async-start | bytes 393216 | tf_op jit(solution)/shard_map/all_to_all | solution.py:429
  37.8 8.7 %collective-permute-start.4 = (bf16[64,128]{1,0:T(8,128)(2,1)S(1)}, bf16[64,128]{1,0:T(8,128)(2,1)S(1)}, u32[]{:S(2)}, u32[]{:S(2)}) collective-permute-start(bf16[64,128]{1,0:T(8,128)(2,1)S(1)} %get-tuple-element.32), channel_id=1, source_target_pairs={{0,1},{1,2},{2,3},{3,4},{4,5},{5,6},{6,7},{7,8},{8,9},{9,10},{10,1... | collective-permute-start | bytes 49160 | tf_op jit(solution)/shard_map/ppermute | solution.py:336
  38.3 8.2 %collective-permute-start.5 = (bf16[64,128]{1,0:T(8,128)(2,1)S(1)}, bf16[64,128]{1,0:T(8,128)(2,1)S(1)}, u32[]{:S(2)}, u32[]{:S(2)}) collective-permute-start(bf16[64,128]{1,0:T(8,128)(2,1)S(1)} %get-tuple-element.33), channel_id=1, source_target_pairs={{0,15},{1,0},{2,1},{3,2},{4,3},{5,4},{6,5},{7,6},{8,7},{9,8},{10,9... | collective-permute-start | bytes 49160 | tf_op jit(solution)/shard_map/ppermute | solution.py:336

commit v11 on v10

--- a/solution.py
+++ b/solution.py
@@ -12,7 +12,7 @@
 CODE_ROWS = 16
 LANES = 128
 FAR = -1e30
-GROUP = 4
+GROUP = 32
 BLOCK = 64
 
 

time: 48.5 us -> 47.5 us (0.979)
  Pallas kernels: 14.2 us -> 13.1 us
    pallas_call x1, Pallas kernels: 8.84 us -> 7.8 us  [shards(): call(layer_kernel, [((1, rows, width), BF16), ((border, width), BF16), ((...]
where the time goes in v11:
time: 47.5 us; the launch traced here: 47.3 us
  starting transfers between devices  14.7 us (31%)
  blocking collectives  13.5 us (28%)
  Pallas kernels  13.1 us (28%)
  waiting for transfers between devices  4.2 us (9%)
  local copies, waits for them, and re-layouts  0.88 us (2%)
  between operations  0.84 us (2%)
    all_to_all x1, blocking collectives, shards(): lax.all_to_all(grads.reshape(devices, share, width), axes, split_axis=0,...  13.5 us
    ppermute x6, starting transfers between devices, shift(): lax.ppermute(array, 'slab', [(i, (i + by) % size) for i in range(size)])  12.1 us
    pallas_call x1, Pallas kernels, shards(): call(layer_kernel, [((1, rows, width), BF16), ((border, width), BF16), ((...  7.8 us
    ppermute x6, waiting for transfers between devices, shift(): lax.ppermute(array, 'slab', [(i, (i + by) % size) for i in range(size)])  4.2 us
    all_to_all x1, starting transfers between devices, shards(): lax.all_to_all(shared, axes, split_axis=0, concat_axis=0, tiled=True)  2.59 us
    pallas_call x1, Pallas kernels, shards(): call(prep_kernel, [((edges, hot_rows), BF16), ((half_rows, edges), BF16),...  2.49 us
  transfers between devices with their start and end apart: 7, of which 1 were waited for; matrix products, arithmetic and copies ran while one was open for 0% of the time, Pallas kernels for 7%

profile of v11, /device:TPU:0, one launch (start us, length us, event | category | flops | bytes accessed | tf_op | source)
XLA Modules:
  0.0 47.3 jit_solution(16373329172903403418)
XLA Ops:
  0.6 0.0 copy-start.12
  0.6 0.0 copy-start.7
  0.7 0.6 %copy-done.12 = s32[1,128]{1,0:T(1,128)S(1)} copy-done((s32[1,128]{1,0:T(1,128)S(1)}, s32[1,128]{1,0:T(1,128)}, u32[]{:S(2)}) %copy-start.12) | copy-done | bytes 536
  1.3 0.0 copy-done.7
  1.3 0.2 copy-done
  1.5 0.0 copy-start.9
  1.5 0.0 copy-start.10
  1.5 0.3 shard_map.149
  1.9 0.0 copy-start.3
  1.9 0.0 copy-start.4
  1.9 0.0 copy-start.5
  1.9 0.0 copy-start.6
  1.9 3.0 %collective-permute-start.1 = (bf16[112,128]{1,0:T(8,128)(2,1)S(1)}, bf16[112,128]{1,0:T(8,128)(2,1)S(1)}, u32[]{:S(2)}, u32[]{:S(2)}) collective-permute-start(bf16[112,128]{1,0:T(8,128)(2,1)S(1)} %get-tuple-element.21), channel_id=1, source_target_pairs={{0,2},{1,3},{2,4},{3,5},{4,6},{5,7},{6,8},{7,9},{8,10},{9,11},{10,... | collective-permute-start | bytes 86024 | tf_op jit(solution)/shard_map/ppermute | solution.py:336
  5.0 0.0 collective-permute-start
  5.0 3.2 %collective-permute-start.3 = (bf16[128,128]{1,0:T(8,128)(2,1)S(1)}, bf16[128,128]{1,0:T(8,128)(2,1)S(1)}, u32[]{:S(2)}, u32[]{:S(2)}) collective-permute-start(bf16[128,128]{1,0:T(8,128)(2,1)S(1)} %get-tuple-element.22), channel_id=1, source_target_pairs={{0,14},{1,15},{2,0},{3,1},{4,2},{5,3},{6,4},{7,5},{8,6},{9,7},{10,... | collective-permute-start | bytes 98312 | tf_op jit(solution)/shard_map/ppermute | solution.py:336
  8.1 1.4 %collective-permute-start.2 = (bf16[128,128]{1,0:T(8,128)(2,1)S(1)}, bf16[128,128]{1,0:T(8,128)(2,1)S(1)}, u32[]{:S(2)}, u32[]{:S(2)}) collective-permute-start(bf16[128,128]{1,0:T(8,128)(2,1)S(1)} %get-tuple-element.20.my_down), channel_id=1, source_target_pairs={{0,15},{1,0},{2,1},{3,2},{4,3},{5,4},{6,5},{7,6},{8,7},{9,8},{10,9... | collective-permute-start | bytes 98312 | tf_op jit(solution)/shard_map/ppermute | solution.py:336
  9.6 2.5 %shard_map.150 = (bf16[8192,256]{1,0:T(8,128)(2,1)S(1)}, bf16[192,8192]{1,0:T(8,128)(2,1)S(1)}, bf16[2,256,256]{2,1,0:T(8,128)(2,1)S(1)}, s32[256,128]{1,0:T(8,128)S(1)}, f32[256,128]{1,0:T(8,128)S(1)}) custom-call(s32[1,32,256]{2,1,0:T(8,128)S(1)} %bitcast.6, s32[1,32,256]{2,1,0:T(8,128)S(1)} %bitcast.7, bf16[128,128]{1,0:T(8,128)(2,1)S(1)} %copy-done.10, ...), custom_call_target="tpu_custom_call" | custom-call | flops 2000000000 | bytes 1024 | tf_op jit(solution)/shard_map/pallas_call | solution.py:354
  12.1 0.0 collective-permute-done.1.low_far
  12.1 0.0 collective-permute-done.low
  12.1 0.0 collective-permute-done.3.high_far
  12.1 0.0 collective-permute-done.2.high
  12.1 7.8 %shard_map.151 = (bf16[1,256,128]{2,1,0:T(8,128)(2,1)}, bf16[64,128]{1,0:T(8,128)(2,1)S(1)}, bf16[64,128]{1,0:T(8,128)(2,1)S(1)}, bf16[768,128]{1,0:T(8,128)(2,1...) custom-call(bf16[1,256,128]{2,1,0:T(8,128)(2,1)S(1)} %copy-done, ...), custom_call_target="tpu_custom_call" | custom-call | flops 2000000000 | bytes 1024 | tf_op jit(solution)/shard_map/pallas_call | solution.py:385
  19.9 13.5 %all_to_all.10.parts = bf16[32,24,128]{2,1,0:T(8,128)(2,1)S(1)} all-to-all(bf16[32,24,128]{2,1,0:T(8,128)(2,1)S(1)} %bitcast.5), channel_id=1, replica_groups=mesh['grp'=2,'slab'=16] {'grp','slab'}, dimensions={0} | all-to-all | bytes 393216 | tf_op jit(solution)/shard_map/all_to_all | solution.py:409
  33.5 0.7 %shard_map.153 = bf16[32,24,128]{2,1,0:T(8,128)(2,1)} custom-call(bf16[32,24,128]{2,1,0:T(8,128)(2,1)S(1)} %all_to_all.10.parts), custom_call_target="tpu_custom_call" | custom-call | flops 2000000000 | bytes 1024 | tf_op jit(solution)/shard_map/pallas_call | solution.py:428
  34.2 2.6 %all-to-all-start.1 = ((bf16[32,24,128]{2,1,0:T(8,128)(2,1)}), bf16[32,24,128]{2,1,0:T(8,128)(2,1)S(1)}, u32[]{:S(2)}, u32[]{:S(2)}) async-start(bf16[32,24,128]{2,1,0:T(8,128)(2,1)} %shard_map.153), calls=%async_computation.1 | async-start | bytes 393216 | tf_op jit(solution)/shard_map/all_to_all | solution.py:429
  36.8 0.4 collective-permute-start.4
  37.2 4.0 %collective-permute-start.5 = (bf16[64,128]{1,0:T(8,128)(2,1)S(1)}, bf16[64,128]{1,0:T(8,128)(2,1)S(1)}, u32[]{:S(2)}, u32[]{:S(2)}) collective-permute-start(bf16[64,128]{1,0:T(8,128)(2,1)S(1)} %get-tuple-element.33), channel_id=1, source_target_pairs={{0,15},{1,0},{2,1},{3,2},{4,3},{5,4},{6,5},{7,6},{8,7},{9,8},{10,9... | collective-permute-start | bytes 49160 | tf_op jit(solution)/shard_map/ppermute | solution.py:336
  41.3 4.2 %collective-permute-done.4.from_low = bf16[64,128]{1,0:T(8,128)(2,1)S(1)} collective-permute-done((bf16[64,128]{1,0:T(8,128)(2,1)S(1)}, bf16[64,128]{1,0:T(8,128)(2,1)S(1)}, u32[]{:S(2)}, u32[]{:S(2)}) %collective-permute-start.4) | collective-permute-done | bytes 16416 | tf_op jit(solution)/shard_map/ppermute | solution.py:336
  45.5 0.0 collective-permute-done.5.from_high
  45.5 0.9 %shard_map.152 = bf16[1,256,128]{2,1,0:T(8,128)(2,1)} custom-call(bf16[1,256,128]{2,1,0:T(8,128)(2,1)S(1)} %copy-done.1, bf16[256,128]{1,0:T(8,128)(2,1)S(1)} %get-tuple-element.29.d_node, bf16[256,128]{1,0:T(8,128)(2,1)S(1)} %get-tuple-element.30.d_centre, bf16[256,128]{1,0:T(8,128)(2,1)S(1)} %get-tuple-element.31.d_neigh, bf16[128,128]{1,0:T(8,128)(2,1)S(1)} %copy-done.6, ...), custom_call_target="tpu_custom_call" | custom-call | flops 2000000000 | bytes 1024 | tf_op jit(solution)/shard_map/pallas_call | solution.py:424
  46.4 0.0 all-to-all-done.1
  46.4 0.9 %shard_map.154 = f32[6,128,128]{2,1,0:T(8,128)} custom-call(bf16[768,128]{1,0:T(8,128)(2,1)S(1)} %bitcast.4), custom_call_target="tpu_custom_call" | custom-call | flops 2000000000 | bytes 1024 | tf_op jit(solution)/shard_map/pallas_call | solution.py:431
  (16 shorter events, 0.0 us)
Async XLA Ops:
  0.6 0.7 %copy-start.12 = (s32[1,128]{1,0:T(1,128)S(1)}, s32[1,128]{1,0:T(1,128)}, u32[]{:S(2)}) copy-start(s32[1,128]{1,0:T(1,128)} %sends.3) | copy-start | bytes 1540
  0.6 0.7 %copy-start.7 = (s32[1,256]{1,0:T(1,128)S(1)}, s32[1,256]{1,0:T(1,128)}, u32[]{:S(2)}) copy-start(s32[1,256]{1,0:T(1,128)} %arrive.3) | copy-start | bytes 3076
  0.7 0.9 %copy-start = (bf16[1,256,128]{2,1,0:T(8,128)(2,1)S(1)}, bf16[1,256,128]{2,1,0:T(8,128)(2,1)}, u32[]{:S(2)}) copy-start(bf16[1,256,128]{2,1,0:T(8,128)(2,1)} %nodes.3) | copy-start | bytes 196612
  0.7 0.8 %copy-start.11 = (s32[1,64]{1,0:T(1,128)S(1)}, s32[1,64]{1,0:T(1,128)}, u32[]{:S(2)}) copy-start(s32[1,64]{1,0:T(1,128)} %leave.1) | copy-start | bytes 772
  1.5 8.0 %copy-start.1 = (bf16[1,256,128]{2,1,0:T(8,128)(2,1)S(1)}, bf16[1,256,128]{2,1,0:T(8,128)(2,1)}, u32[]{:S(2)}) copy-start(bf16[1,256,128]{2,1,0:T(8,128)(2,1)} %cotangent.5) | copy-start | bytes 196612
  1.5 8.0 %copy-start.2 = (bf16[128,128]{1,0:T(8,128)(2,1)S(1)}, bf16[128,128]{1,0:T(8,128)(2,1)}, u32[]{:S(2)}) copy-start(bf16[128,128]{1,0:T(8,128)(2,1)} %w_out.3) | copy-start | bytes 98308
  1.5 8.0 %copy-start.8 = (s32[1,256,32]{1,2,0:T(8,128)S(1)}, s32[1,256,32]{1,2,0:T(8,128)}, u32[]{:S(2)}) copy-start(s32[1,256,32]{1,2,0:T(8,128)} %param.17) | copy-start | bytes 98308
  1.5 8.0 %copy-start.9 = (s32[1,256,32]{1,2,0:T(8,128)S(1)}, s32[1,256,32]{1,2,0:T(8,128)}, u32[]{:S(2)}) copy-start(s32[1,256,32]{1,2,0:T(8,128)} %param.18) | copy-start | bytes 98308
  1.5 8.0 %copy-start.10 = (bf16[128,128]{1,0:T(8,128)(2,1)S(1)}, bf16[128,128]{1,0:T(8,128)(2,1)}, u32[]{:S(2)}) copy-start(bf16[128,128]{1,0:T(8,128)(2,1)} %w_msg.1) | copy-start | bytes 98308
  1.9 10.2 %copy-start.3 = (bf16[128,128]{1,0:T(8,128)(2,1)S(1)}, bf16[128,128]{1,0:T(8,128)(2,1)}, u32[]{:S(2)}) copy-start(bf16[128,128]{1,0:T(8,128)(2,1)} %w_agg.1) | copy-start | bytes 98308
  1.9 10.2 %copy-start.4 = (bf16[128,128]{1,0:T(8,128)(2,1)S(1)}, bf16[128,128]{1,0:T(8,128)(2,1)}, u32[]{:S(2)}) copy-start(bf16[128,128]{1,0:T(8,128)(2,1)} %w_send.3) | copy-start | bytes 98308
  1.9 10.2 %copy-start.5 = (bf16[128,128]{1,0:T(8,128)(2,1)S(1)}, bf16[128,128]{1,0:T(8,128)(2,1)}, u32[]{:S(2)}) copy-start(bf16[128,128]{1,0:T(8,128)(2,1)} %w_recv.3) | copy-start | bytes 98308
  1.9 10.2 %copy-start.6 = (bf16[128,128]{1,0:T(8,128)(2,1)S(1)}, bf16[128,128]{1,0:T(8,128)(2,1)}, u32[]{:S(2)}) copy-start(bf16[128,128]{1,0:T(8,128)(2,1)} %w_self.3) | copy-start | bytes 98308
  1.9 10.1 %collective-permute-start.1 = (bf16[112,128]{1,0:T(8,128)(2,1)S(1)}, bf16[112,128]{1,0:T(8,128)(2,1)S(1)}, u32[]{:S(2)}, u32[]{:S(2)}) collective-permute-start(bf16[112,128]{1,0:T(8,128)(2,1)S(1)} %get-tuple-element.21), channel_id=1, source_target_pairs={{0,2},{1,3},{2,4},{3,5},{4,6},{5,7},{6,8},{7,9},{8,10},{9,11},{10,... | collective-permute-start | bytes 86024 | tf_op jit(solution)/shard_map/ppermute | solution.py:336
  5.0 7.1 %collective-permute-start = (bf16[112,128]{1,0:T(8,128)(2,1)S(1)}, bf16[112,128]{1,0:T(8,128)(2,1)S(1)}, u32[]{:S(2)}, u32[]{:S(2)}) collective-permute-start(bf16[112,128]{1,0:T(8,128)(2,1)S(1)} %get-tuple-element.19.my_up), channel_id=1, source_target_pairs={{0,1},{1,2},{2,3},{3,4},{4,5},{5,6},{6,7},{7,8},{8,9},{9,10},{10,1... | collective-permute-start | bytes 86024 | tf_op jit(solution)/shard_map/ppermute | solution.py:336
  5.0 7.1 %collective-permute-start.3 = (bf16[128,128]{1,0:T(8,128)(2,1)S(1)}, bf16[128,128]{1,0:T(8,128)(2,1)S(1)}, u32[]{:S(2)}, u32[]{:S(2)}) collective-permute-start(bf16[128,128]{1,0:T(8,128)(2,1)S(1)} %get-tuple-element.22), channel_id=1, source_target_pairs={{0,14},{1,15},{2,0},{3,1},{4,2},{5,3},{6,4},{7,5},{8,6},{9,7},{10,... | collective-permute-start | bytes 98312 | tf_op jit(solution)/shard_map/ppermute | solution.py:336
  8.1 4.0 %collective-permute-start.2 = (bf16[128,128]{1,0:T(8,128)(2,1)S(1)}, bf16[128,128]{1,0:T(8,128)(2,1)S(1)}, u32[]{:S(2)}, u32[]{:S(2)}) collective-permute-start(bf16[128,128]{1,0:T(8,128)(2,1)S(1)} %get-tuple-element.20.my_down), channel_id=1, source_target_pairs={{0,15},{1,0},{2,1},{3,2},{4,3},{5,4},{6,5},{7,6},{8,7},{9,8},{10,9... | collective-permute-start | bytes 98312 | tf_op jit(solution)/shard_map/ppermute | solution.py:336
  34.2 12.2 %all-to-all-start.1 = ((bf16[32,24,128]{2,1,0:T(8,128)(2,1)}), bf16[32,24,128]{2,1,0:T(8,128)(2,1)S(1)}, u32[]{:S(2)}, u32[]{:S(2)}) async-start(bf16[32,24,128]{2,1,0:T(8,128)(2,1)} %shard_map.153), calls=%async_computation.1 | async-start | bytes 393216 | tf_op jit(solution)/shard_map/all_to_all | solution.py:429
  36.8 8.7 %collective-permute-start.4 = (bf16[64,128]{1,0:T(8,128)(2,1)S(1)}, bf16[64,128]{1,0:T(8,128)(2,1)S(1)}, u32[]{:S(2)}, u32[]{:S(2)}) collective-permute-start(bf16[64,128]{1,0:T(8,128)(2,1)S(1)} %get-tuple-element.32), channel_id=1, source_target_pairs={{0,1},{1,2},{2,3},{3,4},{4,5},{5,6},{6,7},{7,8},{8,9},{9,10},{10,1... | collective-permute-start | bytes 49160 | tf_op jit(solution)/shard_map/ppermute | solution.py:336
  37.2 8.2 %collective-permute-start.5 = (bf16[64,128]{1,0:T(8,128)(2,1)S(1)}, bf16[64,128]{1,0:T(8,128)(2,1)S(1)}, u32[]{:S(2)}, u32[]{:S(2)}) collective-permute-start(bf16[64,128]{1,0:T(8,128)(2,1)S(1)} %get-tuple-element.33), channel_id=1, source_target_pairs={{0,15},{1,0},{2,1},{3,2},{4,3},{5,4},{6,5},{7,6},{8,7},{9,8},{10,9... | collective-permute-start | bytes 49160 | tf_op jit(solution)/shard_map/ppermute | solution.py:336

commit v12 on v11

--- a/solution.py
+++ b/solution.py
@@ -43,7 +43,13 @@
     out[...] = jnp.zeros_like(out)
 
 
-def pack_kernel(_, nodes, leave, arrive, sends, to_up, far_up, to_down, far_down):
+def parities():
+    slab = lax.axis_index("slab")
+    return lax.rem(slab, 2) == 1, lax.rem(slab // 2, 2) == 1
+
+
+def pack_kernel(_, nodes, leave, arrive, sends, near_off, near_on, far_off, far_on):
+    odd, odd_pair = parities()
     rows = nodes.shape[1]
     migr = leave.shape[1] // 2
     border = sends.shape[1] // 2
@@ -57,15 +63,25 @@
     source = source.astype(jnp.int32)
     rest = tn(hot_columns(source, rows), own).astype(BF16)
     code = jnp.where(source >= rows, source - rows, -1).astype(F32)
-    for out, far, part in ((to_down, far_down, 0), (to_up, far_up, 1)):
-        out[:border] = rest[part * border : (part + 1) * border]
-        moving = leaving[part * migr : (part + 1) * migr]
-        out[border : border + migr] = moving
-        far[:migr] = moving
-        far[migr:] = jnp.zeros_like(far[migr:])
+    messages = []
+    for part in range(2):
         shifted = code if part == 0 else pltpu.roll(code, border, 1)
-        tail = out.shape[0] - border - migr
-        out[border + migr :] = jnp.broadcast_to(shifted, (tail, 2 * border)).astype(BF16)
+        messages.append(
+            jnp.concatenate(
+                [
+                    rest[part * border : (part + 1) * border],
+                    leaving[part * migr : (part + 1) * migr],
+                    jnp.broadcast_to(shifted, (CODE_ROWS, 2 * border)).astype(BF16),
+                ],
+                axis=0,
+            )
+        )
+    down, up = messages
+    near_off[...] = jnp.where(odd, up, down)
+    near_on[...] = jnp.where(odd, down, up)
+    down, up = leaving[:migr], leaving[migr:]
+    far_off[...] = jnp.where(odd_pair, up, down)
+    far_on[...] = jnp.where(odd_pair, down, up)
 
 
 def prep_kernel(nbr, valid, w_msg, w_out, cotangent, hot_o, hot_t_o, wide_o, ids_o, d_hid_o):
@@ -122,12 +138,12 @@
 def layer_kernel(
     nodes,
     arrive,
-    my_up,
-    my_down,
-    low,
-    low_far,
-    high,
-    high_far,
+    my_far_off,
+    my_far_on,
+    got_off,
+    got_on,
+    got_far_off,
+    got_far_on,
     hot,
     hot_t,
     wide,
@@ -140,8 +156,8 @@
     w_out,
     cotangent,
     updated,
-    back_low,
-    back_high,
+    back_off,
+    back_on,
     grads,
     d_node_o,
     d_centre_o,
@@ -157,8 +173,14 @@
 ):
     rows, width = nodes.shape[1:]
     slots = hot.shape[0] // rows
-    border = back_low.shape[0]
-    migr = low.shape[0] - border - CODE_ROWS
+    border, migr = back_off.shape[0], got_far_off.shape[0]
+    odd, odd_pair = parities()
+    low = jnp.where(odd, got_on[...], got_off[...])
+    high = jnp.where(odd, got_off[...], got_on[...])
+    low_far = jnp.where(odd_pair, got_far_on[...], got_far_off[...])
+    high_far = jnp.where(odd_pair, got_far_off[...], got_far_on[...])
+    my_up = jnp.where(odd_pair, my_far_off[...], my_far_on[...])
+    my_down = jnp.where(odd_pair, my_far_on[...], my_far_off[...])
     table_rows = rows + 2 * border
 
     pool = jnp.concatenate(
@@ -173,8 +195,8 @@
         extra = tn(hot_columns(code, 2 * migr), source)
         return (message[:border].astype(F32) + extra[:border]).astype(BF16)
 
-    below = halo(low[...], low_far[:migr], my_down[border : border + migr])
-    above = halo(high[...], my_up[border : border + migr], high_far[:migr])
+    below = halo(low, low_far, my_down)
+    above = halo(high, my_up, high_far)
     table = jnp.concatenate([moved, below, above], axis=0)
 
     half_rows, hot_rows = hot_t.shape[0], hot.shape[1]
@@ -250,8 +272,8 @@
     d_centre = dcen_s[...].astype(BF16)
     d_neigh = jnp.concatenate([d_neigh[:, :width], d_neigh[:, width:]], axis=0)
     d_borrowed = nt(d_neigh[rows:], w_recv[...]).astype(BF16)
-    back_low[...] = d_borrowed[:border]
-    back_high[...] = d_borrowed[border:]
+    back_off[...] = jnp.where(odd, d_borrowed[border:], d_borrowed[:border])
+    back_on[...] = jnp.where(odd, d_borrowed[:border], d_borrowed[border:])
     d_node_o[...] = d_node
     d_centre_o[...] = d_centre
     d_neigh_o[...] = d_neigh[:rows]
@@ -271,10 +293,13 @@
 
 
 def finish_kernel(
-    cotangent, d_node, d_centre, d_neigh, w_self, w_send, w_recv, sends, from_low, from_high, out
+    cotangent, d_node, d_centre, d_neigh, w_self, w_send, w_recv, sends, got_off, got_on, out
 ):
     rows = d_node.shape[0]
-    returned = jnp.concatenate([from_low[...], from_high[...]], axis=0)
+    odd, _ = parities()
+    from_low = jnp.where(odd, got_on[...], got_off[...])
+    from_high = jnp.where(odd, got_off[...], got_on[...])
+    returned = jnp.concatenate([from_low, from_high], axis=0)
     out[0] = (
         cotangent[0].astype(F32)
         + nt(d_node[...], w_self[...])
@@ -332,18 +357,23 @@
     devices = size * lax.axis_size("grp")
     axes = ("grp", "slab")
 
-    def shift(array, by):
-        return lax.ppermute(array, "slab", [(i, (i + by) % size) for i in range(size)])
+    def swap(array, by):
+        step = abs(by)
+        pairs = [
+            (i, (i + by if i // step % 2 == 0 else i - by) % size) for i in range(size)
+        ]
+        return lax.ppermute(array, "slab", pairs)
 
     message = (border + migr + CODE_ROWS, width)
-    message_down = (message[0] + CODE_ROWS, width)
     (token,) = call(first_kernel, [((8, LANES), F32)])()
-    to_up, far_up, to_down, far_down = call(
+    near_off, near_on, far_off, far_on = call(
         pack_kernel,
-        [(message, BF16)] * 2 + [(message_down, BF16)] * 2,
+        [(message, BF16)] * 2 + [((migr, width), BF16)] * 2,
     )(token, nodes, leave_list, arrive_list, send_list)
-    low, low_far = shift(to_up, 1), shift(far_up, 2)
-    high, high_far = shift(to_down, -1), shift(far_down, -2)
+    got_on = swap(near_on, 1)
+    got_off = swap(near_off, -1)
+    got_far_on = swap(far_on, 2)
+    got_far_off = swap(far_off, -2)
 
     matrices = 6
     pair_rows = rows * slots // 2
@@ -364,12 +394,12 @@
     sources = (
         nodes,
         arrive_list,
-        to_up,
-        to_down,
-        low,
-        low_far,
-        high,
-        high_far,
+        far_off,
+        far_on,
+        got_off,
+        got_on,
+        got_far_off,
+        got_far_on,
         hot,
         hot_t,
         wide,
@@ -382,7 +412,7 @@
         w_out,
         cotangent,
     )
-    updated, back_low, back_high, grads, d_node, d_centre, d_neigh = call(
+    updated, back_off, back_on, grads, d_node, d_centre, d_neigh = call(
         layer_kernel,
         [
             ((1, rows, width), BF16),
@@ -404,8 +434,8 @@
             pltpu.VMEM((edges, 2 * width), BF16),
         ],
     )(*sources)
-    from_low = shift(back_high, 1)
-    from_high = shift(back_low, -1)
+    got_on = swap(back_on, 1)
+    got_off = swap(back_off, -1)
     parts = lax.all_to_all(
         grads.reshape(devices, share, width), axes, split_axis=0, concat_axis=0, tiled=True
     )
@@ -418,8 +448,8 @@
         w_send,
         w_recv,
         send_list,
-        from_low,
-        from_high,
+        got_off,
+        got_on,
     )
     (grad_nodes,) = call(
         finish_kernel,

time: 47.5 us -> 47.2 us (level)
  blocking collectives: 13.5 us -> 11.4 us
  waiting for transfers between devices: 4.2 us -> 5.63 us
  starting transfers between devices: 14.7 us -> 15.2 us
    all_to_all x1, blocking collectives: 13.5 us -> 11.4 us  [shards(): lax.all_to_all(grads.reshape(devices, share, width), axes, split_axis=0,...]
    ppermute x6, waiting for transfers between devices: 4.2 us -> 5.63 us  [swap(): return lax.ppermute(array, 'slab', pairs)]
    ppermute x6, starting transfers between devices: 12.1 us -> 12.6 us  [swap(): return lax.ppermute(array, 'slab', pairs)]
  transfers between devices with their start and end apart: 7 -> 7, of which waited for: 1 -> 2; matrix products, arithmetic and copies ran while one was open for 0% -> 0% of each run, Pallas kernels for 7% -> 7%
where the time goes in v12:
time: 47.2 us; the launch traced here: 47 us
  starting transfers between devices  15.2 us (32%)
  Pallas kernels  13.1 us (28%)
  blocking collectives  11.4 us (24%)
  waiting for transfers between devices  5.63 us (12%)
  local copies, waits for them, and re-layouts  0.88 us (2%)
  between operations  0.81 us (2%)
    ppermute x6, starting transfers between devices, swap(): return lax.ppermute(array, 'slab', pairs)  12.6 us
    all_to_all x1, blocking collectives, shards(): lax.all_to_all(grads.reshape(devices, share, width), axes, split_axis=0,...  11.4 us
    pallas_call x1, Pallas kernels, shards(): call(layer_kernel, [((1, rows, width), BF16), ((border, width), BF16), ((...  7.75 us
    ppermute x6, waiting for transfers between devices, swap(): return lax.ppermute(array, 'slab', pairs)  5.63 us
    all_to_all x1, starting transfers between devices, shards(): lax.all_to_all(shared, axes, split_axis=0, concat_axis=0, tiled=True)  2.59 us
    pallas_call x1, Pallas kernels, shards(): call(prep_kernel, [((edges, hot_rows), BF16), ((half_rows, edges), BF16),...  2.49 us
  transfers between devices with their start and end apart: 7, of which 2 were waited for; matrix products, arithmetic and copies ran while one was open for 0% of the time, Pallas kernels for 7%

profile of v12, /device:TPU:0, one launch (start us, length us, event | category | flops | bytes accessed | tf_op | source)
XLA Modules:
  0.0 47.0 jit_solution(9536045849454381369)
XLA Ops:
  0.7 0.6 %copy-done.12 = s32[1,128]{1,0:T(1,128)S(1)} copy-done((s32[1,128]{1,0:T(1,128)S(1)}, s32[1,128]{1,0:T(1,128)}, u32[]{:S(2)}) %copy-start.12) | copy-done | bytes 536
  1.3 0.0 copy-done.7
  1.3 0.2 copy-done
  1.5 0.0 copy-start.9
  1.5 0.0 copy-start.10
  1.5 0.3 shard_map.149
  1.9 0.0 copy-start.3
  1.9 0.0 copy-start.4
  1.9 0.0 copy-start.5
  1.9 0.0 copy-start.6
  1.9 6.1 %collective-permute-start.2 = (bf16[32,128]{1,0:T(8,128)(2,1)S(1)}, bf16[32,128]{1,0:T(8,128)(2,1)S(1)}, u32[]{:S(2)}, u32[]{:S(2)}) collective-permute-start(bf16[32,128]{1,0:T(8,128)(2,1)S(1)} %get-tuple-element.19.my_far_off), channel_id=1, source_target_pairs={{0,14},{1,15},{2,4},{3,5},{4,2},{5,3},{6,8},{7,9},{8,6},{9,7},{10,... | collective-permute-start | bytes 24584 | tf_op jit(solution)/shard_map/ppermute | solution.py:365
  8.0 0.0 collective-permute-start.3
  8.0 0.8 %collective-permute-start = (bf16[112,128]{1,0:T(8,128)(2,1)S(1)}, bf16[112,128]{1,0:T(8,128)(2,1)S(1)}, u32[]{:S(2)}, u32[]{:S(2)}) collective-permute-start(bf16[112,128]{1,0:T(8,128)(2,1)S(1)} %get-tuple-element.21), channel_id=1, source_target_pairs={{0,15},{1,2},{2,1},{3,4},{4,3},{5,6},{6,5},{7,8},{8,7},{9,10},{10,... | collective-permute-start | bytes 86024 | tf_op jit(solution)/shard_map/ppermute | solution.py:365
  8.8 1.4 %collective-permute-start.1 = (bf16[112,128]{1,0:T(8,128)(2,1)S(1)}, bf16[112,128]{1,0:T(8,128)(2,1)S(1)}, u32[]{:S(2)}, u32[]{:S(2)}) collective-permute-start(bf16[112,128]{1,0:T(8,128)(2,1)S(1)} %get-tuple-element.22), channel_id=1, source_target_pairs={{0,1},{1,0},{2,3},{3,2},{4,5},{5,4},{6,7},{7,6},{8,9},{9,8},{10,11... | collective-permute-start | bytes 86024 | tf_op jit(solution)/shard_map/ppermute | solution.py:365
  10.2 0.0 copy-done.1
  10.2 0.0 copy-done.10
  10.2 2.5 %shard_map.150 = (bf16[8192,256]{1,0:T(8,128)(2,1)S(1)}, bf16[192,8192]{1,0:T(8,128)(2,1)S(1)}, bf16[2,256,256]{2,1,0:T(8,128)(2,1)S(1)}, s32[256,128]{1,0:T(8,128)S(1)}, f32[256,128]{1,0:T(8,128)S(1)}) custom-call(s32[1,32,256]{2,1,0:T(8,128)S(1)} %bitcast.6, s32[1,32,256]{2,1,0:T(8,128)S(1)} %bitcast.7, bf16[128,128]{1,0:T(8,128)(2,1)S(1)} %copy-done.10, ...), custom_call_target="tpu_custom_call" | custom-call | flops 2000000000 | bytes 1024 | tf_op jit(solution)/shard_map/pallas_call | solution.py:384
  12.7 0.0 collective-permute-done.2.got_far_off
  12.7 0.0 collective-permute-done.3.got_far_on
  12.7 1.3 %collective-permute-done.got_off = bf16[112,128]{1,0:T(8,128)(2,1)S(1)} collective-permute-done((bf16[112,128]{1,0:T(8,128)(2,1)S(1)}, bf16[112,128]{1,0:T(8,128)(2,1)S(1)}, u32[]{:S(2)}, u32[]{:S(2)}) %collective-permute-start) | collective-permute-done | bytes 28704 | tf_op jit(solution)/shard_map/ppermute | solution.py:365
  14.0 0.0 collective-permute-done.1.got_on
  14.0 7.7 %shard_map.151 = (bf16[1,256,128]{2,1,0:T(8,128)(2,1)}, bf16[64,128]{1,0:T(8,128)(2,1)S(1)}, bf16[64,128]{1,0:T(8,128)(2,1)S(1)}, bf16[768,128]{1,0:T(8,128)(2,1...) custom-call(bf16[1,256,128]{2,1,0:T(8,128)(2,1)S(1)} %copy-done, ...), custom_call_target="tpu_custom_call" | custom-call | flops 2000000000 | bytes 1024 | tf_op jit(solution)/shard_map/pallas_call | solution.py:415
  21.8 11.4 %all_to_all.10.parts = bf16[32,24,128]{2,1,0:T(8,128)(2,1)S(1)} all-to-all(bf16[32,24,128]{2,1,0:T(8,128)(2,1)S(1)} %bitcast.5), channel_id=1, replica_groups=mesh['grp'=2,'slab'=16] {'grp','slab'}, dimensions={0} | all-to-all | bytes 393216 | tf_op jit(solution)/shard_map/all_to_all | solution.py:439
  33.2 0.7 %shard_map.153 = bf16[32,24,128]{2,1,0:T(8,128)(2,1)} custom-call(bf16[32,24,128]{2,1,0:T(8,128)(2,1)S(1)} %all_to_all.10.parts), custom_call_target="tpu_custom_call" | custom-call | flops 2000000000 | bytes 1024 | tf_op jit(solution)/shard_map/pallas_call | solution.py:458
  33.9 2.6 %all-to-all-start.1 = ((bf16[32,24,128]{2,1,0:T(8,128)(2,1)}), bf16[32,24,128]{2,1,0:T(8,128)(2,1)S(1)}, u32[]{:S(2)}, u32[]{:S(2)}) async-start(bf16[32,24,128]{2,1,0:T(8,128)(2,1)} %shard_map.153), calls=%async_computation.1 | async-start | bytes 393216 | tf_op jit(solution)/shard_map/all_to_all | solution.py:459
  36.5 4.4 %collective-permute-start.4 = (bf16[64,128]{1,0:T(8,128)(2,1)S(1)}, bf16[64,128]{1,0:T(8,128)(2,1)S(1)}, u32[]{:S(2)}, u32[]{:S(2)}) collective-permute-start(bf16[64,128]{1,0:T(8,128)(2,1)S(1)} %get-tuple-element.32), channel_id=1, source_target_pairs={{0,15},{1,2},{2,1},{3,4},{4,3},{5,6},{6,5},{7,8},{8,7},{9,10},{10,... | collective-permute-start | bytes 49160 | tf_op jit(solution)/shard_map/ppermute | solution.py:365
  40.9 0.0 collective-permute-start.5
  40.9 4.3 %collective-permute-done.4.got_off = bf16[64,128]{1,0:T(8,128)(2,1)S(1)} collective-permute-done((bf16[64,128]{1,0:T(8,128)(2,1)S(1)}, bf16[64,128]{1,0:T(8,128)(2,1)S(1)}, u32[]{:S(2)}, u32[]{:S(2)}) %collective-permute-start.4) | collective-permute-done | bytes 16416 | tf_op jit(solution)/shard_map/ppermute | solution.py:365
  45.2 0.0 collective-permute-done.5.got_on
  45.2 0.9 %shard_map.152 = bf16[1,256,128]{2,1,0:T(8,128)(2,1)} custom-call(bf16[1,256,128]{2,1,0:T(8,128)(2,1)S(1)} %copy-done.1, bf16[256,128]{1,0:T(8,128)(2,1)S(1)} %get-tuple-element.29.d_node, bf16[256,128]{1,0:T(8,128)(2,1)S(1)} %get-tuple-element.30.d_centre, bf16[256,128]{1,0:T(8,128)(2,1)S(1)} %get-tuple-element.31.d_neigh, bf16[128,128]{1,0:T(8,128)(2,1)S(1)} %copy-done.6, ...), custom_call_target="tpu_custom_call" | custom-call | flops 2000000000 | bytes 1024 | tf_op jit(solution)/shard_map/pallas_call | solution.py:454
  46.1 0.0 all-to-all-done.1
  46.1 0.9 %shard_map.154 = f32[6,128,128]{2,1,0:T(8,128)} custom-call(bf16[768,128]{1,0:T(8,128)(2,1)S(1)} %bitcast.4), custom_call_target="tpu_custom_call" | custom-call | flops 2000000000 | bytes 1024 | tf_op jit(solution)/shard_map/pallas_call | solution.py:461
  (16 shorter events, 0.0 us)
Async XLA Ops:
  0.6 0.7 %copy-start.12 = (s32[1,128]{1,0:T(1,128)S(1)}, s32[1,128]{1,0:T(1,128)}, u32[]{:S(2)}) copy-start(s32[1,128]{1,0:T(1,128)} %sends.3) | copy-start | bytes 1540
  0.6 0.7 %copy-start.7 = (s32[1,256]{1,0:T(1,128)S(1)}, s32[1,256]{1,0:T(1,128)}, u32[]{:S(2)}) copy-start(s32[1,256]{1,0:T(1,128)} %arrive.3) | copy-start | bytes 3076
  0.7 0.9 %copy-start = (bf16[1,256,128]{2,1,0:T(8,128)(2,1)S(1)}, bf16[1,256,128]{2,1,0:T(8,128)(2,1)}, u32[]{:S(2)}) copy-start(bf16[1,256,128]{2,1,0:T(8,128)(2,1)} %nodes.3) | copy-start | bytes 196612
  0.7 0.8 %copy-start.11 = (s32[1,64]{1,0:T(1,128)S(1)}, s32[1,64]{1,0:T(1,128)}, u32[]{:S(2)}) copy-start(s32[1,64]{1,0:T(1,128)} %leave.1) | copy-start | bytes 772
  1.5 8.7 %copy-start.1 = (bf16[1,256,128]{2,1,0:T(8,128)(2,1)S(1)}, bf16[1,256,128]{2,1,0:T(8,128)(2,1)}, u32[]{:S(2)}) copy-start(bf16[1,256,128]{2,1,0:T(8,128)(2,1)} %cotangent.5) | copy-start | bytes 196612
  1.5 8.7 %copy-start.2 = (bf16[128,128]{1,0:T(8,128)(2,1)S(1)}, bf16[128,128]{1,0:T(8,128)(2,1)}, u32[]{:S(2)}) copy-start(bf16[128,128]{1,0:T(8,128)(2,1)} %w_out.3) | copy-start | bytes 98308
  1.5 8.7 %copy-start.8 = (s32[1,256,32]{1,2,0:T(8,128)S(1)}, s32[1,256,32]{1,2,0:T(8,128)}, u32[]{:S(2)}) copy-start(s32[1,256,32]{1,2,0:T(8,128)} %param.17) | copy-start | bytes 98308
  1.5 8.7 %copy-start.9 = (s32[1,256,32]{1,2,0:T(8,128)S(1)}, s32[1,256,32]{1,2,0:T(8,128)}, u32[]{:S(2)}) copy-start(s32[1,256,32]{1,2,0:T(8,128)} %param.18) | copy-start | bytes 98308
  1.5 8.6 %copy-start.10 = (bf16[128,128]{1,0:T(8,128)(2,1)S(1)}, bf16[128,128]{1,0:T(8,128)(2,1)}, u32[]{:S(2)}) copy-start(bf16[128,128]{1,0:T(8,128)(2,1)} %w_msg.1) | copy-start | bytes 98308
  1.9 12.1 %copy-start.3 = (bf16[128,128]{1,0:T(8,128)(2,1)S(1)}, bf16[128,128]{1,0:T(8,128)(2,1)}, u32[]{:S(2)}) copy-start(bf16[128,128]{1,0:T(8,128)(2,1)} %w_agg.1) | copy-start | bytes 98308
  1.9 12.1 %copy-start.4 = (bf16[128,128]{1,0:T(8,128)(2,1)S(1)}, bf16[128,128]{1,0:T(8,128)(2,1)}, u32[]{:S(2)}) copy-start(bf16[128,128]{1,0:T(8,128)(2,1)} %w_send.3) | copy-start | bytes 98308
  1.9 12.1 %copy-start.5 = (bf16[128,128]{1,0:T(8,128)(2,1)S(1)}, bf16[128,128]{1,0:T(8,128)(2,1)}, u32[]{:S(2)}) copy-start(bf16[128,128]{1,0:T(8,128)(2,1)} %w_recv.3) | copy-start | bytes 98308
  1.9 12.1 %copy-start.6 = (bf16[128,128]{1,0:T(8,128)(2,1)S(1)}, bf16[128,128]{1,0:T(8,128)(2,1)}, u32[]{:S(2)}) copy-start(bf16[128,128]{1,0:T(8,128)(2,1)} %w_self.3) | copy-start | bytes 98308
  1.9 10.7 %collective-permute-start.2 = (bf16[32,128]{1,0:T(8,128)(2,1)S(1)}, bf16[32,128]{1,0:T(8,128)(2,1)S(1)}, u32[]{:S(2)}, u32[]{:S(2)}) collective-permute-start(bf16[32,128]{1,0:T(8,128)(2,1)S(1)} %get-tuple-element.19.my_far_off), channel_id=1, source_target_pairs={{0,14},{1,15},{2,4},{3,5},{4,2},{5,3},{6,8},{7,9},{8,6},{9,7},{10,... | collective-permute-start | bytes 24584 | tf_op jit(solution)/shard_map/ppermute | solution.py:365
  8.0 4.7 %collective-permute-start.3 = (bf16[32,128]{1,0:T(8,128)(2,1)S(1)}, bf16[32,128]{1,0:T(8,128)(2,1)S(1)}, u32[]{:S(2)}, u32[]{:S(2)}) collective-permute-start(bf16[32,128]{1,0:T(8,128)(2,1)S(1)} %get-tuple-element.20.my_far_on), channel_id=1, source_target_pairs={{0,2},{1,3},{2,0},{3,1},{4,6},{5,7},{6,4},{7,5},{8,10},{9,11},{10,... | collective-permute-start | bytes 24584 | tf_op jit(solution)/shard_map/ppermute | solution.py:365
  8.0 6.0 %collective-permute-start = (bf16[112,128]{1,0:T(8,128)(2,1)S(1)}, bf16[112,128]{1,0:T(8,128)(2,1)S(1)}, u32[]{:S(2)}, u32[]{:S(2)}) collective-permute-start(bf16[112,128]{1,0:T(8,128)(2,1)S(1)} %get-tuple-element.21), channel_id=1, source_target_pairs={{0,15},{1,2},{2,1},{3,4},{4,3},{5,6},{6,5},{7,8},{8,7},{9,10},{10,... | collective-permute-start | bytes 86024 | tf_op jit(solution)/shard_map/ppermute | solution.py:365
  8.8 5.2 %collective-permute-start.1 = (bf16[112,128]{1,0:T(8,128)(2,1)S(1)}, bf16[112,128]{1,0:T(8,128)(2,1)S(1)}, u32[]{:S(2)}, u32[]{:S(2)}) collective-permute-start(bf16[112,128]{1,0:T(8,128)(2,1)S(1)} %get-tuple-element.22), channel_id=1, source_target_pairs={{0,1},{1,0},{2,3},{3,2},{4,5},{5,4},{6,7},{7,6},{8,9},{9,8},{10,11... | collective-permute-start | bytes 86024 | tf_op jit(solution)/shard_map/ppermute | solution.py:365
  33.9 12.2 %all-to-all-start.1 = ((bf16[32,24,128]{2,1,0:T(8,128)(2,1)}), bf16[32,24,128]{2,1,0:T(8,128)(2,1)S(1)}, u32[]{:S(2)}, u32[]{:S(2)}) async-start(bf16[32,24,128]{2,1,0:T(8,128)(2,1)} %shard_map.153), calls=%async_computation.1 | async-start | bytes 393216 | tf_op jit(solution)/shard_map/all_to_all | solution.py:459
  36.5 8.7 %collective-permute-start.4 = (bf16[64,128]{1,0:T(8,128)(2,1)S(1)}, bf16[64,128]{1,0:T(8,128)(2,1)S(1)}, u32[]{:S(2)}, u32[]{:S(2)}) collective-permute-start(bf16[64,128]{1,0:T(8,128)(2,1)S(1)} %get-tuple-element.32), channel_id=1, source_target_pairs={{0,15},{1,2},{2,1},{3,4},{4,3},{5,6},{6,5},{7,8},{8,7},{9,10},{10,... | collective-permute-start | bytes 49160 | tf_op jit(solution)/shard_map/ppermute | solution.py:365
  40.9 4.3 %collective-permute-start.5 = (bf16[64,128]{1,0:T(8,128)(2,1)S(1)}, bf16[64,128]{1,0:T(8,128)(2,1)S(1)}, u32[]{:S(2)}, u32[]{:S(2)}) collective-permute-start(bf16[64,128]{1,0:T(8,128)(2,1)S(1)} %get-tuple-element.33), channel_id=1, source_target_pairs={{0,1},{1,0},{2,3},{3,2},{4,5},{5,4},{6,7},{7,6},{8,9},{9,8},{10,11... | collective-permute-start | bytes 49160 | tf_op jit(solution)/shard_map/ppermute | solution.py:365

commit v13 on v12

--- a/solution.py
+++ b/solution.py
@@ -80,8 +80,10 @@
     near_off[...] = jnp.where(odd, up, down)
     near_on[...] = jnp.where(odd, down, up)
     down, up = leaving[:migr], leaving[migr:]
-    far_off[...] = jnp.where(odd_pair, up, down)
-    far_on[...] = jnp.where(odd_pair, down, up)
+    far_off[:migr] = jnp.where(odd_pair, up, down)
+    far_on[:migr] = jnp.where(odd_pair, down, up)
+    for out in (far_off, far_on):
+        out[migr:] = jnp.zeros_like(out[migr:])
 
 
 def prep_kernel(nbr, valid, w_msg, w_out, cotangent, hot_o, hot_t_o, wide_o, ids_o, d_hid_o):
@@ -173,14 +175,15 @@
 ):
     rows, width = nodes.shape[1:]
     slots = hot.shape[0] // rows
-    border, migr = back_off.shape[0], got_far_off.shape[0]
+    border = back_off.shape[0]
+    migr = got_off.shape[0] - border - CODE_ROWS
     odd, odd_pair = parities()
     low = jnp.where(odd, got_on[...], got_off[...])
     high = jnp.where(odd, got_off[...], got_on[...])
-    low_far = jnp.where(odd_pair, got_far_on[...], got_far_off[...])
-    high_far = jnp.where(odd_pair, got_far_off[...], got_far_on[...])
-    my_up = jnp.where(odd_pair, my_far_off[...], my_far_on[...])
-    my_down = jnp.where(odd_pair, my_far_on[...], my_far_off[...])
+    low_far = jnp.where(odd_pair, got_far_on[:migr], got_far_off[:migr])
+    high_far = jnp.where(odd_pair, got_far_off[:migr], got_far_on[:migr])
+    my_up = jnp.where(odd_pair, my_far_off[:migr], my_far_on[:migr])
+    my_down = jnp.where(odd_pair, my_far_on[:migr], my_far_off[:migr])
     table_rows = rows + 2 * border
 
     pool = jnp.concatenate(
@@ -368,12 +371,12 @@
     (token,) = call(first_kernel, [((8, LANES), F32)])()
     near_off, near_on, far_off, far_on = call(
         pack_kernel,
-        [(message, BF16)] * 2 + [((migr, width), BF16)] * 2,
+        [(message, BF16)] * 4,
     )(token, nodes, leave_list, arrive_list, send_list)
     got_on = swap(near_on, 1)
-    got_off = swap(near_off, -1)
     got_far_on = swap(far_on, 2)
     got_far_off = swap(far_off, -2)
+    got_off = swap(near_off, -1)
 
     matrices = 6
     pair_rows = rows * slots // 2

time: 47.2 us -> 47.9 us (1.015)
  starting transfers between devices: 15.2 us -> 13.2 us
  waiting for transfers between devices: 5.63 us -> 7.61 us
  blocking collectives: 11.4 us -> 12 us
    ppermute x6, starting transfers between devices: 12.6 us -> 10.6 us  [swap(): return lax.ppermute(array, 'slab', pairs)]
    ppermute x6, waiting for transfers between devices: 5.63 us -> 7.6 us  [swap(): return lax.ppermute(array, 'slab', pairs)]
    all_to_all x1, blocking collectives: 11.4 us -> 12 us  [shards(): lax.all_to_all(grads.reshape(devices, share, width), axes, split_axis=0,...]
where the time goes in v13:
time: 47.9 us; the launch traced here: 47.6 us
  starting transfers between devices  13.2 us (28%)
  Pallas kernels  13.1 us (27%)
  blocking collectives  12 us (25%)
  waiting for transfers between devices  7.61 us (16%)
  local copies, waits for them, and re-layouts  0.88 us (2%)
  between operations  0.82 us (2%)
    all_to_all x1, blocking collectives, shards(): lax.all_to_all(grads.reshape(devices, share, width), axes, split_axis=0,...  12 us
    ppermute x6, starting transfers between devices, swap(): return lax.ppermute(array, 'slab', pairs)  10.6 us
    pallas_call x1, Pallas kernels, shards(): call(layer_kernel, [((1, rows, width), BF16), ((border, width), BF16), ((...  7.79 us
    ppermute x6, waiting for transfers between devices, swap(): return lax.ppermute(array, 'slab', pairs)  7.6 us
    all_to_all x1, starting transfers between devices, shards(): lax.all_to_all(shared, axes, split_axis=0, concat_axis=0, tiled=True)  2.59 us
    pallas_call x1, Pallas kernels, shards(): call(prep_kernel, [((edges, hot_rows), BF16), ((half_rows, edges), BF16),...  2.5 us
  transfers between devices with their start and end apart: 7, of which 2 were waited for; matrix products, arithmetic and copies ran while one was open for 0% of the time, Pallas kernels for 7%

profile of v13, /device:TPU:0, one launch (start us, length us, event | category | flops | bytes accessed | tf_op | source)
XLA Modules:
  0.0 47.6 jit_solution(7533683333265730633)
XLA Ops:
  0.6 0.0 copy-start.12
  0.6 0.0 copy-start.7
  0.7 0.6 %copy-done.12 = s32[1,128]{1,0:T(1,128)S(1)} copy-done((s32[1,128]{1,0:T(1,128)S(1)}, s32[1,128]{1,0:T(1,128)}, u32[]{:S(2)}) %copy-start.12) | copy-done | bytes 536
  1.3 0.0 copy-done.7
  1.3 0.2 copy-done
  1.5 0.0 copy-start.9
  1.5 0.0 copy-start.10
  1.5 0.3 shard_map.149
  1.9 0.0 copy-start.3
  1.9 0.0 copy-start.4
  1.9 0.0 copy-start.5
  1.9 0.0 copy-start.6
  1.9 5.5 %collective-permute-start = (bf16[112,128]{1,0:T(8,128)(2,1)S(1)}, bf16[112,128]{1,0:T(8,128)(2,1)S(1)}, u32[]{:S(2)}, u32[]{:S(2)}) collective-permute-start(bf16[112,128]{1,0:T(8,128)(2,1)S(1)} %get-tuple-element.21), channel_id=1, source_target_pairs={{0,15},{1,2},{2,1},{3,4},{4,3},{5,6},{6,5},{7,8},{8,7},{9,10},{10,... | collective-permute-start | bytes 86024 | tf_op jit(solution)/shard_map/ppermute | solution.py:368
  7.5 0.0 collective-permute-start.1
  7.5 0.7 %collective-permute-start.2 = (bf16[112,128]{1,0:T(8,128)(2,1)S(1)}, bf16[112,128]{1,0:T(8,128)(2,1)S(1)}, u32[]{:S(2)}, u32[]{:S(2)}) collective-permute-start(bf16[112,128]{1,0:T(8,128)(2,1)S(1)} %get-tuple-element.19.my_far_off), channel_id=1, source_target_pairs={{0,14},{1,15},{2,4},{3,5},{4,2},{5,3},{6,8},{7,9},{8,6},{9,7},{10,... | collective-permute-start | bytes 86024 | tf_op jit(solution)/shard_map/ppermute | solution.py:368
  8.2 0.0 collective-permute-start.3
  8.2 2.5 %shard_map.150 = (bf16[8192,256]{1,0:T(8,128)(2,1)S(1)}, bf16[192,8192]{1,0:T(8,128)(2,1)S(1)}, bf16[2,256,256]{2,1,0:T(8,128)(2,1)S(1)}, s32[256,128]{1,0:T(8,128)S(1)}, f32[256,128]{1,0:T(8,128)S(1)}) custom-call(s32[1,32,256]{2,1,0:T(8,128)S(1)} %bitcast.6, s32[1,32,256]{2,1,0:T(8,128)S(1)} %bitcast.7, bf16[128,128]{1,0:T(8,128)(2,1)S(1)} %copy-done.10, ...), custom_call_target="tpu_custom_call" | custom-call | flops 2000000000 | bytes 1024 | tf_op jit(solution)/shard_map/pallas_call | solution.py:387
  10.7 0.0 collective-permute-done.got_off
  10.7 0.0 collective-permute-done.1.got_on
  10.7 3.3 %collective-permute-done.2.got_far_off = bf16[112,128]{1,0:T(8,128)(2,1)S(1)} collective-permute-done((bf16[112,128]{1,0:T(8,128)(2,1)S(1)}, bf16[112,128]{1,0:T(8,128)(2,1)S(1)}, u32[]{:S(2)}, u32[]{:S(2)}) %collective-permute-start.2) | collective-permute-done | bytes 28704 | tf_op jit(solution)/shard_map/ppermute | solution.py:368
  14.0 0.0 collective-permute-done.3.got_far_on
  14.1 7.8 %shard_map.151 = (bf16[1,256,128]{2,1,0:T(8,128)(2,1)}, bf16[64,128]{1,0:T(8,128)(2,1)S(1)}, bf16[64,128]{1,0:T(8,128)(2,1)S(1)}, bf16[768,128]{1,0:T(8,128)(2,1...) custom-call(bf16[1,256,128]{2,1,0:T(8,128)(2,1)S(1)} %copy-done, ...), custom_call_target="tpu_custom_call" | custom-call | flops 2000000000 | bytes 1024 | tf_op jit(solution)/shard_map/pallas_call | solution.py:418
  21.9 12.0 %all_to_all.10.parts = bf16[32,24,128]{2,1,0:T(8,128)(2,1)S(1)} all-to-all(bf16[32,24,128]{2,1,0:T(8,128)(2,1)S(1)} %bitcast.5), channel_id=1, replica_groups=mesh['grp'=2,'slab'=16] {'grp','slab'}, dimensions={0} | all-to-all | bytes 393216 | tf_op jit(solution)/shard_map/all_to_all | solution.py:442
  33.9 0.7 %shard_map.153 = bf16[32,24,128]{2,1,0:T(8,128)(2,1)} custom-call(bf16[32,24,128]{2,1,0:T(8,128)(2,1)S(1)} %all_to_all.10.parts), custom_call_target="tpu_custom_call" | custom-call | flops 2000000000 | bytes 1024 | tf_op jit(solution)/shard_map/pallas_call | solution.py:461
  34.6 2.6 %all-to-all-start.1 = ((bf16[32,24,128]{2,1,0:T(8,128)(2,1)}), bf16[32,24,128]{2,1,0:T(8,128)(2,1)S(1)}, u32[]{:S(2)}, u32[]{:S(2)}) async-start(bf16[32,24,128]{2,1,0:T(8,128)(2,1)} %shard_map.153), calls=%async_computation.1 | async-start | bytes 393216 | tf_op jit(solution)/shard_map/all_to_all | solution.py:462
  37.2 4.4 %collective-permute-start.4 = (bf16[64,128]{1,0:T(8,128)(2,1)S(1)}, bf16[64,128]{1,0:T(8,128)(2,1)S(1)}, u32[]{:S(2)}, u32[]{:S(2)}) collective-permute-start(bf16[64,128]{1,0:T(8,128)(2,1)S(1)} %get-tuple-element.32), channel_id=1, source_target_pairs={{0,15},{1,2},{2,1},{3,4},{4,3},{5,6},{6,5},{7,8},{8,7},{9,10},{10,... | collective-permute-start | bytes 49160 | tf_op jit(solution)/shard_map/ppermute | solution.py:368
  41.5 0.0 collective-permute-start.5
  41.6 4.3 %collective-permute-done.4.got_off = bf16[64,128]{1,0:T(8,128)(2,1)S(1)} collective-permute-done((bf16[64,128]{1,0:T(8,128)(2,1)S(1)}, bf16[64,128]{1,0:T(8,128)(2,1)S(1)}, u32[]{:S(2)}, u32[]{:S(2)}) %collective-permute-start.4) | collective-permute-done | bytes 16416 | tf_op jit(solution)/shard_map/ppermute | solution.py:368
  45.9 0.0 collective-permute-done.5.got_on
  45.9 0.9 %shard_map.152 = bf16[1,256,128]{2,1,0:T(8,128)(2,1)} custom-call(bf16[1,256,128]{2,1,0:T(8,128)(2,1)S(1)} %copy-done.1, bf16[256,128]{1,0:T(8,128)(2,1)S(1)} %get-tuple-element.29.d_node, bf16[256,128]{1,0:T(8,128)(2,1)S(1)} %get-tuple-element.30.d_centre, bf16[256,128]{1,0:T(8,128)(2,1)S(1)} %get-tuple-element.31.d_neigh, bf16[128,128]{1,0:T(8,128)(2,1)S(1)} %copy-done.6, ...), custom_call_target="tpu_custom_call" | custom-call | flops 2000000000 | bytes 1024 | tf_op jit(solution)/shard_map/pallas_call | solution.py:457
  46.7 0.0 all-to-all-done.1
  46.7 0.9 %shard_map.154 = f32[6,128,128]{2,1,0:T(8,128)} custom-call(bf16[768,128]{1,0:T(8,128)(2,1)S(1)} %bitcast.4), custom_call_target="tpu_custom_call" | custom-call | flops 2000000000 | bytes 1024 | tf_op jit(solution)/shard_map/pallas_call | solution.py:464
  (16 shorter events, 0.0 us)
Async XLA Ops:
  0.6 0.7 %copy-start.12 = (s32[1,128]{1,0:T(1,128)S(1)}, s32[1,128]{1,0:T(1,128)}, u32[]{:S(2)}) copy-start(s32[1,128]{1,0:T(1,128)} %sends.3) | copy-start | bytes 1540
  0.6 0.7 %copy-start.7 = (s32[1,256]{1,0:T(1,128)S(1)}, s32[1,256]{1,0:T(1,128)}, u32[]{:S(2)}) copy-start(s32[1,256]{1,0:T(1,128)} %arrive.3) | copy-start | bytes 3076
  0.7 0.9 %copy-start = (bf16[1,256,128]{2,1,0:T(8,128)(2,1)S(1)}, bf16[1,256,128]{2,1,0:T(8,128)(2,1)}, u32[]{:S(2)}) copy-start(bf16[1,256,128]{2,1,0:T(8,128)(2,1)} %nodes.3) | copy-start | bytes 196612
  0.7 0.8 %copy-start.11 = (s32[1,64]{1,0:T(1,128)S(1)}, s32[1,64]{1,0:T(1,128)}, u32[]{:S(2)}) copy-start(s32[1,64]{1,0:T(1,128)} %leave.1) | copy-start | bytes 772
  1.5 6.7 %copy-start.1 = (bf16[1,256,128]{2,1,0:T(8,128)(2,1)S(1)}, bf16[1,256,128]{2,1,0:T(8,128)(2,1)}, u32[]{:S(2)}) copy-start(bf16[1,256,128]{2,1,0:T(8,128)(2,1)} %cotangent.5) | copy-start | bytes 196612
  1.5 6.7 %copy-start.2 = (bf16[128,128]{1,0:T(8,128)(2,1)S(1)}, bf16[128,128]{1,0:T(8,128)(2,1)}, u32[]{:S(2)}) copy-start(bf16[128,128]{1,0:T(8,128)(2,1)} %w_out.3) | copy-start | bytes 98308
  1.5 6.7 %copy-start.8 = (s32[1,256,32]{1,2,0:T(8,128)S(1)}, s32[1,256,32]{1,2,0:T(8,128)}, u32[]{:S(2)}) copy-start(s32[1,256,32]{1,2,0:T(8,128)} %param.17) | copy-start | bytes 98308
  1.5 6.7 %copy-start.9 = (s32[1,256,32]{1,2,0:T(8,128)S(1)}, s32[1,256,32]{1,2,0:T(8,128)}, u32[]{:S(2)}) copy-start(s32[1,256,32]{1,2,0:T(8,128)} %param.18) | copy-start | bytes 98308
  1.5 6.7 %copy-start.10 = (bf16[128,128]{1,0:T(8,128)(2,1)S(1)}, bf16[128,128]{1,0:T(8,128)(2,1)}, u32[]{:S(2)}) copy-start(bf16[128,128]{1,0:T(8,128)(2,1)} %w_msg.1) | copy-start | bytes 98308
  1.9 12.1 %copy-start.3 = (bf16[128,128]{1,0:T(8,128)(2,1)S(1)}, bf16[128,128]{1,0:T(8,128)(2,1)}, u32[]{:S(2)}) copy-start(bf16[128,128]{1,0:T(8,128)(2,1)} %w_agg.1) | copy-start | bytes 98308
  1.9 12.1 %copy-start.4 = (bf16[128,128]{1,0:T(8,128)(2,1)S(1)}, bf16[128,128]{1,0:T(8,128)(2,1)}, u32[]{:S(2)}) copy-start(bf16[128,128]{1,0:T(8,128)(2,1)} %w_send.3) | copy-start | bytes 98308
  1.9 12.1 %copy-start.5 = (bf16[128,128]{1,0:T(8,128)(2,1)S(1)}, bf16[128,128]{1,0:T(8,128)(2,1)}, u32[]{:S(2)}) copy-start(bf16[128,128]{1,0:T(8,128)(2,1)} %w_recv.3) | copy-start | bytes 98308
  1.9 12.1 %copy-start.6 = (bf16[128,128]{1,0:T(8,128)(2,1)S(1)}, bf16[128,128]{1,0:T(8,128)(2,1)}, u32[]{:S(2)}) copy-start(bf16[128,128]{1,0:T(8,128)(2,1)} %w_self.3) | copy-start | bytes 98308
  1.9 8.8 %collective-permute-start = (bf16[112,128]{1,0:T(8,128)(2,1)S(1)}, bf16[112,128]{1,0:T(8,128)(2,1)S(1)}, u32[]{:S(2)}, u32[]{:S(2)}) collective-permute-start(bf16[112,128]{1,0:T(8,128)(2,1)S(1)} %get-tuple-element.21), channel_id=1, source_target_pairs={{0,15},{1,2},{2,1},{3,4},{4,3},{5,6},{6,5},{7,8},{8,7},{9,10},{10,... | collective-permute-start | bytes 86024 | tf_op jit(solution)/shard_map/ppermute | solution.py:368
  7.5 3.3 %collective-permute-start.1 = (bf16[112,128]{1,0:T(8,128)(2,1)S(1)}, bf16[112,128]{1,0:T(8,128)(2,1)S(1)}, u32[]{:S(2)}, u32[]{:S(2)}) collective-permute-start(bf16[112,128]{1,0:T(8,128)(2,1)S(1)} %get-tuple-element.22), channel_id=1, source_target_pairs={{0,1},{1,0},{2,3},{3,2},{4,5},{5,4},{6,7},{7,6},{8,9},{9,8},{10,11... | collective-permute-start | bytes 86024 | tf_op jit(solution)/shard_map/ppermute | solution.py:368
  7.5 6.6 %collective-permute-start.2 = (bf16[112,128]{1,0:T(8,128)(2,1)S(1)}, bf16[112,128]{1,0:T(8,128)(2,1)S(1)}, u32[]{:S(2)}, u32[]{:S(2)}) collective-permute-start(bf16[112,128]{1,0:T(8,128)(2,1)S(1)} %get-tuple-element.19.my_far_off), channel_id=1, source_target_pairs={{0,14},{1,15},{2,4},{3,5},{4,2},{5,3},{6,8},{7,9},{8,6},{9,7},{10,... | collective-permute-start | bytes 86024 | tf_op jit(solution)/shard_map/ppermute | solution.py:368
  8.2 5.9 %collective-permute-start.3 = (bf16[112,128]{1,0:T(8,128)(2,1)S(1)}, bf16[112,128]{1,0:T(8,128)(2,1)S(1)}, u32[]{:S(2)}, u32[]{:S(2)}) collective-permute-start(bf16[112,128]{1,0:T(8,128)(2,1)S(1)} %get-tuple-element.20.my_far_on), channel_id=1, source_target_pairs={{0,2},{1,3},{2,0},{3,1},{4,6},{5,7},{6,4},{7,5},{8,10},{9,11},{10,... | collective-permute-start | bytes 86024 | tf_op jit(solution)/shard_map/ppermute | solution.py:368
  34.6 12.2 %all-to-all-start.1 = ((bf16[32,24,128]{2,1,0:T(8,128)(2,1)}), bf16[32,24,128]{2,1,0:T(8,128)(2,1)S(1)}, u32[]{:S(2)}, u32[]{:S(2)}) async-start(bf16[32,24,128]{2,1,0:T(8,128)(2,1)} %shard_map.153), calls=%async_computation.1 | async-start | bytes 393216 | tf_op jit(solution)/shard_map/all_to_all | solution.py:462
  37.2 8.7 %collective-permute-start.4 = (bf16[64,128]{1,0:T(8,128)(2,1)S(1)}, bf16[64,128]{1,0:T(8,128)(2,1)S(1)}, u32[]{:S(2)}, u32[]{:S(2)}) collective-permute-start(bf16[64,128]{1,0:T(8,128)(2,1)S(1)} %get-tuple-element.32), channel_id=1, source_target_pairs={{0,15},{1,2},{2,1},{3,4},{4,3},{5,6},{6,5},{7,8},{8,7},{9,10},{10,... | collective-permute-start | bytes 49160 | tf_op jit(solution)/shard_map/ppermute | solution.py:368
  41.5 4.3 %collective-permute-start.5 = (bf16[64,128]{1,0:T(8,128)(2,1)S(1)}, bf16[64,128]{1,0:T(8,128)(2,1)S(1)}, u32[]{:S(2)}, u32[]{:S(2)}) collective-permute-start(bf16[64,128]{1,0:T(8,128)(2,1)S(1)} %get-tuple-element.33), channel_id=1, source_target_pairs={{0,1},{1,0},{2,3},{3,2},{4,5},{5,4},{6,7},{7,6},{8,9},{9,8},{10,11... | collective-permute-start | bytes 49160 | tf_op jit(solution)/shard_map/ppermute | solution.py:368

commit v14 on v12

--- a/solution.py
+++ b/solution.py
@@ -11,6 +11,7 @@
 BF16 = jnp.bfloat16
 CODE_ROWS = 16
 LANES = 128
+SLAB = ("chip", "core")
 FAR = -1e30
 GROUP = 32
 BLOCK = 64
@@ -44,8 +45,7 @@
 
 
 def parities():
-    slab = lax.axis_index("slab")
-    return lax.rem(slab, 2) == 1, lax.rem(slab // 2, 2) == 1
+    return lax.axis_index("core") == 1, lax.rem(lax.axis_index("chip"), 2) == 1
 
 
 def pack_kernel(_, nodes, leave, arrive, sends, near_off, near_on, far_off, far_on):
@@ -158,7 +158,8 @@
     updated,
     back_off,
     back_on,
-    grads,
+    keep,
+    give,
     d_node_o,
     d_centre_o,
     d_neigh_o,
@@ -285,11 +286,11 @@
         tn(agg_b, d_node),
         tn(node_hid, cot),
     )
-    for m, part in enumerate(parts):
-        grads[m * width : (m + 1) * width] = part.astype(BF16)
-    used = len(parts) * width
-    if grads.shape[0] > used:
-        grads[used:] = jnp.zeros_like(grads[used:])
+    count = len(parts) // 2
+    for m in range(count):
+        at = slice(m * width, (m + 1) * width)
+        keep[at] = jnp.where(odd, parts[count + m], parts[m])
+        give[at] = jnp.where(odd, parts[m], parts[count + m]).astype(BF16)
 
 
 def finish_kernel(
@@ -309,15 +310,27 @@
     ).astype(BF16)
 
 
-def sum_kernel(parts, out):
+def add_kernel(keep, got, out):
+    used = keep.shape[0]
+    out[:used] = (keep[...] + got[...].astype(F32)).astype(BF16)
+    if out.shape[0] > used:
+        out[used:] = jnp.zeros_like(out[used:])
+
+
+def sum_kernel(parts, back_off, back_on, out, back_off_o, back_on_o):
     total = jnp.sum(parts[...].astype(F32), axis=0).astype(BF16)
     out[...] = jnp.broadcast_to(total[None], out.shape)
-
-
-def norm_kernel(total, steps):
-    count, width = steps.shape[0], steps.shape[1]
-    for m in range(count):
-        part = total[m * width : (m + 1) * width].astype(F32)
+    back_off_o[...] = back_off[...]
+    back_on_o[...] = back_on[...]
+
+
+def norm_kernel(mine, other, steps):
+    count, width = steps.shape[0] // 2, steps.shape[1]
+    odd, _ = parities()
+    for m in range(2 * count):
+        at = slice(m % count * width, (m % count + 1) * width)
+        own, got = mine[at].astype(F32), other[at].astype(F32)
+        part = jnp.where(odd, got, own) if m < count else jnp.where(odd, own, got)
         mean = jnp.sum(jnp.sum(part * part, axis=0, keepdims=True), axis=1, keepdims=True)
         mean = mean / (part.shape[0] * part.shape[1])
         steps[m] = part / jnp.sqrt(mean + 1e-06)
@@ -353,16 +366,16 @@
     migr = leave_list.shape[1] // 2
     border = send_list.shape[1] // 2
     table_rows = rows + 2 * border
-    size = lax.axis_size("slab")
-    devices = size * lax.axis_size("grp")
-    axes = ("grp", "slab")
+    size = lax.axis_size(SLAB)
+    axes = ("grp", "chip")
+    chips = lax.axis_size(axes)
 
     def swap(array, by):
         step = abs(by)
         pairs = [
             (i, (i + by if i // step % 2 == 0 else i - by) % size) for i in range(size)
         ]
-        return lax.ppermute(array, "slab", pairs)
+        return lax.ppermute(array, SLAB, pairs)
 
     message = (border + migr + CODE_ROWS, width)
     (token,) = call(first_kernel, [((8, LANES), F32)])()
@@ -379,7 +392,8 @@
     pair_rows = rows * slots // 2
     half_rows = table_rows // 2
     hot_rows = -(-(half_rows + 1) // LANES) * LANES
-    share = -(-matrices * width // (8 * devices)) * 8
+    half = matrices // 2 * width
+    share = -(-half // (8 * chips)) * 8
     edges = rows * slots
     hot, hot_t, wide, ids, d_hid = call(
         prep_kernel,
@@ -412,13 +426,14 @@
         w_out,
         cotangent,
     )
-    updated, back_off, back_on, grads, d_node, d_centre, d_neigh = call(
+    updated, back_off, back_on, keep, give, d_node, d_centre, d_neigh = call(
         layer_kernel,
         [
             ((1, rows, width), BF16),
             ((border, width), BF16),
             ((border, width), BF16),
-            ((devices * share, width), BF16),
+            ((half, width), F32),
+            ((half, width), BF16),
             ((rows, width), BF16),
             ((rows, width), BF16),
             ((rows, width), BF16),
@@ -434,11 +449,16 @@
             pltpu.VMEM((edges, 2 * width), BF16),
         ],
     )(*sources)
+    (chip,) = call(add_kernel, [((chips * share, width), BF16)])(keep, swap(give, 1))
+    parts = lax.all_to_all(
+        chip.reshape(chips, share, width), axes, split_axis=0, concat_axis=0, tiled=True
+    )
+    shared, back_off, back_on = call(
+        sum_kernel,
+        [((chips, share, width), BF16), ((border, width), BF16), ((border, width), BF16)],
+    )(parts, back_off, back_on)
     got_on = swap(back_on, 1)
     got_off = swap(back_off, -1)
-    parts = lax.all_to_all(
-        grads.reshape(devices, share, width), axes, split_axis=0, concat_axis=0, tiled=True
-    )
     sources = (
         cotangent,
         d_node,
@@ -455,16 +475,17 @@
         finish_kernel,
         [((1, rows, width), BF16)],
     )(*sources)
-    (shared,) = call(sum_kernel, [((devices, share, width), BF16)])(parts)
     total = lax.all_to_all(shared, axes, split_axis=0, concat_axis=0, tiled=True)
-    total = total.reshape(devices * share, width)[: matrices * width]
-    (weight_steps,) = call(norm_kernel, [((matrices, width, width), F32)])(total)
+    total = total.reshape(chips * share, width)[:half]
+    (weight_steps,) = call(norm_kernel, [((matrices, width, width), F32)])(total, swap(total, 1))
     return (updated, grad_nodes, weight_steps)
 
 
 def solution(mesh):
-    rows = P("grp", "slab", None)
-    lists = P("grp", "slab")
+    groups, slabs = mesh.devices.shape
+    mesh = jax.sharding.Mesh(mesh.devices.reshape(groups, slabs // 2, 2), ("grp", *SLAB))
+    rows = P("grp", SLAB, None)
+    lists = P("grp", SLAB)
     in_specs = (rows, lists, lists, lists, rows, rows, P(), P(), P(), P(), P(), P(), rows)
     out_specs = (rows, rows, P())
     return jax.shard_map(shards, mesh=mesh, in_specs=in_specs, out_specs=out_specs, check_vma=False)

time: 47.2 us -> 48.7 us (1.032)
  waiting for transfers between devices: 5.63 us -> 8.06 us
  starting transfers between devices: 15.2 us -> 14.4 us
    all_to_all x1, waiting for transfers between devices: 0.01 us -> 5.03 us  [shards(): lax.all_to_all(shared, axes, split_axis=0, concat_axis=0, tiled=True)]
    ppermute x6 -> x8, waiting for transfers between devices: 5.63 us -> 3.03 us  [swap(): return lax.ppermute(array, SLAB, pairs)]
    ppermute x6 -> x8, starting transfers between devices: 12.6 us -> 10.9 us  [swap(): return lax.ppermute(array, SLAB, pairs)]
    all_to_all x1, starting transfers between devices: 2.59 us -> 3.51 us  [shards(): lax.all_to_all(shared, axes, split_axis=0, concat_axis=0, tiled=True)]
    pallas_call x2 -> x3, Pallas kernels: 1.63 us -> 1.61 us  [the longest x1 0.92 us: shards(): call(norm_kernel, [((matrices, width, width), F32)])(total, swap(total, 1))]
  transfers between devices with their start and end apart: 7 -> 9, of which waited for: 2 -> 4; matrix products, arithmetic and copies ran while one was open for 0% -> 0% of each run, Pallas kernels for 7% -> 7%
where the time goes in v14:
time: 48.7 us; the launch traced here: 48.4 us
  starting transfers between devices  14.4 us (30%)
  Pallas kernels  13.1 us (27%)
  blocking collectives  11.2 us (23%)
  waiting for transfers between devices  8.06 us (17%)
  local copies, waits for them, and re-layouts  0.88 us (2%)
  between operations  0.83 us (2%)
    all_to_all x1, blocking collectives, shards(): lax.all_to_all(chip.reshape(chips, share, width), axes, split_axis=0, con...  11.2 us
    ppermute x8, starting transfers between devices, swap(): return lax.ppermute(array, SLAB, pairs)  10.9 us
    pallas_call x1, Pallas kernels, shards(): call(layer_kernel, [((1, rows, width), BF16), ((border, width), BF16), ((...  7.75 us
    all_to_all x1, waiting for transfers between devices, shards(): lax.all_to_all(shared, axes, split_axis=0, concat_axis=0, tiled=True)  5.03 us
    all_to_all x1, starting transfers between devices, shards(): lax.all_to_all(shared, axes, split_axis=0, concat_axis=0, tiled=True)  3.51 us
    ppermute x8, waiting for transfers between devices, swap(): return lax.ppermute(array, SLAB, pairs)  3.03 us
    pallas_call x1, Pallas kernels, shards(): call(prep_kernel, [((edges, hot_rows), BF16), ((half_rows, edges), BF16),...  2.49 us
  transfers between devices with their start and end apart: 9, of which 4 were waited for; matrix products, arithmetic and copies ran while one was open for 0% of the time, Pallas kernels for 7%

profile of v14, /device:TPU:0, one launch (start us, length us, event | category | flops | bytes accessed | tf_op | source)
XLA Modules:
  0.0 48.4 jit_solution(2325640984432716889)
XLA Ops:
  0.7 0.6 %copy-done.12 = s32[1,128]{1,0:T(1,128)S(1)} copy-done((s32[1,128]{1,0:T(1,128)S(1)}, s32[1,128]{1,0:T(1,128)}, u32[]{:S(2)}) %copy-start.12) | copy-done | bytes 536
  1.3 0.0 copy-done.7
  1.3 0.2 copy-done
  1.5 0.0 copy-start.9
  1.5 0.0 copy-start.10
  1.5 0.3 shard_map.149
  1.9 0.0 copy-start.3
  1.9 0.0 copy-start.4
  1.9 0.0 copy-start.5
  1.9 0.0 copy-start.6
  1.9 6.1 %collective-permute-start.2 = (bf16[32,128]{1,0:T(8,128)(2,1)S(1)}, bf16[32,128]{1,0:T(8,128)(2,1)S(1)}, u32[]{:S(2)}, u32[]{:S(2)}) collective-permute-start(bf16[32,128]{1,0:T(8,128)(2,1)S(1)} %get-tuple-element.23.my_far_off), channel_id=1, source_target_pairs={{0,14},{1,15},{2,4},{3,5},{4,2},{5,3},{6,8},{7,9},{8,6},{9,7},{10,... | collective-permute-start | bytes 24584 | tf_op jit(solution)/shard_map/ppermute | solution.py:378
  8.0 0.0 collective-permute-start.3
  8.0 0.8 %collective-permute-start = (bf16[112,128]{1,0:T(8,128)(2,1)S(1)}, bf16[112,128]{1,0:T(8,128)(2,1)S(1)}, u32[]{:S(2)}, u32[]{:S(2)}) collective-permute-start(bf16[112,128]{1,0:T(8,128)(2,1)S(1)} %get-tuple-element.25), channel_id=1, source_target_pairs={{0,15},{1,2},{2,1},{3,4},{4,3},{5,6},{6,5},{7,8},{8,7},{9,10},{10,... | collective-permute-start | bytes 86024 | tf_op jit(solution)/shard_map/ppermute | solution.py:378
  8.8 1.4 %collective-permute-start.1 = (bf16[112,128]{1,0:T(8,128)(2,1)S(1)}, bf16[112,128]{1,0:T(8,128)(2,1)S(1)}, u32[]{:S(2)}, u32[]{:S(2)}) collective-permute-start(bf16[112,128]{1,0:T(8,128)(2,1)S(1)} %get-tuple-element.26), channel_id=1, source_target_pairs={{0,1},{1,0},{2,3},{3,2},{4,5},{5,4},{6,7},{7,6},{8,9},{9,8},{10,11... | collective-permute-start | bytes 86024 | tf_op jit(solution)/shard_map/ppermute | solution.py:378
  10.2 2.5 %shard_map.150 = (bf16[8192,256]{1,0:T(8,128)(2,1)S(1)}, bf16[192,8192]{1,0:T(8,128)(2,1)S(1)}, bf16[2,256,256]{2,1,0:T(8,128)(2,1)S(1)}, s32[256,128]{1,0:T(8,128)S(1)}, f32[256,128]{1,0:T(8,128)S(1)}) custom-call(s32[1,32,256]{2,1,0:T(8,128)S(1)} %bitcast.7, s32[1,32,256]{2,1,0:T(8,128)S(1)} %bitcast.8, bf16[128,128]{1,0:T(8,128)(2,1)S(1)} %copy-done.10, ...), custom_call_target="tpu_custom_call" | custom-call | flops 2000000000 | bytes 1024 | tf_op jit(solution)/shard_map/pallas_call | solution.py:398
  12.7 0.0 collective-permute-done.2.got_far_off
  12.7 0.0 collective-permute-done.3.got_far_on
  12.7 1.3 %collective-permute-done.got_off = bf16[112,128]{1,0:T(8,128)(2,1)S(1)} collective-permute-done((bf16[112,128]{1,0:T(8,128)(2,1)S(1)}, bf16[112,128]{1,0:T(8,128)(2,1)S(1)}, u32[]{:S(2)}, u32[]{:S(2)}) %collective-permute-start) | collective-permute-done | bytes 28704 | tf_op jit(solution)/shard_map/ppermute | solution.py:378
  14.0 7.8 %shard_map.151 = (bf16[1,256,128]{2,1,0:T(8,128)(2,1)}, bf16[64,128]{1,0:T(8,128)(2,1)S(1)}, bf16[64,128]{1,0:T(8,128)(2,1)S(1)}, f32[384,128]{1,0:T(8,128)S(1)}...) custom-call(bf16[1,256,128]{2,1,0:T(8,128)(2,1)S(1)} %copy-done, ...), custom_call_target="tpu_custom_call" | custom-call | flops 2000000000 | bytes 1024 | tf_op jit(solution)/shard_map/pallas_call | solution.py:429
  21.8 0.1 collective-permute-start.4
  21.9 1.3 %collective-permute-done.4.got = bf16[384,128]{1,0:T(8,128)(2,1)S(1)} collective-permute-done((bf16[384,128]{1,0:T(8,128)(2,1)S(1)}, bf16[384,128]{1,0:T(8,128)(2,1)S(1)}, u32[]{:S(2)}, u32[]{:S(2)}) %collective-permute-start.4) | collective-permute-done | bytes 98336 | tf_op jit(solution)/shard_map/ppermute | solution.py:378
  23.2 11.2 %all_to_all.10.parts = bf16[16,24,128]{2,1,0:T(8,128)(2,1)S(1)} all-to-all(bf16[16,24,128]{2,1,0:T(8,128)(2,1)S(1)} %bitcast.6), channel_id=1, replica_groups=mesh['grp'=2,'chip'=8,'core'=2] {'grp','chip'}, dimensions={0} | all-to-all | bytes 196608 | tf_op jit(solution)/shard_map/all_to_all | solution.py:453
  34.4 0.7 %shard_map.153 = (bf16[16,24,128]{2,1,0:T(8,128)(2,1)}, bf16[64,128]{1,0:T(8,128)(2,1)S(1)}, bf16[64,128]{1,0:T(8,128)(2,1)S(1)}) custom-call(bf16[16,24,128]{2,1,0:T(8,128)(2,1)S(1)} %all_to_all.10.parts, bf16[64,128]{1,0:T(8,128)(2,1)S(1)} %get-tuple-element.38.back_off, bf16[64,128]{1,0:T(8,128)(2,1)S(1)} %get-tuple-element.39.back_on), custom_call_target="tpu_custom_call" | custom-call | flops 2000000000 | bytes 1024 | tf_op jit(solution)/shard_map/pallas_call | solution.py:456
  35.0 3.5 %all-to-all-start.1 = ((bf16[16,24,128]{2,1,0:T(8,128)(2,1)}), bf16[16,24,128]{2,1,0:T(8,128)(2,1)S(1)}, u32[]{:S(2)}, u32[]{:S(2)}) async-start(bf16[16,24,128]{2,1,0:T(8,128)(2,1)} %get-tuple-element.42), calls=%async_computation.1 | async-start | bytes 196608 | tf_op jit(solution)/shard_map/all_to_all | solution.py:478
  38.6 2.6 %collective-permute-start.5 = (bf16[64,128]{1,0:T(8,128)(2,1)S(1)}, bf16[64,128]{1,0:T(8,128)(2,1)S(1)}, u32[]{:S(2)}, u32[]{:S(2)}) collective-permute-start(bf16[64,128]{1,0:T(8,128)(2,1)S(1)} %get-tuple-element.40), channel_id=1, source_target_pairs={{0,15},{1,2},{2,1},{3,4},{4,3},{5,6},{6,5},{7,8},{8,7},{9,10},{10,... | collective-permute-start | bytes 49160 | tf_op jit(solution)/shard_map/ppermute | solution.py:378
  41.2 5.0 %all-to-all-done.1 = bf16[16,24,128]{2,1,0:T(8,128)(2,1)S(1)} async-done(((bf16[16,24,128]{2,1,0:T(8,128)(2,1)}), bf16[16,24,128]{2,1,0:T(8,128)(2,1)S(1)}, u32[]{:S(2)}, u32[]{:S(2)}) %all-to-all-start.1) | async-done | bytes 98336 | tf_op jit(solution)/shard_map/all_to_all | solution.py:478
  46.2 0.0 collective-permute-start.7
  46.2 0.0 collective-permute-done.5.got_off
  46.2 0.0 collective-permute-done.6.got_on
  46.2 0.9 %shard_map.154 = bf16[1,256,128]{2,1,0:T(8,128)(2,1)} custom-call(bf16[1,256,128]{2,1,0:T(8,128)(2,1)S(1)} %copy-done.1, bf16[256,128]{1,0:T(8,128)(2,1)S(1)} %get-tuple-element.33.d_node, bf16[256,128]{1,0:T(8,128)(2,1)S(1)} %get-tuple-element.34.d_centre, bf16[256,128]{1,0:T(8,128)(2,1)S(1)} %get-tuple-element.35.d_neigh, bf16[128,128]{1,0:T(8,128)(2,1)S(1)} %copy-done.6, ...), custom_call_target="tpu_custom_call" | custom-call | flops 2000000000 | bytes 1024 | tf_op jit(solution)/shard_map/pallas_call | solution.py:474
  47.1 0.4 collective-permute-done.7.other
  47.5 0.9 %shard_map.155 = f32[6,128,128]{2,1,0:T(8,128)} custom-call(bf16[384,128]{1,0:T(8,128)(2,1)S(1)} %bitcast.5, bf16[384,128]{1,0:T(8,128)(2,1)S(1)} %collective-permute-done.7.other), custom_call_target="tpu_custom_call" | custom-call | flops 2000000000 | bytes 1024 | tf_op jit(solution)/shard_map/pallas_call | solution.py:480
  (21 shorter events, 0.1 us)
Async XLA Ops:
  0.6 0.7 %copy-start.12 = (s32[1,128]{1,0:T(1,128)S(1)}, s32[1,128]{1,0:T(1,128)}, u32[]{:S(2)}) copy-start(s32[1,128]{1,0:T(1,128)} %sends.3) | copy-start | bytes 1540
  0.6 0.7 %copy-start.7 = (s32[1,256]{1,0:T(1,128)S(1)}, s32[1,256]{1,0:T(1,128)}, u32[]{:S(2)}) copy-start(s32[1,256]{1,0:T(1,128)} %arrive.3) | copy-start | bytes 3076
  0.7 0.9 %copy-start = (bf16[1,256,128]{2,1,0:T(8,128)(2,1)S(1)}, bf16[1,256,128]{2,1,0:T(8,128)(2,1)}, u32[]{:S(2)}) copy-start(bf16[1,256,128]{2,1,0:T(8,128)(2,1)} %nodes.3) | copy-start | bytes 196612
  0.7 0.8 %copy-start.11 = (s32[1,64]{1,0:T(1,128)S(1)}, s32[1,64]{1,0:T(1,128)}, u32[]{:S(2)}) copy-start(s32[1,64]{1,0:T(1,128)} %leave.1) | copy-start | bytes 772
  1.5 8.7 %copy-start.1 = (bf16[1,256,128]{2,1,0:T(8,128)(2,1)S(1)}, bf16[1,256,128]{2,1,0:T(8,128)(2,1)}, u32[]{:S(2)}) copy-start(bf16[1,256,128]{2,1,0:T(8,128)(2,1)} %cotangent.5) | copy-start | bytes 196612
  1.5 8.7 %copy-start.2 = (bf16[128,128]{1,0:T(8,128)(2,1)S(1)}, bf16[128,128]{1,0:T(8,128)(2,1)}, u32[]{:S(2)}) copy-start(bf16[128,128]{1,0:T(8,128)(2,1)} %w_out.3) | copy-start | bytes 98308
  1.5 8.7 %copy-start.8 = (s32[1,256,32]{1,2,0:T(8,128)S(1)}, s32[1,256,32]{1,2,0:T(8,128)}, u32[]{:S(2)}) copy-start(s32[1,256,32]{1,2,0:T(8,128)} %param.17) | copy-start | bytes 98308
  1.5 8.7 %copy-start.9 = (s32[1,256,32]{1,2,0:T(8,128)S(1)}, s32[1,256,32]{1,2,0:T(8,128)}, u32[]{:S(2)}) copy-start(s32[1,256,32]{1,2,0:T(8,128)} %param.18) | copy-start | bytes 98308
  1.5 8.6 %copy-start.10 = (bf16[128,128]{1,0:T(8,128)(2,1)S(1)}, bf16[128,128]{1,0:T(8,128)(2,1)}, u32[]{:S(2)}) copy-start(bf16[128,128]{1,0:T(8,128)(2,1)} %w_msg.1) | copy-start | bytes 98308
  1.9 12.1 %copy-start.3 = (bf16[128,128]{1,0:T(8,128)(2,1)S(1)}, bf16[128,128]{1,0:T(8,128)(2,1)}, u32[]{:S(2)}) copy-start(bf16[128,128]{1,0:T(8,128)(2,1)} %w_agg.1) | copy-start | bytes 98308
  1.9 12.1 %copy-start.4 = (bf16[128,128]{1,0:T(8,128)(2,1)S(1)}, bf16[128,128]{1,0:T(8,128)(2,1)}, u32[]{:S(2)}) copy-start(bf16[128,128]{1,0:T(8,128)(2,1)} %w_send.3) | copy-start | bytes 98308
  1.9 12.1 %copy-start.5 = (bf16[128,128]{1,0:T(8,128)(2,1)S(1)}, bf16[128,128]{1,0:T(8,128)(2,1)}, u32[]{:S(2)}) copy-start(bf16[128,128]{1,0:T(8,128)(2,1)} %w_recv.3) | copy-start | bytes 98308
  1.9 12.1 %copy-start.6 = (bf16[128,128]{1,0:T(8,128)(2,1)S(1)}, bf16[128,128]{1,0:T(8,128)(2,1)}, u32[]{:S(2)}) copy-start(bf16[128,128]{1,0:T(8,128)(2,1)} %w_self.3) | copy-start | bytes 98308
  1.9 10.7 %collective-permute-start.2 = (bf16[32,128]{1,0:T(8,128)(2,1)S(1)}, bf16[32,128]{1,0:T(8,128)(2,1)S(1)}, u32[]{:S(2)}, u32[]{:S(2)}) collective-permute-start(bf16[32,128]{1,0:T(8,128)(2,1)S(1)} %get-tuple-element.23.my_far_off), channel_id=1, source_target_pairs={{0,14},{1,15},{2,4},{3,5},{4,2},{5,3},{6,8},{7,9},{8,6},{9,7},{10,... | collective-permute-start | bytes 24584 | tf_op jit(solution)/shard_map/ppermute | solution.py:378
  8.0 4.7 %collective-permute-start.3 = (bf16[32,128]{1,0:T(8,128)(2,1)S(1)}, bf16[32,128]{1,0:T(8,128)(2,1)S(1)}, u32[]{:S(2)}, u32[]{:S(2)}) collective-permute-start(bf16[32,128]{1,0:T(8,128)(2,1)S(1)} %get-tuple-element.24.my_far_on), channel_id=1, source_target_pairs={{0,2},{1,3},{2,0},{3,1},{4,6},{5,7},{6,4},{7,5},{8,10},{9,11},{10,... | collective-permute-start | bytes 24584 | tf_op jit(solution)/shard_map/ppermute | solution.py:378
  8.0 6.0 %collective-permute-start = (bf16[112,128]{1,0:T(8,128)(2,1)S(1)}, bf16[112,128]{1,0:T(8,128)(2,1)S(1)}, u32[]{:S(2)}, u32[]{:S(2)}) collective-permute-start(bf16[112,128]{1,0:T(8,128)(2,1)S(1)} %get-tuple-element.25), channel_id=1, source_target_pairs={{0,15},{1,2},{2,1},{3,4},{4,3},{5,6},{6,5},{7,8},{8,7},{9,10},{10,... | collective-permute-start | bytes 86024 | tf_op jit(solution)/shard_map/ppermute | solution.py:378
  8.8 5.2 %collective-permute-start.1 = (bf16[112,128]{1,0:T(8,128)(2,1)S(1)}, bf16[112,128]{1,0:T(8,128)(2,1)S(1)}, u32[]{:S(2)}, u32[]{:S(2)}) collective-permute-start(bf16[112,128]{1,0:T(8,128)(2,1)S(1)} %get-tuple-element.26), channel_id=1, source_target_pairs={{0,1},{1,0},{2,3},{3,2},{4,5},{5,4},{6,7},{7,6},{8,9},{9,8},{10,11... | collective-permute-start | bytes 86024 | tf_op jit(solution)/shard_map/ppermute | solution.py:378
  21.8 1.4 %collective-permute-start.4 = (bf16[384,128]{1,0:T(8,128)(2,1)S(1)}, bf16[384,128]{1,0:T(8,128)(2,1)S(1)}, u32[]{:S(2)}, u32[]{:S(2)}) collective-permute-start(bf16[384,128]{1,0:T(8,128)(2,1)S(1)} %get-tuple-element.37), channel_id=1, source_target_pairs={{0,1},{1,0},{2,3},{3,2},{4,5},{5,4},{6,7},{7,6},{8,9},{9,8},{10,11... | collective-permute-start | bytes 294920 | tf_op jit(solution)/shard_map/ppermute | solution.py:378
  35.0 11.1 %all-to-all-start.1 = ((bf16[16,24,128]{2,1,0:T(8,128)(2,1)}), bf16[16,24,128]{2,1,0:T(8,128)(2,1)S(1)}, u32[]{:S(2)}, u32[]{:S(2)}) async-start(bf16[16,24,128]{2,1,0:T(8,128)(2,1)} %get-tuple-element.42), calls=%async_computation.1 | async-start | bytes 196608 | tf_op jit(solution)/shard_map/all_to_all | solution.py:478
  38.6 7.6 %collective-permute-start.5 = (bf16[64,128]{1,0:T(8,128)(2,1)S(1)}, bf16[64,128]{1,0:T(8,128)(2,1)S(1)}, u32[]{:S(2)}, u32[]{:S(2)}) collective-permute-start(bf16[64,128]{1,0:T(8,128)(2,1)S(1)} %get-tuple-element.40), channel_id=1, source_target_pairs={{0,15},{1,2},{2,1},{3,4},{4,3},{5,6},{6,5},{7,8},{8,7},{9,10},{10,... | collective-permute-start | bytes 49160 | tf_op jit(solution)/shard_map/ppermute | solution.py:378
  41.2 5.0 %collective-permute-start.6 = (bf16[64,128]{1,0:T(8,128)(2,1)S(1)}, bf16[64,128]{1,0:T(8,128)(2,1)S(1)}, u32[]{:S(2)}, u32[]{:S(2)}) collective-permute-start(bf16[64,128]{1,0:T(8,128)(2,1)S(1)} %get-tuple-element.41), channel_id=1, source_target_pairs={{0,1},{1,0},{2,3},{3,2},{4,5},{5,4},{6,7},{7,6},{8,9},{9,8},{10,11... | collective-permute-start | bytes 49160 | tf_op jit(solution)/shard_map/ppermute | solution.py:378
  46.2 1.3 %collective-permute-start.7 = (bf16[384,128]{1,0:T(8,128)(2,1)S(1)}, bf16[384,128]{1,0:T(8,128)(2,1)S(1)}, u32[]{:S(2)}, u32[]{:S(2)}) collective-permute-start(bf16[384,128]{1,0:T(8,128)(2,1)S(1)} %bitcast.4), channel_id=1, source_target_pairs={{0,1},{1,0},{2,3},{3,2},{4,5},{5,4},{6,7},{7,6},{8,9},{9,8},{10,11... | collective-permute-start | bytes 294920 | tf_op jit(solution)/shard_map/ppermute | solution.py:378

commit v15 on v12

--- a/solution.py
+++ b/solution.py
@@ -43,13 +43,12 @@
     out[...] = jnp.zeros_like(out)
 
 
-def parities():
-    slab = lax.axis_index("slab")
-    return lax.rem(slab, 2) == 1, lax.rem(slab // 2, 2) == 1
-
-
-def pack_kernel(_, nodes, leave, arrive, sends, near_off, near_on, far_off, far_on):
-    odd, odd_pair = parities()
+def is_odd():
+    return lax.rem(lax.axis_index("slab"), 2) == 1
+
+
+def pack_kernel(_, nodes, leave, arrive, sends, near_off, near_on, far_up, far_down):
+    odd = is_odd()
     rows = nodes.shape[1]
     migr = leave.shape[1] // 2
     border = sends.shape[1] // 2
@@ -79,12 +78,12 @@
     down, up = messages
     near_off[...] = jnp.where(odd, up, down)
     near_on[...] = jnp.where(odd, down, up)
-    down, up = leaving[:migr], leaving[migr:]
-    far_off[...] = jnp.where(odd_pair, up, down)
-    far_on[...] = jnp.where(odd_pair, down, up)
-
-
-def prep_kernel(nbr, valid, w_msg, w_out, cotangent, hot_o, hot_t_o, wide_o, ids_o, d_hid_o):
+    far_down[...], far_up[...] = leaving[:migr], leaving[migr:]
+
+
+def prep_kernel(
+    arrive, nbr, valid, w_msg, w_out, cotangent, hot_o, hot_t_o, wide_o, ids_o, d_hid_o, moves_o
+):
     slots, rows = nbr.shape[1:]
     width = w_msg.shape[0]
     half_rows, hot_rows = hot_t_o.shape[0], hot_o.shape[1]
@@ -100,6 +99,9 @@
             axis=0,
         ).astype(BF16)
     d_hid_o[...] = nt(cotangent[0], w_out[...])
+    sub = lax.broadcasted_iota(jnp.int32, (moves_o.shape[1], rows), 0)
+    moves = jnp.where(sub == arrive[...], 1.0, 0.0)
+    moves_o[...] = jnp.transpose(moves, (1, 0)).astype(BF16)
     upper = nbr[0] >= half_rows
     low_row = jnp.where(upper, nbr[0] - half_rows, nbr[0])
     index = jnp.where(valid[0] == 1, low_row, half_rows) + jnp.where(upper, hot_rows, 0)
@@ -137,13 +139,13 @@
 
 def layer_kernel(
     nodes,
-    arrive,
-    my_far_off,
-    my_far_on,
+    moves,
+    my_up,
+    my_down,
     got_off,
     got_on,
-    got_far_off,
-    got_far_on,
+    low_far,
+    high_far,
     hot,
     hot_t,
     wide,
@@ -173,20 +175,15 @@
 ):
     rows, width = nodes.shape[1:]
     slots = hot.shape[0] // rows
-    border, migr = back_off.shape[0], got_far_off.shape[0]
-    odd, odd_pair = parities()
+    border, migr = back_off.shape[0], low_far.shape[0]
+    odd = is_odd()
     low = jnp.where(odd, got_on[...], got_off[...])
     high = jnp.where(odd, got_off[...], got_on[...])
-    low_far = jnp.where(odd_pair, got_far_on[...], got_far_off[...])
-    high_far = jnp.where(odd_pair, got_far_off[...], got_far_on[...])
-    my_up = jnp.where(odd_pair, my_far_off[...], my_far_on[...])
-    my_down = jnp.where(odd_pair, my_far_on[...], my_far_off[...])
-    table_rows = rows + 2 * border
 
     pool = jnp.concatenate(
         [nodes[0], low[border : border + migr], high[border : border + migr]], axis=0
     )
-    moved = tn(hot_columns(arrive[...], pool.shape[0]), pool).astype(BF16)
+    moved = nn(moves[...], pool).astype(BF16)
 
     def halo(message, first, second):
         code = message[border + migr : border + migr + 8].astype(F32)[:1]
@@ -195,8 +192,8 @@
         extra = tn(hot_columns(code, 2 * migr), source)
         return (message[:border].astype(F32) + extra[:border]).astype(BF16)
 
-    below = halo(low, low_far, my_down)
-    above = halo(high, my_up, high_far)
+    below = halo(low, low_far[...], my_down[...])
+    above = halo(high, my_up[...], high_far[...])
     table = jnp.concatenate([moved, below, above], axis=0)
 
     half_rows, hot_rows = hot_t.shape[0], hot.shape[1]
@@ -241,6 +238,13 @@
     cot = cotangent[0]
     d_node = (d_hid[...] * (0.5 * slope)).astype(BF16)
     half_d_agg = 0.5 * nt(d_node, w_agg[...])
+
+    def store(m, gradient):
+        grads[m * width : (m + 1) * width] = gradient.astype(BF16)
+
+    store(3, tn(moved, d_node))
+    store(4, tn(agg_b, d_node))
+    store(5, tn(node_hid, cot))
 
     none = jnp.zeros((BLOCK, width), BF16)
     border_id = jnp.full((BLOCK, width), hot_rows, jnp.int16)
@@ -277,17 +281,10 @@
     d_node_o[...] = d_node
     d_centre_o[...] = d_centre
     d_neigh_o[...] = d_neigh[:rows]
-    parts = (
-        tn(moved, d_centre),
-        tn(table, d_neigh),
-        gmsg[:width, :width] + gmsg[width:, width:],
-        tn(moved, d_node),
-        tn(agg_b, d_node),
-        tn(node_hid, cot),
-    )
-    for m, part in enumerate(parts):
-        grads[m * width : (m + 1) * width] = part.astype(BF16)
-    used = len(parts) * width
+    store(2, gmsg[:width, :width] + gmsg[width:, width:])
+    store(0, tn(moved, d_centre))
+    store(1, tn(table, d_neigh))
+    used = 6 * width
     if grads.shape[0] > used:
         grads[used:] = jnp.zeros_like(grads[used:])
 
@@ -296,7 +293,7 @@
     cotangent, d_node, d_centre, d_neigh, w_self, w_send, w_recv, sends, got_off, got_on, out
 ):
     rows = d_node.shape[0]
-    odd, _ = parities()
+    odd = is_odd()
     from_low = jnp.where(odd, got_on[...], got_off[...])
     from_high = jnp.where(odd, got_off[...], got_on[...])
     returned = jnp.concatenate([from_low, from_high], axis=0)
@@ -357,23 +354,23 @@
     devices = size * lax.axis_size("grp")
     axes = ("grp", "slab")
 
+    def shift(array, by):
+        return lax.ppermute(array, "slab", [(i, (i + by) % size) for i in range(size)])
+
     def swap(array, by):
-        step = abs(by)
-        pairs = [
-            (i, (i + by if i // step % 2 == 0 else i - by) % size) for i in range(size)
-        ]
+        pairs = [(i, (i + (by if i % 2 == 0 else -by)) % size) for i in range(size)]
         return lax.ppermute(array, "slab", pairs)
 
     message = (border + migr + CODE_ROWS, width)
     (token,) = call(first_kernel, [((8, LANES), F32)])()
-    near_off, near_on, far_off, far_on = call(
+    near_off, near_on, far_up, far_down = call(
         pack_kernel,
         [(message, BF16)] * 2 + [((migr, width), BF16)] * 2,
     )(token, nodes, leave_list, arrive_list, send_list)
     got_on = swap(near_on, 1)
     got_off = swap(near_off, -1)
-    got_far_on = swap(far_on, 2)
-    got_far_off = swap(far_off, -2)
+    high_far = shift(far_down, -2)
+    low_far = shift(far_up, 2)
 
     matrices = 6
     pair_rows = rows * slots // 2
@@ -381,7 +378,7 @@
     hot_rows = -(-(half_rows + 1) // LANES) * LANES
     share = -(-matrices * width // (8 * devices)) * 8
     edges = rows * slots
-    hot, hot_t, wide, ids, d_hid = call(
+    hot, hot_t, wide, ids, d_hid, moves = call(
         prep_kernel,
         [
             ((edges, hot_rows), BF16),
@@ -389,17 +386,18 @@
             ((2, 2 * width, 2 * width), BF16),
             ((rows, LANES), jnp.int32),
             ((rows, width), F32),
+            ((rows, rows + 2 * migr), BF16),
         ],
-    )(jnp.swapaxes(neighbours, 1, 2), jnp.swapaxes(valid, 1, 2), w_msg, w_out, cotangent)
+    )(arrive_list, jnp.swapaxes(neighbours, 1, 2), jnp.swapaxes(valid, 1, 2), w_msg, w_out, cotangent)
     sources = (
         nodes,
-        arrive_list,
-        far_off,
-        far_on,
+        moves,
+        far_up,
+        far_down,
         got_off,
         got_on,
-        got_far_off,
-        got_far_on,
+        low_far,
+        high_far,
         hot,
         hot_t,
         wide,

time: 47.2 us -> 47.4 us (level)
  starting transfers between devices: 15.2 us -> 13.9 us
  waiting for transfers between devices: 5.63 us -> 6.89 us
    ppermute x6 -> x4, starting transfers between devices: 12.6 us -> 5.22 us  [swap(): return lax.ppermute(array, 'slab', pairs)]
    ppermute x0 -> x2, starting transfers between devices: none -> 6.12 us  [shift(): lax.ppermute(array, 'slab', [(i, (i + by) % size) for i in range(size)])]
    ppermute x6 -> x4, waiting for transfers between devices: 5.63 us -> 6.88 us  [swap(): return lax.ppermute(array, 'slab', pairs)]
where the time goes in v15:
time: 47.4 us; the launch traced here: 47.2 us
  starting transfers between devices  13.9 us (29%)
  Pallas kernels  13.1 us (28%)
  blocking collectives  11.5 us (24%)
  waiting for transfers between devices  6.89 us (15%)
  local copies, waits for them, and re-layouts  0.88 us (2%)
  between operations  0.83 us (2%)
    all_to_all x1, blocking collectives, shards(): lax.all_to_all(grads.reshape(devices, share, width), axes, split_axis=0,...  11.5 us
    pallas_call x1, Pallas kernels, shards(): call(layer_kernel, [((1, rows, width), BF16), ((border, width), BF16), ((...  7.79 us
    ppermute x4, waiting for transfers between devices, swap(): return lax.ppermute(array, 'slab', pairs)  6.88 us
    ppermute x2, starting transfers between devices, shift(): lax.ppermute(array, 'slab', [(i, (i + by) % size) for i in range(size)])  6.12 us
    ppermute x4, starting transfers between devices, swap(): return lax.ppermute(array, 'slab', pairs)  5.22 us
    all_to_all x1, starting transfers between devices, shards(): lax.all_to_all(shared, axes, split_axis=0, concat_axis=0, tiled=True)  2.59 us
    pallas_call x1, Pallas kernels, shards(): call(prep_kernel, [((edges, hot_rows), BF16), ((half_rows, edges), BF16),...  2.51 us
  transfers between devices with their start and end apart: 7, of which 2 were waited for; matrix products, arithmetic and copies ran while one was open for 0% of the time, Pallas kernels for 7%

profile of v15, /device:TPU:0, one launch (start us, length us, event | category | flops | bytes accessed | tf_op | source)
XLA Modules:
  0.0 47.2 jit_solution(2634441137735608728)
XLA Ops:
  0.7 0.6 %copy-done.12 = s32[1,128]{1,0:T(1,128)S(1)} copy-done((s32[1,128]{1,0:T(1,128)S(1)}, s32[1,128]{1,0:T(1,128)}, u32[]{:S(2)}) %copy-start.12) | copy-done | bytes 536
  1.3 0.0 copy-done.10
  1.3 0.2 copy-done
  1.5 0.0 copy-start.8
  1.5 0.0 copy-start.9
  1.5 0.3 shard_map.150
  1.9 0.0 copy-start.3
  1.9 0.0 copy-start.4
  1.9 0.0 copy-start.5
  1.9 0.0 copy-start.6
  1.9 3.0 %collective-permute-start.2 = (bf16[32,128]{1,0:T(8,128)(2,1)S(1)}, bf16[32,128]{1,0:T(8,128)(2,1)S(1)}, u32[]{:S(2)}, u32[]{:S(2)}) collective-permute-start(bf16[32,128]{1,0:T(8,128)(2,1)S(1)} %get-tuple-element.21.my_up), channel_id=1, source_target_pairs={{0,2},{1,3},{2,4},{3,5},{4,6},{5,7},{6,8},{7,9},{8,10},{9,11},{10,... | collective-permute-start | bytes 24584 | tf_op jit(solution)/shard_map/ppermute | solution.py:358
  5.0 3.1 %collective-permute-start.3 = (bf16[32,128]{1,0:T(8,128)(2,1)S(1)}, bf16[32,128]{1,0:T(8,128)(2,1)S(1)}, u32[]{:S(2)}, u32[]{:S(2)}) collective-permute-start(bf16[32,128]{1,0:T(8,128)(2,1)S(1)} %get-tuple-element.22.my_down), channel_id=1, source_target_pairs={{0,14},{1,15},{2,0},{3,1},{4,2},{5,3},{6,4},{7,5},{8,6},{9,7},{10,... | collective-permute-start | bytes 24584 | tf_op jit(solution)/shard_map/ppermute | solution.py:358
  8.1 0.8 %collective-permute-start = (bf16[112,128]{1,0:T(8,128)(2,1)S(1)}, bf16[112,128]{1,0:T(8,128)(2,1)S(1)}, u32[]{:S(2)}, u32[]{:S(2)}) collective-permute-start(bf16[112,128]{1,0:T(8,128)(2,1)S(1)} %get-tuple-element.23), channel_id=1, source_target_pairs={{0,15},{1,2},{2,1},{3,4},{4,3},{5,6},{6,5},{7,8},{8,7},{9,10},{10,... | collective-permute-start | bytes 86024 | tf_op jit(solution)/shard_map/ppermute | solution.py:362
  8.9 0.0 collective-permute-start.1
  8.9 0.0 copy-done.2
  8.9 2.5 %shard_map.148 = (bf16[8192,256]{1,0:T(8,128)(2,1)S(1)}, bf16[192,8192]{1,0:T(8,128)(2,1)S(1)}, bf16[2,256,256]{2,1,0:T(8,128)(2,1)S(1)}, s32[256,128]{1,0:T(8,1...) custom-call(s32[1,256]{1,0:T(1,128)S(1)} %copy-done.10, s32[1,32,256]{2,1,0:T(8,128)S(1)} %bitcast.6, ...), custom_call_target="tpu_custom_call" | custom-call | flops 2000000000 | bytes 1024 | tf_op jit(solution)/shard_map/pallas_call | solution.py:381
  11.5 0.0 collective-permute-done.2.low_far
  11.5 0.0 collective-permute-done.3.high_far
  11.5 2.6 %collective-permute-done.got_off = bf16[112,128]{1,0:T(8,128)(2,1)S(1)} collective-permute-done((bf16[112,128]{1,0:T(8,128)(2,1)S(1)}, bf16[112,128]{1,0:T(8,128)(2,1)S(1)}, u32[]{:S(2)}, u32[]{:S(2)}) %collective-permute-start) | collective-permute-done | bytes 28704 | tf_op jit(solution)/shard_map/ppermute | solution.py:362
  14.1 0.0 collective-permute-done.1.got_on
  14.1 0.0 copy-done.4
  14.1 7.8 %shard_map.151 = (bf16[1,256,128]{2,1,0:T(8,128)(2,1)}, bf16[64,128]{1,0:T(8,128)(2,1)S(1)}, bf16[64,128]{1,0:T(8,128)(2,1)S(1)}, bf16[768,128]{1,0:T(8,128)(2,1...) custom-call(bf16[1,256,128]{2,1,0:T(8,128)(2,1)S(1)} %copy-done, ...), custom_call_target="tpu_custom_call" | custom-call | flops 2000000000 | bytes 1024 | tf_op jit(solution)/shard_map/pallas_call | solution.py:413
  21.9 11.5 %all_to_all.10.parts = bf16[32,24,128]{2,1,0:T(8,128)(2,1)S(1)} all-to-all(bf16[32,24,128]{2,1,0:T(8,128)(2,1)S(1)} %bitcast.5), channel_id=1, replica_groups=mesh['grp'=2,'slab'=16] {'grp','slab'}, dimensions={0} | all-to-all | bytes 393216 | tf_op jit(solution)/shard_map/all_to_all | solution.py:437
  33.4 0.7 %shard_map.153 = bf16[32,24,128]{2,1,0:T(8,128)(2,1)} custom-call(bf16[32,24,128]{2,1,0:T(8,128)(2,1)S(1)} %all_to_all.10.parts), custom_call_target="tpu_custom_call" | custom-call | flops 2000000000 | bytes 1024 | tf_op jit(solution)/shard_map/pallas_call | solution.py:456
  34.1 2.6 %all-to-all-start.1 = ((bf16[32,24,128]{2,1,0:T(8,128)(2,1)}), bf16[32,24,128]{2,1,0:T(8,128)(2,1)S(1)}, u32[]{:S(2)}, u32[]{:S(2)}) async-start(bf16[32,24,128]{2,1,0:T(8,128)(2,1)} %shard_map.153), calls=%async_computation.1 | async-start | bytes 393216 | tf_op jit(solution)/shard_map/all_to_all | solution.py:457
  36.7 4.4 %collective-permute-start.4 = (bf16[64,128]{1,0:T(8,128)(2,1)S(1)}, bf16[64,128]{1,0:T(8,128)(2,1)S(1)}, u32[]{:S(2)}, u32[]{:S(2)}) collective-permute-start(bf16[64,128]{1,0:T(8,128)(2,1)S(1)} %get-tuple-element.34), channel_id=1, source_target_pairs={{0,15},{1,2},{2,1},{3,4},{4,3},{5,6},{6,5},{7,8},{8,7},{9,10},{10,... | collective-permute-start | bytes 49160 | tf_op jit(solution)/shard_map/ppermute | solution.py:362
  41.1 0.0 collective-permute-start.5
  41.1 4.3 %collective-permute-done.4.got_off = bf16[64,128]{1,0:T(8,128)(2,1)S(1)} collective-permute-done((bf16[64,128]{1,0:T(8,128)(2,1)S(1)}, bf16[64,128]{1,0:T(8,128)(2,1)S(1)}, u32[]{:S(2)}, u32[]{:S(2)}) %collective-permute-start.4) | collective-permute-done | bytes 16416 | tf_op jit(solution)/shard_map/ppermute | solution.py:362
  45.4 0.0 collective-permute-done.5.got_on
  45.4 0.9 %shard_map.152 = bf16[1,256,128]{2,1,0:T(8,128)(2,1)} custom-call(bf16[1,256,128]{2,1,0:T(8,128)(2,1)S(1)} %copy-done.1, bf16[256,128]{1,0:T(8,128)(2,1)S(1)} %get-tuple-element.31.d_node, bf16[256,128]{1,0:T(8,128)(2,1)S(1)} %get-tuple-element.32.d_centre, bf16[256,128]{1,0:T(8,128)(2,1)S(1)} %get-tuple-element.33.d_neigh, bf16[128,128]{1,0:T(8,128)(2,1)S(1)} %copy-done.6, ...), custom_call_target="tpu_custom_call" | custom-call | flops 2000000000 | bytes 1024 | tf_op jit(solution)/shard_map/pallas_call | solution.py:452
  46.3 0.0 all-to-all-done.1
  46.3 0.9 %shard_map.154 = f32[6,128,128]{2,1,0:T(8,128)} custom-call(bf16[768,128]{1,0:T(8,128)(2,1)S(1)} %bitcast.4), custom_call_target="tpu_custom_call" | custom-call | flops 2000000000 | bytes 1024 | tf_op jit(solution)/shard_map/pallas_call | solution.py:459
  (16 shorter events, 0.0 us)
Async XLA Ops:
  0.6 0.7 %copy-start.12 = (s32[1,128]{1,0:T(1,128)S(1)}, s32[1,128]{1,0:T(1,128)}, u32[]{:S(2)}) copy-start(s32[1,128]{1,0:T(1,128)} %sends.3) | copy-start | bytes 1540
  0.6 0.7 %copy-start.10 = (s32[1,256]{1,0:T(1,128)S(1)}, s32[1,256]{1,0:T(1,128)}, u32[]{:S(2)}) copy-start(s32[1,256]{1,0:T(1,128)} %arrive.3) | copy-start | bytes 3076
  0.7 0.9 %copy-start = (bf16[1,256,128]{2,1,0:T(8,128)(2,1)S(1)}, bf16[1,256,128]{2,1,0:T(8,128)(2,1)}, u32[]{:S(2)}) copy-start(bf16[1,256,128]{2,1,0:T(8,128)(2,1)} %nodes.3) | copy-start | bytes 196612
  0.7 0.8 %copy-start.11 = (s32[1,64]{1,0:T(1,128)S(1)}, s32[1,64]{1,0:T(1,128)}, u32[]{:S(2)}) copy-start(s32[1,64]{1,0:T(1,128)} %leave.1) | copy-start | bytes 772
  1.5 7.4 %copy-start.1 = (bf16[1,256,128]{2,1,0:T(8,128)(2,1)S(1)}, bf16[1,256,128]{2,1,0:T(8,128)(2,1)}, u32[]{:S(2)}) copy-start(bf16[1,256,128]{2,1,0:T(8,128)(2,1)} %cotangent.5) | copy-start | bytes 196612
  1.5 7.4 %copy-start.2 = (bf16[128,128]{1,0:T(8,128)(2,1)S(1)}, bf16[128,128]{1,0:T(8,128)(2,1)}, u32[]{:S(2)}) copy-start(bf16[128,128]{1,0:T(8,128)(2,1)} %w_out.3) | copy-start | bytes 98308
  1.5 7.4 %copy-start.7 = (s32[1,256,32]{1,2,0:T(8,128)S(1)}, s32[1,256,32]{1,2,0:T(8,128)}, u32[]{:S(2)}) copy-start(s32[1,256,32]{1,2,0:T(8,128)} %param.17) | copy-start | bytes 98308
  1.5 7.4 %copy-start.8 = (s32[1,256,32]{1,2,0:T(8,128)S(1)}, s32[1,256,32]{1,2,0:T(8,128)}, u32[]{:S(2)}) copy-start(s32[1,256,32]{1,2,0:T(8,128)} %param.18) | copy-start | bytes 98308
  1.5 7.4 %copy-start.9 = (bf16[128,128]{1,0:T(8,128)(2,1)S(1)}, bf16[128,128]{1,0:T(8,128)(2,1)}, u32[]{:S(2)}) copy-start(bf16[128,128]{1,0:T(8,128)(2,1)} %w_msg.1) | copy-start | bytes 98308
  1.9 12.2 %copy-start.3 = (bf16[128,128]{1,0:T(8,128)(2,1)S(1)}, bf16[128,128]{1,0:T(8,128)(2,1)}, u32[]{:S(2)}) copy-start(bf16[128,128]{1,0:T(8,128)(2,1)} %w_agg.1) | copy-start | bytes 98308
  1.9 12.2 %copy-start.4 = (bf16[128,128]{1,0:T(8,128)(2,1)S(1)}, bf16[128,128]{1,0:T(8,128)(2,1)}, u32[]{:S(2)}) copy-start(bf16[128,128]{1,0:T(8,128)(2,1)} %w_send.3) | copy-start | bytes 98308
  1.9 12.2 %copy-start.5 = (bf16[128,128]{1,0:T(8,128)(2,1)S(1)}, bf16[128,128]{1,0:T(8,128)(2,1)}, u32[]{:S(2)}) copy-start(bf16[128,128]{1,0:T(8,128)(2,1)} %w_recv.3) | copy-start | bytes 98308
  1.9 12.2 %copy-start.6 = (bf16[128,128]{1,0:T(8,128)(2,1)S(1)}, bf16[128,128]{1,0:T(8,128)(2,1)}, u32[]{:S(2)}) copy-start(bf16[128,128]{1,0:T(8,128)(2,1)} %w_self.3) | copy-start | bytes 98308
  1.9 9.5 %collective-permute-start.2 = (bf16[32,128]{1,0:T(8,128)(2,1)S(1)}, bf16[32,128]{1,0:T(8,128)(2,1)S(1)}, u32[]{:S(2)}, u32[]{:S(2)}) collective-permute-start(bf16[32,128]{1,0:T(8,128)(2,1)S(1)} %get-tuple-element.21.my_up), channel_id=1, source_target_pairs={{0,2},{1,3},{2,4},{3,5},{4,6},{5,7},{6,8},{7,9},{8,10},{9,11},{10,... | collective-permute-start | bytes 24584 | tf_op jit(solution)/shard_map/ppermute | solution.py:358
  5.0 6.5 %collective-permute-start.3 = (bf16[32,128]{1,0:T(8,128)(2,1)S(1)}, bf16[32,128]{1,0:T(8,128)(2,1)S(1)}, u32[]{:S(2)}, u32[]{:S(2)}) collective-permute-start(bf16[32,128]{1,0:T(8,128)(2,1)S(1)} %get-tuple-element.22.my_down), channel_id=1, source_target_pairs={{0,14},{1,15},{2,0},{3,1},{4,2},{5,3},{6,4},{7,5},{8,6},{9,7},{10,... | collective-permute-start | bytes 24584 | tf_op jit(solution)/shard_map/ppermute | solution.py:358
  8.1 6.0 %collective-permute-start = (bf16[112,128]{1,0:T(8,128)(2,1)S(1)}, bf16[112,128]{1,0:T(8,128)(2,1)S(1)}, u32[]{:S(2)}, u32[]{:S(2)}) collective-permute-start(bf16[112,128]{1,0:T(8,128)(2,1)S(1)} %get-tuple-element.23), channel_id=1, source_target_pairs={{0,15},{1,2},{2,1},{3,4},{4,3},{5,6},{6,5},{7,8},{8,7},{9,10},{10,... | collective-permute-start | bytes 86024 | tf_op jit(solution)/shard_map/ppermute | solution.py:362
  8.9 5.2 %collective-permute-start.1 = (bf16[112,128]{1,0:T(8,128)(2,1)S(1)}, bf16[112,128]{1,0:T(8,128)(2,1)S(1)}, u32[]{:S(2)}, u32[]{:S(2)}) collective-permute-start(bf16[112,128]{1,0:T(8,128)(2,1)S(1)} %get-tuple-element.24), channel_id=1, source_target_pairs={{0,1},{1,0},{2,3},{3,2},{4,5},{5,4},{6,7},{7,6},{8,9},{9,8},{10,11... | collective-permute-start | bytes 86024 | tf_op jit(solution)/shard_map/ppermute | solution.py:362
  34.1 12.2 %all-to-all-start.1 = ((bf16[32,24,128]{2,1,0:T(8,128)(2,1)}), bf16[32,24,128]{2,1,0:T(8,128)(2,1)S(1)}, u32[]{:S(2)}, u32[]{:S(2)}) async-start(bf16[32,24,128]{2,1,0:T(8,128)(2,1)} %shard_map.153), calls=%async_computation.1 | async-start | bytes 393216 | tf_op jit(solution)/shard_map/all_to_all | solution.py:457
  36.7 8.7 %collective-permute-start.4 = (bf16[64,128]{1,0:T(8,128)(2,1)S(1)}, bf16[64,128]{1,0:T(8,128)(2,1)S(1)}, u32[]{:S(2)}, u32[]{:S(2)}) collective-permute-start(bf16[64,128]{1,0:T(8,128)(2,1)S(1)} %get-tuple-element.34), channel_id=1, source_target_pairs={{0,15},{1,2},{2,1},{3,4},{4,3},{5,6},{6,5},{7,8},{8,7},{9,10},{10,... | collective-permute-start | bytes 49160 | tf_op jit(solution)/shard_map/ppermute | solution.py:362
  41.1 4.3 %collective-permute-start.5 = (bf16[64,128]{1,0:T(8,128)(2,1)S(1)}, bf16[64,128]{1,0:T(8,128)(2,1)S(1)}, u32[]{:S(2)}, u32[]{:S(2)}) collective-permute-start(bf16[64,128]{1,0:T(8,128)(2,1)S(1)} %get-tuple-element.35), channel_id=1, source_target_pairs={{0,1},{1,0},{2,3},{3,2},{4,5},{5,4},{6,7},{7,6},{8,9},{9,8},{10,11... | collective-permute-start | bytes 49160 | tf_op jit(solution)/shard_map/ppermute | solution.py:362

commit v16 on v12

--- a/solution.py
+++ b/solution.py
@@ -34,7 +34,7 @@
 
 
 def silu_parts(half):
-    tan = jnp.tanh(half)
+    tan = jnp.tanh(half.astype(BF16)).astype(F32)
     part = half * tan
     return half + part, (1.0 + tan) * ((1.0 + half) - part)
 
@@ -219,7 +219,7 @@
                 )
                 act, slope = silu_parts(half_centre[block] + pick)
                 at = slice(pair * rows + block.start, pair * rows + block.stop)
-                ds1_s[at, sides[side]] = slope
+                ds1_s[at, sides[side]] = slope.astype(BF16)
                 hid_s[at, sides[side]] = act.astype(BF16)
         base = first // 2 * rows
         halves = nn(hid_s[base : base + GROUP // 2 * rows], wide[0])
@@ -230,7 +230,7 @@
                 at = slice(pair * rows + block.start, pair * rows + block.stop)
                 act, slope = silu_parts(halves[at, sides[side]])
                 total = total + act
-                ds2_s[base + at.start : base + at.stop, sides[side]] = slope
+                ds2_s[base + at.start : base + at.stop, sides[side]] = slope.astype(BF16)
             agg_s[block] = total
 
     agg_b = agg_s[...].astype(BF16)
@@ -426,8 +426,8 @@
         [
             pltpu.VMEM((hot_rows, 2 * width), BF16),
             pltpu.VMEM((pair_rows, 2 * width), BF16),
-            pltpu.VMEM((pair_rows, 2 * width), F32),
-            pltpu.VMEM((pair_rows, 2 * width), F32),
+            pltpu.VMEM((pair_rows, 2 * width), BF16),
+            pltpu.VMEM((pair_rows, 2 * width), BF16),
             pltpu.VMEM((rows, width), F32),
             pltpu.VMEM((rows, width), F32),
             pltpu.VMEM((pair_rows, 2 * width), BF16),

time: 47.2 us -> 48.1 us (1.019)
  Pallas kernels: 13.1 us -> 14 us
    pallas_call x1, Pallas kernels: 7.75 us -> 8.62 us  [shards(): call(layer_kernel, [((1, rows, width), BF16), ((border, width), BF16), ((...]
where the time goes in v16:
time: 48.1 us; the launch traced here: 47.9 us
  starting transfers between devices  15.2 us (32%)
  Pallas kernels  14 us (29%)
  blocking collectives  11.4 us (24%)
  waiting for transfers between devices  5.63 us (12%)
  local copies, waits for them, and re-layouts  0.88 us (2%)
  between operations  0.81 us (2%)
    ppermute x6, starting transfers between devices, swap(): return lax.ppermute(array, 'slab', pairs)  12.6 us
    all_to_all x1, blocking collectives, shards(): lax.all_to_all(grads.reshape(devices, share, width), axes, split_axis=0,...  11.4 us
    pallas_call x1, Pallas kernels, shards(): call(layer_kernel, [((1, rows, width), BF16), ((border, width), BF16), ((...  8.62 us
    ppermute x6, waiting for transfers between devices, swap(): return lax.ppermute(array, 'slab', pairs)  5.63 us
    all_to_all x1, starting transfers between devices, shards(): lax.all_to_all(shared, axes, split_axis=0, concat_axis=0, tiled=True)  2.59 us
    pallas_call x1, Pallas kernels, shards(): call(prep_kernel, [((edges, hot_rows), BF16), ((half_rows, edges), BF16),...  2.49 us
  transfers between devices with their start and end apart: 7, of which 2 were waited for; matrix products, arithmetic and copies ran while one was open for 0% of the time, Pallas kernels for 7%

profile of v16, /device:TPU:0, one launch (start us, length us, event | category | flops | bytes accessed | tf_op | source)
XLA Modules:
  0.0 47.9 jit_solution(16475924750543845927)
XLA Ops:
  0.7 0.6 %copy-done.12 = s32[1,128]{1,0:T(1,128)S(1)} copy-done((s32[1,128]{1,0:T(1,128)S(1)}, s32[1,128]{1,0:T(1,128)}, u32[]{:S(2)}) %copy-start.12) | copy-done | bytes 536
  1.3 0.0 copy-done.7
  1.3 0.2 copy-done
  1.5 0.0 copy-start.9
  1.5 0.0 copy-start.10
  1.5 0.3 shard_map.149
  1.9 0.0 copy-start.3
  1.9 0.0 copy-start.4
  1.9 0.0 copy-start.5
  1.9 0.0 copy-start.6
  1.9 6.1 %collective-permute-start.2 = (bf16[32,128]{1,0:T(8,128)(2,1)S(1)}, bf16[32,128]{1,0:T(8,128)(2,1)S(1)}, u32[]{:S(2)}, u32[]{:S(2)}) collective-permute-start(bf16[32,128]{1,0:T(8,128)(2,1)S(1)} %get-tuple-element.19.my_far_off), channel_id=1, source_target_pairs={{0,14},{1,15},{2,4},{3,5},{4,2},{5,3},{6,8},{7,9},{8,6},{9,7},{10,... | collective-permute-start | bytes 24584 | tf_op jit(solution)/shard_map/ppermute | solution.py:365
  8.0 0.0 collective-permute-start.3
  8.0 0.8 %collective-permute-start = (bf16[112,128]{1,0:T(8,128)(2,1)S(1)}, bf16[112,128]{1,0:T(8,128)(2,1)S(1)}, u32[]{:S(2)}, u32[]{:S(2)}) collective-permute-start(bf16[112,128]{1,0:T(8,128)(2,1)S(1)} %get-tuple-element.21), channel_id=1, source_target_pairs={{0,15},{1,2},{2,1},{3,4},{4,3},{5,6},{6,5},{7,8},{8,7},{9,10},{10,... | collective-permute-start | bytes 86024 | tf_op jit(solution)/shard_map/ppermute | solution.py:365
  8.8 1.4 %collective-permute-start.1 = (bf16[112,128]{1,0:T(8,128)(2,1)S(1)}, bf16[112,128]{1,0:T(8,128)(2,1)S(1)}, u32[]{:S(2)}, u32[]{:S(2)}) collective-permute-start(bf16[112,128]{1,0:T(8,128)(2,1)S(1)} %get-tuple-element.22), channel_id=1, source_target_pairs={{0,1},{1,0},{2,3},{3,2},{4,5},{5,4},{6,7},{7,6},{8,9},{9,8},{10,11... | collective-permute-start | bytes 86024 | tf_op jit(solution)/shard_map/ppermute | solution.py:365
  10.2 0.0 copy-done.1
  10.2 0.0 copy-done.10
  10.2 2.5 %shard_map.150 = (bf16[8192,256]{1,0:T(8,128)(2,1)S(1)}, bf16[192,8192]{1,0:T(8,128)(2,1)S(1)}, bf16[2,256,256]{2,1,0:T(8,128)(2,1)S(1)}, s32[256,128]{1,0:T(8,128)S(1)}, f32[256,128]{1,0:T(8,128)S(1)}) custom-call(s32[1,32,256]{2,1,0:T(8,128)S(1)} %bitcast.6, s32[1,32,256]{2,1,0:T(8,128)S(1)} %bitcast.7, bf16[128,128]{1,0:T(8,128)(2,1)S(1)} %copy-done.10, ...), custom_call_target="tpu_custom_call" | custom-call | flops 2000000000 | bytes 1024 | tf_op jit(solution)/shard_map/pallas_call | solution.py:384
  12.7 0.0 collective-permute-done.2.got_far_off
  12.7 0.0 collective-permute-done.3.got_far_on
  12.7 1.3 %collective-permute-done.got_off = bf16[112,128]{1,0:T(8,128)(2,1)S(1)} collective-permute-done((bf16[112,128]{1,0:T(8,128)(2,1)S(1)}, bf16[112,128]{1,0:T(8,128)(2,1)S(1)}, u32[]{:S(2)}, u32[]{:S(2)}) %collective-permute-start) | collective-permute-done | bytes 28704 | tf_op jit(solution)/shard_map/ppermute | solution.py:365
  14.0 0.0 collective-permute-done.1.got_on
  14.0 8.6 %shard_map.151 = (bf16[1,256,128]{2,1,0:T(8,128)(2,1)}, bf16[64,128]{1,0:T(8,128)(2,1)S(1)}, bf16[64,128]{1,0:T(8,128)(2,1)S(1)}, bf16[768,128]{1,0:T(8,128)(2,1...) custom-call(bf16[1,256,128]{2,1,0:T(8,128)(2,1)S(1)} %copy-done, ...), custom_call_target="tpu_custom_call" | custom-call | flops 2000000000 | bytes 1024 | tf_op jit(solution)/shard_map/pallas_call | solution.py:415
  22.7 11.4 %all_to_all.10.parts = bf16[32,24,128]{2,1,0:T(8,128)(2,1)S(1)} all-to-all(bf16[32,24,128]{2,1,0:T(8,128)(2,1)S(1)} %bitcast.5), channel_id=1, replica_groups=mesh['grp'=2,'slab'=16] {'grp','slab'}, dimensions={0} | all-to-all | bytes 393216 | tf_op jit(solution)/shard_map/all_to_all | solution.py:439
  34.1 0.7 %shard_map.153 = bf16[32,24,128]{2,1,0:T(8,128)(2,1)} custom-call(bf16[32,24,128]{2,1,0:T(8,128)(2,1)S(1)} %all_to_all.10.parts), custom_call_target="tpu_custom_call" | custom-call | flops 2000000000 | bytes 1024 | tf_op jit(solution)/shard_map/pallas_call | solution.py:458
  34.8 2.6 %all-to-all-start.1 = ((bf16[32,24,128]{2,1,0:T(8,128)(2,1)}), bf16[32,24,128]{2,1,0:T(8,128)(2,1)S(1)}, u32[]{:S(2)}, u32[]{:S(2)}) async-start(bf16[32,24,128]{2,1,0:T(8,128)(2,1)} %shard_map.153), calls=%async_computation.1 | async-start | bytes 393216 | tf_op jit(solution)/shard_map/all_to_all | solution.py:459
  37.4 4.4 %collective-permute-start.4 = (bf16[64,128]{1,0:T(8,128)(2,1)S(1)}, bf16[64,128]{1,0:T(8,128)(2,1)S(1)}, u32[]{:S(2)}, u32[]{:S(2)}) collective-permute-start(bf16[64,128]{1,0:T(8,128)(2,1)S(1)} %get-tuple-element.32), channel_id=1, source_target_pairs={{0,15},{1,2},{2,1},{3,4},{4,3},{5,6},{6,5},{7,8},{8,7},{9,10},{10,... | collective-permute-start | bytes 49160 | tf_op jit(solution)/shard_map/ppermute | solution.py:365
  41.8 0.0 collective-permute-start.5
  41.8 4.3 %collective-permute-done.4.got_off = bf16[64,128]{1,0:T(8,128)(2,1)S(1)} collective-permute-done((bf16[64,128]{1,0:T(8,128)(2,1)S(1)}, bf16[64,128]{1,0:T(8,128)(2,1)S(1)}, u32[]{:S(2)}, u32[]{:S(2)}) %collective-permute-start.4) | collective-permute-done | bytes 16416 | tf_op jit(solution)/shard_map/ppermute | solution.py:365
  46.1 0.0 collective-permute-done.5.got_on
  46.1 0.9 %shard_map.152 = bf16[1,256,128]{2,1,0:T(8,128)(2,1)} custom-call(bf16[1,256,128]{2,1,0:T(8,128)(2,1)S(1)} %copy-done.1, bf16[256,128]{1,0:T(8,128)(2,1)S(1)} %get-tuple-element.29.d_node, bf16[256,128]{1,0:T(8,128)(2,1)S(1)} %get-tuple-element.30.d_centre, bf16[256,128]{1,0:T(8,128)(2,1)S(1)} %get-tuple-element.31.d_neigh, bf16[128,128]{1,0:T(8,128)(2,1)S(1)} %copy-done.6, ...), custom_call_target="tpu_custom_call" | custom-call | flops 2000000000 | bytes 1024 | tf_op jit(solution)/shard_map/pallas_call | solution.py:454
  46.9 0.0 all-to-all-done.1
  47.0 0.9 %shard_map.154 = f32[6,128,128]{2,1,0:T(8,128)} custom-call(bf16[768,128]{1,0:T(8,128)(2,1)S(1)} %bitcast.4), custom_call_target="tpu_custom_call" | custom-call | flops 2000000000 | bytes 1024 | tf_op jit(solution)/shard_map/pallas_call | solution.py:461
  (16 shorter events, 0.0 us)
Async XLA Ops:
  0.6 0.7 %copy-start.12 = (s32[1,128]{1,0:T(1,128)S(1)}, s32[1,128]{1,0:T(1,128)}, u32[]{:S(2)}) copy-start(s32[1,128]{1,0:T(1,128)} %sends.3) | copy-start | bytes 1540
  0.6 0.7 %copy-start.7 = (s32[1,256]{1,0:T(1,128)S(1)}, s32[1,256]{1,0:T(1,128)}, u32[]{:S(2)}) copy-start(s32[1,256]{1,0:T(1,128)} %arrive.3) | copy-start | bytes 3076
  0.7 0.9 %copy-start = (bf16[1,256,128]{2,1,0:T(8,128)(2,1)S(1)}, bf16[1,256,128]{2,1,0:T(8,128)(2,1)}, u32[]{:S(2)}) copy-start(bf16[1,256,128]{2,1,0:T(8,128)(2,1)} %nodes.3) | copy-start | bytes 196612
  0.7 0.8 %copy-start.11 = (s32[1,64]{1,0:T(1,128)S(1)}, s32[1,64]{1,0:T(1,128)}, u32[]{:S(2)}) copy-start(s32[1,64]{1,0:T(1,128)} %leave.1) | copy-start | bytes 772
  1.5 8.7 %copy-start.1 = (bf16[1,256,128]{2,1,0:T(8,128)(2,1)S(1)}, bf16[1,256,128]{2,1,0:T(8,128)(2,1)}, u32[]{:S(2)}) copy-start(bf16[1,256,128]{2,1,0:T(8,128)(2,1)} %cotangent.5) | copy-start | bytes 196612
  1.5 8.7 %copy-start.2 = (bf16[128,128]{1,0:T(8,128)(2,1)S(1)}, bf16[128,128]{1,0:T(8,128)(2,1)}, u32[]{:S(2)}) copy-start(bf16[128,128]{1,0:T(8,128)(2,1)} %w_out.3) | copy-start | bytes 98308
  1.5 8.7 %copy-start.8 = (s32[1,256,32]{1,2,0:T(8,128)S(1)}, s32[1,256,32]{1,2,0:T(8,128)}, u32[]{:S(2)}) copy-start(s32[1,256,32]{1,2,0:T(8,128)} %param.17) | copy-start | bytes 98308
  1.5 8.7 %copy-start.9 = (s32[1,256,32]{1,2,0:T(8,128)S(1)}, s32[1,256,32]{1,2,0:T(8,128)}, u32[]{:S(2)}) copy-start(s32[1,256,32]{1,2,0:T(8,128)} %param.18) | copy-start | bytes 98308
  1.5 8.6 %copy-start.10 = (bf16[128,128]{1,0:T(8,128)(2,1)S(1)}, bf16[128,128]{1,0:T(8,128)(2,1)}, u32[]{:S(2)}) copy-start(bf16[128,128]{1,0:T(8,128)(2,1)} %w_msg.1) | copy-start | bytes 98308
  1.9 12.1 %copy-start.3 = (bf16[128,128]{1,0:T(8,128)(2,1)S(1)}, bf16[128,128]{1,0:T(8,128)(2,1)}, u32[]{:S(2)}) copy-start(bf16[128,128]{1,0:T(8,128)(2,1)} %w_agg.1) | copy-start | bytes 98308
  1.9 12.1 %copy-start.4 = (bf16[128,128]{1,0:T(8,128)(2,1)S(1)}, bf16[128,128]{1,0:T(8,128)(2,1)}, u32[]{:S(2)}) copy-start(bf16[128,128]{1,0:T(8,128)(2,1)} %w_send.3) | copy-start | bytes 98308
  1.9 12.1 %copy-start.5 = (bf16[128,128]{1,0:T(8,128)(2,1)S(1)}, bf16[128,128]{1,0:T(8,128)(2,1)}, u32[]{:S(2)}) copy-start(bf16[128,128]{1,0:T(8,128)(2,1)} %w_recv.3) | copy-start | bytes 98308
  1.9 12.1 %copy-start.6 = (bf16[128,128]{1,0:T(8,128)(2,1)S(1)}, bf16[128,128]{1,0:T(8,128)(2,1)}, u32[]{:S(2)}) copy-start(bf16[128,128]{1,0:T(8,128)(2,1)} %w_self.3) | copy-start | bytes 98308
  1.9 10.7 %collective-permute-start.2 = (bf16[32,128]{1,0:T(8,128)(2,1)S(1)}, bf16[32,128]{1,0:T(8,128)(2,1)S(1)}, u32[]{:S(2)}, u32[]{:S(2)}) collective-permute-start(bf16[32,128]{1,0:T(8,128)(2,1)S(1)} %get-tuple-element.19.my_far_off), channel_id=1, source_target_pairs={{0,14},{1,15},{2,4},{3,5},{4,2},{5,3},{6,8},{7,9},{8,6},{9,7},{10,... | collective-permute-start | bytes 24584 | tf_op jit(solution)/shard_map/ppermute | solution.py:365
  8.0 4.7 %collective-permute-start.3 = (bf16[32,128]{1,0:T(8,128)(2,1)S(1)}, bf16[32,128]{1,0:T(8,128)(2,1)S(1)}, u32[]{:S(2)}, u32[]{:S(2)}) collective-permute-start(bf16[32,128]{1,0:T(8,128)(2,1)S(1)} %get-tuple-element.20.my_far_on), channel_id=1, source_target_pairs={{0,2},{1,3},{2,0},{3,1},{4,6},{5,7},{6,4},{7,5},{8,10},{9,11},{10,... | collective-permute-start | bytes 24584 | tf_op jit(solution)/shard_map/ppermute | solution.py:365
  8.0 6.0 %collective-permute-start = (bf16[112,128]{1,0:T(8,128)(2,1)S(1)}, bf16[112,128]{1,0:T(8,128)(2,1)S(1)}, u32[]{:S(2)}, u32[]{:S(2)}) collective-permute-start(bf16[112,128]{1,0:T(8,128)(2,1)S(1)} %get-tuple-element.21), channel_id=1, source_target_pairs={{0,15},{1,2},{2,1},{3,4},{4,3},{5,6},{6,5},{7,8},{8,7},{9,10},{10,... | collective-permute-start | bytes 86024 | tf_op jit(solution)/shard_map/ppermute | solution.py:365
  8.8 5.2 %collective-permute-start.1 = (bf16[112,128]{1,0:T(8,128)(2,1)S(1)}, bf16[112,128]{1,0:T(8,128)(2,1)S(1)}, u32[]{:S(2)}, u32[]{:S(2)}) collective-permute-start(bf16[112,128]{1,0:T(8,128)(2,1)S(1)} %get-tuple-element.22), channel_id=1, source_target_pairs={{0,1},{1,0},{2,3},{3,2},{4,5},{5,4},{6,7},{7,6},{8,9},{9,8},{10,11... | collective-permute-start | bytes 86024 | tf_op jit(solution)/shard_map/ppermute | solution.py:365
  34.8 12.2 %all-to-all-start.1 = ((bf16[32,24,128]{2,1,0:T(8,128)(2,1)}), bf16[32,24,128]{2,1,0:T(8,128)(2,1)S(1)}, u32[]{:S(2)}, u32[]{:S(2)}) async-start(bf16[32,24,128]{2,1,0:T(8,128)(2,1)} %shard_map.153), calls=%async_computation.1 | async-start | bytes 393216 | tf_op jit(solution)/shard_map/all_to_all | solution.py:459
  37.4 8.7 %collective-permute-start.4 = (bf16[64,128]{1,0:T(8,128)(2,1)S(1)}, bf16[64,128]{1,0:T(8,128)(2,1)S(1)}, u32[]{:S(2)}, u32[]{:S(2)}) collective-permute-start(bf16[64,128]{1,0:T(8,128)(2,1)S(1)} %get-tuple-element.32), channel_id=1, source_target_pairs={{0,15},{1,2},{2,1},{3,4},{4,3},{5,6},{6,5},{7,8},{8,7},{9,10},{10,... | collective-permute-start | bytes 49160 | tf_op jit(solution)/shard_map/ppermute | solution.py:365
  41.8 4.3 %collective-permute-start.5 = (bf16[64,128]{1,0:T(8,128)(2,1)S(1)}, bf16[64,128]{1,0:T(8,128)(2,1)S(1)}, u32[]{:S(2)}, u32[]{:S(2)}) collective-permute-start(bf16[64,128]{1,0:T(8,128)(2,1)S(1)} %get-tuple-element.33), channel_id=1, source_target_pairs={{0,1},{1,0},{2,3},{3,2},{4,5},{5,4},{6,7},{7,6},{8,9},{9,8},{10,11... | collective-permute-start | bytes 49160 | tf_op jit(solution)/shard_map/ppermute | solution.py:365

commit v17 on v12

--- a/solution.py
+++ b/solution.py
@@ -35,8 +35,9 @@
 
 def silu_parts(half):
     tan = jnp.tanh(half)
-    part = half * tan
-    return half + part, (1.0 + tan) * ((1.0 + half) - part)
+    twice = 1.0 + tan
+    act = half * twice
+    return act, twice + act * (1.0 - tan)
 
 
 def first_kernel(out):
@@ -84,7 +85,7 @@
     far_on[...] = jnp.where(odd_pair, down, up)
 
 
-def prep_kernel(nbr, valid, w_msg, w_out, cotangent, hot_o, hot_t_o, wide_o, ids_o, d_hid_o):
+def prep_kernel(nbr, valid, w_msg, w_out, cotangent, hot_o, hot_t_o, up_o, wide_o, ids_o, d_hid_o):
     slots, rows = nbr.shape[1:]
     width = w_msg.shape[0]
     half_rows, hot_rows = hot_t_o.shape[0], hot_o.shape[1]
@@ -113,10 +114,14 @@
     one_t = jnp.ones((half_rows, rows), BF16)
     zero_t = jnp.zeros((half_rows, rows), BF16)
 
+    border_id = jnp.full((rows, LANES), hot_rows, jnp.int16)
+
     @pl.loop(0, slots // chunk)
     def build(step):
         for j, short in enumerate(slot_ids(ids_o, step, chunk)):
             slot = step * chunk + j
+            at_up = short.astype(jnp.int16) >= border_id
+            up_o[pl.ds(slot * rows, rows)] = jnp.where(at_up, one[:, :LANES], zero[:, :LANES])
             short = (short & (hot_rows - 1)).astype(jnp.int16)
             short = jnp.concatenate([short] * (hot_rows // LANES), axis=1)
             hot_o[pl.ds(slot * rows, rows)] = jnp.where(short == lane, one, zero)
@@ -146,6 +151,7 @@
     got_far_on,
     hot,
     hot_t,
+    upper,
     wide,
     nbr_ids,
     d_hid,
@@ -242,8 +248,6 @@
     d_node = (d_hid[...] * (0.5 * slope)).astype(BF16)
     half_d_agg = 0.5 * nt(d_node, w_agg[...])
 
-    none = jnp.zeros((BLOCK, width), BF16)
-    border_id = jnp.full((BLOCK, width), hot_rows, jnp.int16)
     for first in range(0, slots, GROUP):
         base = first // 2 * rows
         span = slice(base, base + GROUP // 2 * rows)
@@ -261,10 +265,10 @@
                 part = d_hids[at, sides[side]] * ds1_s[base + at.start : base + at.stop, sides[side]]
                 total = total + part
                 part = part.astype(BF16)
-                is_up = ids[first + j][block].astype(jnp.int16) >= border_id
                 at = slice((first + j) * rows + block.start, (first + j) * rows + block.stop)
-                dpre_s[at, sides[0]] = jnp.where(is_up, none, part)
-                dpre_s[at, sides[1]] = jnp.where(is_up, part, none)
+                part_up = part * upper[at]
+                dpre_s[at, sides[0]] = part - part_up
+                dpre_s[at, sides[1]] = part_up
             dcen_s[block] = total
     gmsg = tn(hid_s[...], dpre2_s[...])
     d_neigh = nn(hot_t[...], dpre_s[...]).astype(BF16)
@@ -381,11 +385,12 @@
     hot_rows = -(-(half_rows + 1) // LANES) * LANES
     share = -(-matrices * width // (8 * devices)) * 8
     edges = rows * slots
-    hot, hot_t, wide, ids, d_hid = call(
+    hot, hot_t, upper, wide, ids, d_hid = call(
         prep_kernel,
         [
             ((edges, hot_rows), BF16),
             ((half_rows, edges), BF16),
+            ((edges, width), BF16),
             ((2, 2 * width, 2 * width), BF16),
             ((rows, LANES), jnp.int32),
             ((rows, width), F32),
@@ -402,6 +407,7 @@
         got_far_on,
         hot,
         hot_t,
+        upper,
         wide,
         ids,
         d_hid,

time: 47.2 us -> 47 us (level)
  no operation moved by 1% of the time
where the time goes in v17:
time: 47 us; the launch traced here: 46.7 us
  starting transfers between devices  15.2 us (32%)
  Pallas kernels  12.8 us (27%)
  blocking collectives  11.5 us (24%)
  waiting for transfers between devices  5.57 us (12%)
  local copies, waits for them, and re-layouts  0.88 us (2%)
  between operations  0.81 us (2%)
    ppermute x6, starting transfers between devices, swap(): return lax.ppermute(array, 'slab', pairs)  12.6 us
    all_to_all x1, blocking collectives, shards(): lax.all_to_all(grads.reshape(devices, share, width), axes, split_axis=0,...  11.5 us
    pallas_call x1, Pallas kernels, shards(): call(layer_kernel, [((1, rows, width), BF16), ((border, width), BF16), ((...  7.5 us
    ppermute x6, waiting for transfers between devices, swap(): return lax.ppermute(array, 'slab', pairs)  5.57 us
    all_to_all x1, starting transfers between devices, shards(): lax.all_to_all(shared, axes, split_axis=0, concat_axis=0, tiled=True)  2.59 us
    pallas_call x1, Pallas kernels, shards(): call(prep_kernel, [((edges, hot_rows), BF16), ((half_rows, edges), BF16),...  2.5 us
  transfers between devices with their start and end apart: 7, of which 2 were waited for; matrix products, arithmetic and copies ran while one was open for 0% of the time, Pallas kernels for 7%

profile of v17, /device:TPU:0, one launch (start us, length us, event | category | flops | bytes accessed | tf_op | source)
XLA Modules:
  0.0 46.7 jit_solution(15583267860436897723)
XLA Ops:
  0.6 0.0 copy-start.12
  0.6 0.0 copy-start.7
  0.7 0.6 %copy-done.12 = s32[1,128]{1,0:T(1,128)S(1)} copy-done((s32[1,128]{1,0:T(1,128)S(1)}, s32[1,128]{1,0:T(1,128)}, u32[]{:S(2)}) %copy-start.12) | copy-done | bytes 536
  1.3 0.0 copy-done.7
  1.3 0.2 copy-done
  1.5 0.0 copy-start.9
  1.5 0.0 copy-start.10
  1.5 0.3 shard_map.149
  1.9 6.1 %collective-permute-start.2 = (bf16[32,128]{1,0:T(8,128)(2,1)S(1)}, bf16[32,128]{1,0:T(8,128)(2,1)S(1)}, u32[]{:S(2)}, u32[]{:S(2)}) collective-permute-start(bf16[32,128]{1,0:T(8,128)(2,1)S(1)} %get-tuple-element.20.my_far_off), channel_id=1, source_target_pairs={{0,14},{1,15},{2,4},{3,5},{4,2},{5,3},{6,8},{7,9},{8,6},{9,7},{10,... | collective-permute-start | bytes 24584 | tf_op jit(solution)/shard_map/ppermute | solution.py:369
  8.0 0.0 collective-permute-start.3
  8.0 0.8 %collective-permute-start = (bf16[112,128]{1,0:T(8,128)(2,1)S(1)}, bf16[112,128]{1,0:T(8,128)(2,1)S(1)}, u32[]{:S(2)}, u32[]{:S(2)}) collective-permute-start(bf16[112,128]{1,0:T(8,128)(2,1)S(1)} %get-tuple-element.22), channel_id=1, source_target_pairs={{0,15},{1,2},{2,1},{3,4},{4,3},{5,6},{6,5},{7,8},{8,7},{9,10},{10,... | collective-permute-start | bytes 86024 | tf_op jit(solution)/shard_map/ppermute | solution.py:369
  8.8 1.4 %collective-permute-start.1 = (bf16[112,128]{1,0:T(8,128)(2,1)S(1)}, bf16[112,128]{1,0:T(8,128)(2,1)S(1)}, u32[]{:S(2)}, u32[]{:S(2)}) collective-permute-start(bf16[112,128]{1,0:T(8,128)(2,1)S(1)} %get-tuple-element.23), channel_id=1, source_target_pairs={{0,1},{1,0},{2,3},{3,2},{4,5},{5,4},{6,7},{7,6},{8,9},{9,8},{10,11... | collective-permute-start | bytes 86024 | tf_op jit(solution)/shard_map/ppermute | solution.py:369
  10.1 0.0 copy-start.3
  10.1 0.0 copy-start.4
  10.2 0.0 copy-start.5
  10.2 0.0 copy-start.6
  10.2 2.5 %shard_map.150 = (bf16[8192,256]{1,0:T(8,128)(2,1)S(1)}, bf16[192,8192]{1,0:T(8,128)(2,1)S(1)}, bf16[8192,128]{1,0:T(8,128)(2,1)S(1)}, bf16[2,256,256]{2,1,0:T(8...) custom-call(s32[1,32,256]{2,1,0:T(8,128)S(1)} %bitcast.6, s32[1,32,256]{2,1,0:T(8,128)S(1)} %bitcast.7, ...), custom_call_target="tpu_custom_call" | custom-call | flops 2000000000 | bytes 1024 | tf_op jit(solution)/shard_map/pallas_call | solution.py:388
  12.7 0.0 collective-permute-done.2.got_far_off
  12.7 0.0 collective-permute-done.3.got_far_on
  12.7 1.3 %collective-permute-done.got_off = bf16[112,128]{1,0:T(8,128)(2,1)S(1)} collective-permute-done((bf16[112,128]{1,0:T(8,128)(2,1)S(1)}, bf16[112,128]{1,0:T(8,128)(2,1)S(1)}, u32[]{:S(2)}, u32[]{:S(2)}) %collective-permute-start) | collective-permute-done | bytes 28704 | tf_op jit(solution)/shard_map/ppermute | solution.py:369
  14.0 0.0 collective-permute-done.1.got_on
  14.0 7.5 %shard_map.151 = (bf16[1,256,128]{2,1,0:T(8,128)(2,1)}, bf16[64,128]{1,0:T(8,128)(2,1)S(1)}, bf16[64,128]{1,0:T(8,128)(2,1)S(1)}, bf16[768,128]{1,0:T(8,128)(2,1...) custom-call(bf16[1,256,128]{2,1,0:T(8,128)(2,1)S(1)} %copy-done, ...), custom_call_target="tpu_custom_call" | custom-call | flops 2000000000 | bytes 1024 | tf_op jit(solution)/shard_map/pallas_call | solution.py:421
  21.5 11.5 %all_to_all.10.parts = bf16[32,24,128]{2,1,0:T(8,128)(2,1)S(1)} all-to-all(bf16[32,24,128]{2,1,0:T(8,128)(2,1)S(1)} %bitcast.5), channel_id=1, replica_groups=mesh['grp'=2,'slab'=16] {'grp','slab'}, dimensions={0} | all-to-all | bytes 393216 | tf_op jit(solution)/shard_map/all_to_all | solution.py:445
  33.0 0.7 %shard_map.153 = bf16[32,24,128]{2,1,0:T(8,128)(2,1)} custom-call(bf16[32,24,128]{2,1,0:T(8,128)(2,1)S(1)} %all_to_all.10.parts), custom_call_target="tpu_custom_call" | custom-call | flops 2000000000 | bytes 1024 | tf_op jit(solution)/shard_map/pallas_call | solution.py:464
  33.7 2.6 %all-to-all-start.1 = ((bf16[32,24,128]{2,1,0:T(8,128)(2,1)}), bf16[32,24,128]{2,1,0:T(8,128)(2,1)S(1)}, u32[]{:S(2)}, u32[]{:S(2)}) async-start(bf16[32,24,128]{2,1,0:T(8,128)(2,1)} %shard_map.153), calls=%async_computation.1 | async-start | bytes 393216 | tf_op jit(solution)/shard_map/all_to_all | solution.py:465
  36.3 4.4 %collective-permute-start.4 = (bf16[64,128]{1,0:T(8,128)(2,1)S(1)}, bf16[64,128]{1,0:T(8,128)(2,1)S(1)}, u32[]{:S(2)}, u32[]{:S(2)}) collective-permute-start(bf16[64,128]{1,0:T(8,128)(2,1)S(1)} %get-tuple-element.34), channel_id=1, source_target_pairs={{0,15},{1,2},{2,1},{3,4},{4,3},{5,6},{6,5},{7,8},{8,7},{9,10},{10,... | collective-permute-start | bytes 49160 | tf_op jit(solution)/shard_map/ppermute | solution.py:369
  40.7 0.0 collective-permute-start.5
  40.7 4.3 %collective-permute-done.4.got_off = bf16[64,128]{1,0:T(8,128)(2,1)S(1)} collective-permute-done((bf16[64,128]{1,0:T(8,128)(2,1)S(1)}, bf16[64,128]{1,0:T(8,128)(2,1)S(1)}, u32[]{:S(2)}, u32[]{:S(2)}) %collective-permute-start.4) | collective-permute-done | bytes 16416 | tf_op jit(solution)/shard_map/ppermute | solution.py:369
  45.0 0.0 collective-permute-done.5.got_on
  45.0 0.9 %shard_map.152 = bf16[1,256,128]{2,1,0:T(8,128)(2,1)} custom-call(bf16[1,256,128]{2,1,0:T(8,128)(2,1)S(1)} %copy-done.1, bf16[256,128]{1,0:T(8,128)(2,1)S(1)} %get-tuple-element.31.d_node, bf16[256,128]{1,0:T(8,128)(2,1)S(1)} %get-tuple-element.32.d_centre, bf16[256,128]{1,0:T(8,128)(2,1)S(1)} %get-tuple-element.33.d_neigh, bf16[128,128]{1,0:T(8,128)(2,1)S(1)} %copy-done.6, ...), custom_call_target="tpu_custom_call" | custom-call | flops 2000000000 | bytes 1024 | tf_op jit(solution)/shard_map/pallas_call | solution.py:460
  45.8 0.0 all-to-all-done.1
  45.8 0.9 %shard_map.154 = f32[6,128,128]{2,1,0:T(8,128)} custom-call(bf16[768,128]{1,0:T(8,128)(2,1)S(1)} %bitcast.4), custom_call_target="tpu_custom_call" | custom-call | flops 2000000000 | bytes 1024 | tf_op jit(solution)/shard_map/pallas_call | solution.py:467
  (16 shorter events, 0.0 us)
Async XLA Ops:
  0.6 0.7 %copy-start.12 = (s32[1,128]{1,0:T(1,128)S(1)}, s32[1,128]{1,0:T(1,128)}, u32[]{:S(2)}) copy-start(s32[1,128]{1,0:T(1,128)} %sends.3) | copy-start | bytes 1540
  0.6 0.7 %copy-start.7 = (s32[1,256]{1,0:T(1,128)S(1)}, s32[1,256]{1,0:T(1,128)}, u32[]{:S(2)}) copy-start(s32[1,256]{1,0:T(1,128)} %arrive.3) | copy-start | bytes 3076
  0.7 0.9 %copy-start = (bf16[1,256,128]{2,1,0:T(8,128)(2,1)S(1)}, bf16[1,256,128]{2,1,0:T(8,128)(2,1)}, u32[]{:S(2)}) copy-start(bf16[1,256,128]{2,1,0:T(8,128)(2,1)} %nodes.3) | copy-start | bytes 196612
  0.7 0.8 %copy-start.11 = (s32[1,64]{1,0:T(1,128)S(1)}, s32[1,64]{1,0:T(1,128)}, u32[]{:S(2)}) copy-start(s32[1,64]{1,0:T(1,128)} %leave.1) | copy-start | bytes 772
  1.5 8.6 %copy-start.1 = (bf16[1,256,128]{2,1,0:T(8,128)(2,1)S(1)}, bf16[1,256,128]{2,1,0:T(8,128)(2,1)}, u32[]{:S(2)}) copy-start(bf16[1,256,128]{2,1,0:T(8,128)(2,1)} %cotangent.5) | copy-start | bytes 196612
  1.5 8.6 %copy-start.2 = (bf16[128,128]{1,0:T(8,128)(2,1)S(1)}, bf16[128,128]{1,0:T(8,128)(2,1)}, u32[]{:S(2)}) copy-start(bf16[128,128]{1,0:T(8,128)(2,1)} %w_out.3) | copy-start | bytes 98308
  1.5 8.6 %copy-start.8 = (s32[1,256,32]{1,2,0:T(8,128)S(1)}, s32[1,256,32]{1,2,0:T(8,128)}, u32[]{:S(2)}) copy-start(s32[1,256,32]{1,2,0:T(8,128)} %param.17) | copy-start | bytes 98308
  1.5 8.6 %copy-start.9 = (s32[1,256,32]{1,2,0:T(8,128)S(1)}, s32[1,256,32]{1,2,0:T(8,128)}, u32[]{:S(2)}) copy-start(s32[1,256,32]{1,2,0:T(8,128)} %param.18) | copy-start | bytes 98308
  1.5 8.6 %copy-start.10 = (bf16[128,128]{1,0:T(8,128)(2,1)S(1)}, bf16[128,128]{1,0:T(8,128)(2,1)}, u32[]{:S(2)}) copy-start(bf16[128,128]{1,0:T(8,128)(2,1)} %w_msg.1) | copy-start | bytes 98308
  1.9 10.8 %collective-permute-start.2 = (bf16[32,128]{1,0:T(8,128)(2,1)S(1)}, bf16[32,128]{1,0:T(8,128)(2,1)S(1)}, u32[]{:S(2)}, u32[]{:S(2)}) collective-permute-start(bf16[32,128]{1,0:T(8,128)(2,1)S(1)} %get-tuple-element.20.my_far_off), channel_id=1, source_target_pairs={{0,14},{1,15},{2,4},{3,5},{4,2},{5,3},{6,8},{7,9},{8,6},{9,7},{10,... | collective-permute-start | bytes 24584 | tf_op jit(solution)/shard_map/ppermute | solution.py:369
  8.0 4.7 %collective-permute-start.3 = (bf16[32,128]{1,0:T(8,128)(2,1)S(1)}, bf16[32,128]{1,0:T(8,128)(2,1)S(1)}, u32[]{:S(2)}, u32[]{:S(2)}) collective-permute-start(bf16[32,128]{1,0:T(8,128)(2,1)S(1)} %get-tuple-element.21.my_far_on), channel_id=1, source_target_pairs={{0,2},{1,3},{2,0},{3,1},{4,6},{5,7},{6,4},{7,5},{8,10},{9,11},{10,... | collective-permute-start | bytes 24584 | tf_op jit(solution)/shard_map/ppermute | solution.py:369
  8.0 6.0 %collective-permute-start = (bf16[112,128]{1,0:T(8,128)(2,1)S(1)}, bf16[112,128]{1,0:T(8,128)(2,1)S(1)}, u32[]{:S(2)}, u32[]{:S(2)}) collective-permute-start(bf16[112,128]{1,0:T(8,128)(2,1)S(1)} %get-tuple-element.22), channel_id=1, source_target_pairs={{0,15},{1,2},{2,1},{3,4},{4,3},{5,6},{6,5},{7,8},{8,7},{9,10},{10,... | collective-permute-start | bytes 86024 | tf_op jit(solution)/shard_map/ppermute | solution.py:369
  8.8 5.2 %collective-permute-start.1 = (bf16[112,128]{1,0:T(8,128)(2,1)S(1)}, bf16[112,128]{1,0:T(8,128)(2,1)S(1)}, u32[]{:S(2)}, u32[]{:S(2)}) collective-permute-start(bf16[112,128]{1,0:T(8,128)(2,1)S(1)} %get-tuple-element.23), channel_id=1, source_target_pairs={{0,1},{1,0},{2,3},{3,2},{4,5},{5,4},{6,7},{7,6},{8,9},{9,8},{10,11... | collective-permute-start | bytes 86024 | tf_op jit(solution)/shard_map/ppermute | solution.py:369
  10.1 3.8 %copy-start.3 = (bf16[128,128]{1,0:T(8,128)(2,1)S(1)}, bf16[128,128]{1,0:T(8,128)(2,1)}, u32[]{:S(2)}) copy-start(bf16[128,128]{1,0:T(8,128)(2,1)} %w_agg.1) | copy-start | bytes 98308
  10.1 3.8 %copy-start.4 = (bf16[128,128]{1,0:T(8,128)(2,1)S(1)}, bf16[128,128]{1,0:T(8,128)(2,1)}, u32[]{:S(2)}) copy-start(bf16[128,128]{1,0:T(8,128)(2,1)} %w_send.3) | copy-start | bytes 98308
  10.2 3.8 %copy-start.5 = (bf16[128,128]{1,0:T(8,128)(2,1)S(1)}, bf16[128,128]{1,0:T(8,128)(2,1)}, u32[]{:S(2)}) copy-start(bf16[128,128]{1,0:T(8,128)(2,1)} %w_recv.3) | copy-start | bytes 98308
  10.2 3.8 %copy-start.6 = (bf16[128,128]{1,0:T(8,128)(2,1)S(1)}, bf16[128,128]{1,0:T(8,128)(2,1)}, u32[]{:S(2)}) copy-start(bf16[128,128]{1,0:T(8,128)(2,1)} %w_self.3) | copy-start | bytes 98308
  33.7 12.2 %all-to-all-start.1 = ((bf16[32,24,128]{2,1,0:T(8,128)(2,1)}), bf16[32,24,128]{2,1,0:T(8,128)(2,1)S(1)}, u32[]{:S(2)}, u32[]{:S(2)}) async-start(bf16[32,24,128]{2,1,0:T(8,128)(2,1)} %shard_map.153), calls=%async_computation.1 | async-start | bytes 393216 | tf_op jit(solution)/shard_map/all_to_all | solution.py:465
  36.3 8.7 %collective-permute-start.4 = (bf16[64,128]{1,0:T(8,128)(2,1)S(1)}, bf16[64,128]{1,0:T(8,128)(2,1)S(1)}, u32[]{:S(2)}, u32[]{:S(2)}) collective-permute-start(bf16[64,128]{1,0:T(8,128)(2,1)S(1)} %get-tuple-element.34), channel_id=1, source_target_pairs={{0,15},{1,2},{2,1},{3,4},{4,3},{5,6},{6,5},{7,8},{8,7},{9,10},{10,... | collective-permute-start | bytes 49160 | tf_op jit(solution)/shard_map/ppermute | solution.py:369
  40.7 4.3 %collective-permute-start.5 = (bf16[64,128]{1,0:T(8,128)(2,1)S(1)}, bf16[64,128]{1,0:T(8,128)(2,1)S(1)}, u32[]{:S(2)}, u32[]{:S(2)}) collective-permute-start(bf16[64,128]{1,0:T(8,128)(2,1)S(1)} %get-tuple-element.35), channel_id=1, source_target_pairs={{0,1},{1,0},{2,3},{3,2},{4,5},{5,4},{6,7},{7,6},{8,9},{9,8},{10,11... | collective-permute-start | bytes 49160 | tf_op jit(solution)/shard_map/ppermute | solution.py:369

commit v18 on v17

--- a/solution.py
+++ b/solution.py
@@ -12,7 +12,7 @@
 CODE_ROWS = 16
 LANES = 128
 FAR = -1e30
-GROUP = 32
+GROUP = 16
 BLOCK = 64
 
 
@@ -214,8 +214,10 @@
     blocks = [slice(start, start + BLOCK) for start in range(0, rows, BLOCK)]
     sides = (slice(0, width), slice(width, 2 * width))
 
-    for first in range(0, slots, GROUP):
-        gathered = nn(hot[first * rows : (first + GROUP) * rows], neigh_s[...])
+    firsts = range(0, slots, GROUP)
+    group_rows = GROUP // 2 * rows
+
+    def first_half(first, gathered):
         for j in range(GROUP):
             pair, side = divmod(first + j, 2)
             for block in blocks:
@@ -227,8 +229,9 @@
                 at = slice(pair * rows + block.start, pair * rows + block.stop)
                 ds1_s[at, sides[side]] = slope
                 hid_s[at, sides[side]] = act.astype(BF16)
+
+    def second_half(first, halves):
         base = first // 2 * rows
-        halves = nn(hid_s[base : base + GROUP // 2 * rows], wide[0])
         for block in blocks:
             total = jnp.zeros((BLOCK, width), F32) if first == 0 else agg_s[block]
             for j in range(GROUP):
@@ -239,6 +242,18 @@
                 ds2_s[base + at.start : base + at.stop, sides[side]] = slope
             agg_s[block] = total
 
+    def staggered(matmul, arithmetic):
+        ready = matmul(firsts[0])
+        for first, after in zip(firsts, [*firsts[1:], None]):
+            held, ready = ready, None if after is None else matmul(after)
+            arithmetic(first, held)
+
+    staggered(lambda first: nn(hot[first * rows : (first + GROUP) * rows], neigh_s[...]), first_half)
+    staggered(
+        lambda first: nn(hid_s[first // 2 * rows : first // 2 * rows + group_rows], wide[0]),
+        second_half,
+    )
+
     agg_b = agg_s[...].astype(BF16)
     node_pre = nn(moved, w_self[...]) + nn(agg_b, w_agg[...])
     act, slope = silu_parts(0.5 * node_pre)
@@ -248,15 +263,17 @@
     d_node = (d_hid[...] * (0.5 * slope)).astype(BF16)
     half_d_agg = 0.5 * nt(d_node, w_agg[...])
 
-    for first in range(0, slots, GROUP):
+    def message_slope(first):
         base = first // 2 * rows
-        span = slice(base, base + GROUP // 2 * rows)
         for pair in range(GROUP // 2):
             for block in blocks:
                 at = slice(base + pair * rows + block.start, base + pair * rows + block.stop)
                 for side in sides:
                     dpre2_s[at, side] = (half_d_agg[block] * ds2_s[at, side]).astype(BF16)
-        d_hids = nn(dpre2_s[span], wide[1])
+        return nn(dpre2_s[base : base + group_rows], wide[1])
+
+    def edge_slope(first, d_hids):
+        base = first // 2 * rows
         for block in blocks:
             total = jnp.zeros((BLOCK, width), F32) if first == 0 else dcen_s[block]
             for j in range(GROUP):
@@ -270,6 +287,8 @@
                 dpre_s[at, sides[0]] = part - part_up
                 dpre_s[at, sides[1]] = part_up
             dcen_s[block] = total
+
+    staggered(message_slope, edge_slope)
     gmsg = tn(hid_s[...], dpre2_s[...])
     d_neigh = nn(hot_t[...], dpre_s[...]).astype(BF16)
 

time: 47 us -> 46.6 us (level)
  no operation moved by 1% of the time
where the time goes in v18:
time: 46.6 us; the launch traced here: 46.3 us
  starting transfers between devices  15.2 us (33%)
  Pallas kernels  12.4 us (27%)
  blocking collectives  11.5 us (25%)
  waiting for transfers between devices  5.57 us (12%)
  local copies, waits for them, and re-layouts  0.88 us (2%)
  between operations  0.81 us (2%)
    ppermute x6, starting transfers between devices, swap(): return lax.ppermute(array, 'slab', pairs)  12.6 us
    all_to_all x1, blocking collectives, shards(): lax.all_to_all(grads.reshape(devices, share, width), axes, split_axis=0,...  11.5 us
    pallas_call x1, Pallas kernels, shards(): call(layer_kernel, [((1, rows, width), BF16), ((border, width), BF16), ((...  7.1 us
    ppermute x6, waiting for transfers between devices, swap(): return lax.ppermute(array, 'slab', pairs)  5.57 us
    all_to_all x1, starting transfers between devices, shards(): lax.all_to_all(shared, axes, split_axis=0, concat_axis=0, tiled=True)  2.59 us
    pallas_call x1, Pallas kernels, shards(): call(prep_kernel, [((edges, hot_rows), BF16), ((half_rows, edges), BF16),...  2.5 us
  transfers between devices with their start and end apart: 7, of which 2 were waited for; matrix products, arithmetic and copies ran while one was open for 0% of the time, Pallas kernels for 7%

profile of v18, /device:TPU:0, one launch (start us, length us, event | category | flops | bytes accessed | tf_op | source)
XLA Modules:
  0.0 46.3 jit_solution(2741917779867737421)
XLA Ops:
  0.7 0.6 %copy-done.12 = s32[1,128]{1,0:T(1,128)S(1)} copy-done((s32[1,128]{1,0:T(1,128)S(1)}, s32[1,128]{1,0:T(1,128)}, u32[]{:S(2)}) %copy-start.12) | copy-done | bytes 536
  1.3 0.0 copy-done.7
  1.3 0.2 copy-done
  1.5 0.0 copy-start.9
  1.5 0.0 copy-start.10
  1.5 0.3 shard_map.149
  1.9 6.1 %collective-permute-start.2 = (bf16[32,128]{1,0:T(8,128)(2,1)S(1)}, bf16[32,128]{1,0:T(8,128)(2,1)S(1)}, u32[]{:S(2)}, u32[]{:S(2)}) collective-permute-start(bf16[32,128]{1,0:T(8,128)(2,1)S(1)} %get-tuple-element.20.my_far_off), channel_id=1, source_target_pairs={{0,14},{1,15},{2,4},{3,5},{4,2},{5,3},{6,8},{7,9},{8,6},{9,7},{10,... | collective-permute-start | bytes 24584 | tf_op jit(solution)/shard_map/ppermute | solution.py:388
  8.0 0.0 collective-permute-start.3
  8.0 0.8 %collective-permute-start = (bf16[112,128]{1,0:T(8,128)(2,1)S(1)}, bf16[112,128]{1,0:T(8,128)(2,1)S(1)}, u32[]{:S(2)}, u32[]{:S(2)}) collective-permute-start(bf16[112,128]{1,0:T(8,128)(2,1)S(1)} %get-tuple-element.22), channel_id=1, source_target_pairs={{0,15},{1,2},{2,1},{3,4},{4,3},{5,6},{6,5},{7,8},{8,7},{9,10},{10,... | collective-permute-start | bytes 86024 | tf_op jit(solution)/shard_map/ppermute | solution.py:388
  8.8 1.4 %collective-permute-start.1 = (bf16[112,128]{1,0:T(8,128)(2,1)S(1)}, bf16[112,128]{1,0:T(8,128)(2,1)S(1)}, u32[]{:S(2)}, u32[]{:S(2)}) collective-permute-start(bf16[112,128]{1,0:T(8,128)(2,1)S(1)} %get-tuple-element.23), channel_id=1, source_target_pairs={{0,1},{1,0},{2,3},{3,2},{4,5},{5,4},{6,7},{7,6},{8,9},{9,8},{10,11... | collective-permute-start | bytes 86024 | tf_op jit(solution)/shard_map/ppermute | solution.py:388
  10.1 0.0 copy-done.1
  10.1 0.0 copy-done.10
  10.1 0.0 copy-start.3
  10.1 0.0 copy-start.4
  10.2 0.0 copy-start.5
  10.2 0.0 copy-start.6
  10.2 2.5 %shard_map.150 = (bf16[8192,256]{1,0:T(8,128)(2,1)S(1)}, bf16[192,8192]{1,0:T(8,128)(2,1)S(1)}, bf16[8192,128]{1,0:T(8,128)(2,1)S(1)}, bf16[2,256,256]{2,1,0:T(8...) custom-call(s32[1,32,256]{2,1,0:T(8,128)S(1)} %bitcast.6, s32[1,32,256]{2,1,0:T(8,128)S(1)} %bitcast.7, ...), custom_call_target="tpu_custom_call" | custom-call | flops 2000000000 | bytes 1024 | tf_op jit(solution)/shard_map/pallas_call | solution.py:407
  12.7 0.0 collective-permute-done.2.got_far_off
  12.7 0.0 collective-permute-done.3.got_far_on
  12.7 1.3 %collective-permute-done.got_off = bf16[112,128]{1,0:T(8,128)(2,1)S(1)} collective-permute-done((bf16[112,128]{1,0:T(8,128)(2,1)S(1)}, bf16[112,128]{1,0:T(8,128)(2,1)S(1)}, u32[]{:S(2)}, u32[]{:S(2)}) %collective-permute-start) | collective-permute-done | bytes 28704 | tf_op jit(solution)/shard_map/ppermute | solution.py:388
  14.0 0.0 collective-permute-done.1.got_on
  14.0 7.1 %shard_map.151 = (bf16[1,256,128]{2,1,0:T(8,128)(2,1)}, bf16[64,128]{1,0:T(8,128)(2,1)S(1)}, bf16[64,128]{1,0:T(8,128)(2,1)S(1)}, bf16[768,128]{1,0:T(8,128)(2,1...) custom-call(bf16[1,256,128]{2,1,0:T(8,128)(2,1)S(1)} %copy-done, ...), custom_call_target="tpu_custom_call" | custom-call | flops 2000000000 | bytes 1024 | tf_op jit(solution)/shard_map/pallas_call | solution.py:440
  21.1 11.5 %all_to_all.10.parts = bf16[32,24,128]{2,1,0:T(8,128)(2,1)S(1)} all-to-all(bf16[32,24,128]{2,1,0:T(8,128)(2,1)S(1)} %bitcast.5), channel_id=1, replica_groups=mesh['grp'=2,'slab'=16] {'grp','slab'}, dimensions={0} | all-to-all | bytes 393216 | tf_op jit(solution)/shard_map/all_to_all | solution.py:464
  32.6 0.7 %shard_map.153 = bf16[32,24,128]{2,1,0:T(8,128)(2,1)} custom-call(bf16[32,24,128]{2,1,0:T(8,128)(2,1)S(1)} %all_to_all.10.parts), custom_call_target="tpu_custom_call" | custom-call | flops 2000000000 | bytes 1024 | tf_op jit(solution)/shard_map/pallas_call | solution.py:483
  33.3 2.6 %all-to-all-start.1 = ((bf16[32,24,128]{2,1,0:T(8,128)(2,1)}), bf16[32,24,128]{2,1,0:T(8,128)(2,1)S(1)}, u32[]{:S(2)}, u32[]{:S(2)}) async-start(bf16[32,24,128]{2,1,0:T(8,128)(2,1)} %shard_map.153), calls=%async_computation.1 | async-start | bytes 393216 | tf_op jit(solution)/shard_map/all_to_all | solution.py:484
  35.9 4.4 %collective-permute-start.4 = (bf16[64,128]{1,0:T(8,128)(2,1)S(1)}, bf16[64,128]{1,0:T(8,128)(2,1)S(1)}, u32[]{:S(2)}, u32[]{:S(2)}) collective-permute-start(bf16[64,128]{1,0:T(8,128)(2,1)S(1)} %get-tuple-element.34), channel_id=1, source_target_pairs={{0,15},{1,2},{2,1},{3,4},{4,3},{5,6},{6,5},{7,8},{8,7},{9,10},{10,... | collective-permute-start | bytes 49160 | tf_op jit(solution)/shard_map/ppermute | solution.py:388
  40.3 0.0 collective-permute-start.5
  40.3 4.3 %collective-permute-done.4.got_off = bf16[64,128]{1,0:T(8,128)(2,1)S(1)} collective-permute-done((bf16[64,128]{1,0:T(8,128)(2,1)S(1)}, bf16[64,128]{1,0:T(8,128)(2,1)S(1)}, u32[]{:S(2)}, u32[]{:S(2)}) %collective-permute-start.4) | collective-permute-done | bytes 16416 | tf_op jit(solution)/shard_map/ppermute | solution.py:388
  44.6 0.0 collective-permute-done.5.got_on
  44.6 0.9 %shard_map.152 = bf16[1,256,128]{2,1,0:T(8,128)(2,1)} custom-call(bf16[1,256,128]{2,1,0:T(8,128)(2,1)S(1)} %copy-done.1, bf16[256,128]{1,0:T(8,128)(2,1)S(1)} %get-tuple-element.31.d_node, bf16[256,128]{1,0:T(8,128)(2,1)S(1)} %get-tuple-element.32.d_centre, bf16[256,128]{1,0:T(8,128)(2,1)S(1)} %get-tuple-element.33.d_neigh, bf16[128,128]{1,0:T(8,128)(2,1)S(1)} %copy-done.6, ...), custom_call_target="tpu_custom_call" | custom-call | flops 2000000000 | bytes 1024 | tf_op jit(solution)/shard_map/pallas_call | solution.py:479
  45.4 0.0 all-to-all-done.1
  45.4 0.9 %shard_map.154 = f32[6,128,128]{2,1,0:T(8,128)} custom-call(bf16[768,128]{1,0:T(8,128)(2,1)S(1)} %bitcast.4), custom_call_target="tpu_custom_call" | custom-call | flops 2000000000 | bytes 1024 | tf_op jit(solution)/shard_map/pallas_call | solution.py:486
  (16 shorter events, 0.0 us)
Async XLA Ops:
  0.6 0.7 %copy-start.12 = (s32[1,128]{1,0:T(1,128)S(1)}, s32[1,128]{1,0:T(1,128)}, u32[]{:S(2)}) copy-start(s32[1,128]{1,0:T(1,128)} %sends.3) | copy-start | bytes 1540
  0.6 0.7 %copy-start.7 = (s32[1,256]{1,0:T(1,128)S(1)}, s32[1,256]{1,0:T(1,128)}, u32[]{:S(2)}) copy-start(s32[1,256]{1,0:T(1,128)} %arrive.3) | copy-start | bytes 3076
  0.7 0.9 %copy-start = (bf16[1,256,128]{2,1,0:T(8,128)(2,1)S(1)}, bf16[1,256,128]{2,1,0:T(8,128)(2,1)}, u32[]{:S(2)}) copy-start(bf16[1,256,128]{2,1,0:T(8,128)(2,1)} %nodes.3) | copy-start | bytes 196612
  0.7 0.8 %copy-start.11 = (s32[1,64]{1,0:T(1,128)S(1)}, s32[1,64]{1,0:T(1,128)}, u32[]{:S(2)}) copy-start(s32[1,64]{1,0:T(1,128)} %leave.1) | copy-start | bytes 772
  1.5 8.6 %copy-start.1 = (bf16[1,256,128]{2,1,0:T(8,128)(2,1)S(1)}, bf16[1,256,128]{2,1,0:T(8,128)(2,1)}, u32[]{:S(2)}) copy-start(bf16[1,256,128]{2,1,0:T(8,128)(2,1)} %cotangent.5) | copy-start | bytes 196612
  1.5 8.6 %copy-start.2 = (bf16[128,128]{1,0:T(8,128)(2,1)S(1)}, bf16[128,128]{1,0:T(8,128)(2,1)}, u32[]{:S(2)}) copy-start(bf16[128,128]{1,0:T(8,128)(2,1)} %w_out.3) | copy-start | bytes 98308
  1.5 8.6 %copy-start.8 = (s32[1,256,32]{1,2,0:T(8,128)S(1)}, s32[1,256,32]{1,2,0:T(8,128)}, u32[]{:S(2)}) copy-start(s32[1,256,32]{1,2,0:T(8,128)} %param.17) | copy-start | bytes 98308
  1.5 8.6 %copy-start.9 = (s32[1,256,32]{1,2,0:T(8,128)S(1)}, s32[1,256,32]{1,2,0:T(8,128)}, u32[]{:S(2)}) copy-start(s32[1,256,32]{1,2,0:T(8,128)} %param.18) | copy-start | bytes 98308
  1.5 8.6 %copy-start.10 = (bf16[128,128]{1,0:T(8,128)(2,1)S(1)}, bf16[128,128]{1,0:T(8,128)(2,1)}, u32[]{:S(2)}) copy-start(bf16[128,128]{1,0:T(8,128)(2,1)} %w_msg.1) | copy-start | bytes 98308
  1.9 10.8 %collective-permute-start.2 = (bf16[32,128]{1,0:T(8,128)(2,1)S(1)}, bf16[32,128]{1,0:T(8,128)(2,1)S(1)}, u32[]{:S(2)}, u32[]{:S(2)}) collective-permute-start(bf16[32,128]{1,0:T(8,128)(2,1)S(1)} %get-tuple-element.20.my_far_off), channel_id=1, source_target_pairs={{0,14},{1,15},{2,4},{3,5},{4,2},{5,3},{6,8},{7,9},{8,6},{9,7},{10,... | collective-permute-start | bytes 24584 | tf_op jit(solution)/shard_map/ppermute | solution.py:388
  8.0 4.7 %collective-permute-start.3 = (bf16[32,128]{1,0:T(8,128)(2,1)S(1)}, bf16[32,128]{1,0:T(8,128)(2,1)S(1)}, u32[]{:S(2)}, u32[]{:S(2)}) collective-permute-start(bf16[32,128]{1,0:T(8,128)(2,1)S(1)} %get-tuple-element.21.my_far_on), channel_id=1, source_target_pairs={{0,2},{1,3},{2,0},{3,1},{4,6},{5,7},{6,4},{7,5},{8,10},{9,11},{10,... | collective-permute-start | bytes 24584 | tf_op jit(solution)/shard_map/ppermute | solution.py:388
  8.0 6.0 %collective-permute-start = (bf16[112,128]{1,0:T(8,128)(2,1)S(1)}, bf16[112,128]{1,0:T(8,128)(2,1)S(1)}, u32[]{:S(2)}, u32[]{:S(2)}) collective-permute-start(bf16[112,128]{1,0:T(8,128)(2,1)S(1)} %get-tuple-element.22), channel_id=1, source_target_pairs={{0,15},{1,2},{2,1},{3,4},{4,3},{5,6},{6,5},{7,8},{8,7},{9,10},{10,... | collective-permute-start | bytes 86024 | tf_op jit(solution)/shard_map/ppermute | solution.py:388
  8.8 5.2 %collective-permute-start.1 = (bf16[112,128]{1,0:T(8,128)(2,1)S(1)}, bf16[112,128]{1,0:T(8,128)(2,1)S(1)}, u32[]{:S(2)}, u32[]{:S(2)}) collective-permute-start(bf16[112,128]{1,0:T(8,128)(2,1)S(1)} %get-tuple-element.23), channel_id=1, source_target_pairs={{0,1},{1,0},{2,3},{3,2},{4,5},{5,4},{6,7},{7,6},{8,9},{9,8},{10,11... | collective-permute-start | bytes 86024 | tf_op jit(solution)/shard_map/ppermute | solution.py:388
  10.1 3.8 %copy-start.3 = (bf16[128,128]{1,0:T(8,128)(2,1)S(1)}, bf16[128,128]{1,0:T(8,128)(2,1)}, u32[]{:S(2)}) copy-start(bf16[128,128]{1,0:T(8,128)(2,1)} %w_agg.1) | copy-start | bytes 98308
  10.1 3.8 %copy-start.4 = (bf16[128,128]{1,0:T(8,128)(2,1)S(1)}, bf16[128,128]{1,0:T(8,128)(2,1)}, u32[]{:S(2)}) copy-start(bf16[128,128]{1,0:T(8,128)(2,1)} %w_send.3) | copy-start | bytes 98308
  10.2 3.8 %copy-start.5 = (bf16[128,128]{1,0:T(8,128)(2,1)S(1)}, bf16[128,128]{1,0:T(8,128)(2,1)}, u32[]{:S(2)}) copy-start(bf16[128,128]{1,0:T(8,128)(2,1)} %w_recv.3) | copy-start | bytes 98308
  10.2 3.8 %copy-start.6 = (bf16[128,128]{1,0:T(8,128)(2,1)S(1)}, bf16[128,128]{1,0:T(8,128)(2,1)}, u32[]{:S(2)}) copy-start(bf16[128,128]{1,0:T(8,128)(2,1)} %w_self.3) | copy-start | bytes 98308
  33.3 12.2 %all-to-all-start.1 = ((bf16[32,24,128]{2,1,0:T(8,128)(2,1)}), bf16[32,24,128]{2,1,0:T(8,128)(2,1)S(1)}, u32[]{:S(2)}, u32[]{:S(2)}) async-start(bf16[32,24,128]{2,1,0:T(8,128)(2,1)} %shard_map.153), calls=%async_computation.1 | async-start | bytes 393216 | tf_op jit(solution)/shard_map/all_to_all | solution.py:484
  35.9 8.7 %collective-permute-start.4 = (bf16[64,128]{1,0:T(8,128)(2,1)S(1)}, bf16[64,128]{1,0:T(8,128)(2,1)S(1)}, u32[]{:S(2)}, u32[]{:S(2)}) collective-permute-start(bf16[64,128]{1,0:T(8,128)(2,1)S(1)} %get-tuple-element.34), channel_id=1, source_target_pairs={{0,15},{1,2},{2,1},{3,4},{4,3},{5,6},{6,5},{7,8},{8,7},{9,10},{10,... | collective-permute-start | bytes 49160 | tf_op jit(solution)/shard_map/ppermute | solution.py:388
  40.3 4.3 %collective-permute-start.5 = (bf16[64,128]{1,0:T(8,128)(2,1)S(1)}, bf16[64,128]{1,0:T(8,128)(2,1)S(1)}, u32[]{:S(2)}, u32[]{:S(2)}) collective-permute-start(bf16[64,128]{1,0:T(8,128)(2,1)S(1)} %get-tuple-element.35), channel_id=1, source_target_pairs={{0,1},{1,0},{2,3},{3,2},{4,5},{5,4},{6,7},{7,6},{8,9},{9,8},{10,11... | collective-permute-start | bytes 49160 | tf_op jit(solution)/shard_map/ppermute | solution.py:388

commit v19 on v18

--- a/solution.py
+++ b/solution.py
@@ -12,7 +12,7 @@
 CODE_ROWS = 16
 LANES = 128
 FAR = -1e30
-GROUP = 16
+GROUP = 8
 BLOCK = 64
 
 
@@ -242,17 +242,18 @@
                 ds2_s[base + at.start : base + at.stop, sides[side]] = slope
             agg_s[block] = total
 
-    def staggered(matmul, arithmetic):
-        ready = matmul(firsts[0])
-        for first, after in zip(firsts, [*firsts[1:], None]):
-            held, ready = ready, None if after is None else matmul(after)
-            arithmetic(first, held)
-
-    staggered(lambda first: nn(hot[first * rows : (first + GROUP) * rows], neigh_s[...]), first_half)
-    staggered(
-        lambda first: nn(hid_s[first // 2 * rows : first // 2 * rows + group_rows], wide[0]),
-        second_half,
-    )
+    def gather(first):
+        return nn(hot[first * rows : (first + GROUP) * rows], neigh_s[...])
+
+    ready, message = gather(0), None
+    for first in firsts:
+        held, ready = ready, None if first + GROUP == slots else gather(first + GROUP)
+        first_half(first, held)
+        base = first // 2 * rows
+        held, message = message, nn(hid_s[base : base + group_rows], wide[0])
+        if first > 0:
+            second_half(first - GROUP, held)
+    second_half(slots - GROUP, message)
 
     agg_b = agg_s[...].astype(BF16)
     node_pre = nn(moved, w_self[...]) + nn(agg_b, w_agg[...])
@@ -288,9 +289,27 @@
                 dpre_s[at, sides[1]] = part_up
             dcen_s[block] = total
 
-    staggered(message_slope, edge_slope)
-    gmsg = tn(hid_s[...], dpre2_s[...])
-    d_neigh = nn(hot_t[...], dpre_s[...]).astype(BF16)
+    def message_gradient(first, last):
+        pairs = slice(first // 2 * rows, last // 2 * rows)
+        return tn(hid_s[pairs], dpre2_s[pairs])
+
+    def scatter(first, last):
+        at = slice(first * rows, last * rows)
+        return nn(hot_t[:, at], dpre_s[at])
+
+    middle = slots // (2 * GROUP) * GROUP
+    ready = message_slope(0)
+    for first in firsts:
+        after = first + GROUP
+        held, ready = ready, None if after == slots else message_slope(after)
+        if after == middle:
+            gmsg = message_gradient(0, middle)
+        elif after == slots:
+            gmsg = gmsg + message_gradient(middle, slots)
+        edge_slope(first, held)
+        if after == middle:
+            scattered = scatter(0, middle)
+    d_neigh = (scattered + scatter(middle, slots)).astype(BF16)
 
     d_centre = dcen_s[...].astype(BF16)
     d_neigh = jnp.concatenate([d_neigh[:, :width], d_neigh[:, width:]], axis=0)

time: 46.6 us -> 46.6 us (level)
  no operation moved by 1% of the time
where the time goes in v19:
time: 46.6 us; the launch traced here: 46.4 us
  starting transfers between devices  15.2 us (33%)
  Pallas kernels  12.5 us (27%)
  blocking collectives  11.5 us (25%)
  waiting for transfers between devices  5.57 us (12%)
  local copies, waits for them, and re-layouts  0.88 us (2%)
  between operations  0.81 us (2%)
    ppermute x6, starting transfers between devices, swap(): return lax.ppermute(array, 'slab', pairs)  12.6 us
    all_to_all x1, blocking collectives, shards(): lax.all_to_all(grads.reshape(devices, share, width), axes, split_axis=0,...  11.5 us
    pallas_call x1, Pallas kernels, shards(): call(layer_kernel, [((1, rows, width), BF16), ((border, width), BF16), ((...  7.16 us
    ppermute x6, waiting for transfers between devices, swap(): return lax.ppermute(array, 'slab', pairs)  5.57 us
    all_to_all x1, starting transfers between devices, shards(): lax.all_to_all(shared, axes, split_axis=0, concat_axis=0, tiled=True)  2.59 us
    pallas_call x1, Pallas kernels, shards(): call(prep_kernel, [((edges, hot_rows), BF16), ((half_rows, edges), BF16),...  2.5 us
  transfers between devices with their start and end apart: 7, of which 2 were waited for; matrix products, arithmetic and copies ran while one was open for 0% of the time, Pallas kernels for 7%

profile of v19, /device:TPU:0, one launch (start us, length us, event | category | flops | bytes accessed | tf_op | source)
XLA Modules:
  0.0 46.4 jit_solution(13024899595792141954)
XLA Ops:
  0.7 0.6 %copy-done.12 = s32[1,128]{1,0:T(1,128)S(1)} copy-done((s32[1,128]{1,0:T(1,128)S(1)}, s32[1,128]{1,0:T(1,128)}, u32[]{:S(2)}) %copy-start.12) | copy-done | bytes 536
  1.3 0.0 copy-done.7
  1.3 0.2 copy-done
  1.5 0.0 copy-start.9
  1.5 0.0 copy-start.10
  1.5 0.3 shard_map.149
  1.9 6.1 %collective-permute-start.2 = (bf16[32,128]{1,0:T(8,128)(2,1)S(1)}, bf16[32,128]{1,0:T(8,128)(2,1)S(1)}, u32[]{:S(2)}, u32[]{:S(2)}) collective-permute-start(bf16[32,128]{1,0:T(8,128)(2,1)S(1)} %get-tuple-element.20.my_far_off), channel_id=1, source_target_pairs={{0,14},{1,15},{2,4},{3,5},{4,2},{5,3},{6,8},{7,9},{8,6},{9,7},{10,... | collective-permute-start | bytes 24584 | tf_op jit(solution)/shard_map/ppermute | solution.py:407
  8.0 0.0 collective-permute-start.3
  8.0 0.8 %collective-permute-start = (bf16[112,128]{1,0:T(8,128)(2,1)S(1)}, bf16[112,128]{1,0:T(8,128)(2,1)S(1)}, u32[]{:S(2)}, u32[]{:S(2)}) collective-permute-start(bf16[112,128]{1,0:T(8,128)(2,1)S(1)} %get-tuple-element.22), channel_id=1, source_target_pairs={{0,15},{1,2},{2,1},{3,4},{4,3},{5,6},{6,5},{7,8},{8,7},{9,10},{10,... | collective-permute-start | bytes 86024 | tf_op jit(solution)/shard_map/ppermute | solution.py:407
  8.8 1.4 %collective-permute-start.1 = (bf16[112,128]{1,0:T(8,128)(2,1)S(1)}, bf16[112,128]{1,0:T(8,128)(2,1)S(1)}, u32[]{:S(2)}, u32[]{:S(2)}) collective-permute-start(bf16[112,128]{1,0:T(8,128)(2,1)S(1)} %get-tuple-element.23), channel_id=1, source_target_pairs={{0,1},{1,0},{2,3},{3,2},{4,5},{5,4},{6,7},{7,6},{8,9},{9,8},{10,11... | collective-permute-start | bytes 86024 | tf_op jit(solution)/shard_map/ppermute | solution.py:407
  10.1 0.0 copy-done.2
  10.1 0.0 copy-done.9
  10.1 0.0 copy-start.3
  10.1 0.0 copy-start.4
  10.2 0.0 copy-start.5
  10.2 0.0 copy-start.6
  10.2 2.5 %shard_map.150 = (bf16[8192,256]{1,0:T(8,128)(2,1)S(1)}, bf16[192,8192]{1,0:T(8,128)(2,1)S(1)}, bf16[8192,128]{1,0:T(8,128)(2,1)S(1)}, bf16[2,256,256]{2,1,0:T(8...) custom-call(s32[1,32,256]{2,1,0:T(8,128)S(1)} %bitcast.6, s32[1,32,256]{2,1,0:T(8,128)S(1)} %bitcast.7, ...), custom_call_target="tpu_custom_call" | custom-call | flops 2000000000 | bytes 1024 | tf_op jit(solution)/shard_map/pallas_call | solution.py:426
  12.7 0.0 collective-permute-done.2.got_far_off
  12.7 0.0 collective-permute-done.3.got_far_on
  12.7 1.3 %collective-permute-done.got_off = bf16[112,128]{1,0:T(8,128)(2,1)S(1)} collective-permute-done((bf16[112,128]{1,0:T(8,128)(2,1)S(1)}, bf16[112,128]{1,0:T(8,128)(2,1)S(1)}, u32[]{:S(2)}, u32[]{:S(2)}) %collective-permute-start) | collective-permute-done | bytes 28704 | tf_op jit(solution)/shard_map/ppermute | solution.py:407
  14.0 0.0 collective-permute-done.1.got_on
  14.0 7.2 %shard_map.151 = (bf16[1,256,128]{2,1,0:T(8,128)(2,1)}, bf16[64,128]{1,0:T(8,128)(2,1)S(1)}, bf16[64,128]{1,0:T(8,128)(2,1)S(1)}, bf16[768,128]{1,0:T(8,128)(2,1...) custom-call(bf16[1,256,128]{2,1,0:T(8,128)(2,1)S(1)} %copy-done, ...), custom_call_target="tpu_custom_call" | custom-call | flops 2000000000 | bytes 1024 | tf_op jit(solution)/shard_map/pallas_call | solution.py:459
  21.2 11.5 %all_to_all.10.parts = bf16[32,24,128]{2,1,0:T(8,128)(2,1)S(1)} all-to-all(bf16[32,24,128]{2,1,0:T(8,128)(2,1)S(1)} %bitcast.5), channel_id=1, replica_groups=mesh['grp'=2,'slab'=16] {'grp','slab'}, dimensions={0} | all-to-all | bytes 393216 | tf_op jit(solution)/shard_map/all_to_all | solution.py:483
  32.6 0.7 %shard_map.153 = bf16[32,24,128]{2,1,0:T(8,128)(2,1)} custom-call(bf16[32,24,128]{2,1,0:T(8,128)(2,1)S(1)} %all_to_all.10.parts), custom_call_target="tpu_custom_call" | custom-call | flops 2000000000 | bytes 1024 | tf_op jit(solution)/shard_map/pallas_call | solution.py:502
  33.4 2.6 %all-to-all-start.1 = ((bf16[32,24,128]{2,1,0:T(8,128)(2,1)}), bf16[32,24,128]{2,1,0:T(8,128)(2,1)S(1)}, u32[]{:S(2)}, u32[]{:S(2)}) async-start(bf16[32,24,128]{2,1,0:T(8,128)(2,1)} %shard_map.153), calls=%async_computation.1 | async-start | bytes 393216 | tf_op jit(solution)/shard_map/all_to_all | solution.py:503
  36.0 4.4 %collective-permute-start.4 = (bf16[64,128]{1,0:T(8,128)(2,1)S(1)}, bf16[64,128]{1,0:T(8,128)(2,1)S(1)}, u32[]{:S(2)}, u32[]{:S(2)}) collective-permute-start(bf16[64,128]{1,0:T(8,128)(2,1)S(1)} %get-tuple-element.34), channel_id=1, source_target_pairs={{0,15},{1,2},{2,1},{3,4},{4,3},{5,6},{6,5},{7,8},{8,7},{9,10},{10,... | collective-permute-start | bytes 49160 | tf_op jit(solution)/shard_map/ppermute | solution.py:407
  40.3 0.0 collective-permute-start.5
  40.3 4.3 %collective-permute-done.4.got_off = bf16[64,128]{1,0:T(8,128)(2,1)S(1)} collective-permute-done((bf16[64,128]{1,0:T(8,128)(2,1)S(1)}, bf16[64,128]{1,0:T(8,128)(2,1)S(1)}, u32[]{:S(2)}, u32[]{:S(2)}) %collective-permute-start.4) | collective-permute-done | bytes 16416 | tf_op jit(solution)/shard_map/ppermute | solution.py:407
  44.6 0.0 collective-permute-done.5.got_on
  44.6 0.9 %shard_map.152 = bf16[1,256,128]{2,1,0:T(8,128)(2,1)} custom-call(bf16[1,256,128]{2,1,0:T(8,128)(2,1)S(1)} %copy-done.1, bf16[256,128]{1,0:T(8,128)(2,1)S(1)} %get-tuple-element.31.d_node, bf16[256,128]{1,0:T(8,128)(2,1)S(1)} %get-tuple-element.32.d_centre, bf16[256,128]{1,0:T(8,128)(2,1)S(1)} %get-tuple-element.33.d_neigh, bf16[128,128]{1,0:T(8,128)(2,1)S(1)} %copy-done.6, ...), custom_call_target="tpu_custom_call" | custom-call | flops 2000000000 | bytes 1024 | tf_op jit(solution)/shard_map/pallas_call | solution.py:498
  45.5 0.0 all-to-all-done.1
  45.5 0.9 %shard_map.154 = f32[6,128,128]{2,1,0:T(8,128)} custom-call(bf16[768,128]{1,0:T(8,128)(2,1)S(1)} %bitcast.4), custom_call_target="tpu_custom_call" | custom-call | flops 2000000000 | bytes 1024 | tf_op jit(solution)/shard_map/pallas_call | solution.py:505
  (16 shorter events, 0.0 us)
Async XLA Ops:
  0.6 0.7 %copy-start.12 = (s32[1,128]{1,0:T(1,128)S(1)}, s32[1,128]{1,0:T(1,128)}, u32[]{:S(2)}) copy-start(s32[1,128]{1,0:T(1,128)} %sends.3) | copy-start | bytes 1540
  0.6 0.7 %copy-start.7 = (s32[1,256]{1,0:T(1,128)S(1)}, s32[1,256]{1,0:T(1,128)}, u32[]{:S(2)}) copy-start(s32[1,256]{1,0:T(1,128)} %arrive.3) | copy-start | bytes 3076
  0.7 0.9 %copy-start = (bf16[1,256,128]{2,1,0:T(8,128)(2,1)S(1)}, bf16[1,256,128]{2,1,0:T(8,128)(2,1)}, u32[]{:S(2)}) copy-start(bf16[1,256,128]{2,1,0:T(8,128)(2,1)} %nodes.3) | copy-start | bytes 196612
  0.7 0.8 %copy-start.11 = (s32[1,64]{1,0:T(1,128)S(1)}, s32[1,64]{1,0:T(1,128)}, u32[]{:S(2)}) copy-start(s32[1,64]{1,0:T(1,128)} %leave.1) | copy-start | bytes 772
  1.5 8.6 %copy-start.1 = (bf16[1,256,128]{2,1,0:T(8,128)(2,1)S(1)}, bf16[1,256,128]{2,1,0:T(8,128)(2,1)}, u32[]{:S(2)}) copy-start(bf16[1,256,128]{2,1,0:T(8,128)(2,1)} %cotangent.5) | copy-start | bytes 196612
  1.5 8.6 %copy-start.2 = (bf16[128,128]{1,0:T(8,128)(2,1)S(1)}, bf16[128,128]{1,0:T(8,128)(2,1)}, u32[]{:S(2)}) copy-start(bf16[128,128]{1,0:T(8,128)(2,1)} %w_out.3) | copy-start | bytes 98308
  1.5 8.6 %copy-start.8 = (s32[1,256,32]{1,2,0:T(8,128)S(1)}, s32[1,256,32]{1,2,0:T(8,128)}, u32[]{:S(2)}) copy-start(s32[1,256,32]{1,2,0:T(8,128)} %param.17) | copy-start | bytes 98308
  1.5 8.6 %copy-start.9 = (s32[1,256,32]{1,2,0:T(8,128)S(1)}, s32[1,256,32]{1,2,0:T(8,128)}, u32[]{:S(2)}) copy-start(s32[1,256,32]{1,2,0:T(8,128)} %param.18) | copy-start | bytes 98308
  1.5 8.6 %copy-start.10 = (bf16[128,128]{1,0:T(8,128)(2,1)S(1)}, bf16[128,128]{1,0:T(8,128)(2,1)}, u32[]{:S(2)}) copy-start(bf16[128,128]{1,0:T(8,128)(2,1)} %w_msg.1) | copy-start | bytes 98308
  1.9 10.8 %collective-permute-start.2 = (bf16[32,128]{1,0:T(8,128)(2,1)S(1)}, bf16[32,128]{1,0:T(8,128)(2,1)S(1)}, u32[]{:S(2)}, u32[]{:S(2)}) collective-permute-start(bf16[32,128]{1,0:T(8,128)(2,1)S(1)} %get-tuple-element.20.my_far_off), channel_id=1, source_target_pairs={{0,14},{1,15},{2,4},{3,5},{4,2},{5,3},{6,8},{7,9},{8,6},{9,7},{10,... | collective-permute-start | bytes 24584 | tf_op jit(solution)/shard_map/ppermute | solution.py:407
  8.0 4.7 %collective-permute-start.3 = (bf16[32,128]{1,0:T(8,128)(2,1)S(1)}, bf16[32,128]{1,0:T(8,128)(2,1)S(1)}, u32[]{:S(2)}, u32[]{:S(2)}) collective-permute-start(bf16[32,128]{1,0:T(8,128)(2,1)S(1)} %get-tuple-element.21.my_far_on), channel_id=1, source_target_pairs={{0,2},{1,3},{2,0},{3,1},{4,6},{5,7},{6,4},{7,5},{8,10},{9,11},{10,... | collective-permute-start | bytes 24584 | tf_op jit(solution)/shard_map/ppermute | solution.py:407
  8.0 6.0 %collective-permute-start = (bf16[112,128]{1,0:T(8,128)(2,1)S(1)}, bf16[112,128]{1,0:T(8,128)(2,1)S(1)}, u32[]{:S(2)}, u32[]{:S(2)}) collective-permute-start(bf16[112,128]{1,0:T(8,128)(2,1)S(1)} %get-tuple-element.22), channel_id=1, source_target_pairs={{0,15},{1,2},{2,1},{3,4},{4,3},{5,6},{6,5},{7,8},{8,7},{9,10},{10,... | collective-permute-start | bytes 86024 | tf_op jit(solution)/shard_map/ppermute | solution.py:407
  8.8 5.2 %collective-permute-start.1 = (bf16[112,128]{1,0:T(8,128)(2,1)S(1)}, bf16[112,128]{1,0:T(8,128)(2,1)S(1)}, u32[]{:S(2)}, u32[]{:S(2)}) collective-permute-start(bf16[112,128]{1,0:T(8,128)(2,1)S(1)} %get-tuple-element.23), channel_id=1, source_target_pairs={{0,1},{1,0},{2,3},{3,2},{4,5},{5,4},{6,7},{7,6},{8,9},{9,8},{10,11... | collective-permute-start | bytes 86024 | tf_op jit(solution)/shard_map/ppermute | solution.py:407
  10.1 3.8 %copy-start.3 = (bf16[128,128]{1,0:T(8,128)(2,1)S(1)}, bf16[128,128]{1,0:T(8,128)(2,1)}, u32[]{:S(2)}) copy-start(bf16[128,128]{1,0:T(8,128)(2,1)} %w_agg.1) | copy-start | bytes 98308
  10.1 3.8 %copy-start.4 = (bf16[128,128]{1,0:T(8,128)(2,1)S(1)}, bf16[128,128]{1,0:T(8,128)(2,1)}, u32[]{:S(2)}) copy-start(bf16[128,128]{1,0:T(8,128)(2,1)} %w_send.3) | copy-start | bytes 98308
  10.2 3.8 %copy-start.5 = (bf16[128,128]{1,0:T(8,128)(2,1)S(1)}, bf16[128,128]{1,0:T(8,128)(2,1)}, u32[]{:S(2)}) copy-start(bf16[128,128]{1,0:T(8,128)(2,1)} %w_recv.3) | copy-start | bytes 98308
  10.2 3.8 %copy-start.6 = (bf16[128,128]{1,0:T(8,128)(2,1)S(1)}, bf16[128,128]{1,0:T(8,128)(2,1)}, u32[]{:S(2)}) copy-start(bf16[128,128]{1,0:T(8,128)(2,1)} %w_self.3) | copy-start | bytes 98308
  33.4 12.2 %all-to-all-start.1 = ((bf16[32,24,128]{2,1,0:T(8,128)(2,1)}), bf16[32,24,128]{2,1,0:T(8,128)(2,1)S(1)}, u32[]{:S(2)}, u32[]{:S(2)}) async-start(bf16[32,24,128]{2,1,0:T(8,128)(2,1)} %shard_map.153), calls=%async_computation.1 | async-start | bytes 393216 | tf_op jit(solution)/shard_map/all_to_all | solution.py:503
  36.0 8.7 %collective-permute-start.4 = (bf16[64,128]{1,0:T(8,128)(2,1)S(1)}, bf16[64,128]{1,0:T(8,128)(2,1)S(1)}, u32[]{:S(2)}, u32[]{:S(2)}) collective-permute-start(bf16[64,128]{1,0:T(8,128)(2,1)S(1)} %get-tuple-element.34), channel_id=1, source_target_pairs={{0,15},{1,2},{2,1},{3,4},{4,3},{5,6},{6,5},{7,8},{8,7},{9,10},{10,... | collective-permute-start | bytes 49160 | tf_op jit(solution)/shard_map/ppermute | solution.py:407
  40.3 4.3 %collective-permute-start.5 = (bf16[64,128]{1,0:T(8,128)(2,1)S(1)}, bf16[64,128]{1,0:T(8,128)(2,1)S(1)}, u32[]{:S(2)}, u32[]{:S(2)}) collective-permute-start(bf16[64,128]{1,0:T(8,128)(2,1)S(1)} %get-tuple-element.35), channel_id=1, source_target_pairs={{0,1},{1,0},{2,3},{3,2},{4,5},{5,4},{6,7},{7,6},{8,9},{9,8},{10,11... | collective-permute-start | bytes 49160 | tf_op jit(solution)/shard_map/ppermute | solution.py:407

commit v20 on v19

--- a/solution.py
+++ b/solution.py
@@ -12,7 +12,7 @@
 CODE_ROWS = 16
 LANES = 128
 FAR = -1e30
-GROUP = 8
+GROUP = 16
 BLOCK = 64
 
 

time: 46.6 us -> 46.6 us (level)
  no operation moved by 1% of the time
where the time goes in v20:
time: 46.6 us; the launch traced here: 46.4 us
  starting transfers between devices  15.2 us (33%)
  Pallas kernels  12.4 us (27%)
  blocking collectives  11.5 us (25%)
  waiting for transfers between devices  5.57 us (12%)
  local copies, waits for them, and re-layouts  0.88 us (2%)
  between operations  0.81 us (2%)
    ppermute x6, starting transfers between devices, swap(): return lax.ppermute(array, 'slab', pairs)  12.6 us
    all_to_all x1, blocking collectives, shards(): lax.all_to_all(grads.reshape(devices, share, width), axes, split_axis=0,...  11.5 us
    pallas_call x1, Pallas kernels, shards(): call(layer_kernel, [((1, rows, width), BF16), ((border, width), BF16), ((...  7.1 us
    ppermute x6, waiting for transfers between devices, swap(): return lax.ppermute(array, 'slab', pairs)  5.57 us
    all_to_all x1, starting transfers between devices, shards(): lax.all_to_all(shared, axes, split_axis=0, concat_axis=0, tiled=True)  2.59 us
    pallas_call x1, Pallas kernels, shards(): call(prep_kernel, [((edges, hot_rows), BF16), ((half_rows, edges), BF16),...  2.5 us
  transfers between devices with their start and end apart: 7, of which 2 were waited for; matrix products, arithmetic and copies ran while one was open for 0% of the time, Pallas kernels for 7%

profile of v20, /device:TPU:0, one launch (start us, length us, event | category | flops | bytes accessed | tf_op | source)
XLA Modules:
  0.0 46.4 jit_solution(12435110275103943889)
XLA Ops:
  0.7 0.6 %copy-done.12 = s32[1,128]{1,0:T(1,128)S(1)} copy-done((s32[1,128]{1,0:T(1,128)S(1)}, s32[1,128]{1,0:T(1,128)}, u32[]{:S(2)}) %copy-start.12) | copy-done | bytes 536
  1.3 0.0 copy-done.7
  1.3 0.2 copy-done
  1.5 0.0 copy-start.9
  1.5 0.0 copy-start.10
  1.5 0.3 shard_map.149
  1.9 6.1 %collective-permute-start.2 = (bf16[32,128]{1,0:T(8,128)(2,1)S(1)}, bf16[32,128]{1,0:T(8,128)(2,1)S(1)}, u32[]{:S(2)}, u32[]{:S(2)}) collective-permute-start(bf16[32,128]{1,0:T(8,128)(2,1)S(1)} %get-tuple-element.20.my_far_off), channel_id=1, source_target_pairs={{0,14},{1,15},{2,4},{3,5},{4,2},{5,3},{6,8},{7,9},{8,6},{9,7},{10,... | collective-permute-start | bytes 24584 | tf_op jit(solution)/shard_map/ppermute | solution.py:407
  8.0 0.0 collective-permute-start.3
  8.0 0.8 %collective-permute-start = (bf16[112,128]{1,0:T(8,128)(2,1)S(1)}, bf16[112,128]{1,0:T(8,128)(2,1)S(1)}, u32[]{:S(2)}, u32[]{:S(2)}) collective-permute-start(bf16[112,128]{1,0:T(8,128)(2,1)S(1)} %get-tuple-element.22), channel_id=1, source_target_pairs={{0,15},{1,2},{2,1},{3,4},{4,3},{5,6},{6,5},{7,8},{8,7},{9,10},{10,... | collective-permute-start | bytes 86024 | tf_op jit(solution)/shard_map/ppermute | solution.py:407
  8.8 1.4 %collective-permute-start.1 = (bf16[112,128]{1,0:T(8,128)(2,1)S(1)}, bf16[112,128]{1,0:T(8,128)(2,1)S(1)}, u32[]{:S(2)}, u32[]{:S(2)}) collective-permute-start(bf16[112,128]{1,0:T(8,128)(2,1)S(1)} %get-tuple-element.23), channel_id=1, source_target_pairs={{0,1},{1,0},{2,3},{3,2},{4,5},{5,4},{6,7},{7,6},{8,9},{9,8},{10,11... | collective-permute-start | bytes 86024 | tf_op jit(solution)/shard_map/ppermute | solution.py:407
  10.1 0.0 copy-done.2
  10.1 0.0 copy-done.9
  10.1 0.0 copy-start.3
  10.1 0.0 copy-start.4
  10.2 0.0 copy-start.5
  10.2 0.0 copy-start.6
  10.2 2.5 %shard_map.150 = (bf16[8192,256]{1,0:T(8,128)(2,1)S(1)}, bf16[192,8192]{1,0:T(8,128)(2,1)S(1)}, bf16[8192,128]{1,0:T(8,128)(2,1)S(1)}, bf16[2,256,256]{2,1,0:T(8...) custom-call(s32[1,32,256]{2,1,0:T(8,128)S(1)} %bitcast.6, s32[1,32,256]{2,1,0:T(8,128)S(1)} %bitcast.7, ...), custom_call_target="tpu_custom_call" | custom-call | flops 2000000000 | bytes 1024 | tf_op jit(solution)/shard_map/pallas_call | solution.py:426
  12.7 0.0 collective-permute-done.2.got_far_off
  12.7 0.0 collective-permute-done.3.got_far_on
  12.7 1.3 %collective-permute-done.got_off = bf16[112,128]{1,0:T(8,128)(2,1)S(1)} collective-permute-done((bf16[112,128]{1,0:T(8,128)(2,1)S(1)}, bf16[112,128]{1,0:T(8,128)(2,1)S(1)}, u32[]{:S(2)}, u32[]{:S(2)}) %collective-permute-start) | collective-permute-done | bytes 28704 | tf_op jit(solution)/shard_map/ppermute | solution.py:407
  14.0 0.0 collective-permute-done.1.got_on
  14.0 7.1 %shard_map.151 = (bf16[1,256,128]{2,1,0:T(8,128)(2,1)}, bf16[64,128]{1,0:T(8,128)(2,1)S(1)}, bf16[64,128]{1,0:T(8,128)(2,1)S(1)}, bf16[768,128]{1,0:T(8,128)(2,1...) custom-call(bf16[1,256,128]{2,1,0:T(8,128)(2,1)S(1)} %copy-done, ...), custom_call_target="tpu_custom_call" | custom-call | flops 2000000000 | bytes 1024 | tf_op jit(solution)/shard_map/pallas_call | solution.py:459
  21.1 11.5 %all_to_all.10.parts = bf16[32,24,128]{2,1,0:T(8,128)(2,1)S(1)} all-to-all(bf16[32,24,128]{2,1,0:T(8,128)(2,1)S(1)} %bitcast.5), channel_id=1, replica_groups=mesh['grp'=2,'slab'=16] {'grp','slab'}, dimensions={0} | all-to-all | bytes 393216 | tf_op jit(solution)/shard_map/all_to_all | solution.py:483
  32.6 0.7 %shard_map.153 = bf16[32,24,128]{2,1,0:T(8,128)(2,1)} custom-call(bf16[32,24,128]{2,1,0:T(8,128)(2,1)S(1)} %all_to_all.10.parts), custom_call_target="tpu_custom_call" | custom-call | flops 2000000000 | bytes 1024 | tf_op jit(solution)/shard_map/pallas_call | solution.py:502
  33.3 2.6 %all-to-all-start.1 = ((bf16[32,24,128]{2,1,0:T(8,128)(2,1)}), bf16[32,24,128]{2,1,0:T(8,128)(2,1)S(1)}, u32[]{:S(2)}, u32[]{:S(2)}) async-start(bf16[32,24,128]{2,1,0:T(8,128)(2,1)} %shard_map.153), calls=%async_computation.1 | async-start | bytes 393216 | tf_op jit(solution)/shard_map/all_to_all | solution.py:503
  35.9 4.4 %collective-permute-start.4 = (bf16[64,128]{1,0:T(8,128)(2,1)S(1)}, bf16[64,128]{1,0:T(8,128)(2,1)S(1)}, u32[]{:S(2)}, u32[]{:S(2)}) collective-permute-start(bf16[64,128]{1,0:T(8,128)(2,1)S(1)} %get-tuple-element.34), channel_id=1, source_target_pairs={{0,15},{1,2},{2,1},{3,4},{4,3},{5,6},{6,5},{7,8},{8,7},{9,10},{10,... | collective-permute-start | bytes 49160 | tf_op jit(solution)/shard_map/ppermute | solution.py:407
  40.3 0.0 collective-permute-start.5
  40.3 4.3 %collective-permute-done.4.got_off = bf16[64,128]{1,0:T(8,128)(2,1)S(1)} collective-permute-done((bf16[64,128]{1,0:T(8,128)(2,1)S(1)}, bf16[64,128]{1,0:T(8,128)(2,1)S(1)}, u32[]{:S(2)}, u32[]{:S(2)}) %collective-permute-start.4) | collective-permute-done | bytes 16416 | tf_op jit(solution)/shard_map/ppermute | solution.py:407
  44.6 0.0 collective-permute-done.5.got_on
  44.6 0.9 %shard_map.152 = bf16[1,256,128]{2,1,0:T(8,128)(2,1)} custom-call(bf16[1,256,128]{2,1,0:T(8,128)(2,1)S(1)} %copy-done.1, bf16[256,128]{1,0:T(8,128)(2,1)S(1)} %get-tuple-element.31.d_node, bf16[256,128]{1,0:T(8,128)(2,1)S(1)} %get-tuple-element.32.d_centre, bf16[256,128]{1,0:T(8,128)(2,1)S(1)} %get-tuple-element.33.d_neigh, bf16[128,128]{1,0:T(8,128)(2,1)S(1)} %copy-done.6, ...), custom_call_target="tpu_custom_call" | custom-call | flops 2000000000 | bytes 1024 | tf_op jit(solution)/shard_map/pallas_call | solution.py:498
  45.4 0.0 all-to-all-done.1
  45.4 0.9 %shard_map.154 = f32[6,128,128]{2,1,0:T(8,128)} custom-call(bf16[768,128]{1,0:T(8,128)(2,1)S(1)} %bitcast.4), custom_call_target="tpu_custom_call" | custom-call | flops 2000000000 | bytes 1024 | tf_op jit(solution)/shard_map/pallas_call | solution.py:505
  (16 shorter events, 0.0 us)
Async XLA Ops:
  0.6 0.7 %copy-start.12 = (s32[1,128]{1,0:T(1,128)S(1)}, s32[1,128]{1,0:T(1,128)}, u32[]{:S(2)}) copy-start(s32[1,128]{1,0:T(1,128)} %sends.3) | copy-start | bytes 1540
  0.6 0.7 %copy-start.7 = (s32[1,256]{1,0:T(1,128)S(1)}, s32[1,256]{1,0:T(1,128)}, u32[]{:S(2)}) copy-start(s32[1,256]{1,0:T(1,128)} %arrive.3) | copy-start | bytes 3076
  0.7 0.9 %copy-start = (bf16[1,256,128]{2,1,0:T(8,128)(2,1)S(1)}, bf16[1,256,128]{2,1,0:T(8,128)(2,1)}, u32[]{:S(2)}) copy-start(bf16[1,256,128]{2,1,0:T(8,128)(2,1)} %nodes.3) | copy-start | bytes 196612
  0.7 0.8 %copy-start.11 = (s32[1,64]{1,0:T(1,128)S(1)}, s32[1,64]{1,0:T(1,128)}, u32[]{:S(2)}) copy-start(s32[1,64]{1,0:T(1,128)} %leave.1) | copy-start | bytes 772
  1.5 8.6 %copy-start.1 = (bf16[1,256,128]{2,1,0:T(8,128)(2,1)S(1)}, bf16[1,256,128]{2,1,0:T(8,128)(2,1)}, u32[]{:S(2)}) copy-start(bf16[1,256,128]{2,1,0:T(8,128)(2,1)} %cotangent.5) | copy-start | bytes 196612
  1.5 8.6 %copy-start.2 = (bf16[128,128]{1,0:T(8,128)(2,1)S(1)}, bf16[128,128]{1,0:T(8,128)(2,1)}, u32[]{:S(2)}) copy-start(bf16[128,128]{1,0:T(8,128)(2,1)} %w_out.3) | copy-start | bytes 98308
  1.5 8.6 %copy-start.8 = (s32[1,256,32]{1,2,0:T(8,128)S(1)}, s32[1,256,32]{1,2,0:T(8,128)}, u32[]{:S(2)}) copy-start(s32[1,256,32]{1,2,0:T(8,128)} %param.17) | copy-start | bytes 98308
  1.5 8.6 %copy-start.9 = (s32[1,256,32]{1,2,0:T(8,128)S(1)}, s32[1,256,32]{1,2,0:T(8,128)}, u32[]{:S(2)}) copy-start(s32[1,256,32]{1,2,0:T(8,128)} %param.18) | copy-start | bytes 98308
  1.5 8.6 %copy-start.10 = (bf16[128,128]{1,0:T(8,128)(2,1)S(1)}, bf16[128,128]{1,0:T(8,128)(2,1)}, u32[]{:S(2)}) copy-start(bf16[128,128]{1,0:T(8,128)(2,1)} %w_msg.1) | copy-start | bytes 98308
  1.9 10.8 %collective-permute-start.2 = (bf16[32,128]{1,0:T(8,128)(2,1)S(1)}, bf16[32,128]{1,0:T(8,128)(2,1)S(1)}, u32[]{:S(2)}, u32[]{:S(2)}) collective-permute-start(bf16[32,128]{1,0:T(8,128)(2,1)S(1)} %get-tuple-element.20.my_far_off), channel_id=1, source_target_pairs={{0,14},{1,15},{2,4},{3,5},{4,2},{5,3},{6,8},{7,9},{8,6},{9,7},{10,... | collective-permute-start | bytes 24584 | tf_op jit(solution)/shard_map/ppermute | solution.py:407
  8.0 4.7 %collective-permute-start.3 = (bf16[32,128]{1,0:T(8,128)(2,1)S(1)}, bf16[32,128]{1,0:T(8,128)(2,1)S(1)}, u32[]{:S(2)}, u32[]{:S(2)}) collective-permute-start(bf16[32,128]{1,0:T(8,128)(2,1)S(1)} %get-tuple-element.21.my_far_on), channel_id=1, source_target_pairs={{0,2},{1,3},{2,0},{3,1},{4,6},{5,7},{6,4},{7,5},{8,10},{9,11},{10,... | collective-permute-start | bytes 24584 | tf_op jit(solution)/shard_map/ppermute | solution.py:407
  8.0 6.0 %collective-permute-start = (bf16[112,128]{1,0:T(8,128)(2,1)S(1)}, bf16[112,128]{1,0:T(8,128)(2,1)S(1)}, u32[]{:S(2)}, u32[]{:S(2)}) collective-permute-start(bf16[112,128]{1,0:T(8,128)(2,1)S(1)} %get-tuple-element.22), channel_id=1, source_target_pairs={{0,15},{1,2},{2,1},{3,4},{4,3},{5,6},{6,5},{7,8},{8,7},{9,10},{10,... | collective-permute-start | bytes 86024 | tf_op jit(solution)/shard_map/ppermute | solution.py:407
  8.8 5.2 %collective-permute-start.1 = (bf16[112,128]{1,0:T(8,128)(2,1)S(1)}, bf16[112,128]{1,0:T(8,128)(2,1)S(1)}, u32[]{:S(2)}, u32[]{:S(2)}) collective-permute-start(bf16[112,128]{1,0:T(8,128)(2,1)S(1)} %get-tuple-element.23), channel_id=1, source_target_pairs={{0,1},{1,0},{2,3},{3,2},{4,5},{5,4},{6,7},{7,6},{8,9},{9,8},{10,11... | collective-permute-start | bytes 86024 | tf_op jit(solution)/shard_map/ppermute | solution.py:407
  10.1 3.8 %copy-start.3 = (bf16[128,128]{1,0:T(8,128)(2,1)S(1)}, bf16[128,128]{1,0:T(8,128)(2,1)}, u32[]{:S(2)}) copy-start(bf16[128,128]{1,0:T(8,128)(2,1)} %w_agg.1) | copy-start | bytes 98308
  10.1 3.8 %copy-start.4 = (bf16[128,128]{1,0:T(8,128)(2,1)S(1)}, bf16[128,128]{1,0:T(8,128)(2,1)}, u32[]{:S(2)}) copy-start(bf16[128,128]{1,0:T(8,128)(2,1)} %w_send.3) | copy-start | bytes 98308
  10.2 3.8 %copy-start.5 = (bf16[128,128]{1,0:T(8,128)(2,1)S(1)}, bf16[128,128]{1,0:T(8,128)(2,1)}, u32[]{:S(2)}) copy-start(bf16[128,128]{1,0:T(8,128)(2,1)} %w_recv.3) | copy-start | bytes 98308
  10.2 3.8 %copy-start.6 = (bf16[128,128]{1,0:T(8,128)(2,1)S(1)}, bf16[128,128]{1,0:T(8,128)(2,1)}, u32[]{:S(2)}) copy-start(bf16[128,128]{1,0:T(8,128)(2,1)} %w_self.3) | copy-start | bytes 98308
  33.3 12.2 %all-to-all-start.1 = ((bf16[32,24,128]{2,1,0:T(8,128)(2,1)}), bf16[32,24,128]{2,1,0:T(8,128)(2,1)S(1)}, u32[]{:S(2)}, u32[]{:S(2)}) async-start(bf16[32,24,128]{2,1,0:T(8,128)(2,1)} %shard_map.153), calls=%async_computation.1 | async-start | bytes 393216 | tf_op jit(solution)/shard_map/all_to_all | solution.py:503
  35.9 8.7 %collective-permute-start.4 = (bf16[64,128]{1,0:T(8,128)(2,1)S(1)}, bf16[64,128]{1,0:T(8,128)(2,1)S(1)}, u32[]{:S(2)}, u32[]{:S(2)}) collective-permute-start(bf16[64,128]{1,0:T(8,128)(2,1)S(1)} %get-tuple-element.34), channel_id=1, source_target_pairs={{0,15},{1,2},{2,1},{3,4},{4,3},{5,6},{6,5},{7,8},{8,7},{9,10},{10,... | collective-permute-start | bytes 49160 | tf_op jit(solution)/shard_map/ppermute | solution.py:407
  40.3 4.3 %collective-permute-start.5 = (bf16[64,128]{1,0:T(8,128)(2,1)S(1)}, bf16[64,128]{1,0:T(8,128)(2,1)S(1)}, u32[]{:S(2)}, u32[]{:S(2)}) collective-permute-start(bf16[64,128]{1,0:T(8,128)(2,1)S(1)} %get-tuple-element.35), channel_id=1, source_target_pairs={{0,1},{1,0},{2,3},{3,2},{4,5},{5,4},{6,7},{7,6},{8,9},{9,8},{10,11... | collective-permute-start | bytes 49160 | tf_op jit(solution)/shard_map/ppermute | solution.py:407

commit v21 on v18

--- a/solution.py
+++ b/solution.py
@@ -13,7 +13,7 @@
 LANES = 128
 FAR = -1e30
 GROUP = 16
-BLOCK = 64
+BLOCK = 128
 
 
 def nn(left, right):
@@ -343,7 +343,7 @@
         part = total[m * width : (m + 1) * width].astype(F32)
         mean = jnp.sum(jnp.sum(part * part, axis=0, keepdims=True), axis=1, keepdims=True)
         mean = mean / (part.shape[0] * part.shape[1])
-        steps[m] = part / jnp.sqrt(mean + 1e-06)
+        steps[m] = part * (1.0 / jnp.sqrt(mean + 1e-06))
 
 
 def call(kernel, outs, scratch=()):

time: 46.6 us -> 46.6 us (level)
  no operation moved by 1% of the time
where the time goes in v21:
time: 46.6 us; the launch traced here: 46.3 us
  starting transfers between devices  15.2 us (33%)
  Pallas kernels  12.4 us (27%)
  blocking collectives  11.5 us (25%)
  waiting for transfers between devices  5.57 us (12%)
  local copies, waits for them, and re-layouts  0.88 us (2%)
  between operations  0.81 us (2%)
    ppermute x6, starting transfers between devices, swap(): return lax.ppermute(array, 'slab', pairs)  12.6 us
    all_to_all x1, blocking collectives, shards(): lax.all_to_all(grads.reshape(devices, share, width), axes, split_axis=0,...  11.5 us
    pallas_call x1, Pallas kernels, shards(): call(layer_kernel, [((1, rows, width), BF16), ((border, width), BF16), ((...  7.1 us
    ppermute x6, waiting for transfers between devices, swap(): return lax.ppermute(array, 'slab', pairs)  5.57 us
    all_to_all x1, starting transfers between devices, shards(): lax.all_to_all(shared, axes, split_axis=0, concat_axis=0, tiled=True)  2.59 us
    pallas_call x1, Pallas kernels, shards(): call(prep_kernel, [((edges, hot_rows), BF16), ((half_rows, edges), BF16),...  2.5 us
  transfers between devices with their start and end apart: 7, of which 2 were waited for; matrix products, arithmetic and copies ran while one was open for 0% of the time, Pallas kernels for 7%

profile of v21, /device:TPU:0, one launch (start us, length us, event | category | flops | bytes accessed | tf_op | source)
XLA Modules:
  0.0 46.3 jit_solution(2741917779867737421)
XLA Ops:
  0.7 0.6 %copy-done.12 = s32[1,128]{1,0:T(1,128)S(1)} copy-done((s32[1,128]{1,0:T(1,128)S(1)}, s32[1,128]{1,0:T(1,128)}, u32[]{:S(2)}) %copy-start.12) | copy-done | bytes 536
  1.3 0.0 copy-done.7
  1.3 0.2 copy-done
  1.5 0.0 copy-start.9
  1.5 0.0 copy-start.10
  1.5 0.3 shard_map.149
  1.9 6.1 %collective-permute-start.2 = (bf16[32,128]{1,0:T(8,128)(2,1)S(1)}, bf16[32,128]{1,0:T(8,128)(2,1)S(1)}, u32[]{:S(2)}, u32[]{:S(2)}) collective-permute-start(bf16[32,128]{1,0:T(8,128)(2,1)S(1)} %get-tuple-element.20.my_far_off), channel_id=1, source_target_pairs={{0,14},{1,15},{2,4},{3,5},{4,2},{5,3},{6,8},{7,9},{8,6},{9,7},{10,... | collective-permute-start | bytes 24584 | tf_op jit(solution)/shard_map/ppermute | solution.py:388
  8.0 0.0 collective-permute-start.3
  8.0 0.8 %collective-permute-start = (bf16[112,128]{1,0:T(8,128)(2,1)S(1)}, bf16[112,128]{1,0:T(8,128)(2,1)S(1)}, u32[]{:S(2)}, u32[]{:S(2)}) collective-permute-start(bf16[112,128]{1,0:T(8,128)(2,1)S(1)} %get-tuple-element.22), channel_id=1, source_target_pairs={{0,15},{1,2},{2,1},{3,4},{4,3},{5,6},{6,5},{7,8},{8,7},{9,10},{10,... | collective-permute-start | bytes 86024 | tf_op jit(solution)/shard_map/ppermute | solution.py:388
  8.8 1.4 %collective-permute-start.1 = (bf16[112,128]{1,0:T(8,128)(2,1)S(1)}, bf16[112,128]{1,0:T(8,128)(2,1)S(1)}, u32[]{:S(2)}, u32[]{:S(2)}) collective-permute-start(bf16[112,128]{1,0:T(8,128)(2,1)S(1)} %get-tuple-element.23), channel_id=1, source_target_pairs={{0,1},{1,0},{2,3},{3,2},{4,5},{5,4},{6,7},{7,6},{8,9},{9,8},{10,11... | collective-permute-start | bytes 86024 | tf_op jit(solution)/shard_map/ppermute | solution.py:388
  10.1 0.0 copy-done.1
  10.1 0.0 copy-done.10
  10.1 0.0 copy-start.3
  10.1 0.0 copy-start.4
  10.2 0.0 copy-start.5
  10.2 0.0 copy-start.6
  10.2 2.5 %shard_map.150 = (bf16[8192,256]{1,0:T(8,128)(2,1)S(1)}, bf16[192,8192]{1,0:T(8,128)(2,1)S(1)}, bf16[8192,128]{1,0:T(8,128)(2,1)S(1)}, bf16[2,256,256]{2,1,0:T(8...) custom-call(s32[1,32,256]{2,1,0:T(8,128)S(1)} %bitcast.6, s32[1,32,256]{2,1,0:T(8,128)S(1)} %bitcast.7, ...), custom_call_target="tpu_custom_call" | custom-call | flops 2000000000 | bytes 1024 | tf_op jit(solution)/shard_map/pallas_call | solution.py:407
  12.7 0.0 collective-permute-done.2.got_far_off
  12.7 0.0 collective-permute-done.3.got_far_on
  12.7 1.3 %collective-permute-done.got_off = bf16[112,128]{1,0:T(8,128)(2,1)S(1)} collective-permute-done((bf16[112,128]{1,0:T(8,128)(2,1)S(1)}, bf16[112,128]{1,0:T(8,128)(2,1)S(1)}, u32[]{:S(2)}, u32[]{:S(2)}) %collective-permute-start) | collective-permute-done | bytes 28704 | tf_op jit(solution)/shard_map/ppermute | solution.py:388
  14.0 0.0 collective-permute-done.1.got_on
  14.0 7.1 %shard_map.151 = (bf16[1,256,128]{2,1,0:T(8,128)(2,1)}, bf16[64,128]{1,0:T(8,128)(2,1)S(1)}, bf16[64,128]{1,0:T(8,128)(2,1)S(1)}, bf16[768,128]{1,0:T(8,128)(2,1...) custom-call(bf16[1,256,128]{2,1,0:T(8,128)(2,1)S(1)} %copy-done, ...), custom_call_target="tpu_custom_call" | custom-call | flops 2000000000 | bytes 1024 | tf_op jit(solution)/shard_map/pallas_call | solution.py:440
  21.1 11.5 %all_to_all.10.parts = bf16[32,24,128]{2,1,0:T(8,128)(2,1)S(1)} all-to-all(bf16[32,24,128]{2,1,0:T(8,128)(2,1)S(1)} %bitcast.5), channel_id=1, replica_groups=mesh['grp'=2,'slab'=16] {'grp','slab'}, dimensions={0} | all-to-all | bytes 393216 | tf_op jit(solution)/shard_map/all_to_all | solution.py:464
  32.6 0.7 %shard_map.153 = bf16[32,24,128]{2,1,0:T(8,128)(2,1)} custom-call(bf16[32,24,128]{2,1,0:T(8,128)(2,1)S(1)} %all_to_all.10.parts), custom_call_target="tpu_custom_call" | custom-call | flops 2000000000 | bytes 1024 | tf_op jit(solution)/shard_map/pallas_call | solution.py:483
  33.3 2.6 %all-to-all-start.1 = ((bf16[32,24,128]{2,1,0:T(8,128)(2,1)}), bf16[32,24,128]{2,1,0:T(8,128)(2,1)S(1)}, u32[]{:S(2)}, u32[]{:S(2)}) async-start(bf16[32,24,128]{2,1,0:T(8,128)(2,1)} %shard_map.153), calls=%async_computation.1 | async-start | bytes 393216 | tf_op jit(solution)/shard_map/all_to_all | solution.py:484
  35.9 4.4 %collective-permute-start.4 = (bf16[64,128]{1,0:T(8,128)(2,1)S(1)}, bf16[64,128]{1,0:T(8,128)(2,1)S(1)}, u32[]{:S(2)}, u32[]{:S(2)}) collective-permute-start(bf16[64,128]{1,0:T(8,128)(2,1)S(1)} %get-tuple-element.34), channel_id=1, source_target_pairs={{0,15},{1,2},{2,1},{3,4},{4,3},{5,6},{6,5},{7,8},{8,7},{9,10},{10,... | collective-permute-start | bytes 49160 | tf_op jit(solution)/shard_map/ppermute | solution.py:388
  40.3 0.0 collective-permute-start.5
  40.3 4.3 %collective-permute-done.4.got_off = bf16[64,128]{1,0:T(8,128)(2,1)S(1)} collective-permute-done((bf16[64,128]{1,0:T(8,128)(2,1)S(1)}, bf16[64,128]{1,0:T(8,128)(2,1)S(1)}, u32[]{:S(2)}, u32[]{:S(2)}) %collective-permute-start.4) | collective-permute-done | bytes 16416 | tf_op jit(solution)/shard_map/ppermute | solution.py:388
  44.6 0.0 collective-permute-done.5.got_on
  44.6 0.9 %shard_map.152 = bf16[1,256,128]{2,1,0:T(8,128)(2,1)} custom-call(bf16[1,256,128]{2,1,0:T(8,128)(2,1)S(1)} %copy-done.1, bf16[256,128]{1,0:T(8,128)(2,1)S(1)} %get-tuple-element.31.d_node, bf16[256,128]{1,0:T(8,128)(2,1)S(1)} %get-tuple-element.32.d_centre, bf16[256,128]{1,0:T(8,128)(2,1)S(1)} %get-tuple-element.33.d_neigh, bf16[128,128]{1,0:T(8,128)(2,1)S(1)} %copy-done.6, ...), custom_call_target="tpu_custom_call" | custom-call | flops 2000000000 | bytes 1024 | tf_op jit(solution)/shard_map/pallas_call | solution.py:479
  45.4 0.0 all-to-all-done.1
  45.4 0.9 %shard_map.154 = f32[6,128,128]{2,1,0:T(8,128)} custom-call(bf16[768,128]{1,0:T(8,128)(2,1)S(1)} %bitcast.4), custom_call_target="tpu_custom_call" | custom-call | flops 2000000000 | bytes 1024 | tf_op jit(solution)/shard_map/pallas_call | solution.py:486
  (16 shorter events, 0.0 us)
Async XLA Ops:
  0.6 0.7 %copy-start.12 = (s32[1,128]{1,0:T(1,128)S(1)}, s32[1,128]{1,0:T(1,128)}, u32[]{:S(2)}) copy-start(s32[1,128]{1,0:T(1,128)} %sends.3) | copy-start | bytes 1540
  0.6 0.7 %copy-start.7 = (s32[1,256]{1,0:T(1,128)S(1)}, s32[1,256]{1,0:T(1,128)}, u32[]{:S(2)}) copy-start(s32[1,256]{1,0:T(1,128)} %arrive.3) | copy-start | bytes 3076
  0.7 0.9 %copy-start = (bf16[1,256,128]{2,1,0:T(8,128)(2,1)S(1)}, bf16[1,256,128]{2,1,0:T(8,128)(2,1)}, u32[]{:S(2)}) copy-start(bf16[1,256,128]{2,1,0:T(8,128)(2,1)} %nodes.3) | copy-start | bytes 196612
  0.7 0.8 %copy-start.11 = (s32[1,64]{1,0:T(1,128)S(1)}, s32[1,64]{1,0:T(1,128)}, u32[]{:S(2)}) copy-start(s32[1,64]{1,0:T(1,128)} %leave.1) | copy-start | bytes 772
  1.5 8.6 %copy-start.1 = (bf16[1,256,128]{2,1,0:T(8,128)(2,1)S(1)}, bf16[1,256,128]{2,1,0:T(8,128)(2,1)}, u32[]{:S(2)}) copy-start(bf16[1,256,128]{2,1,0:T(8,128)(2,1)} %cotangent.5) | copy-start | bytes 196612
  1.5 8.6 %copy-start.2 = (bf16[128,128]{1,0:T(8,128)(2,1)S(1)}, bf16[128,128]{1,0:T(8,128)(2,1)}, u32[]{:S(2)}) copy-start(bf16[128,128]{1,0:T(8,128)(2,1)} %w_out.3) | copy-start | bytes 98308
  1.5 8.6 %copy-start.8 = (s32[1,256,32]{1,2,0:T(8,128)S(1)}, s32[1,256,32]{1,2,0:T(8,128)}, u32[]{:S(2)}) copy-start(s32[1,256,32]{1,2,0:T(8,128)} %param.17) | copy-start | bytes 98308
  1.5 8.6 %copy-start.9 = (s32[1,256,32]{1,2,0:T(8,128)S(1)}, s32[1,256,32]{1,2,0:T(8,128)}, u32[]{:S(2)}) copy-start(s32[1,256,32]{1,2,0:T(8,128)} %param.18) | copy-start | bytes 98308
  1.5 8.6 %copy-start.10 = (bf16[128,128]{1,0:T(8,128)(2,1)S(1)}, bf16[128,128]{1,0:T(8,128)(2,1)}, u32[]{:S(2)}) copy-start(bf16[128,128]{1,0:T(8,128)(2,1)} %w_msg.1) | copy-start | bytes 98308
  1.9 10.8 %collective-permute-start.2 = (bf16[32,128]{1,0:T(8,128)(2,1)S(1)}, bf16[32,128]{1,0:T(8,128)(2,1)S(1)}, u32[]{:S(2)}, u32[]{:S(2)}) collective-permute-start(bf16[32,128]{1,0:T(8,128)(2,1)S(1)} %get-tuple-element.20.my_far_off), channel_id=1, source_target_pairs={{0,14},{1,15},{2,4},{3,5},{4,2},{5,3},{6,8},{7,9},{8,6},{9,7},{10,... | collective-permute-start | bytes 24584 | tf_op jit(solution)/shard_map/ppermute | solution.py:388
  8.0 4.7 %collective-permute-start.3 = (bf16[32,128]{1,0:T(8,128)(2,1)S(1)}, bf16[32,128]{1,0:T(8,128)(2,1)S(1)}, u32[]{:S(2)}, u32[]{:S(2)}) collective-permute-start(bf16[32,128]{1,0:T(8,128)(2,1)S(1)} %get-tuple-element.21.my_far_on), channel_id=1, source_target_pairs={{0,2},{1,3},{2,0},{3,1},{4,6},{5,7},{6,4},{7,5},{8,10},{9,11},{10,... | collective-permute-start | bytes 24584 | tf_op jit(solution)/shard_map/ppermute | solution.py:388
  8.0 6.0 %collective-permute-start = (bf16[112,128]{1,0:T(8,128)(2,1)S(1)}, bf16[112,128]{1,0:T(8,128)(2,1)S(1)}, u32[]{:S(2)}, u32[]{:S(2)}) collective-permute-start(bf16[112,128]{1,0:T(8,128)(2,1)S(1)} %get-tuple-element.22), channel_id=1, source_target_pairs={{0,15},{1,2},{2,1},{3,4},{4,3},{5,6},{6,5},{7,8},{8,7},{9,10},{10,... | collective-permute-start | bytes 86024 | tf_op jit(solution)/shard_map/ppermute | solution.py:388
  8.8 5.2 %collective-permute-start.1 = (bf16[112,128]{1,0:T(8,128)(2,1)S(1)}, bf16[112,128]{1,0:T(8,128)(2,1)S(1)}, u32[]{:S(2)}, u32[]{:S(2)}) collective-permute-start(bf16[112,128]{1,0:T(8,128)(2,1)S(1)} %get-tuple-element.23), channel_id=1, source_target_pairs={{0,1},{1,0},{2,3},{3,2},{4,5},{5,4},{6,7},{7,6},{8,9},{9,8},{10,11... | collective-permute-start | bytes 86024 | tf_op jit(solution)/shard_map/ppermute | solution.py:388
  10.1 3.8 %copy-start.3 = (bf16[128,128]{1,0:T(8,128)(2,1)S(1)}, bf16[128,128]{1,0:T(8,128)(2,1)}, u32[]{:S(2)}) copy-start(bf16[128,128]{1,0:T(8,128)(2,1)} %w_agg.1) | copy-start | bytes 98308
  10.1 3.8 %copy-start.4 = (bf16[128,128]{1,0:T(8,128)(2,1)S(1)}, bf16[128,128]{1,0:T(8,128)(2,1)}, u32[]{:S(2)}) copy-start(bf16[128,128]{1,0:T(8,128)(2,1)} %w_send.3) | copy-start | bytes 98308
  10.2 3.8 %copy-start.5 = (bf16[128,128]{1,0:T(8,128)(2,1)S(1)}, bf16[128,128]{1,0:T(8,128)(2,1)}, u32[]{:S(2)}) copy-start(bf16[128,128]{1,0:T(8,128)(2,1)} %w_recv.3) | copy-start | bytes 98308
  10.2 3.8 %copy-start.6 = (bf16[128,128]{1,0:T(8,128)(2,1)S(1)}, bf16[128,128]{1,0:T(8,128)(2,1)}, u32[]{:S(2)}) copy-start(bf16[128,128]{1,0:T(8,128)(2,1)} %w_self.3) | copy-start | bytes 98308
  33.3 12.2 %all-to-all-start.1 = ((bf16[32,24,128]{2,1,0:T(8,128)(2,1)}), bf16[32,24,128]{2,1,0:T(8,128)(2,1)S(1)}, u32[]{:S(2)}, u32[]{:S(2)}) async-start(bf16[32,24,128]{2,1,0:T(8,128)(2,1)} %shard_map.153), calls=%async_computation.1 | async-start | bytes 393216 | tf_op jit(solution)/shard_map/all_to_all | solution.py:484
  35.9 8.7 %collective-permute-start.4 = (bf16[64,128]{1,0:T(8,128)(2,1)S(1)}, bf16[64,128]{1,0:T(8,128)(2,1)S(1)}, u32[]{:S(2)}, u32[]{:S(2)}) collective-permute-start(bf16[64,128]{1,0:T(8,128)(2,1)S(1)} %get-tuple-element.34), channel_id=1, source_target_pairs={{0,15},{1,2},{2,1},{3,4},{4,3},{5,6},{6,5},{7,8},{8,7},{9,10},{10,... | collective-permute-start | bytes 49160 | tf_op jit(solution)/shard_map/ppermute | solution.py:388
  40.3 4.3 %collective-permute-start.5 = (bf16[64,128]{1,0:T(8,128)(2,1)S(1)}, bf16[64,128]{1,0:T(8,128)(2,1)S(1)}, u32[]{:S(2)}, u32[]{:S(2)}) collective-permute-start(bf16[64,128]{1,0:T(8,128)(2,1)S(1)} %get-tuple-element.35), channel_id=1, source_target_pairs={{0,1},{1,0},{2,3},{3,2},{4,5},{5,4},{6,7},{7,6},{8,9},{9,8},{10,11... | collective-permute-start | bytes 49160 | tf_op jit(solution)/shard_map/ppermute | solution.py:388
